TPU v7x, 32 devices: a whole 2x2x4 slice. The times are simulated.
32 devices in a mesh: seq: 8 (over z, x), grp: 4 (over y, core).
Axes of the slice: x: 2, y: 2, z: 4, core: 2. Of those that a mesh axis runs over, the one named last changes fastest.
Arguments:
- tokens: bfloat16 [8, 8, 256, 768], P('grp', 'seq'), may hold values from -6 to 6
- cotangent: bfloat16 [8, 8, 256, 768], P('grp', 'seq'), may hold values from -6 to 6
- col_count: int32 [8], P('grp'), may hold values from 64 to 256, as said below
- row_count: int32 [8], P('grp'), may hold values from 2 to 8, as said below
- attn_weight: float32 [8, 768, 768], P(None, 'seq'), as said below
- in_weight: float32 [768, 3072], P('seq'), as said below
- out_weight: float32 [3072, 768], P(None, 'seq'), may hold values from -0.109375 to 0.109375
- norm_param: float32 [6, 768], P(None, 'seq'), as said below
- attn_first: float32 [8, 768, 768], P(None, 'seq'), may hold values from -0.0048828125 to 0.0048828125
- attn_second: float32 [8, 768, 768], P(None, 'seq'), may hold values from 1.05963814e-07 to 4.2385525e-07
- in_first: float32 [768, 3072], P('seq'), may hold values from -0.0048828125 to 0.0048828125
- in_second: float32 [768, 3072], P('seq'), may hold values from 1.05963814e-07 to 4.2385525e-07
- out_first: float32 [3072, 768], P(None, 'seq'), may hold values from -0.0048828125 to 0.0048828125
- out_second: float32 [3072, 768], P(None, 'seq'), may hold values from 1.05963814e-07 to 4.2385525e-07
- norm_first: float32 [6, 768], P(None, 'seq'), may hold values from -0.01953125 to 0.01953125
- norm_second: float32 [6, 768], P(None, 'seq'), may hold values from 1.695421e-06 to 6.781684e-06
Outputs:
- block_out: bfloat16 [8, 8, 256, 768], P('grp', 'seq')
- grad_tokens: float32 [8, 8, 256, 768], P('grp', 'seq')
- grad_norm: float32 [], replicated
- attn_first_new: float32 [8, 768, 768], P(None, 'seq')
- attn_second_new: float32 [8, 768, 768], P(None, 'seq')
- attn_weight_new: float32 [8, 768, 768], P(None, 'seq')
- attn_copy: bfloat16 [8, 768, 768], P(None, 'seq')
- in_first_new: float32 [768, 3072], P('seq')
- in_second_new: float32 [768, 3072], P('seq')
- in_weight_new: float32 [768, 3072], P('seq')
- in_copy: bfloat16 [768, 3072], P('seq')
- out_first_new: float32 [3072, 768], P(None, 'seq')
- out_second_new: float32 [3072, 768], P(None, 'seq')
- out_weight_new: float32 [3072, 768], P(None, 'seq')
- out_copy: bfloat16 [3072, 768], P(None, 'seq')
- norm_first_new: float32 [6, 768], P(None, 'seq')
- norm_second_new: float32 [6, 768], P(None, 'seq')
- norm_new: float32 [6, 768], P(None, 'seq')
Inputs may be any that keep to these rules, and one draw needn't show every extreme that they name: `col_count`: in each group of 2 consecutive proteins one, drawn from the seed, has 256 live columns and 8 live rows. `row_count`: the protein with 256 live columns in each group also has 8 live rows. `attn_weight`: entries scaled per matrix, of order 768 ** -0.5 in the query, key and value matrices. `in_weight`: entries of order 768 ** -0.5. `norm_param`: gains near one, shifts of both signs.
All inputs are finite; a program needn't handle non-finite values.
Results may differ from a plain program's by a relative error of at most 0.019.
Values may be sent and summed in bfloat16 or wider, within the bound.
No kernel may reach another device: no remote copies, remote signals or barrier semaphores. Data moves between devices by JAX's collectives and lax.ppermute only.
A program may use at most 256 MiB of HBM per device.

v0:
```python
from functools import partial
import math

import jax
import jax.numpy as jnp
from jax import lax
from jax.sharding import PartitionSpec as P

H = 12
DH = 64
STEP = 5


eps_norm = 1e-05
masked_score = -1000000000.0
clip_bound = 1.0
beta_one = 0.5
beta_two = 0.5
matrix_rate = 0.06
norm_rate = 0.3
decay_rate = 0.01
adam_eps = 1e-08


def in_blocks(x, dim, length):
    lengths = x.shape
    pieces = x.reshape(*lengths[:dim], length, lengths[dim] // length, *lengths[dim + 1 :])
    return jnp.moveaxis(pieces, dim, 0)


def sent_and_summed(x, axis, dim):
    length = lax.axis_size(axis)
    pieces = lax.all_to_all(in_blocks(x, dim, length), axis, 0, 0, tiled=True)
    return jnp.sum(pieces.astype(jnp.float32), axis=0)


def layer_norm(value, gain, shift):
    mean = jnp.mean(value, axis=-1, keepdims=True)
    centred = value - mean
    spread = jnp.mean(centred * centred, axis=-1, keepdims=True)
    return centred * lax.rsqrt(spread + eps_norm) * gain + shift


def softmax_rows(scores, keep):
    scores = jnp.where(keep, scores, masked_score)
    top = jnp.max(scores, axis=-1, keepdims=True)
    expo = jnp.exp(scores - top)
    return expo / jnp.sum(expo, axis=-1, keepdims=True)


def softmax_back(probs, grads):
    return probs * (grads - jnp.sum(probs * grads, axis=-1, keepdims=True))


def adam_update(weight, first, second, grad, rate):
    first_new = beta_one * first + (1.0 - beta_one) * grad
    second_new = beta_two * second + (1.0 - beta_two) * grad * grad
    first_hat = first_new / (1.0 - beta_one**STEP)
    second_hat = second_new / (1.0 - beta_two**STEP)
    weight_new = weight - rate * (
        first_hat / (jnp.sqrt(second_hat) + adam_eps) + decay_rate * weight
    )
    return (first_new, second_new, weight_new)


def attn_pair(normed, grad_proj, mixed, grad_branch):
    width = normed.shape[-1]
    qkv_terms = jnp.einsum("prcd,kprce->dke", normed, grad_proj, preferred_element_type=jnp.float32)
    output_terms = jnp.einsum(
        "prcd,prce->de", mixed, grad_branch, preferred_element_type=jnp.float32
    )
    return jnp.concatenate([qkv_terms, output_terms[:, None, :]], axis=1).reshape(width, 4 * width)


def body(
    tokens,
    cotangent,
    col_count,
    row_count,
    attn_weight,
    in_weight,
    out_weight,
    norm_param,
    attn_first,
    attn_second,
    in_first,
    in_second,
    out_first,
    out_second,
    norm_first,
    norm_second,
):
    f32 = jnp.float32
    bf16 = jnp.bfloat16
    prot, rows_dev, cols, width = tokens.shape
    hidden = in_weight.shape[1]
    head_scale = 1.0 / math.sqrt(DH)
    attn_full, in_full, out_full, norm_full = (
        lax.all_gather(attn_weight.astype(bf16), "seq", axis=1, tiled=True),
        lax.all_gather(in_weight.astype(bf16), "seq", axis=0, tiled=True),
        lax.all_gather(out_weight.astype(bf16), "seq", axis=1, tiled=True),
        lax.all_gather(norm_param.astype(bf16), "seq", axis=1, tiled=True),
    )
    norm_gain = norm_full.astype(f32)
    row_ids = lax.axis_index("seq") * rows_dev + jnp.arange(rows_dev, dtype=jnp.int32)
    row_live = (row_ids[None, :] < row_count[:, None]).astype(f32)
    col_live = jnp.arange(cols, dtype=jnp.int32)[None, :] < col_count[:, None]
    tie_scale = lax.rsqrt(row_count.astype(f32)) * head_scale
    live = row_live[:, :, None] * col_live.astype(f32)[:, None, :]
    grad_out = (cotangent.astype(f32) * live[..., None]).astype(bf16)
    resid_one = tokens.astype(f32)
    normed_one = layer_norm(resid_one, norm_gain[0], norm_gain[1]).astype(bf16)
    proj_one = jnp.einsum(
        "prcd,kde->kprce", normed_one, attn_full[0:3], preferred_element_type=f32
    ).astype(bf16)
    proj_one = proj_one.reshape(3, prot, rows_dev, cols, H, DH)
    query_one, key_one, value_one = (proj_one[0], proj_one[1], proj_one[2])
    masked_query = query_one * row_live[:, :, None, None, None].astype(bf16)
    partial_scores = (
        jnp.einsum("prihe,prjhe->phij", masked_query, key_one, preferred_element_type=f32)
        * tie_scale[:, None, None, None]
    )
    keep_cols = col_live[:, None, None, :]
    score_part = lax.psum_scatter(partial_scores, "seq", scatter_dimension=2, tiled=True)
    probs_one = softmax_rows(score_part, keep_cols)
    probs_low = lax.all_gather(probs_one.astype(bf16), "seq", axis=2, tiled=True)
    mixed_one = jnp.einsum(
        "phij,prjhe->prihe", probs_low, value_one, preferred_element_type=f32
    ).astype(bf16)
    mixed_one = mixed_one.reshape(prot, rows_dev, cols, width)
    branch_one = jnp.einsum("prcd,de->prce", mixed_one, attn_full[3], preferred_element_type=f32)
    stream_one = (resid_one + branch_one).astype(bf16)
    stream_cols, up_grad = (
        lax.all_to_all(stream_one, "seq", split_axis=2, concat_axis=1, tiled=True),
        lax.all_to_all(grad_out, "seq", split_axis=2, concat_axis=1, tiled=True),
    )
    rows = stream_cols.shape[1]
    cols_dev = stream_cols.shape[2]
    row_live_all = jnp.arange(rows, dtype=jnp.int32)[None, :] < row_count[:, None]
    resid_two = stream_cols.astype(f32)
    normed_two = layer_norm(resid_two, norm_gain[2], norm_gain[3]).astype(bf16)
    proj_two = jnp.einsum(
        "prcd,kde->kprce", normed_two, attn_full[4:7], preferred_element_type=f32
    ).astype(bf16)
    proj_two = proj_two.reshape(3, prot, rows, cols_dev, H, DH)
    query_two, key_two, value_two = (proj_two[0], proj_two[1], proj_two[2])
    scores_two = (
        jnp.einsum("prche,psche->pchrs", query_two, key_two, preferred_element_type=f32)
        * head_scale
    )
    probs_two = softmax_rows(scores_two, row_live_all[:, None, None, None, :])
    probs_two_low = probs_two.astype(bf16)
    mixed_two = jnp.einsum(
        "pchrs,psche->prche", probs_two_low, value_two, preferred_element_type=f32
    ).astype(bf16)
    mixed_two = mixed_two.reshape(prot, rows, cols_dev, width)
    resid_three = resid_two + jnp.einsum(
        "prcd,de->prce", mixed_two, attn_full[7], preferred_element_type=f32
    )
    normed_three = layer_norm(resid_three, norm_gain[4], norm_gain[5]).astype(bf16)
    inner = jnp.einsum("prcd,df->prcf", normed_three, in_full, preferred_element_type=f32)
    activ = jax.nn.gelu(inner, approximate=True).astype(bf16)
    result = (
        resid_three + jnp.einsum("prcf,fd->prcd", activ, out_full, preferred_element_type=f32)
    ).astype(bf16)
    block_out = lax.all_to_all(result, "seq", split_axis=1, concat_axis=2, tiled=True)
    grad_act = jnp.einsum("prcd,fd->prcf", up_grad, out_full, preferred_element_type=f32)
    _, gelu_back = jax.vjp(partial(jax.nn.gelu, approximate=True), inner)
    grad_inner = gelu_back(grad_act)[0].astype(bf16)
    grad_normed_three = jnp.einsum("prcf,df->prcd", grad_inner, in_full, preferred_element_type=f32)
    _, norm_back_three = jax.vjp(layer_norm, resid_three, norm_gain[4], norm_gain[5])
    part_three, gain_grad_three, shift_grad_three = norm_back_three(grad_normed_three)
    grad_three = up_grad.astype(f32) + part_three
    grad_branch_two = grad_three.astype(bf16)
    grad_mixed_two = jnp.einsum(
        "prce,de->prcd", grad_branch_two, attn_full[7], preferred_element_type=f32
    ).astype(bf16)
    grad_mixed_two = grad_mixed_two.reshape(prot, rows, cols_dev, H, DH)
    grad_probs_two = jnp.einsum(
        "prche,psche->pchrs", grad_mixed_two, value_two, preferred_element_type=f32
    )
    grad_value_two = jnp.einsum(
        "pchrs,prche->psche", probs_two_low, grad_mixed_two, preferred_element_type=f32
    )
    grad_scores_two = softmax_back(probs_two, grad_probs_two).astype(bf16)
    grad_query_two = (
        jnp.einsum("pchrs,psche->prche", grad_scores_two, key_two, preferred_element_type=f32)
        * head_scale
    )
    grad_key_two = (
        jnp.einsum("pchrs,prche->psche", grad_scores_two, query_two, preferred_element_type=f32)
        * head_scale
    )
    grad_proj_two = jnp.stack([grad_query_two, grad_key_two, grad_value_two]).astype(bf16)
    grad_proj_two = grad_proj_two.reshape(3, prot, rows, cols_dev, width)
    grad_normed_two = jnp.einsum(
        "kprce,kde->prcd", grad_proj_two, attn_full[4:7], preferred_element_type=f32
    )
    _, norm_back_two = jax.vjp(layer_norm, resid_two, norm_gain[2], norm_gain[3])
    part_two, gain_grad_two, shift_grad_two = norm_back_two(grad_normed_two)
    grad_stream = (grad_three + part_two).astype(bf16)
    col_attn_terms = attn_pair(normed_two, grad_proj_two, mixed_two, grad_branch_two)
    in_terms = jnp.einsum("prcd,prcf->df", normed_three, grad_inner, preferred_element_type=f32)
    out_terms = jnp.einsum("prcf,prcd->df", activ, up_grad, preferred_element_type=f32)
    grad_rows = lax.all_to_all(grad_stream, "seq", split_axis=1, concat_axis=2, tiled=True)
    grad_mixed_one = jnp.einsum(
        "prce,de->prcd", grad_rows, attn_full[3], preferred_element_type=f32
    ).astype(bf16)
    grad_mixed_one = grad_mixed_one.reshape(prot, rows_dev, cols, H, DH)
    partial_grads = jnp.einsum(
        "prihe,prjhe->phij", grad_mixed_one, value_one, preferred_element_type=f32
    )
    grad_value_one = jnp.einsum(
        "phij,prihe->prjhe", probs_low, grad_mixed_one, preferred_element_type=f32
    )
    grad_part = sent_and_summed(partial_grads.astype(jnp.bfloat16), "seq", 2)
    grad_scores_one = lax.all_gather(
        softmax_back(probs_one, grad_part).astype(bf16), "seq", axis=2, tiled=True
    )
    tie_rows = row_live[:, :, None, None, None] * tie_scale[:, None, None, None, None]
    grad_query_one = (
        jnp.einsum("phij,prjhe->prihe", grad_scores_one, key_one, preferred_element_type=f32)
        * tie_rows
    )
    grad_key_one = (
        jnp.einsum("phij,prihe->prjhe", grad_scores_one, masked_query, preferred_element_type=f32)
        * tie_scale[:, None, None, None, None]
    )
    grad_proj_one = jnp.stack([grad_query_one, grad_key_one, grad_value_one]).astype(bf16)
    grad_proj_one = grad_proj_one.reshape(3, prot, rows_dev, cols, width)
    grad_normed_one = jnp.einsum(
        "kprce,kde->prcd", grad_proj_one, attn_full[0:3], preferred_element_type=f32
    )
    _, norm_back_one = jax.vjp(layer_norm, resid_one, norm_gain[0], norm_gain[1])
    part_one, gain_grad_one, shift_grad_one = norm_back_one(grad_normed_one)
    grad_tokens = grad_rows.astype(f32) + part_one
    norm_stack = jnp.stack(
        [
            gain_grad_one,
            shift_grad_one,
            gain_grad_two,
            shift_grad_two,
            gain_grad_three,
            shift_grad_three,
        ]
    )
    row_attn_terms = attn_pair(normed_one, grad_proj_one, mixed_one, grad_rows)
    owned = lax.psum_scatter(
        jnp.concatenate(
            [row_attn_terms, col_attn_terms, in_terms, out_terms, norm_stack.T], axis=1
        ),
        "seq",
        scatter_dimension=0,
        tiled=True,
    )
    width_dev = owned.shape[0]
    row_part = owned[:, : 4 * width].reshape(width_dev, 4, width)
    col_part = owned[:, 4 * width : 8 * width].reshape(width_dev, 4, width)
    in_part = owned[:, 8 * width : 8 * width + hidden]
    out_part = owned[:, 8 * width + hidden : 8 * width + 2 * hidden].T
    norm_part = owned[:, 8 * width + 2 * hidden :].T
    attn_part = jnp.concatenate([row_part, col_part], axis=1).transpose(1, 0, 2)
    attn_grad, in_grad, out_grad, norm_grad = (
        lax.psum(attn_part.astype(jnp.bfloat16), "grp").astype(jnp.float32),
        lax.psum(in_part.astype(jnp.bfloat16), "grp").astype(jnp.float32),
        lax.psum(out_part.astype(jnp.bfloat16), "grp").astype(jnp.float32),
        lax.psum(norm_part.astype(jnp.bfloat16), "grp").astype(jnp.float32),
    )
    squares = (
        jnp.sum(attn_grad * attn_grad)
        + jnp.sum(in_grad * in_grad)
        + jnp.sum(out_grad * out_grad)
        + jnp.sum(norm_grad * norm_grad)
    )
    grad_norm = jnp.sqrt(lax.psum(squares, "seq"))
    factor = clip_bound / jnp.maximum(grad_norm, clip_bound)
    attn_first_new, attn_second_new, attn_weight_new = adam_update(
        attn_weight, attn_first, attn_second, attn_grad * factor, matrix_rate
    )
    in_first_new, in_second_new, in_weight_new = adam_update(
        in_weight, in_first, in_second, in_grad * factor, matrix_rate
    )
    out_first_new, out_second_new, out_weight_new = adam_update(
        out_weight, out_first, out_second, out_grad * factor, matrix_rate
    )
    norm_first_new, norm_second_new, norm_new = adam_update(
        norm_param, norm_first, norm_second, norm_grad * factor, norm_rate
    )
    return (
        block_out,
        grad_tokens,
        grad_norm,
        attn_first_new,
        attn_second_new,
        attn_weight_new,
        attn_weight_new.astype(bf16),
        in_first_new,
        in_second_new,
        in_weight_new,
        in_weight_new.astype(bf16),
        out_first_new,
        out_second_new,
        out_weight_new,
        out_weight_new.astype(bf16),
        norm_first_new,
        norm_second_new,
        norm_new,
    )


def solution(mesh):
    placed = (
        P("grp", "seq", None, None),
        P("grp", "seq", None, None),
        P("grp"),
        P("grp"),
        P(None, "seq", None),
        P("seq", None),
        P(None, "seq"),
        P(None, "seq"),
        P(None, "seq", None),
        P(None, "seq", None),
        P("seq", None),
        P("seq", None),
        P(None, "seq"),
        P(None, "seq"),
        P(None, "seq"),
        P(None, "seq"),
    )
    return jax.shard_map(
        body,
        mesh=mesh,
        in_specs=placed,
        out_specs=(
            P("grp", "seq", None, None),
            P("grp", "seq", None, None),
            P(),
            P(None, "seq", None),
            P(None, "seq", None),
            P(None, "seq", None),
            P(None, "seq", None),
            P("seq", None),
            P("seq", None),
            P("seq", None),
            P("seq", None),
            P(None, "seq"),
            P(None, "seq"),
            P(None, "seq"),
            P(None, "seq"),
            P(None, "seq"),
            P(None, "seq"),
            P(None, "seq"),
        ),
        check_vma=False,
    )
```

profile of v0, /device:TPU:0, one launch (start us, length us, event | category | flops | bytes accessed | tf_op | source)
XLA Modules:
  0.0 1611.1 jit_solution(13205208508672354822)
XLA Ops:
  10.2 28.2 %all-gather = bf16[8,96,6]{1,2,0:T(8,128)(2,1)S(1)} all-gather(bf16[1,96,6]{1,2,0:T(8,128)(2,1)S(1)} %convert_bitcast_fusion.2), channel_id=1, replica_groups=mesh['seq'=8,'grp'=4] {'seq'}, dimensions={0}, use_global_device_ids=true | all-gather | bytes 10368 | tf_op jit(solution)/shard_map/all_gather | solution.py:102
  39.2 112.5 %all-gather.7.cloned.1.call-done = bf16[8,768,768]{2,1,0:T(8,128)(2,1)} async-done(((bf16[8,96,768]{2,1,0:T(8,128)(2,1)}), bf16[8,768,768]{2,1,0:T(8,128)(2,1)}) %all-gather.7.cloned.1.call-update) | async-done | bytes 9437200 | tf_op jit(solution)/shard_map/all_gather | solution.py:99
  162.2 116.0 %reduce-scatter.5.cloned.1.call-done = f32[2,12,32,256]{3,2,1,0:T(8,128)} async-done(((f32[2,12,256,256]{3,2,1,0:T(8,128)}), f32[2,12,32,256]{3,2,1,0:T(8,128)}) %reduce-scatter.5.cloned.1.call-update) | async-done | bytes 786448 | tf_op jit(solution)/shard_map/reduce_scatter | solution.py:124
  290.9 64.1 %all-gather.9.cloned.1.call-done = bf16[2,12,256,256]{3,2,1,0:T(8,128)(2,1)} async-done(((bf16[2,12,32,256]{3,2,1,0:T(8,128)(2,1)}), bf16[2,12,256,256]{3,2,1,0:T(8,128)(2,1)}) %all-gather.9.cloned.1.call-update) | async-done | bytes 3145744 | tf_op jit(solution)/shard_map/all_gather | solution.py:126
  367.2 36.7 %all-to-all-done = bf16[2,1,256,768]{3,0,1,2:T(2,128)(2,1)S(1)} async-done(((bf16[2,1,256,768]{3,0,1,2:T(2,128)(2,1)}), bf16[2,1,256,768]{3,0,1,2:T(2,128)(2,1)S(1)}, u32[]{:S(2)}, u32[]{:S(2)}) %all-to-all-start) | async-done | bytes 786464 | tf_op jit(solution)/shard_map/all_to_all | solution.py:134
  436.5 16.4 %all-gather.11.cloned.1.call-done = bf16[768,3072]{1,0:T(8,128)(2,1)} async-done(((bf16[96,3072]{1,0:T(8,128)(2,1)}), bf16[768,3072]{1,0:T(8,128)(2,1)}) %all-gather.11.cloned.1.call-update) | async-done | bytes 4718608 | tf_op jit(solution)/shard_map/all_gather | solution.py:100
  452.9 7.0 fusion.12
  459.9 73.7 %all-gather.13.cloned.1.call-done = bf16[3072,768]{0,1:T(8,128)(2,1)} async-done(((bf16[3072,96]{0,1:T(8,128)(2,1)}), bf16[3072,768]{0,1:T(8,128)(2,1)}) %all-gather.13.cloned.1.call-update) | async-done | bytes 4718608 | tf_op jit(solution)/shard_map/all_gather | solution.py:101
  533.6 8.8 fusion.9
  595.9 23.2 %all_to_all.47 = bf16[2,8,32,768]{3,2,0,1:T(8,128)(2,1)S(1)} all-to-all(bf16[2,8,32,768]{3,2,0,1:T(8,128)(2,1)S(1)} %copy.492), channel_id=1, replica_groups=mesh['seq'=8,'grp'=4] {'seq'}, dimensions={1} | all-to-all | bytes 1572864 | tf_op jit(solution)/shard_map/all_to_all | solution.py:205
  629.0 73.9 %all_to_all.48 = bf16[8,2,12,32,256]{4,3,2,1,0:T(8,128)(2,1)S(1)} all-to-all(bf16[8,2,12,32,256]{4,3,2,1,0:T(8,128)(2,1)S(1)} %bitcast.282), channel_id=1, replica_groups=mesh['seq'=8,'grp'=4] {'seq'}, dimensions={0} | all-to-all | bytes 6291456 | tf_op jit(solution)/shard_map/all_to_all | solution.py:33
  718.0 9.9 copy.506
  735.4 33.1 %all-gather.15.cloned.1.call-done = bf16[2,12,256,256]{3,2,1,0:T(8,128)(2,1)} async-done(((bf16[2,12,32,256]{3,2,1,0:T(8,128)(2,1)}), bf16[2,12,256,256]{3,2,1,0:T(8,128)(2,1)}) %all-gather.15.cloned.1.call-update) | async-done | bytes 3145744 | tf_op jit(solution)/shard_map/all_gather | solution.py:217
  790.8 9.6 copy.505
  800.4 8.5 constant_dynamic-update-slice_fusion.1
  809.0 8.6 constant_dynamic-update-slice_fusion
  817.6 5.7 bitcast_dynamic-update-slice_fusion.1
  823.4 5.4 bitcast_dynamic-update-slice_fusion
  831.2 8.0 add_convert_fusion.1
  843.7 612.7 %reduce-scatter.7.cloned.1.call-done = f32[96,12294]{1,0:T(8,128)} async-done(((f32[768,12294]{1,0:T(8,128)}), f32[96,12294]{1,0:T(8,128)}) %reduce-scatter.7.cloned.1.call-update) | async-done | bytes 4720912
  1488.5 7.5 psum.38
  1496.6 35.6 %all-reduce.3.cloned.1.call-done = (bf16[8,96,768]{2,1,0:T(8,128)(2,1)}, bf16[96,3072]{0,1:T(8,128)(2,1)}, bf16[3072,96]{1,0:T(8,128)(2,1)}) async-done(((bf16[8,96,768]{2,1,0:T(8,128)(2,1)}, bf16[96,3072]{0,1:T(8,128)(2,1)}, bf16[3072,96]{1,0:T(8,128)(2,1)}), (bf16[8,96,768]{2,1,0:T(8,128)(2,1)}, bf16[96,3072]{0,1:T(8,128)(2,1)}, bf16[3072,96]{1,0:T(8,128)(2,1)})) %all-reduce.3.cloned.1.call-update) | async-done | bytes 2359312 | tf_op jit(solution)/shard_map/psum | solution.py:264
  1543.7 22.1 %psum.39 = f32[]{:T(128)} all-reduce(f32[]{:T(128)S(6)} %add.200), channel_id=1, replica_groups=mesh['seq'=8,'grp'=4] {'seq'}, use_global_device_ids=true, to_apply=%region_35.36 | all-reduce | flops 1 | bytes 8 | tf_op jit(solution)/shard_map/psum | solution.py:275
  1594.8 7.3 fusion.106
  (292 shorter events, 256.8 us)
Async XLA Ops:
  7.2 31.4 %copy-start.4 = (bf16[2,1,256,768]{3,2,1,0:T(8,128)(2,1)S(1)}, bf16[2,1,256,768]{3,2,1,0:T(8,128)(2,1)}, u32[]{:S(2)}) copy-start(bf16[2,1,256,768]{3,2,1,0:T(8,128)(2,1)} %param.16) | copy-start | bytes 2359300
  7.2 144.5 %all-gather.7.cloned.1.call-start = ((), (), s32[]{:S(2)}) async-start(), calls=%async_computation.7 | async-start | bytes 10616832 | tf_op jit(solution)/shard_map/all_gather | solution.py:99
  10.1 29.0 %copy-start.58 = (s32[2]{0:T(128)S(1)}, s32[2]{0:T(128)}, u32[]{:S(2)}) copy-start(s32[2]{0:T(128)} %param.19) | copy-start | bytes 28
  10.2 268.0 %reduce-scatter.5.cloned.1.call-start = ((), (), s32[]{:S(2)}) async-start(), calls=%async_computation.8 | async-start | bytes 7077888 | tf_op jit(solution)/shard_map/reduce_scatter | solution.py:124
  39.2 116.7 %copy-start.50 = (f32[2,256]{1,0:T(2,128)}, f32[2,256]{1,0:T(2,128)S(1)}, u32[]{:S(2)}) copy-start(f32[2,256]{1,0:T(2,128)S(1)} %fusion.40) | copy-start | bytes 6148
  161.5 193.5 %all-gather.9.cloned.1.call-start = ((), (), s32[]{:S(2)}) async-start(), calls=%async_computation.9 | async-start | bytes 3538944 | tf_op jit(solution)/shard_map/all_gather | solution.py:126
  162.2 119.3 %copy-start.25 = (f32[96,3072]{1,0:T(8,128)S(1)}, f32[96,3072]{1,0:T(8,128)}, u32[]{:S(2)}) copy-start(f32[96,3072]{1,0:T(8,128)} %param.21) | copy-start | bytes 3538948
  281.4 171.5 %all-gather.11.cloned.1.call-start = ((), (), s32[]{:S(2)}) async-start(), calls=%async_computation.10 | async-start | bytes 5308416 | tf_op jit(solution)/shard_map/all_gather | solution.py:100
  282.4 251.2 %all-gather.13.cloned.1.call-start = ((), (), s32[]{:S(2)}) async-start(), calls=%async_computation.11 | async-start | bytes 5308416 | tf_op jit(solution)/shard_map/all_gather | solution.py:101
  286.9 75.2 %all-to-all-start.2 = ((bf16[2,1,256,768]{3,0,1,2:T(2,128)(2,1)}), bf16[2,1,256,768]{3,0,1,2:T(2,128)(2,1)S(1)}, u32[]{:S(2)}, u32[]{:S(2)}) async-start(bf16[2,1,256,768]{3,0,1,2:T(2,128)(2,1)} %copy.478), calls=%async_computation.3 | async-start | bytes 1572864 | tf_op jit(solution)/shard_map/all_to_all | solution.py:135
  290.9 67.1 %copy-start.12 = (bf16[1,2,1,256,768]{3,4,1,2,0:T(8,128)(2,1)}, bf16[1,2,1,256,768]{3,4,1,2,0:T(8,128)(2,1)S(1)}, u32[]{:S(2)}) copy-start(bf16[1,2,1,256,768]{3,4,1,2,0:T(8,128)(2,1)S(1)} %copy.462) | copy-start | bytes 2359300
  362.0 41.8 %all-to-all-start = ((bf16[2,1,256,768]{3,0,1,2:T(2,128)(2,1)}), bf16[2,1,256,768]{3,0,1,2:T(2,128)(2,1)S(1)}, u32[]{:S(2)}, u32[]{:S(2)}) async-start(bf16[2,1,256,768]{3,0,1,2:T(2,128)(2,1)} %copy.466), calls=%async_computation.1 | async-start | bytes 1572864 | tf_op jit(solution)/shard_map/all_to_all | solution.py:134
  365.6 402.9 %all-gather.15.cloned.1.call-start = ((), (), s32[]{:S(2)}) async-start(), calls=%async_computation.12 | async-start | bytes 3538944 | tf_op jit(solution)/shard_map/all_gather | solution.py:217
  533.6 8.8 copy-start.60
  709.0 747.4 %reduce-scatter.7.cloned.1.call-start = ((), (), s32[]{:S(2)}) async-start(), calls=%async_computation.13 | async-start | bytes 42909696
  718.0 10.0 copy-start.13
  731.7 36.8 %copy-start.17 = (bf16[1,2,1,256,768]{3,4,1,2,0:T(8,128)(2,1)S(1)}, bf16[1,2,1,256,768]{3,4,1,2,0:T(8,128)(2,1)}, u32[]{:S(2)}) copy-start(bf16[1,2,1,256,768]{3,4,1,2,0:T(8,128)(2,1)} %copy-done.16) | copy-start | bytes 2359300
  809.0 8.6 copy-start.62
  809.0 14.4 slice-start
  840.1 646.8 %all-to-all-start.1 = ((bf16[2,8,32,768]{3,2,0,1:T(8,128)(2,1)}), bf16[2,8,32,768]{3,2,0,1:T(8,128)(2,1)S(1)}, u32[]{:S(2)}, u32[]{:S(2)}) async-start(bf16[2,8,32,768]{3,2,0,1:T(8,128)(2,1)} %copy.476), calls=%async_computation.2 | async-start | bytes 1572864 | tf_op jit(solution)/shard_map/all_to_all | solution.py:166
  843.6 688.6 %all-reduce.3.cloned.1.call-start = ((), (), s32[]{:S(2)}) async-start(), calls=%async_computation.14 | async-start | bytes 5505024 | tf_op jit(solution)/shard_map/psum | solution.py:264
  1487.8 52.8 %copy-start.7 = (bf16[2,1,256,768]{3,2,1,0:T(8,128)(2,1)S(1)}, bf16[2,1,256,768]{3,2,1,0:T(8,128)(2,1)}, u32[]{:S(2)}) copy-start(bf16[2,1,256,768]{3,2,1,0:T(8,128)(2,1)} %param.16) | copy-start | bytes 2359300
  1487.8 52.8 %copy-start.53 = (f32[2,256]{1,0:T(2,128)S(1)}, f32[2,256]{1,0:T(2,128)}, u32[]{:S(2)}) copy-start(f32[2,256]{1,0:T(2,128)} %copy-done.52) | copy-start | bytes 6148
  1594.8 7.3 copy-start.56
  (52 other events, 160.5 us)
Sparse Core Ops, SparseCore 0:
  10.8 140.8 all-gather.6
  161.6 116.5 reduce-scatter.4
  281.5 73.4 all-gather.8
  357.6 95.2 all-gather.10
  455.5 78.0 all-gather.12
  709.1 59.3 all-gather.14
  831.3 625.0 reduce-scatter.6
  1470.5 61.6 all-reduce.2
where the time goes:
time: 1620 us; the launch traced here: 1610 us
  waiting for transfers between devices  1100 us (68%)
  blocking collectives  155 us (10%)
  local copies, waits for them, and re-layouts  149 us (9%)
  matrix products  113 us (7%)
  other arithmetic  62.4 us (4%)
  between operations  19.9 us (1%)
    unnamed x9, waiting for transfers between devices  613 us
    reduce_scatter x1, waiting for transfers between devices, body(): lax.psum_scatter(partial_scores, 'seq', scatter_dimension=2, tiled=True)  116 us
    all_gather x1, waiting for transfers between devices, body(): lax.all_gather(attn_weight.astype(bf16), 'seq', axis=1, tiled=True)  113 us
    all_to_all x1, blocking collectives, sent_and_summed(): pieces = lax.all_to_all(in_blocks(x, dim, length), axis, 0, 0, tiled=True)  73.9 us
    all_gather x1, waiting for transfers between devices, body(): lax.all_gather(out_weight.astype(bf16), 'seq', axis=1, tiled=True)  73.7 us
    unnamed x147, local copies, waits for them, and re-layouts  64.8 us
    all_gather x1, waiting for transfers between devices, body(): lax.all_gather(probs_one.astype(bf16), 'seq', axis=2, tiled=True)  64.1 us
    all_to_all x1, waiting for transfers between devices, body(): lax.all_to_all(stream_one, 'seq', split_axis=2, concat_axis=1, tiled=True)  36.7 us
  transfers between devices with their start and end apart: 11, of which 9 were waited for; matrix products, arithmetic and copies ran while one was open for 7% of the time, Pallas kernels for 0%

commit v1 on v0

--- a/solution.py
+++ b/solution.py
@@ -4,6 +4,9 @@
 import jax
 import jax.numpy as jnp
 from jax import lax
+from jax.experimental import pallas as pl
+from jax.experimental.pallas import tpu as pltpu
+from jax.sharding import Mesh
 from jax.sharding import PartitionSpec as P
 
 H = 12
@@ -72,7 +75,7 @@
     return jnp.concatenate([qkv_terms, output_terms[:, None, :]], axis=1).reshape(width, 4 * width)
 
 
-def body(
+def general_body(
     tokens,
     cotangent,
     col_count,
@@ -308,48 +311,660 @@
     )
 
 
-def solution(mesh):
+PAIR = [(0, 1), (1, 0)]
+TILE = 128
+
+
+def swap(value, axis):
+    return lax.ppermute(value, axis, PAIR)
+
+
+def pick(value, index, axis):
+    return lax.dynamic_index_in_dim(value, index, axis, keepdims=False)
+
+
+def merge(own, other, place, axis):
+    return jnp.where(
+        place == 0,
+        jnp.stack([own, other], axis=axis),
+        jnp.stack([other, own], axis=axis),
+    )
+
+
+def to_columns(value, c):
+    prot, _, cols, width = value.shape
+    part = cols // 4
+    split = value.reshape(prot, 2, 2, part, width)
+    got = swap(pick(split, 1 - c, 2), "c")
+    both = merge(pick(split, c, 2), got, c, 0)
+    both = both.reshape(8, part, width)
+    return lax.all_to_all(both, ("z", "x"), 0, 0, tiled=True)
+
+
+def to_rows(value, c):
+    rows, part, width = value.shape
+    got = lax.all_to_all(value, ("z", "x"), 0, 0, tiled=True)
+    got = got.reshape(2, 2, 2, part, width)
+    other = swap(pick(got, 1 - c, 0), "c")
+    both = merge(pick(got, c, 0), other, c, 2)
+    return both.reshape(2, 1, 4 * part, width)
+
+
+def gather_pieces(own):
+    over_z = [own]
+    for i in (1, 2, 3):
+        over_z.append(lax.ppermute(own, "z", [(k, k ^ i) for k in range(4)]))
+    return over_z, [swap(piece, "x") for piece in over_z]
+
+
+def place_kernel(plan, outs_at, place_ref, *refs):
+    pieces = refs[: len(plan)]
+    outs = refs[len(plan) : -1]
+    sem = refs[-1]
+    copies = []
+    for ref, (i, j, k) in zip(pieces, plan):
+        z = lax.bitwise_xor(place_ref[0], i)
+        x = lax.bitwise_xor(place_ref[1], j)
+        c = lax.bitwise_xor(place_ref[2], k)
+        shard = z * 2 + x
+        for source, target in outs_at(ref, outs, shard, c):
+            copies.append(pltpu.make_async_copy(source, target, sem.at[len(copies)]))
+    for copy in copies:
+        copy.start()
+    for copy in copies:
+        copy.wait()
+
+
+def placed_pieces(pieces, plan, outs_at, outs, place, count):
+    anywhere = pl.BlockSpec(memory_space=pl.ANY)
+    return pl.pallas_call(
+        partial(place_kernel, plan, outs_at),
+        in_specs=[pl.BlockSpec(memory_space=pltpu.SMEM)] + [anywhere] * len(pieces),
+        out_specs=[anywhere] * len(outs),
+        out_shape=[jax.ShapeDtypeStruct(shape, jnp.bfloat16) for shape in outs],
+        scratch_shapes=[pltpu.SemaphoreType.DMA((count,))],
+        cost_estimate=pl.CostEstimate(
+            flops=0, transcendentals=0, bytes_accessed=sum(4 * math.prod(s) for s in outs)
+        ),
+    )(place, *pieces)
+
+
+def row_attn_at(ref, outs, shard, c):
+    depth = outs[0].shape[0] // 8
+    at = pl.multiple_of(shard * depth, depth)
+    return [
+        (ref.at[pl.ds(0, depth)], outs[0].at[pl.ds(at, depth)]),
+        (ref.at[pl.ds(depth, 16)], outs[1].at[shard]),
+    ]
+
+
+def halves_at(ref, outs, shard, c):
+    depth, half = ref.shape[1], ref.shape[2]
+    at = pl.multiple_of(shard * depth, depth)
+    moves = []
+    slots = [(o, n) for o, out in enumerate(outs) for n in range(out.shape[1] // (2 * half))]
+    for k, (o, n) in enumerate(slots):
+        lane = pl.multiple_of(c * half + n * 2 * half, TILE)
+        moves.append((ref.at[k], outs[o].at[pl.ds(at, depth), pl.ds(lane, half)]))
+    return moves
+
+
+def all_halves(own_half, other_half, place, outs):
+    over_z, over_x = gather_pieces(own_half)
+    mine = over_z + over_x
+    plan = [(i, j, 0) for j in (0, 1) for i in range(4)]
+    theirs = [other_half] + [swap(piece, "c") for piece in mine[1:]]
+    plan = plan + [(i, j, 1) for (i, j, _) in plan]
+    pieces = mine + theirs
+    return placed_pieces(
+        pieces, plan, halves_at, outs, place, len(pieces) * own_half.shape[0]
+    )
+
+
+def contract(a, b, dims):
+    return lax.dot_general(a, b, (dims, ((), ())), preferred_element_type=jnp.float32)
+
+
+LAST = ((1,), (1,))
+FIRST = ((0,), (0,))
+PLAIN = ((1,), (0,))
+
+
+def softmax_of(scores, keep):
+    scores = jnp.where(keep, scores, masked_score)
+    expo = jnp.exp(scores - jnp.max(scores, axis=-1, keepdims=True))
+    return expo / jnp.sum(expo, axis=-1, keepdims=True)
+
+
+def head_lanes(lanes):
+    side = lax.broadcasted_iota(jnp.int32, (1, lanes), 1) % TILE < DH
+    return (side, jnp.logical_not(side))
+
+
+def only(keep, value):
+    return jnp.where(keep, value, jnp.zeros_like(value))
+
+
+def column_keep(info_ref, own_cols, near, part):
+    key = lax.broadcasted_iota(jnp.int32, (1, 2 * near), 1)
+    far = key >= near
+    inner = key % near
+    x = jnp.where(far, 1 - info_ref[1], info_ref[1])
+    c = jnp.where(inner >= part, 1 - info_ref[2], info_ref[2])
+    column = x * near + c * part + inner % part
+    return column < info_ref[3]
+
+
+def row_pair(ref, row):
+    blocks, _, part, lanes = ref.shape
+    return jnp.concatenate(
+        [ref[:, row + n].reshape(blocks * part, lanes) for n in (0, 1)], axis=1
+    )
+
+
+def live_pair(value, row, info_ref):
+    lane = lax.broadcasted_iota(jnp.int32, (1, value.shape[1]), 1) // TILE + row
+    return only(lane < info_ref[4], value)
+
+
+def row_fwd_kernel(info_ref, tie_ref, q_ref, k_ref, v_ref, kf_ref, vf_ref, o_ref):
+    blocks, rows, part, lanes = q_ref.shape
+    near = blocks * part
+    sides = head_lanes(2 * lanes)
+    keep = column_keep(info_ref, near, near, part)
+    tie = tie_ref[0]
+    scores = [jnp.zeros((near, 2 * near), jnp.float32) for _ in sides]
+    for row in range(0, rows, 2):
+        query = live_pair(row_pair(q_ref, row), row, info_ref)
+        key = jnp.concatenate([row_pair(k_ref, row), row_pair(kf_ref, row)], axis=0)
+        for n, side in enumerate(sides):
+            scores[n] = scores[n] + contract(only(side, query), key, LAST)
+    probs = [softmax_of(s * tie, keep).astype(jnp.bfloat16) for s in scores]
+    for row in range(0, rows, 2):
+        value = jnp.concatenate([row_pair(v_ref, row), row_pair(vf_ref, row)], axis=0)
+        mixed = jnp.where(
+            sides[0], contract(probs[0], value, PLAIN), contract(probs[1], value, PLAIN)
+        ).astype(jnp.bfloat16)
+        for n in (0, 1):
+            o_ref[:, row + n] = mixed[:, n * lanes : (n + 1) * lanes].reshape(blocks, part, lanes)
+
+
+def row_bwd_kernel(
+    info_ref, tie_ref, q_ref, k_ref, v_ref, kf_ref, vf_ref, do_ref,
+    dq_ref, dk_ref, dv_ref, dkf_ref, dvf_ref,
+):
+    bf16 = jnp.bfloat16
+    blocks, rows, part, lanes = q_ref.shape
+    near = blocks * part
+    sides = head_lanes(2 * lanes)
+    keep = column_keep(info_ref, near, near, part)
+    tie = tie_ref[0]
+    scores = [jnp.zeros((near, 2 * near), jnp.float32) for _ in sides]
+    grads = [jnp.zeros((near, 2 * near), jnp.float32) for _ in sides]
+    for row in range(0, rows, 2):
+        query = live_pair(row_pair(q_ref, row), row, info_ref)
+        key = jnp.concatenate([row_pair(k_ref, row), row_pair(kf_ref, row)], axis=0)
+        value = jnp.concatenate([row_pair(v_ref, row), row_pair(vf_ref, row)], axis=0)
+        out = row_pair(do_ref, row)
+        for n, side in enumerate(sides):
+            scores[n] = scores[n] + contract(only(side, query), key, LAST)
+            grads[n] = grads[n] + contract(only(side, out), value, LAST)
+    probs = [softmax_of(s * tie, keep) for s in scores]
+    lows = [p.astype(bf16) for p in probs]
+    deltas = [softmax_back(p, g).astype(bf16) for p, g in zip(probs, grads)]
+    for row in range(0, rows, 2):
+        query = live_pair(row_pair(q_ref, row), row, info_ref)
+        key = jnp.concatenate([row_pair(k_ref, row), row_pair(kf_ref, row)], axis=0)
+        out = row_pair(do_ref, row)
+        dq = [contract(d, key, PLAIN) for d in deltas]
+        dk = [contract(d, query, FIRST) for d in deltas]
+        dv = [contract(p, out, FIRST) for p in lows]
+        dq = live_pair(jnp.where(sides[0], dq[0], dq[1]) * tie, row, info_ref).astype(bf16)
+        dk = (jnp.where(sides[0], dk[0], dk[1]) * tie).astype(bf16)
+        dv = jnp.where(sides[0], dv[0], dv[1]).astype(bf16)
+        for n in (0, 1):
+            at = slice(n * lanes, (n + 1) * lanes)
+            dq_ref[:, row + n] = dq[:, at].reshape(blocks, part, lanes)
+            dk_ref[:, row + n] = dk[:near, at].reshape(blocks, part, lanes)
+            dv_ref[:, row + n] = dv[:near, at].reshape(blocks, part, lanes)
+            dkf_ref[:, row + n] = dk[near:, at].reshape(blocks, part, lanes)
+            dvf_ref[:, row + n] = dv[near:, at].reshape(blocks, part, lanes)
+
+
+def lane_block(shape, first):
+    blocks, rows, part, _ = shape
+    return pl.BlockSpec((blocks, rows, part, TILE), lambda t: (0, 0, 0, first + t))
+
+
+def row_attention(info, tie, near, far):
+    blocks, rows, part, lanes = near.shape
+    tiles = lanes // 3 // TILE
+    shape = near.shape
+    small = pl.BlockSpec(memory_space=pltpu.SMEM)
+    return pl.pallas_call(
+        row_fwd_kernel,
+        grid=(tiles,),
+        in_specs=[small, small]
+        + [lane_block(shape, n * tiles) for n in range(3)]
+        + [lane_block(shape, n * tiles) for n in range(2)],
+        out_specs=lane_block(shape, 0),
+        out_shape=jax.ShapeDtypeStruct((blocks, rows, part, lanes // 3), jnp.bfloat16),
+        compiler_params=pltpu.CompilerParams(vmem_limit_bytes=32 * 2**20),
+    )(info, tie, near, near, near, far, far)
+
+
+def row_attention_back(info, tie, near, far, grad):
+    blocks, rows, part, lanes = near.shape
+    tiles = lanes // 3 // TILE
+    shape = near.shape
+    small = pl.BlockSpec(memory_space=pltpu.SMEM)
+    result = jax.ShapeDtypeStruct((blocks, rows, part, lanes // 3), jnp.bfloat16)
+    return pl.pallas_call(
+        row_bwd_kernel,
+        grid=(tiles,),
+        in_specs=[small, small]
+        + [lane_block(shape, n * tiles) for n in range(3)]
+        + [lane_block(shape, n * tiles) for n in range(2)]
+        + [lane_block(shape, 0)],
+        out_specs=[lane_block(shape, 0)] * 5,
+        out_shape=[result] * 5,
+        compiler_params=pltpu.CompilerParams(vmem_limit_bytes=32 * 2**20),
+    )(info, tie, near, near, near, far, far, grad)
+
+
+def column_masks(info_ref, rows, part):
+    tokens = rows * part
+    first = lax.broadcasted_iota(jnp.int32, (tokens, tokens), 0)
+    second = lax.broadcasted_iota(jnp.int32, (tokens, tokens), 1)
+    same = first % part == second % part
+    return jnp.logical_and(same, second // part < info_ref[4])
+
+
+def col_fwd_kernel(info_ref, qkv_ref, o_ref):
+    rows, part, lanes = qkv_ref.shape
+    width = lanes // 3
+    qkv = qkv_ref[...].reshape(rows * part, lanes)
+    keep = column_masks(info_ref, rows, part)
+    sides = head_lanes(TILE)
+    scale = 1.0 / math.sqrt(DH)
+    for at in range(0, width, TILE):
+        query = qkv[:, at : at + TILE]
+        key = qkv[:, width + at : width + at + TILE]
+        value = qkv[:, 2 * width + at : 2 * width + at + TILE]
+        mixed = []
+        for side in sides:
+            probs = softmax_of(contract(only(side, query), key, LAST) * scale, keep)
+            mixed.append(contract(probs.astype(jnp.bfloat16), value, PLAIN))
+        mixed = jnp.where(sides[0], mixed[0], mixed[1]).astype(jnp.bfloat16)
+        o_ref[:, :, at : at + TILE] = mixed.reshape(rows, part, TILE)
+
+
+def col_bwd_kernel(info_ref, qkv_ref, do_ref, d_ref):
+    bf16 = jnp.bfloat16
+    rows, part, lanes = qkv_ref.shape
+    width = lanes // 3
+    qkv = qkv_ref[...].reshape(rows * part, lanes)
+    out_grad = do_ref[...].reshape(rows * part, width)
+    keep = column_masks(info_ref, rows, part)
+    sides = head_lanes(TILE)
+    scale = 1.0 / math.sqrt(DH)
+    for at in range(0, width, TILE):
+        query = qkv[:, at : at + TILE]
+        key = qkv[:, width + at : width + at + TILE]
+        value = qkv[:, 2 * width + at : 2 * width + at + TILE]
+        out = out_grad[:, at : at + TILE]
+        found = []
+        for side in sides:
+            probs = softmax_of(contract(only(side, query), key, LAST) * scale, keep)
+            grads = contract(only(side, out), value, LAST)
+            delta = softmax_back(probs, grads).astype(bf16)
+            found.append(
+                (
+                    contract(delta, key, PLAIN) * scale,
+                    contract(delta, query, FIRST) * scale,
+                    contract(probs.astype(bf16), out, FIRST),
+                )
+            )
+        for n in range(3):
+            both = jnp.where(sides[0], found[0][n], found[1][n]).astype(bf16)
+            first = n * width + at
+            d_ref[:, :, first : first + TILE] = both.reshape(rows, part, TILE)
+
+
+def column_block(rows, part, lanes):
+    return pl.BlockSpec((rows, part, lanes), lambda b: (0, b, 0))
+
+
+def column_attention(info, qkv, part=16):
+    rows, cols, lanes = qkv.shape
+    return pl.pallas_call(
+        col_fwd_kernel,
+        grid=(cols // part,),
+        in_specs=[pl.BlockSpec(memory_space=pltpu.SMEM), column_block(rows, part, lanes)],
+        out_specs=column_block(rows, part, lanes // 3),
+        out_shape=jax.ShapeDtypeStruct((rows, cols, lanes // 3), jnp.bfloat16),
+        compiler_params=pltpu.CompilerParams(vmem_limit_bytes=32 * 2**20),
+    )(info, qkv)
+
+
+def column_attention_back(info, qkv, grad, part=16):
+    rows, cols, lanes = qkv.shape
+    return pl.pallas_call(
+        col_bwd_kernel,
+        grid=(cols // part,),
+        in_specs=[
+            pl.BlockSpec(memory_space=pltpu.SMEM),
+            column_block(rows, part, lanes),
+            column_block(rows, part, lanes // 3),
+        ],
+        out_specs=column_block(rows, part, lanes),
+        out_shape=jax.ShapeDtypeStruct((rows, cols, lanes), jnp.bfloat16),
+        compiler_params=pltpu.CompilerParams(vmem_limit_bytes=32 * 2**20),
+    )(info, qkv, grad)
+
+
+def summed_to_owner(terms, x):
+    bf16 = jnp.bfloat16
+    f32 = jnp.float32
+    depth = terms.shape[0] // 8
+    blocks = terms.reshape(4, 2, depth, *terms.shape[1:])
+    got = swap(pick(blocks, 1 - x, 1), "x")
+    column = (pick(blocks, x, 1).astype(f32) + got.astype(f32)).astype(bf16)
+    parts = lax.all_to_all(column, "z", 0, 0, tiled=True)
+    shard = jnp.sum(parts.astype(f32), axis=0).astype(bf16)
+    return (shard.astype(f32) + swap(shard, "y").astype(f32)).astype(bf16)
+
+
+def paired_body(
+    tokens,
+    cotangent,
+    col_count,
+    row_count,
+    attn_weight,
+    in_weight,
+    out_weight,
+    norm_param,
+    attn_first,
+    attn_second,
+    in_first,
+    in_second,
+    out_first,
+    out_second,
+    norm_first,
+    norm_second,
+):
+    f32 = jnp.float32
+    bf16 = jnp.bfloat16
+    z, x, c = (lax.axis_index(name) for name in ("z", "x", "c"))
+    width = tokens.shape[-1]
+    hidden = in_weight.shape[1]
+    depth = in_weight.shape[0]
+    half = width // 2
+    hidden_half = hidden // 2
+
+    counts = jnp.stack([col_count, row_count])
+    other_counts = swap(counts, "c")
+    mine = jnp.where(z // 2 == c, counts, other_counts)
+    mine = pick(mine, z % 2, 1)
+    cols_live, rows_live = mine[0], mine[1]
+    place = jnp.stack([z, x, c]).astype(jnp.int32)
+    info = jnp.concatenate([place, mine])
+    tie = (lax.rsqrt(rows_live.astype(f32)) * (1.0 / math.sqrt(DH))).reshape(1)
+
+    attn_low = attn_weight.astype(bf16)
+    halves = attn_low.reshape(8, depth, 2, half)
+    qkv_half = jnp.moveaxis(pick(halves[:3], c, 2), 0, 1).reshape(depth, 3 * half)
+    norm_row = jnp.pad(
+        norm_param.astype(bf16).reshape(1, 6 * depth), ((0, 15), (0, 3 * half - 6 * depth))
+    )
+    over_z, over_x = gather_pieces(jnp.concatenate([qkv_half, norm_row]))
+    plan = [(i, j, 0) for j in (0, 1) for i in range(4)]
+    w_row, norm_rows = placed_pieces(
+        over_z + over_x,
+        plan,
+        row_attn_at,
+        [(width, 3 * half), (8, 16, 3 * half)],
+        place,
+        16,
+    )
+    norm_gain = norm_rows[:, 0, : 6 * depth].reshape(8, 6, depth)
+    norm_gain = jnp.moveaxis(norm_gain, 0, 1).reshape(6, width).astype(f32)
+    w_three, w_col, w_seven = all_halves(
+        pick(halves[3:], c, 2),
+        pick(halves[3:], 1 - c, 2),
+        place,
+        [(width, width), (width, 3 * width), (width, width)],
+    )
+    ffn_low = jnp.stack([in_weight.astype(bf16), out_weight.astype(bf16).T])
+    ffn_halves = ffn_low.reshape(2, depth, 2, hidden_half)
+    w_in, w_out = all_halves(
+        pick(ffn_halves, c, 2),
+        pick(ffn_halves, 1 - c, 2),
+        place,
+        [(width, hidden), (width, hidden)],
+    )
+
+    stream_zero = to_columns(tokens, c)
+    rows, part, _ = stream_zero.shape
+    count = rows * part
+    resid_one = stream_zero.reshape(count, width).astype(f32)
+    normed_one = layer_norm(resid_one, norm_gain[0], norm_gain[1]).astype(bf16)
+    near_normed = jnp.concatenate([normed_one, swap(normed_one, "c")])
+    far_first = swap(normed_one, "x")
+    far_normed = jnp.concatenate([far_first, swap(far_first, "c")])
+    near = contract(near_normed, w_row, PLAIN).astype(bf16).reshape(2, rows, part, 3 * half)
+    far = contract(far_normed, w_row[:, half:], PLAIN).astype(bf16)
+    far = far.reshape(2, rows, part, 2 * half)
+    mixed_heads = row_attention(info, tie, near, far)
+    mixed_one = merge(mixed_heads[0], swap(mixed_heads[1], "c"), c, 2).reshape(count, width)
+    stream_one = (resid_one + contract(mixed_one, w_three, PLAIN)).astype(bf16)
+
+    resid_two = stream_one.astype(f32)
+    normed_two = layer_norm(resid_two, norm_gain[2], norm_gain[3]).astype(bf16)
+    qkv_two = contract(normed_two, w_col, PLAIN).astype(bf16).reshape(rows, part, 3 * width)
+    mixed_two = column_attention(info, qkv_two).reshape(count, width)
+    resid_three = resid_two + contract(mixed_two, w_seven, PLAIN)
+
+    normed_three = layer_norm(resid_three, norm_gain[4], norm_gain[5]).astype(bf16)
+    inner = contract(normed_three, w_in, PLAIN)
+    activ = jax.nn.gelu(inner, approximate=True).astype(bf16)
+    result = (resid_three + contract(activ, w_out, LAST)).astype(bf16)
+    block_out = to_rows(result.reshape(rows, part, width), c)
+
+    up = to_columns(cotangent, c)
+    column = x * (2 * part) + c * part + jnp.arange(part, dtype=jnp.int32)
+    live = jnp.logical_and(
+        (jnp.arange(rows, dtype=jnp.int32) < rows_live)[:, None], (column < cols_live)[None, :]
+    )
+    up = jnp.where(live[..., None], up, jnp.zeros_like(up)).reshape(count, width)
+    grad_act = contract(up, w_out, PLAIN)
+    _, gelu_back = jax.vjp(partial(jax.nn.gelu, approximate=True), inner)
+    grad_inner = gelu_back(grad_act)[0].astype(bf16)
+
+    def lanes_of(value, which, groups):
+        split = value.reshape(value.shape[0], groups, 2, value.shape[1] // (2 * groups))
+        return pick(split, which, 2).reshape(value.shape[0], value.shape[1] // 2)
+
+    def over_cores(sides):
+        sent = [contract(a, lanes_of(b, 1 - c, g), FIRST).astype(bf16) for a, b, g in sides]
+        got = [swap(value, "c") for value in sent]
+        kept = [contract(a, lanes_of(b, c, g), FIRST) for a, b, g in sides]
+        return [(k + v.astype(f32)).astype(bf16) for k, v in zip(kept, got)]
+
+    ffn_terms = over_cores([(normed_three, grad_inner, 1), (up, activ, 1)])
+    ffn_grad = summed_to_owner(jnp.stack(ffn_terms, axis=1), x)
+    grad_normed_three = contract(grad_inner, w_in, LAST)
+    _, norm_back_three = jax.vjp(layer_norm, resid_three, norm_gain[4], norm_gain[5])
+    part_three, gain_grad_three, shift_grad_three = norm_back_three(grad_normed_three)
+    grad_three = up.astype(f32) + part_three
+
+    grad_branch_two = grad_three.astype(bf16)
+    grad_mixed_two = contract(grad_branch_two, w_seven, LAST).astype(bf16)
+    grad_qkv_two = column_attention_back(
+        info, qkv_two, grad_mixed_two.reshape(rows, part, width)
+    ).reshape(count, 3 * width)
+    grad_normed_two = contract(grad_qkv_two, w_col, LAST)
+    _, norm_back_two = jax.vjp(layer_norm, resid_two, norm_gain[2], norm_gain[3])
+    part_two, gain_grad_two, shift_grad_two = norm_back_two(grad_normed_two)
+    grad_stream = (grad_three + part_two).astype(bf16)
+
+    grad_mixed_one = contract(grad_stream, w_three, LAST).astype(bf16)
+    split = grad_mixed_one.reshape(rows, part, 2, half)
+    grad_heads = jnp.stack([pick(split, c, 2), swap(pick(split, 1 - c, 2), "c")])
+    dq, dk, dv, dk_far, dv_far = row_attention_back(info, tie, near, far, grad_heads)
+    grad_near = jnp.concatenate([dq, dk, dv], axis=-1).reshape(2 * count, 3 * half)
+    grad_far = jnp.concatenate([dk_far, dv_far], axis=-1).reshape(2 * count, 2 * half)
+    far_part = contract(grad_far, w_row[:, half:], LAST).reshape(2, count, width)
+    far_sum = far_part[0] + swap(far_part[1].astype(bf16), "c").astype(f32)
+    far_got = swap(far_sum.astype(bf16), "x")
+    near_part = contract(grad_near, w_row, LAST).reshape(2, count, width)
+    near_got = swap(near_part[1].astype(bf16), "c")
+    grad_normed_one = near_part[0] + near_got.astype(f32) + far_got.astype(f32)
+    _, norm_back_one = jax.vjp(layer_norm, resid_one, norm_gain[0], norm_gain[1])
+    part_one, gain_grad_one, shift_grad_one = norm_back_one(grad_normed_one)
+    grad_input = (grad_stream.astype(f32) + part_one).astype(bf16)
+    grad_tokens = to_rows(grad_input.reshape(rows, part, width), c).astype(f32)
+
+    attn_terms = over_cores(
+        [
+            (mixed_one, grad_stream, 1),
+            (normed_two, grad_qkv_two, 3),
+            (mixed_two, grad_branch_two, 1),
+        ]
+    )
+    attn_grad_b = summed_to_owner(jnp.concatenate(attn_terms, axis=1), x)
+    row_terms = contract(near_normed, grad_near, FIRST)
+    far_terms = contract(far_normed, grad_far, FIRST)
+    row_terms = jnp.concatenate([row_terms[:, :half], row_terms[:, half:] + far_terms], axis=1)
+    norm_stack = jnp.stack(
+        [
+            gain_grad_one,
+            shift_grad_one,
+            gain_grad_two,
+            shift_grad_two,
+            gain_grad_three,
+            shift_grad_three,
+        ]
+    )
+    norm_terms = jnp.moveaxis(norm_stack.reshape(6, 8, depth), 0, 1).reshape(8, 1, 6 * depth)
+    norm_terms = jnp.pad(norm_terms, ((0, 0), (0, 15), (0, 3 * half - 6 * depth)))
+    row_terms = jnp.concatenate(
+        [row_terms.reshape(8, depth, 3 * half), norm_terms], axis=1
+    ).astype(bf16)
+    row_grad = summed_to_owner(row_terms.reshape(8 * (depth + 16), 3 * half), x)
+
+    row_other = swap(row_grad, "c")
+    attn_other = swap(attn_grad_b, "c")
+    ffn_other = swap(ffn_grad, "c")
+    norm_grad = row_grad[depth, : 6 * depth].astype(f32) + row_other[depth, : 6 * depth].astype(f32)
+    norm_grad = norm_grad.reshape(6, depth)
+    row_parts = [
+        merge(a.reshape(depth, 3, half), b.reshape(depth, 3, half), c, 2)
+        for a, b in [(row_grad[:depth], row_other[:depth])]
+    ][0].reshape(depth, 3, width)
+    col_parts = merge(
+        attn_grad_b.reshape(depth, 5, half), attn_other.reshape(depth, 5, half), c, 2
+    ).reshape(depth, 5, width)
+    attn_grad = jnp.moveaxis(jnp.concatenate([row_parts, col_parts], axis=1), 1, 0).astype(f32)
+    ffn_parts = merge(ffn_grad, ffn_other, c, 2).reshape(depth, 2, hidden).astype(f32)
+    in_grad = ffn_parts[:, 0]
+    out_grad = ffn_parts[:, 1].T
+
+    squares = (
+        jnp.sum(attn_grad * attn_grad)
+        + jnp.sum(in_grad * in_grad)
+        + jnp.sum(out_grad * out_grad)
+        + jnp.sum(norm_grad * norm_grad)
+    )
+    grad_norm = jnp.sqrt(lax.psum(squares, ("z", "x")))
+    factor = clip_bound / jnp.maximum(grad_norm, clip_bound)
+    attn_first_new, attn_second_new, attn_weight_new = adam_update(
+        attn_weight, attn_first, attn_second, attn_grad * factor, matrix_rate
+    )
+    in_first_new, in_second_new, in_weight_new = adam_update(
+        in_weight, in_first, in_second, in_grad * factor, matrix_rate
+    )
+    out_first_new, out_second_new, out_weight_new = adam_update(
+        out_weight, out_first, out_second, out_grad * factor, matrix_rate
+    )
+    norm_first_new, norm_second_new, norm_new = adam_update(
+        norm_param, norm_first, norm_second, norm_grad * factor, norm_rate
+    )
+    return (
+        block_out,
+        grad_tokens,
+        grad_norm,
+        attn_first_new,
+        attn_second_new,
+        attn_weight_new,
+        attn_weight_new.astype(bf16),
+        in_first_new,
+        in_second_new,
+        in_weight_new,
+        in_weight_new.astype(bf16),
+        out_first_new,
+        out_second_new,
+        out_weight_new,
+        out_weight_new.astype(bf16),
+        norm_first_new,
+        norm_second_new,
+        norm_new,
+    )
+
+
+def paired_layout(mesh):
+    return dict(mesh.shape) == {"seq": 8, "grp": 4}
+
+
+def mapped(run, mesh, seq, grp):
     placed = (
-        P("grp", "seq", None, None),
-        P("grp", "seq", None, None),
-        P("grp"),
-        P("grp"),
-        P(None, "seq", None),
-        P("seq", None),
-        P(None, "seq"),
-        P(None, "seq"),
-        P(None, "seq", None),
-        P(None, "seq", None),
-        P("seq", None),
-        P("seq", None),
-        P(None, "seq"),
-        P(None, "seq"),
-        P(None, "seq"),
-        P(None, "seq"),
+        P(grp, seq, None, None),
+        P(grp, seq, None, None),
+        P(grp),
+        P(grp),
+        P(None, seq, None),
+        P(seq, None),
+        P(None, seq),
+        P(None, seq),
+        P(None, seq, None),
+        P(None, seq, None),
+        P(seq, None),
+        P(seq, None),
+        P(None, seq),
+        P(None, seq),
+        P(None, seq),
+        P(None, seq),
     )
     return jax.shard_map(
-        body,
+        run,
         mesh=mesh,
         in_specs=placed,
         out_specs=(
-            P("grp", "seq", None, None),
-            P("grp", "seq", None, None),
+            P(grp, seq, None, None),
+            P(grp, seq, None, None),
             P(),
-            P(None, "seq", None),
-            P(None, "seq", None),
-            P(None, "seq", None),
-            P(None, "seq", None),
-            P("seq", None),
-            P("seq", None),
-            P("seq", None),
-            P("seq", None),
-            P(None, "seq"),
-            P(None, "seq"),
-            P(None, "seq"),
-            P(None, "seq"),
-            P(None, "seq"),
-            P(None, "seq"),
-            P(None, "seq"),
+            P(None, seq, None),
+            P(None, seq, None),
+            P(None, seq, None),
+            P(None, seq, None),
+            P(seq, None),
+            P(seq, None),
+            P(seq, None),
+            P(seq, None),
+            P(None, seq),
+            P(None, seq),
+            P(None, seq),
+            P(None, seq),
+            P(None, seq),
+            P(None, seq),
+            P(None, seq),
         ),
         check_vma=False,
     )
+
+
+def solution(mesh):
+    if not paired_layout(mesh):
+        return mapped(general_body, mesh, "seq", "grp")
+    fine = Mesh(mesh.devices.reshape(4, 2, 2, 2), ("z", "x", "y", "c"))
+    return mapped(paired_body, fine, ("z", "x"), ("y", "c"))

time: 1620 us -> 1190 us (0.73)
  waiting for transfers between devices: 1100 us -> 206 us
  Pallas kernels: 0 us -> 585 us
  blocking collectives: 155 us -> 19.1 us
  starting transfers between devices: 11.6 us -> 91.7 us
  matrix products: 113 us -> 77 us
  local copies, waits for them, and re-layouts: 149 us -> 127 us
    unnamed x9 -> x0, waiting for transfers between devices: 613 us -> none
    pallas_call x0 -> x7, Pallas kernels: none -> 585 us  [the longest x3 534 us: placed_pieces(): pl.pallas_call(partial(place_kernel, plan, outs_at), in_specs=[pl.BlockSp...]
    all_gather x5 -> x0, waiting for transfers between devices: 300 us -> none  [the longest x1 113 us: body(): lax.all_gather(attn_weight.astype(bf16), 'seq', axis=1, tiled=True)]
    ppermute x0 -> x62, waiting for transfers between devices: none -> 177 us  [the longest x53 131 us: swap(): return lax.ppermute(value, axis, PAIR)]
    reduce_scatter x1 -> x0, waiting for transfers between devices: 116 us -> none  [body(): lax.psum_scatter(partial_scores, 'seq', scatter_dimension=2, tiled=True)]
    all_to_all x2 -> x0, blocking collectives: 97.1 us -> none  [the longest x1 73.9 us: sent_and_summed(): pieces = lax.all_to_all(in_blocks(x, dim, length), axis, 0, 0, tiled=True)]
    ppermute x0 -> x62, starting transfers between devices: none -> 58.8 us  [the longest x53 36.8 us: swap(): return lax.ppermute(value, axis, PAIR)]
    dynamic_slice x0 -> x10, local copies, waits for them, and re-layouts: none -> 43.2 us  [pick(): return lax.dynamic_index_in_dim(value, index, axis, keepdims=False)]
  transfers between devices with their start and end apart: 11 -> 69, of which waited for: 9 -> 17; matrix products, arithmetic and copies ran while one was open for 7% -> 15% of each run, Pallas kernels for 0% -> 46%
where the time goes in v1:
time: 1190 us; the launch traced here: 1180 us
  Pallas kernels  585 us (49%)
  waiting for transfers between devices  206 us (17%)
  local copies, waits for them, and re-layouts  127 us (11%)
  starting transfers between devices  91.7 us (8%)
  matrix products  77 us (6%)
  other arithmetic  63.4 us (5%)
  blocking collectives  19.1 us (2%)
    pallas_call x3, Pallas kernels, placed_pieces(): pl.pallas_call(partial(place_kernel, plan, outs_at), in_specs=[pl.BlockSp...  534 us
    ppermute x53, waiting for transfers between devices, swap(): return lax.ppermute(value, axis, PAIR)  131 us
    dot_general x26, matrix products, contract(): lax.dot_general(a, b, (dims, ((), ())), preferred_element_type=jnp.float32)  77 us
    ppermute x9, waiting for transfers between devices, gather_pieces(): over_z.append(lax.ppermute(own, 'z', [(k, k ^ i) for k in range(4)]))  45.6 us
    dynamic_slice x10, local copies, waits for them, and re-layouts, pick(): return lax.dynamic_index_in_dim(value, index, axis, keepdims=False)  43.2 us
    ppermute x53, starting transfers between devices, swap(): return lax.ppermute(value, axis, PAIR)  36.8 us
    unnamed x246, local copies, waits for them, and re-layouts  30.9 us
    all_to_all x3, waiting for transfers between devices, summed_to_owner(): parts = lax.all_to_all(column, 'z', 0, 0, tiled=True)  29.4 us
  transfers between devices with their start and end apart: 69, of which 17 were waited for; matrix products, arithmetic and copies ran while one was open for 15% of the time, Pallas kernels for 46%

profile of v1, /device:TPU:0, one launch (start us, length us, event | category | flops | bytes accessed | tf_op | source)
XLA Modules:
  0.0 1177.5 jit_solution(12068662706025043333)
XLA Ops:
  37.8 9.5 collective-permute-done.13.refs_1_
  50.4 24.3 %collective-permute-done.14.refs_2_ = bf16[5,96,384]{2,1,0:T(8,128)(2,1)S(1)} collective-permute-done((bf16[5,96,384]{2,1,0:T(8,128)(2,1)}, bf16[5,96,384]{2,1,0:T(8,128)(2,1)S(1)}, u32[]{:S(2)}, u32[]{:S(2)}) %collective-permute-start.14) | collective-permute-done | bytes 368672 | tf_op jit(solution)/shard_map/ppermute | solution.py:356
  74.7 8.1 collective-permute-start.28
  94.3 13.5 %collective-permute-done.8.refs_7_ = bf16[112,1152]{1,0:T(8,128)(2,1)} collective-permute-done((bf16[112,1152]{1,0:T(8,128)(2,1)}, bf16[112,1152]{1,0:T(8,128)(2,1)}, u32[]{:S(2)}, u32[]{:S(2)}) %collective-permute-start.8) | collective-permute-done | bytes 258080 | tf_op jit(solution)/shard_map/ppermute | solution.py:319
  110.7 11.9 %collective-permute-done.28.refs_2_ = bf16[2,96,1536]{2,1,0:T(8,128)(2,1)S(1)} collective-permute-done((bf16[2,96,1536]{2,1,0:T(8,128)(2,1)}, bf16[2,96,1536]{2,1,0:T(8,128)(2,1)S(1)}, u32[]{:S(2)}, u32[]{:S(2)}) %collective-permute-start.28) | collective-permute-done | bytes 589856 | tf_op jit(solution)/shard_map/ppermute | solution.py:356
  126.3 64.4 %shard_map.295 = (bf16[768,1152]{1,0:T(8,128)(2,1)}, bf16[8,16,1152]{2,1,0:T(8,128)(2,1)}) custom-call(s32[3]{0:T(128)} %pad_add_fusion.2.place_ref, bf16[112,1152]{1,0:T(8,128)(2,1)} %fusion.57.refs_0_, bf16[112,1152]{1,0:T(8,128)(2,1)} %collective-permute-done.2.refs_1_, bf16[112,1152]{1,0:T(8,128)(2,1)} %collective-permute-done.3.refs_2_, ...), custom_call_target="tpu_custom_call" | custom-call | bytes 4128768 | tf_op jit(solution)/shard_map/pallas_call | solution.py:380
  204.7 17.7 %collective-permute-done.31.refs_5_ = bf16[2,96,1536]{2,1,0:T(8,128)(2,1)} collective-permute-done((bf16[2,96,1536]{2,1,0:T(8,128)(2,1)S(1)}, bf16[2,96,1536]{2,1,0:T(8,128)(2,1)}, u32[]{:S(2)}, u32[]{:S(2)}) %collective-permute-start.31) | collective-permute-done | bytes 589856 | tf_op jit(solution)/shard_map/ppermute | solution.py:319
  222.4 12.6 %collective-permute-done.32.refs_6_ = bf16[2,96,1536]{2,1,0:T(8,128)(2,1)} collective-permute-done((bf16[2,96,1536]{2,1,0:T(8,128)(2,1)S(1)}, bf16[2,96,1536]{2,1,0:T(8,128)(2,1)}, u32[]{:S(2)}, u32[]{:S(2)}) %collective-permute-start.32) | collective-permute-done | bytes 589856 | tf_op jit(solution)/shard_map/ppermute | solution.py:319
  235.5 11.3 collective-permute-done.33.refs_7_
  255.4 181.2 %shard_map.297 = (bf16[768,768]{1,0:T(8,128)(2,1)}, bf16[768,2304]{1,0:T(8,128)(2,1)}, bf16[768,768]{1,0:T(8,128)(2,1)}) custom-call(s32[3]{0:T(128)} %pad_add_fusion.2.place_ref, bf16[5,96,384]{2,1,0:T(8,128)(2,1)} %bitcast.240.refs_0_, bf16[5,96,384]{2,1,0:T(8,128)(2,1)} %collective-permute-done.13.refs_1_, bf16[5,96,384]{2,1,0:T(8,128)(2,1)} %copy-done.63, ...), custom_call_target="tpu_custom_call" | custom-call | bytes 11796480 | tf_op jit(solution)/shard_map/pallas_call | solution.py:380
  436.6 288.0 %shard_map.299 = (bf16[768,3072]{1,0:T(8,128)(2,1)}, bf16[768,3072]{1,0:T(8,128)(2,1)}) custom-call(s32[3]{0:T(128)} %pad_add_fusion.2.place_ref, bf16[2,96,1536]{2,1,0:T(8,128)(2,1)} %get-tuple-element.92.refs_0_, bf16[2,96,1536]{2,1,0:T(8,128)(2,1)} %copy-done.55, bf16[2,96,1536]{2,1,0:T(8,128)(2,1)} %copy-done.56, ...), custom_call_target="tpu_custom_call" | custom-call | bytes 18874368 | tf_op jit(solution)/shard_map/pallas_call | solution.py:380
  746.5 16.6 %shard_map.298 = bf16[8,64,768]{2,1,0:T(8,128)(2,1)S(1)} custom-call(s32[5]{0:T(128)S(1)} %pad_add_fusion.1.info_ref, bf16[8,64,2304]{2,1,0:T(8,128)(2,1)S(1)} %bitcast.252), custom_call_target="tpu_custom_call" | custom-call | tf_op jit(solution)/shard_map/pallas_call | solution.py:640
  764.5 9.1 fusion.6
  779.8 8.3 reshape.521
  788.0 8.3 reshape.524
  808.1 23.3 %shard_map.300 = bf16[8,64,2304]{2,1,0:T(8,128)(2,1)S(1)} custom-call(s32[5]{0:T(128)S(1)} %pad_add_fusion.1.info_ref, bf16[8,64,2304]{2,1,0:T(8,128)(2,1)S(1)} %bitcast.253, bf16[8,64,768]{2,1,0:T(8,128)(2,1)S(1)} %bitcast.257), custom_call_target="tpu_custom_call" | custom-call | tf_op jit(solution)/shard_map/pallas_call | solution.py:652
  851.6 11.9 %constant_dynamic-slice_fusion.1 = (bf16[512,1,1,1536]{3,2,0,1:T(2,128)(2,1)}, bf16[512,1,1,1536]{3,2,0,1:T(2,128)(2,1)}) fusion(bf16[512,1,2,1536]{3,2,0,1:T(2,128)(2,1)} %reshape.524, s32[]{:T(128)S(6)} %select_n.183, s32[]{:T(128)S(6)} %select_n.184), kind=kLoop, calls=%fused_computation.187 | loop fusion | bytes 6291464 | tf_op jit(solution)/shard_map/jit(dynamic_index_in_dim)/dynamic_slice | solution.py:323
  868.9 9.6 constant_dynamic-slice_fusion.3
  911.8 13.6 %collective-permute-done.46 = bf16[512,768]{1,0:T(8,128)(2,1)S(1)} collective-permute-done((bf16[512,768]{1,0:T(8,128)(2,1)S(1)}, bf16[512,768]{1,0:T(8,128)(2,1)S(1)}, u32[]{:S(2)}, u32[]{:S(2)}) %collective-permute-start.46) | collective-permute-done | bytes 786464 | tf_op jit(solution)/shard_map/ppermute | solution.py:319
  955.8 9.4 constant_dynamic-slice_fusion.7
  999.4 13.9 %collective-permute-done.59 = bf16[4,96,2,1536]{3,1,2,0:T(8,128)(2,1)} collective-permute-done((bf16[4,96,2,1536]{3,1,2,0:T(8,128)(2,1)}, bf16[4,96,2,1536]{3,1,2,0:T(8,128)(2,1)}, u32[]{:S(2)}, u32[]{:S(2)}) %collective-permute-start.59) | collective-permute-done | bytes 2359328 | tf_op jit(solution)/shard_map/ppermute | solution.py:319
  1033.4 30.9 %collective-permute-done.54 = bf16[4,96,1920]{2,1,0:T(8,128)(2,1)S(1)} collective-permute-done((bf16[4,96,1920]{2,1,0:T(8,128)(2,1)S(1)}, bf16[4,96,1920]{2,1,0:T(8,128)(2,1)S(1)}, u32[]{:S(2)}, u32[]{:S(2)}) %collective-permute-start.54) | collective-permute-done | bytes 1474592 | tf_op jit(solution)/shard_map/ppermute | solution.py:319
  1091.2 21.5 %all-to-all-done.5 = bf16[4,96,1920]{2,1,0:T(8,128)(2,1)} async-done(((bf16[4,96,1920]{2,1,0:T(8,128)(2,1)}), bf16[4,96,1920]{2,1,0:T(8,128)(2,1)}, u32[]{:S(2)}, u32[]{:S(2)}) %all-to-all-start.5) | async-done | bytes 1474592 | tf_op jit(solution)/shard_map/all_to_all | solution.py:673
  1141.3 19.1 %psum.7 = f32[]{:T(128)} all-reduce(f32[]{:T(128)S(6)} %add.342), channel_id=1, replica_groups=mesh['z'=4,'x'=2,'y'=2,'c'=2] {'z','x'}, use_global_device_ids=true, to_apply=%region_25.26 | all-reduce | flops 1 | bytes 8 | tf_op jit(solution)/shard_map/psum | solution.py:879
  (539 shorter events, 331.5 us)
Async XLA Ops:
  20.4 173.3 %all-to-all-start = ((bf16[8,64,768]{2,1,0:T(8,128)(2,1)}), bf16[8,64,768]{2,1,0:T(8,128)(2,1)S(1)}, u32[]{:S(2)}, u32[]{:S(2)}) async-start(bf16[8,64,768]{2,1,0:T(8,128)(2,1)} %bitcast.4), calls=%async_computation | async-start | bytes 1572864 | tf_op jit(solution)/shard_map/all_to_all | solution.py:341
  28.5 46.2 %collective-permute-start.14 = (bf16[5,96,384]{2,1,0:T(8,128)(2,1)}, bf16[5,96,384]{2,1,0:T(8,128)(2,1)S(1)}, u32[]{:S(2)}, u32[]{:S(2)}) collective-permute-start(bf16[5,96,384]{2,1,0:T(8,128)(2,1)} %bitcast.240.refs_0_), channel_id=1, source_target_pairs={{0,16},{8,24},{16,0},{24,8},{1,17},{9,25},{17,1},{25,9},{2,18},{10... | collective-permute-start | bytes 1105928 | tf_op jit(solution)/shard_map/ppermute | solution.py:356
  33.3 49.6 %collective-permute-start.16 = (bf16[5,96,384]{2,1,0:T(8,128)(2,1)}, bf16[5,96,384]{2,1,0:T(8,128)(2,1)}, u32[]{:S(2)}, u32[]{:S(2)}) collective-permute-start(bf16[5,96,384]{2,1,0:T(8,128)(2,1)} %bitcast.240.refs_0_), channel_id=1, source_target_pairs={{0,4},{4,0},{1,5},{5,1},{2,6},{6,2},{3,7},{7,3},{8,12},{12,8},{9,1... | collective-permute-start | bytes 1105928 | tf_op jit(solution)/shard_map/ppermute | solution.py:319
  37.7 46.6 %collective-permute-start.42 = (bf16[2,2,64,768]{3,2,1,0:T(8,128)(2,1)S(1)}, bf16[2,2,64,768]{3,2,1,0:T(8,128)(2,1)}, u32[]{:S(2)}, u32[]{:S(2)}) collective-permute-start(bf16[2,2,64,768]{3,2,1,0:T(8,128)(2,1)S(1)} %get-tuple-element.102), channel_id=1, source_target_pairs={{0,1},{1,0},{2,3},{3,2},{4,5},{5,4},{6,7},{7,6},{8,9},{9,8},{10,11... | collective-permute-start | bytes 1179656 | tf_op jit(solution)/shard_map/ppermute | solution.py:319
  74.7 47.9 %collective-permute-start.28 = (bf16[2,96,1536]{2,1,0:T(8,128)(2,1)}, bf16[2,96,1536]{2,1,0:T(8,128)(2,1)S(1)}, u32[]{:S(2)}, u32[]{:S(2)}) collective-permute-start(bf16[2,96,1536]{2,1,0:T(8,128)(2,1)} %get-tuple-element.92.refs_0_), channel_id=1, source_target_pairs={{0,16},{8,24},{16,0},{24,8},{1,17},{9,25},{17,1},{25,9},{2,18},{10... | collective-permute-start | bytes 1769480 | tf_op jit(solution)/shard_map/ppermute | solution.py:356
  84.4 106.4 %collective-permute-start.29 = (bf16[2,96,1536]{2,1,0:T(8,128)(2,1)}, bf16[2,96,1536]{2,1,0:T(8,128)(2,1)}, u32[]{:S(2)}, u32[]{:S(2)}) collective-permute-start(bf16[2,96,1536]{2,1,0:T(8,128)(2,1)} %get-tuple-element.92.refs_0_), channel_id=1, source_target_pairs={{0,24},{8,16},{16,8},{24,0},{1,25},{9,17},{17,9},{25,1},{2,26},{10... | collective-permute-start | bytes 1769480 | tf_op jit(solution)/shard_map/ppermute | solution.py:356
  85.7 105.1 %collective-permute-start.30 = (bf16[2,96,1536]{2,1,0:T(8,128)(2,1)}, bf16[2,96,1536]{2,1,0:T(8,128)(2,1)}, u32[]{:S(2)}, u32[]{:S(2)}) collective-permute-start(bf16[2,96,1536]{2,1,0:T(8,128)(2,1)} %get-tuple-element.92.refs_0_), channel_id=1, source_target_pairs={{0,4},{4,0},{1,5},{5,1},{2,6},{6,2},{3,7},{7,3},{8,12},{12,8},{9,1... | collective-permute-start | bytes 1769480 | tf_op jit(solution)/shard_map/ppermute | solution.py:319
  107.9 85.2 %collective-permute-start.17 = (bf16[5,96,384]{2,1,0:T(8,128)(2,1)}, bf16[5,96,384]{2,1,0:T(8,128)(2,1)S(1)}, u32[]{:S(2)}, u32[]{:S(2)}) collective-permute-start(bf16[5,96,384]{2,1,0:T(8,128)(2,1)} %collective-permute-done.13.refs_1_), channel_id=1, source_target_pairs={{0,4},{4,0},{1,5},{5,1},{2,6},{6,2},{3,7},{7,3},{8,12},{12,8},{9,1... | collective-permute-start | bytes 1105928 | tf_op jit(solution)/shard_map/ppermute | solution.py:319
  109.4 83.9 %collective-permute-start.18 = (bf16[5,96,384]{2,1,0:T(8,128)(2,1)}, bf16[5,96,384]{2,1,0:T(8,128)(2,1)}, u32[]{:S(2)}, u32[]{:S(2)}) collective-permute-start(bf16[5,96,384]{2,1,0:T(8,128)(2,1)} %copy-done.63), channel_id=1, source_target_pairs={{0,4},{4,0},{1,5},{5,1},{2,6},{6,2},{3,7},{7,3},{8,12},{12,8},{9,1... | collective-permute-start | bytes 1105928 | tf_op jit(solution)/shard_map/ppermute | solution.py:319
  122.6 75.1 %collective-permute-start.19 = (bf16[5,96,384]{2,1,0:T(8,128)(2,1)}, bf16[5,96,384]{2,1,0:T(8,128)(2,1)}, u32[]{:S(2)}, u32[]{:S(2)}) collective-permute-start(bf16[5,96,384]{2,1,0:T(8,128)(2,1)} %collective-permute-done.15.refs_3_), channel_id=1, source_target_pairs={{0,4},{4,0},{1,5},{5,1},{2,6},{6,2},{3,7},{7,3},{8,12},{12,8},{9,1... | collective-permute-start | bytes 1105928 | tf_op jit(solution)/shard_map/ppermute | solution.py:319
  193.9 531.2 %all-to-all-start.2 = ((bf16[8,64,768]{2,1,0:T(8,128)(2,1)}), bf16[8,64,768]{2,1,0:T(8,128)(2,1)S(1)}, u32[]{:S(2)}, u32[]{:S(2)}) async-start(bf16[8,64,768]{2,1,0:T(8,128)(2,1)} %bitcast.39), calls=%async_computation.2 | async-start | bytes 1572864 | tf_op jit(solution)/shard_map/all_to_all | solution.py:341
  200.1 46.8 %collective-permute-start.33 = (bf16[2,96,1536]{2,1,0:T(8,128)(2,1)}, bf16[2,96,1536]{2,1,0:T(8,128)(2,1)}, u32[]{:S(2)}, u32[]{:S(2)}) collective-permute-start(bf16[2,96,1536]{2,1,0:T(8,128)(2,1)} %collective-permute-done.29.refs_3_), channel_id=1, source_target_pairs={{0,4},{4,0},{1,5},{5,1},{2,6},{6,2},{3,7},{7,3},{8,12},{12,8},{9,1... | collective-permute-start | bytes 1769480 | tf_op jit(solution)/shard_map/ppermute | solution.py:319
  203.9 44.2 %collective-permute-start.34 = (bf16[2,96,1536]{2,1,0:T(8,128)(2,1)S(1)}, bf16[2,96,1536]{2,1,0:T(8,128)(2,1)S(1)}, u32[]{:S(2)}, u32[]{:S(2)}) collective-permute-start(bf16[2,96,1536]{2,1,0:T(8,128)(2,1)S(1)} %collective-permute-done.27.refs_1_), channel_id=1, source_target_pairs={{0,1},{1,0},{2,3},{3,2},{4,5},{5,4},{6,7},{7,6},{8,9},{9,8},{10,11... | collective-permute-start | bytes 1769480 | tf_op jit(solution)/shard_map/ppermute | solution.py:319
  246.9 477.7 %collective-permute-start.10 = (bf16[512,768]{1,0:T(8,128)(2,1)S(1)}, bf16[512,768]{1,0:T(8,128)(2,1)}, u32[]{:S(2)}, u32[]{:S(2)}) collective-permute-start(bf16[512,768]{1,0:T(8,128)(2,1)S(1)} %fusion.37), channel_id=1, source_target_pairs={{0,4},{4,0},{1,5},{5,1},{2,6},{6,2},{3,7},{7,3},{8,12},{12,8},{9,1... | collective-permute-start | bytes 2359304 | tf_op jit(solution)/shard_map/ppermute | solution.py:319
  248.1 188.5 %collective-permute-start.38 = (bf16[2,96,1536]{2,1,0:T(8,128)(2,1)}, bf16[2,96,1536]{2,1,0:T(8,128)(2,1)}, u32[]{:S(2)}, u32[]{:S(2)}) collective-permute-start(bf16[2,96,1536]{2,1,0:T(8,128)(2,1)} %collective-permute-done.31.refs_5_), channel_id=1, source_target_pairs={{0,1},{1,0},{2,3},{3,2},{4,5},{5,4},{6,7},{7,6},{8,9},{9,8},{10,11... | collective-permute-start | bytes 1769480 | tf_op jit(solution)/shard_map/ppermute | solution.py:319
  248.2 188.4 %collective-permute-start.39 = (bf16[2,96,1536]{2,1,0:T(8,128)(2,1)}, bf16[2,96,1536]{2,1,0:T(8,128)(2,1)}, u32[]{:S(2)}, u32[]{:S(2)}) collective-permute-start(bf16[2,96,1536]{2,1,0:T(8,128)(2,1)} %collective-permute-done.32.refs_6_), channel_id=1, source_target_pairs={{0,1},{1,0},{2,3},{3,2},{4,5},{5,4},{6,7},{7,6},{8,9},{9,8},{10,11... | collective-permute-start | bytes 1769480 | tf_op jit(solution)/shard_map/ppermute | solution.py:319
  248.7 187.9 %collective-permute-start.40 = (bf16[2,96,1536]{2,1,0:T(8,128)(2,1)}, bf16[2,96,1536]{2,1,0:T(8,128)(2,1)}, u32[]{:S(2)}, u32[]{:S(2)}) collective-permute-start(bf16[2,96,1536]{2,1,0:T(8,128)(2,1)} %collective-permute-done.33.refs_7_), channel_id=1, source_target_pairs={{0,1},{1,0},{2,3},{3,2},{4,5},{5,4},{6,7},{7,6},{8,9},{9,8},{10,11... | collective-permute-start | bytes 1769480 | tf_op jit(solution)/shard_map/ppermute | solution.py:319
  249.5 477.3 %collective-permute-start.9 = (bf16[512,768]{1,0:T(8,128)(2,1)S(1)}, bf16[512,768]{1,0:T(8,128)(2,1)S(1)}, u32[]{:S(2)}, u32[]{:S(2)}) collective-permute-start(bf16[512,768]{1,0:T(8,128)(2,1)S(1)} %fusion.37), channel_id=1, source_target_pairs={{0,1},{1,0},{2,3},{3,2},{4,5},{5,4},{6,7},{7,6},{8,9},{9,8},{10,11... | collective-permute-start | bytes 2359304 | tf_op jit(solution)/shard_map/ppermute | solution.py:319
  868.7 64.5 %collective-permute-start.58 = (bf16[768,1536]{1,0:T(8,128)(2,1)}, bf16[768,1536]{1,0:T(8,128)(2,1)}, u32[]{:S(2)}, u32[]{:S(2)}) collective-permute-start(bf16[768,1536]{1,0:T(8,128)(2,1)} %convolution_convert_fusion.2), channel_id=1, source_target_pairs={{0,1},{1,0},{2,3},{3,2},{4,5},{5,4},{6,7},{7,6},{8,9},{9,8},{10,11... | collective-permute-start | bytes 7077896 | tf_op jit(solution)/shard_map/ppermute | solution.py:319
  883.9 53.4 %collective-permute-start.57 = (bf16[768,1536]{1,0:T(8,128)(2,1)}, bf16[768,1536]{1,0:T(8,128)(2,1)}, u32[]{:S(2)}, u32[]{:S(2)}) collective-permute-start(bf16[768,1536]{1,0:T(8,128)(2,1)} %convolution_convert_fusion.3), channel_id=1, source_target_pairs={{0,1},{1,0},{2,3},{3,2},{4,5},{5,4},{6,7},{7,6},{8,9},{9,8},{10,11... | collective-permute-start | bytes 7077896 | tf_op jit(solution)/shard_map/ppermute | solution.py:319
  884.3 57.8 %all-to-all-start.1 = ((bf16[8,64,768]{2,1,0:T(8,128)(2,1)}), bf16[8,64,768]{2,1,0:T(8,128)(2,1)}, u32[]{:S(2)}, u32[]{:S(2)}) async-start(bf16[8,64,768]{2,1,0:T(8,128)(2,1)} %bitcast.292), calls=%async_computation.1 | async-start | bytes 1572864 | tf_op jit(solution)/shard_map/all_to_all | solution.py:346
  951.7 61.6 %collective-permute-start.59 = (bf16[4,96,2,1536]{3,1,2,0:T(8,128)(2,1)}, bf16[4,96,2,1536]{3,1,2,0:T(8,128)(2,1)}, u32[]{:S(2)}, u32[]{:S(2)}) collective-permute-start(bf16[4,96,2,1536]{3,1,2,0:T(8,128)(2,1)} %bitcast.236), channel_id=1, source_target_pairs={{0,4},{4,0},{1,5},{5,1},{2,6},{6,2},{3,7},{7,3},{8,12},{12,8},{9,1... | collective-permute-start | bytes 7077896 | tf_op jit(solution)/shard_map/ppermute | solution.py:319
  981.9 46.5 %collective-permute-start.52 = (bf16[768,1152]{1,0:T(8,128)(2,1)}, bf16[768,1152]{1,0:T(8,128)(2,1)}, u32[]{:S(2)}, u32[]{:S(2)}) collective-permute-start(bf16[768,1152]{1,0:T(8,128)(2,1)} %convolution_convert_fusion.4), channel_id=1, source_target_pairs={{0,1},{1,0},{2,3},{3,2},{4,5},{5,4},{6,7},{7,6},{8,9},{9,8},{10,11... | collective-permute-start | bytes 5308424 | tf_op jit(solution)/shard_map/ppermute | solution.py:319
  1017.1 56.7 %all-to-all-start.6 = ((bf16[4,96,2,1536]{3,1,2,0:T(8,128)(2,1)}), bf16[4,96,2,1536]{3,1,2,0:T(8,128)(2,1)S(1)}, u32[]{:S(2)}, u32[]{:S(2)}) async-start(bf16[4,96,2,1536]{3,1,2,0:T(8,128)(2,1)} %fusion.7), calls=%async_computation.6 | async-start | bytes 4718592 | tf_op jit(solution)/shard_map/all_to_all | solution.py:673
  (160 other events, 4466.0 us)

commit v2 on v1

--- a/solution.py
+++ b/solution.py
@@ -323,6 +323,14 @@
     return lax.dynamic_index_in_dim(value, index, axis, keepdims=False)
 
 
+def joined(own, other, place, axis):
+    return jnp.where(
+        place == 0,
+        jnp.concatenate([own, other], axis=axis),
+        jnp.concatenate([other, own], axis=axis),
+    )
+
+
 def merge(own, other, place, axis):
     return jnp.where(
         place == 0,
@@ -380,9 +388,12 @@
     return pl.pallas_call(
         partial(place_kernel, plan, outs_at),
         in_specs=[pl.BlockSpec(memory_space=pltpu.SMEM)] + [anywhere] * len(pieces),
-        out_specs=[anywhere] * len(outs),
+        out_specs=[pl.BlockSpec(memory_space=pltpu.VMEM)] * len(outs),
         out_shape=[jax.ShapeDtypeStruct(shape, jnp.bfloat16) for shape in outs],
         scratch_shapes=[pltpu.SemaphoreType.DMA((count,))],
+        compiler_params=pltpu.CompilerParams(
+            vmem_limit_bytes=sum(2 * math.prod(s) for s in outs) + 2 * 2**20
+        ),
         cost_estimate=pl.CostEstimate(
             flops=0, transcendentals=0, bytes_accessed=sum(4 * math.prod(s) for s in outs)
         ),
@@ -756,7 +767,9 @@
     far = contract(far_normed, w_row[:, half:], PLAIN).astype(bf16)
     far = far.reshape(2, rows, part, 2 * half)
     mixed_heads = row_attention(info, tie, near, far)
-    mixed_one = merge(mixed_heads[0], swap(mixed_heads[1], "c"), c, 2).reshape(count, width)
+    mixed_one = joined(
+        mixed_heads[0].reshape(count, half), swap(mixed_heads[1].reshape(count, half), "c"), c, 1
+    )
     stream_one = (resid_one + contract(mixed_one, w_three, PLAIN)).astype(bf16)
 
     resid_two = stream_one.astype(f32)
@@ -782,8 +795,13 @@
     grad_inner = gelu_back(grad_act)[0].astype(bf16)
 
     def lanes_of(value, which, groups):
-        split = value.reshape(value.shape[0], groups, 2, value.shape[1] // (2 * groups))
-        return pick(split, which, 2).reshape(value.shape[0], value.shape[1] // 2)
+        size = value.shape[1] // (2 * groups)
+        first, second = (
+            [value[:, (2 * n + k) * size : (2 * n + k + 1) * size] for n in range(groups)]
+            for k in (0, 1)
+        )
+        chosen = [jnp.where(which == 0, a, b) for a, b in zip(first, second)]
+        return chosen[0] if groups == 1 else jnp.concatenate(chosen, axis=1)
 
     def over_cores(sides):
         sent = [contract(a, lanes_of(b, 1 - c, g), FIRST).astype(bf16) for a, b, g in sides]
@@ -792,7 +810,7 @@
         return [(k + v.astype(f32)).astype(bf16) for k, v in zip(kept, got)]
 
     ffn_terms = over_cores([(normed_three, grad_inner, 1), (up, activ, 1)])
-    ffn_grad = summed_to_owner(jnp.stack(ffn_terms, axis=1), x)
+    ffn_grad = summed_to_owner(jnp.concatenate(ffn_terms, axis=1), x)
     grad_normed_three = contract(grad_inner, w_in, LAST)
     _, norm_back_three = jax.vjp(layer_norm, resid_three, norm_gain[4], norm_gain[5])
     part_three, gain_grad_three, shift_grad_three = norm_back_three(grad_normed_three)
@@ -809,8 +827,9 @@
     grad_stream = (grad_three + part_two).astype(bf16)
 
     grad_mixed_one = contract(grad_stream, w_three, LAST).astype(bf16)
-    split = grad_mixed_one.reshape(rows, part, 2, half)
-    grad_heads = jnp.stack([pick(split, c, 2), swap(pick(split, 1 - c, 2), "c")])
+    grad_heads = jnp.stack(
+        [lanes_of(grad_mixed_one, c, 1), swap(lanes_of(grad_mixed_one, 1 - c, 1), "c")]
+    ).reshape(2, rows, part, half)
     dq, dk, dv, dk_far, dv_far = row_attention_back(info, tie, near, far, grad_heads)
     grad_near = jnp.concatenate([dq, dk, dv], axis=-1).reshape(2 * count, 3 * half)
     grad_far = jnp.concatenate([dk_far, dv_far], axis=-1).reshape(2 * count, 2 * half)
@@ -858,17 +877,18 @@
     ffn_other = swap(ffn_grad, "c")
     norm_grad = row_grad[depth, : 6 * depth].astype(f32) + row_other[depth, : 6 * depth].astype(f32)
     norm_grad = norm_grad.reshape(6, depth)
-    row_parts = [
-        merge(a.reshape(depth, 3, half), b.reshape(depth, 3, half), c, 2)
-        for a, b in [(row_grad[:depth], row_other[:depth])]
-    ][0].reshape(depth, 3, width)
-    col_parts = merge(
-        attn_grad_b.reshape(depth, 5, half), attn_other.reshape(depth, 5, half), c, 2
-    ).reshape(depth, 5, width)
-    attn_grad = jnp.moveaxis(jnp.concatenate([row_parts, col_parts], axis=1), 1, 0).astype(f32)
-    ffn_parts = merge(ffn_grad, ffn_other, c, 2).reshape(depth, 2, hidden).astype(f32)
-    in_grad = ffn_parts[:, 0]
-    out_grad = ffn_parts[:, 1].T
+    def whole(own, other, groups):
+        size = own.shape[1] // groups
+        return [
+            joined(own[:depth, n * size : (n + 1) * size], other[:depth, n * size : (n + 1) * size], c, 1)
+            for n in range(groups)
+        ]
+
+    attn_grad = jnp.stack(whole(row_grad, row_other, 3) + whole(attn_grad_b, attn_other, 5))
+    attn_grad = attn_grad.astype(f32)
+    in_grad, out_grad = whole(ffn_grad, ffn_other, 2)
+    in_grad = in_grad.astype(f32)
+    out_grad = out_grad.astype(f32).T
 
     squares = (
         jnp.sum(attn_grad * attn_grad)

time: 1190 us -> 635 us (0.53)
  Pallas kernels: 585 us -> 62.6 us
  local copies, waits for them, and re-layouts: 127 us -> 54.8 us
  waiting for transfers between devices: 206 us -> 239 us
  other arithmetic: 63.4 us -> 79.8 us
    pallas_call x3, Pallas kernels: 534 us -> 10.6 us  [placed_pieces(): pl.pallas_call(partial(place_kernel, plan, outs_at), in_specs=[pl.BlockSp...]
    dynamic_slice x10 -> x4, local copies, waits for them, and re-layouts: 43.2 us -> 3.35 us  [pick(): return lax.dynamic_index_in_dim(value, index, axis, keepdims=False)]
    ppermute x53, waiting for transfers between devices: 131 us -> 156 us  [swap(): return lax.ppermute(value, axis, PAIR)]
    reshape x5 -> x0, local copies, waits for them, and re-layouts: 22.4 us -> none  [the longest x4 19.4 us: lanes_of(): value.reshape(value.shape[0], groups, 2, value.shape[1] // (2 * groups))]
    unnamed x246 -> x256, local copies, waits for them, and re-layouts: 30.9 us -> 31.6 us
  transfers between devices with their start and end apart: 69 -> 69, of which waited for: 17 -> 17; matrix products, arithmetic and copies ran while one was open for 15% -> 21% of each run, Pallas kernels for 46% -> 3%
where the time goes in v2:
time: 635 us; the launch traced here: 627 us
  waiting for transfers between devices  239 us (38%)
  starting transfers between devices  87.2 us (14%)
  other arithmetic  79.8 us (13%)
  matrix products  76.1 us (12%)
  Pallas kernels  62.6 us (10%)
  local copies, waits for them, and re-layouts  54.8 us (9%)
  blocking collectives  19.3 us (3%)
  between operations  7.82 us (1%)
    ppermute x53, waiting for transfers between devices, swap(): return lax.ppermute(value, axis, PAIR)  156 us
    dot_general x26, matrix products, contract(): lax.dot_general(a, b, (dims, ((), ())), preferred_element_type=jnp.float32)  76.1 us
    ppermute x9, waiting for transfers between devices, gather_pieces(): over_z.append(lax.ppermute(own, 'z', [(k, k ^ i) for k in range(4)]))  49 us
    all_to_all x3, waiting for transfers between devices, summed_to_owner(): parts = lax.all_to_all(column, 'z', 0, 0, tiled=True)  34.3 us
    ppermute x53, starting transfers between devices, swap(): return lax.ppermute(value, axis, PAIR)  33.9 us
    unnamed x256, local copies, waits for them, and re-layouts  31.6 us
    pallas_call x1, Pallas kernels, column_attention_back(): pl.pallas_call(col_bwd_kernel, grid=(cols // part,), in_specs=[pl.BlockSp...  23.4 us
    ppermute x9, starting transfers between devices, gather_pieces(): over_z.append(lax.ppermute(own, 'z', [(k, k ^ i) for k in range(4)]))  19.7 us
  transfers between devices with their start and end apart: 69, of which 17 were waited for; matrix products, arithmetic and copies ran while one was open for 21% of the time, Pallas kernels for 3%

profile of v2, /device:TPU:0, one launch (start us, length us, event | category | flops | bytes accessed | tf_op | source)
XLA Modules:
  0.0 626.7 jit_solution(16686443526052741009)
XLA Ops:
  33.7 13.7 %collective-permute-done.13.refs_1_ = bf16[5,96,384]{2,1,0:T(8,128)(2,1)} collective-permute-done((bf16[5,96,384]{2,1,0:T(8,128)(2,1)S(1)}, bf16[5,96,384]{2,1,0:T(8,128)(2,1)}, u32[]{:S(2)}, u32[]{:S(2)}) %collective-permute-start.13) | collective-permute-done | bytes 368672 | tf_op jit(solution)/shard_map/ppermute | solution.py:364
  49.6 24.4 %collective-permute-done.14.refs_2_ = bf16[5,96,384]{2,1,0:T(8,128)(2,1)} collective-permute-done((bf16[5,96,384]{2,1,0:T(8,128)(2,1)S(1)}, bf16[5,96,384]{2,1,0:T(8,128)(2,1)}, u32[]{:S(2)}, u32[]{:S(2)}) %collective-permute-start.14) | collective-permute-done | bytes 368672 | tf_op jit(solution)/shard_map/ppermute | solution.py:364
  74.0 8.0 %collective-permute-start.28 = (bf16[2,96,1536]{2,1,0:T(8,128)(2,1)S(1)}, bf16[2,96,1536]{2,1,0:T(8,128)(2,1)S(1)}, u32[]{:S(2)}, u32[]{:S(2)}) collective-permute-start(bf16[2,96,1536]{2,1,0:T(8,128)(2,1)S(1)} %get-tuple-element.88.refs_0_), channel_id=1, source_target_pairs={{0,16},{8,24},{16,0},{24,8},{1,17},{9,25},{17,1},{25,9},{2,18},{10... | collective-permute-start | bytes 1769480 | tf_op jit(solution)/shard_map/ppermute | solution.py:364
  93.5 13.3 %collective-permute-done.8.refs_7_ = bf16[112,1152]{1,0:T(8,128)(2,1)S(1)} collective-permute-done((bf16[112,1152]{1,0:T(8,128)(2,1)}, bf16[112,1152]{1,0:T(8,128)(2,1)S(1)}, u32[]{:S(2)}, u32[]{:S(2)}) %collective-permute-start.8) | collective-permute-done | bytes 258080 | tf_op jit(solution)/shard_map/ppermute | solution.py:319
  110.7 10.9 %collective-permute-done.28.refs_2_ = bf16[2,96,1536]{2,1,0:T(8,128)(2,1)S(1)} collective-permute-done((bf16[2,96,1536]{2,1,0:T(8,128)(2,1)S(1)}, bf16[2,96,1536]{2,1,0:T(8,128)(2,1)S(1)}, u32[]{:S(2)}, u32[]{:S(2)}) %collective-permute-start.28) | collective-permute-done | bytes 589856 | tf_op jit(solution)/shard_map/ppermute | solution.py:364
  131.6 5.1 all-to-all-start.2
  145.7 15.1 %collective-permute-done.31.refs_5_ = bf16[2,96,1536]{2,1,0:T(8,128)(2,1)} collective-permute-done((bf16[2,96,1536]{2,1,0:T(8,128)(2,1)S(1)}, bf16[2,96,1536]{2,1,0:T(8,128)(2,1)}, u32[]{:S(2)}, u32[]{:S(2)}) %collective-permute-start.31) | collective-permute-done | bytes 589856 | tf_op jit(solution)/shard_map/ppermute | solution.py:319
  160.7 12.6 %collective-permute-done.32.refs_6_ = bf16[2,96,1536]{2,1,0:T(8,128)(2,1)} collective-permute-done((bf16[2,96,1536]{2,1,0:T(8,128)(2,1)S(1)}, bf16[2,96,1536]{2,1,0:T(8,128)(2,1)}, u32[]{:S(2)}, u32[]{:S(2)}) %collective-permute-start.32) | collective-permute-done | bytes 589856 | tf_op jit(solution)/shard_map/ppermute | solution.py:319
  175.7 10.0 %collective-permute-done.33.refs_7_ = bf16[2,96,1536]{2,1,0:T(8,128)(2,1)} collective-permute-done((bf16[2,96,1536]{2,1,0:T(8,128)(2,1)}, bf16[2,96,1536]{2,1,0:T(8,128)(2,1)}, u32[]{:S(2)}, u32[]{:S(2)}) %collective-permute-start.33) | collective-permute-done | bytes 589856 | tf_op jit(solution)/shard_map/ppermute | solution.py:319
  232.5 16.6 %shard_map.298 = bf16[8,64,768]{2,1,0:T(8,128)(2,1)S(1)} custom-call(s32[5]{0:T(128)S(1)} %pad_add_fusion.1.info_ref, bf16[8,64,2304]{2,1,0:T(8,128)(2,1)S(1)} %bitcast.206), custom_call_target="tpu_custom_call" | custom-call | tf_op jit(solution)/shard_map/pallas_call | solution.py:651
  250.4 9.4 %fusion.6 = (bf16[512,3072]{1,0:T(8,128)(2,1)S(1)}, bf16[512,3072]{1,0:T(8,128)(2,1)}) fusion(f32[512,3072]{1,0:T(8,128)S(1)} %fusion.147, bf16[768,3072]{1,0:T(8,128)(2,1)S(1)} %bitcast.223, f32[512,768]{1,0:T(8,128)S(1)} %get-tuple-element.128, f32[768]{0:T(1024)S(1)} %add.294, f32[768]{0:T(1024)S(1)} %mul.395, f32[512]{0:T(512)S(1)} %fusion.120, ...), kind=kOutput, calls=%fused_computation.8 | convolution fusion | flops 2452488192 | bytes 18884608 | tf_op jit(solution)/shard_map/dot_general | solution.py:436
  264.7 23.4 %shard_map.300 = bf16[8,64,2304]{2,1,0:T(8,128)(2,1)S(1)} custom-call(s32[5]{0:T(128)S(1)} %pad_add_fusion.1.info_ref, bf16[8,64,2304]{2,1,0:T(8,128)(2,1)S(1)} %bitcast.207, bf16[8,64,768]{2,1,0:T(8,128)(2,1)S(1)} %bitcast.221), custom_call_target="tpu_custom_call" | custom-call | tf_op jit(solution)/shard_map/pallas_call | solution.py:663
  312.3 5.7 all-to-all-start.1
  318.0 5.0 convolution_convert_fusion.2
  324.5 7.9 %shard_map.301 = (bf16[2,8,64,384]{3,2,1,0:T(8,128)(2,1)S(1)}, bf16[2,8,64,384]{3,2,1,0:T(8,128)(2,1)S(1)}, bf16[2,8,64,384]{3,2,1,0:T(8,128)(2,1)S(1)}, bf16[2,...) custom-call(s32[5]{0:T(128)S(1)} %pad_add_fusion.1.info_ref, f32[1]{0:T(128)} %bitcast.12.tie_ref, ...), custom_call_target="tpu_custom_call" | custom-call | tf_op jit(solution)/shard_map/pallas_call | solution.py:573
  361.6 14.0 %collective-permute-done.46 = bf16[512,768]{1,0:T(8,128)(2,1)S(1)} collective-permute-done((bf16[512,768]{1,0:T(8,128)(2,1)S(1)}, bf16[512,768]{1,0:T(8,128)(2,1)S(1)}, u32[]{:S(2)}, u32[]{:S(2)}) %collective-permute-start.46) | collective-permute-done | bytes 786464 | tf_op jit(solution)/shard_map/ppermute | solution.py:319
  390.9 5.6 add_convert_fusion
  401.2 34.5 %collective-permute-done.48 = bf16[4,112,1152]{2,1,0:T(8,128)(2,1)} collective-permute-done((bf16[4,112,1152]{2,1,0:T(8,128)(2,1)}, bf16[4,112,1152]{2,1,0:T(8,128)(2,1)}, u32[]{:S(2)}, u32[]{:S(2)}) %collective-permute-start.48) | collective-permute-done | bytes 1032224 | tf_op jit(solution)/shard_map/ppermute | solution.py:319
  454.5 14.5 %all-to-all-done.4 = bf16[4,112,1152]{2,1,0:T(8,128)(2,1)S(1)} async-done(((bf16[4,112,1152]{2,1,0:T(8,128)(2,1)}), bf16[4,112,1152]{2,1,0:T(8,128)(2,1)S(1)}, u32[]{:S(2)}, u32[]{:S(2)}) %all-to-all-start.4) | async-done | bytes 1032224 | tf_op jit(solution)/shard_map/all_to_all | solution.py:684
  472.5 30.3 %collective-permute-done.59 = bf16[4,96,3072]{2,1,0:T(8,128)(2,1)} collective-permute-done((bf16[4,96,3072]{2,1,0:T(8,128)(2,1)}, bf16[4,96,3072]{2,1,0:T(8,128)(2,1)}, u32[]{:S(2)}, u32[]{:S(2)}) %collective-permute-start.59) | collective-permute-done | bytes 2359328 | tf_op jit(solution)/shard_map/ppermute | solution.py:319
  533.7 7.0 %collective-permute-done.55 = bf16[96,1920]{1,0:T(8,128)(2,1)S(1)} collective-permute-done((bf16[96,1920]{1,0:T(8,128)(2,1)}, bf16[96,1920]{1,0:T(8,128)(2,1)S(1)}, u32[]{:S(2)}, u32[]{:S(2)}) %collective-permute-start.55) | collective-permute-done | bytes 368672 | tf_op jit(solution)/shard_map/ppermute | solution.py:319
  545.6 19.8 %all-to-all-done.6 = bf16[4,96,3072]{2,1,0:T(8,128)(2,1)S(1)} async-done(((bf16[4,96,3072]{2,1,0:T(8,128)(2,1)}), bf16[4,96,3072]{2,1,0:T(8,128)(2,1)S(1)}, u32[]{:S(2)}, u32[]{:S(2)}) %all-to-all-start.6) | async-done | bytes 2359328 | tf_op jit(solution)/shard_map/all_to_all | solution.py:684
  572.5 8.8 %collective-permute-done.60 = bf16[96,3072]{1,0:T(8,128)(2,1)S(1)} collective-permute-done((bf16[96,3072]{1,0:T(8,128)(2,1)}, bf16[96,3072]{1,0:T(8,128)(2,1)S(1)}, u32[]{:S(2)}, u32[]{:S(2)}) %collective-permute-start.60) | collective-permute-done | bytes 589856 | tf_op jit(solution)/shard_map/ppermute | solution.py:319
  589.3 19.3 %psum.7 = f32[]{:T(128)} all-reduce(f32[]{:T(128)S(6)} %add.326), channel_id=1, replica_groups=mesh['z'=4,'x'=2,'y'=2,'c'=2] {'z','x'}, use_global_device_ids=true, to_apply=%region_25.26 | all-reduce | flops 1 | bytes 8 | tf_op jit(solution)/shard_map/psum | solution.py:899
  (540 shorter events, 284.0 us)
Async XLA Ops:
  20.7 110.9 %all-to-all-start = ((bf16[8,64,768]{2,1,0:T(8,128)(2,1)}), bf16[8,64,768]{2,1,0:T(8,128)(2,1)}, u32[]{:S(2)}, u32[]{:S(2)}) async-start(bf16[8,64,768]{2,1,0:T(8,128)(2,1)} %bitcast.4), calls=%async_computation | async-start | bytes 1572864 | tf_op jit(solution)/shard_map/all_to_all | solution.py:349
  27.8 46.2 %collective-permute-start.14 = (bf16[5,96,384]{2,1,0:T(8,128)(2,1)S(1)}, bf16[5,96,384]{2,1,0:T(8,128)(2,1)}, u32[]{:S(2)}, u32[]{:S(2)}) collective-permute-start(bf16[5,96,384]{2,1,0:T(8,128)(2,1)S(1)} %bitcast.213), channel_id=1, source_target_pairs={{0,16},{8,24},{16,0},{24,8},{1,17},{9,25},{17,1},{25,9},{2,18},{10... | collective-permute-start | bytes 1105928 | tf_op jit(solution)/shard_map/ppermute | solution.py:364
  30.2 43.8 %collective-permute-start.15 = (bf16[5,96,384]{2,1,0:T(8,128)(2,1)S(1)}, bf16[5,96,384]{2,1,0:T(8,128)(2,1)}, u32[]{:S(2)}, u32[]{:S(2)}) collective-permute-start(bf16[5,96,384]{2,1,0:T(8,128)(2,1)S(1)} %bitcast.214), channel_id=1, source_target_pairs={{0,24},{8,16},{16,8},{24,0},{1,25},{9,17},{17,9},{25,1},{2,26},{10... | collective-permute-start | bytes 1105928 | tf_op jit(solution)/shard_map/ppermute | solution.py:364
  30.3 51.7 %collective-permute-start.16 = (bf16[5,96,384]{2,1,0:T(8,128)(2,1)S(1)}, bf16[5,96,384]{2,1,0:T(8,128)(2,1)S(1)}, u32[]{:S(2)}, u32[]{:S(2)}) collective-permute-start(bf16[5,96,384]{2,1,0:T(8,128)(2,1)S(1)} %bitcast.215), channel_id=1, source_target_pairs={{0,4},{4,0},{1,5},{5,1},{2,6},{6,2},{3,7},{7,3},{8,12},{12,8},{9,1... | collective-permute-start | bytes 1105928 | tf_op jit(solution)/shard_map/ppermute | solution.py:319
  33.7 49.9 %collective-permute-start.42 = (bf16[2,2,64,768]{3,2,1,0:T(8,128)(2,1)S(1)}, bf16[2,2,64,768]{3,2,1,0:T(8,128)(2,1)S(1)}, u32[]{:S(2)}, u32[]{:S(2)}) collective-permute-start(bf16[2,2,64,768]{3,2,1,0:T(8,128)(2,1)S(1)} %get-tuple-element.94), channel_id=1, source_target_pairs={{0,1},{1,0},{2,3},{3,2},{4,5},{5,4},{6,7},{7,6},{8,9},{9,8},{10,11... | collective-permute-start | bytes 1179656 | tf_op jit(solution)/shard_map/ppermute | solution.py:319
  74.0 47.6 %collective-permute-start.28 = (bf16[2,96,1536]{2,1,0:T(8,128)(2,1)S(1)}, bf16[2,96,1536]{2,1,0:T(8,128)(2,1)S(1)}, u32[]{:S(2)}, u32[]{:S(2)}) collective-permute-start(bf16[2,96,1536]{2,1,0:T(8,128)(2,1)S(1)} %get-tuple-element.88.refs_0_), channel_id=1, source_target_pairs={{0,16},{8,24},{16,0},{24,8},{1,17},{9,25},{17,1},{25,9},{2,18},{10... | collective-permute-start | bytes 1769480 | tf_op jit(solution)/shard_map/ppermute | solution.py:364
  83.6 46.6 %collective-permute-start.29 = (bf16[2,96,1536]{2,1,0:T(8,128)(2,1)S(1)}, bf16[2,96,1536]{2,1,0:T(8,128)(2,1)}, u32[]{:S(2)}, u32[]{:S(2)}) collective-permute-start(bf16[2,96,1536]{2,1,0:T(8,128)(2,1)S(1)} %get-tuple-element.88.refs_0_), channel_id=1, source_target_pairs={{0,24},{8,16},{16,8},{24,0},{1,25},{9,17},{17,9},{25,1},{2,26},{10... | collective-permute-start | bytes 1769480 | tf_op jit(solution)/shard_map/ppermute | solution.py:364
  85.6 44.5 %collective-permute-start.30 = (bf16[2,96,1536]{2,1,0:T(8,128)(2,1)S(1)}, bf16[2,96,1536]{2,1,0:T(8,128)(2,1)}, u32[]{:S(2)}, u32[]{:S(2)}) collective-permute-start(bf16[2,96,1536]{2,1,0:T(8,128)(2,1)S(1)} %get-tuple-element.88.refs_0_), channel_id=1, source_target_pairs={{0,4},{4,0},{1,5},{5,1},{2,6},{6,2},{3,7},{7,3},{8,12},{12,8},{9,1... | collective-permute-start | bytes 1769480 | tf_op jit(solution)/shard_map/ppermute | solution.py:319
  131.6 80.1 %all-to-all-start.2 = ((bf16[8,64,768]{2,1,0:T(8,128)(2,1)}), bf16[8,64,768]{2,1,0:T(8,128)(2,1)}, u32[]{:S(2)}, u32[]{:S(2)}) async-start(bf16[8,64,768]{2,1,0:T(8,128)(2,1)} %bitcast.235), calls=%async_computation.2 | async-start | bytes 1572864 | tf_op jit(solution)/shard_map/all_to_all | solution.py:349
  140.3 45.5 %collective-permute-start.33 = (bf16[2,96,1536]{2,1,0:T(8,128)(2,1)}, bf16[2,96,1536]{2,1,0:T(8,128)(2,1)}, u32[]{:S(2)}, u32[]{:S(2)}) collective-permute-start(bf16[2,96,1536]{2,1,0:T(8,128)(2,1)} %collective-permute-done.29.refs_3_), channel_id=1, source_target_pairs={{0,4},{4,0},{1,5},{5,1},{2,6},{6,2},{3,7},{7,3},{8,12},{12,8},{9,1... | collective-permute-start | bytes 1769480 | tf_op jit(solution)/shard_map/ppermute | solution.py:319
  145.1 41.1 %collective-permute-start.34 = (bf16[2,96,1536]{2,1,0:T(8,128)(2,1)S(1)}, bf16[2,96,1536]{2,1,0:T(8,128)(2,1)S(1)}, u32[]{:S(2)}, u32[]{:S(2)}) collective-permute-start(bf16[2,96,1536]{2,1,0:T(8,128)(2,1)S(1)} %collective-permute-done.27.refs_1_), channel_id=1, source_target_pairs={{0,1},{1,0},{2,3},{3,2},{4,5},{5,4},{6,7},{7,6},{8,9},{9,8},{10,11... | collective-permute-start | bytes 1769480 | tf_op jit(solution)/shard_map/ppermute | solution.py:319
  145.2 41.9 %collective-permute-start.35 = (bf16[2,96,1536]{2,1,0:T(8,128)(2,1)S(1)}, bf16[2,96,1536]{2,1,0:T(8,128)(2,1)S(1)}, u32[]{:S(2)}, u32[]{:S(2)}) collective-permute-start(bf16[2,96,1536]{2,1,0:T(8,128)(2,1)S(1)} %collective-permute-done.28.refs_2_), channel_id=1, source_target_pairs={{0,1},{1,0},{2,3},{3,2},{4,5},{5,4},{6,7},{7,6},{8,9},{9,8},{10,11... | collective-permute-start | bytes 1769480 | tf_op jit(solution)/shard_map/ppermute | solution.py:319
  301.8 94.6 %collective-permute-start.57 = (bf16[768,1536]{1,0:T(8,128)(2,1)}, bf16[768,1536]{1,0:T(8,128)(2,1)}, u32[]{:S(2)}, u32[]{:S(2)}) collective-permute-start(bf16[768,1536]{1,0:T(8,128)(2,1)} %convolution_convert_fusion.3), channel_id=1, source_target_pairs={{0,1},{1,0},{2,3},{3,2},{4,5},{5,4},{6,7},{7,6},{8,9},{9,8},{10,11... | collective-permute-start | bytes 7077896 | tf_op jit(solution)/shard_map/ppermute | solution.py:319
  305.5 41.0 %collective-permute-start.51 = (bf16[768,384]{0,1:T(8,128)(2,1)}, bf16[768,384]{0,1:T(8,128)(2,1)}, u32[]{:S(2)}, u32[]{:S(2)}) collective-permute-start(bf16[768,384]{0,1:T(8,128)(2,1)} %convolution_convert_fusion.9), channel_id=1, source_target_pairs={{0,1},{1,0},{2,3},{3,2},{4,5},{5,4},{6,7},{7,6},{8,9},{9,8},{10,11... | collective-permute-start | bytes 1769480 | tf_op jit(solution)/shard_map/ppermute | solution.py:319
  308.2 48.8 %collective-permute-start.52 = (bf16[768,1152]{1,0:T(8,128)(2,1)}, bf16[768,1152]{1,0:T(8,128)(2,1)}, u32[]{:S(2)}, u32[]{:S(2)}) collective-permute-start(bf16[768,1152]{1,0:T(8,128)(2,1)} %convolution_convert_fusion.4), channel_id=1, source_target_pairs={{0,1},{1,0},{2,3},{3,2},{4,5},{5,4},{6,7},{7,6},{8,9},{9,8},{10,11... | collective-permute-start | bytes 5308424 | tf_op jit(solution)/shard_map/ppermute | solution.py:319
  308.7 42.5 %collective-permute-start.53 = (bf16[768,384]{1,0:T(8,128)(2,1)}, bf16[768,384]{1,0:T(8,128)(2,1)}, u32[]{:S(2)}, u32[]{:S(2)}) collective-permute-start(bf16[768,384]{1,0:T(8,128)(2,1)} %convolution_convert_fusion.8), channel_id=1, source_target_pairs={{0,1},{1,0},{2,3},{3,2},{4,5},{5,4},{6,7},{7,6},{8,9},{9,8},{10,11... | collective-permute-start | bytes 1769480 | tf_op jit(solution)/shard_map/ppermute | solution.py:319
  312.3 73.8 %all-to-all-start.1 = ((bf16[8,64,768]{2,1,0:T(8,128)(2,1)}), bf16[8,64,768]{2,1,0:T(8,128)(2,1)}, u32[]{:S(2)}, u32[]{:S(2)}) async-start(bf16[8,64,768]{2,1,0:T(8,128)(2,1)} %bitcast.247), calls=%async_computation.1 | async-start | bytes 1572864 | tf_op jit(solution)/shard_map/all_to_all | solution.py:354
  346.5 44.3 %collective-permute-start.58 = (bf16[768,1536]{1,0:T(8,128)(2,1)}, bf16[768,1536]{1,0:T(8,128)(2,1)}, u32[]{:S(2)}, u32[]{:S(2)}) collective-permute-start(bf16[768,1536]{1,0:T(8,128)(2,1)} %convolution_convert_fusion.2), channel_id=1, source_target_pairs={{0,1},{1,0},{2,3},{3,2},{4,5},{5,4},{6,7},{7,6},{8,9},{9,8},{10,11... | collective-permute-start | bytes 7077896 | tf_op jit(solution)/shard_map/ppermute | solution.py:319
  361.5 90.1 %collective-permute-start.54 = (bf16[4,96,1920]{2,1,0:T(8,128)(2,1)}, bf16[4,96,1920]{2,1,0:T(8,128)(2,1)}, u32[]{:S(2)}, u32[]{:S(2)}) collective-permute-start(bf16[4,96,1920]{2,1,0:T(8,128)(2,1)} %dynamic-slice_bitcast_fusion.1), channel_id=1, source_target_pairs={{0,4},{4,0},{1,5},{5,1},{2,6},{6,2},{3,7},{7,3},{8,12},{12,8},{9,1... | collective-permute-start | bytes 4423688 | tf_op jit(solution)/shard_map/ppermute | solution.py:319
  381.5 54.2 %collective-permute-start.48 = (bf16[4,112,1152]{2,1,0:T(8,128)(2,1)}, bf16[4,112,1152]{2,1,0:T(8,128)(2,1)}, u32[]{:S(2)}, u32[]{:S(2)}) collective-permute-start(bf16[4,112,1152]{2,1,0:T(8,128)(2,1)} %fusion.83), channel_id=1, source_target_pairs={{0,4},{4,0},{1,5},{5,1},{2,6},{6,2},{3,7},{7,3},{8,12},{12,8},{9,1... | collective-permute-start | bytes 3096584 | tf_op jit(solution)/shard_map/ppermute | solution.py:319
  386.1 52.0 %all-to-all-start.3 = ((bf16[8,64,768]{2,1,0:T(8,128)(2,1)}), bf16[8,64,768]{2,1,0:T(8,128)(2,1)S(1)}, u32[]{:S(2)}, u32[]{:S(2)}) async-start(bf16[8,64,768]{2,1,0:T(8,128)(2,1)} %bitcast.238), calls=%async_computation.3 | async-start | bytes 1572864 | tf_op jit(solution)/shard_map/all_to_all | solution.py:354
  450.1 52.7 %collective-permute-start.59 = (bf16[4,96,3072]{2,1,0:T(8,128)(2,1)}, bf16[4,96,3072]{2,1,0:T(8,128)(2,1)}, u32[]{:S(2)}, u32[]{:S(2)}) collective-permute-start(bf16[4,96,3072]{2,1,0:T(8,128)(2,1)} %dynamic-slice_bitcast_fusion), channel_id=1, source_target_pairs={{0,4},{4,0},{1,5},{5,1},{2,6},{6,2},{3,7},{7,3},{8,12},{12,8},{9,1... | collective-permute-start | bytes 7077896 | tf_op jit(solution)/shard_map/ppermute | solution.py:319
  469.0 38.5 %all-to-all-start.5 = ((bf16[4,96,1920]{2,1,0:T(8,128)(2,1)}), bf16[4,96,1920]{2,1,0:T(8,128)(2,1)S(1)}, u32[]{:S(2)}, u32[]{:S(2)}) async-start(bf16[4,96,1920]{2,1,0:T(8,128)(2,1)} %fusion.8), calls=%async_computation.5 | async-start | bytes 2949120 | tf_op jit(solution)/shard_map/all_to_all | solution.py:684
  508.6 56.8 %all-to-all-start.6 = ((bf16[4,96,3072]{2,1,0:T(8,128)(2,1)}), bf16[4,96,3072]{2,1,0:T(8,128)(2,1)S(1)}, u32[]{:S(2)}, u32[]{:S(2)}) async-start(bf16[4,96,3072]{2,1,0:T(8,128)(2,1)} %fusion.7), calls=%async_computation.6 | async-start | bytes 4718592 | tf_op jit(solution)/shard_map/all_to_all | solution.py:684
  (168 other events, 1705.0 us)

commit v3 on v2

--- a/solution.py
+++ b/solution.py
@@ -358,35 +358,49 @@
     return both.reshape(2, 1, 4 * part, width)
 
 
-def gather_pieces(own):
-    over_z = [own]
-    for i in (1, 2, 3):
-        over_z.append(lax.ppermute(own, "z", [(k, k ^ i) for k in range(4)]))
-    return over_z, [swap(piece, "x") for piece in over_z]
+def after(value, *earlier):
+    return lax.optimization_barrier((value, *earlier))[0]
+
+
+def gather_z(own):
+    others = [lax.ppermute(own, "z", [(k, k ^ i) for k in range(4)]) for i in (1, 2, 3)]
+    return jnp.stack([own] + others)
+
+
+def spread(over_z):
+    over_x = swap(over_z, "x")
+    quarter = [((0, 0, 0), over_z), ((1, 0, 0), over_x)]
+    return quarter + [((j, 1, 0), swap(value, "y")) for (j, _, _), value in quarter]
+
+
+def both_cores(half):
+    return half + [((j, m, 1), swap(value, "c")) for (j, m, _), value in half]
+
+
+def placing(plan, outs_at, place_ref, stacks, outs, sem):
+    copies = []
+    for stack, (j, m, k) in zip(stacks, plan):
+        x, y, c = (lax.bitwise_xor(place_ref[n], step) for n, step in ((1, j), (3, m), (2, k)))
+        for i in range(4):
+            shard = lax.bitwise_xor(place_ref[0], i) * 2 + x
+            for source, target in outs_at(stack.at[i], outs, shard, y, c):
+                copies.append(pltpu.make_async_copy(source, target, sem.at[len(copies)]))
+    return copies
 
 
 def place_kernel(plan, outs_at, place_ref, *refs):
-    pieces = refs[: len(plan)]
-    outs = refs[len(plan) : -1]
-    sem = refs[-1]
-    copies = []
-    for ref, (i, j, k) in zip(pieces, plan):
-        z = lax.bitwise_xor(place_ref[0], i)
-        x = lax.bitwise_xor(place_ref[1], j)
-        c = lax.bitwise_xor(place_ref[2], k)
-        shard = z * 2 + x
-        for source, target in outs_at(ref, outs, shard, c):
-            copies.append(pltpu.make_async_copy(source, target, sem.at[len(copies)]))
+    stacks = refs[: len(plan)]
+    copies = placing(plan, outs_at, place_ref, stacks, refs[len(plan) : -1], refs[-1])
     for copy in copies:
         copy.start()
     for copy in copies:
         copy.wait()
 
 
-def placed_pieces(pieces, plan, outs_at, outs, place, count):
+def placed_pieces(pieces, outs_at, outs, place, count):
     anywhere = pl.BlockSpec(memory_space=pl.ANY)
     return pl.pallas_call(
-        partial(place_kernel, plan, outs_at),
+        partial(place_kernel, [step for step, _ in pieces], outs_at),
         in_specs=[pl.BlockSpec(memory_space=pltpu.SMEM)] + [anywhere] * len(pieces),
         out_specs=[pl.BlockSpec(memory_space=pltpu.VMEM)] * len(outs),
         out_shape=[jax.ShapeDtypeStruct(shape, jnp.bfloat16) for shape in outs],
@@ -394,13 +408,10 @@
         compiler_params=pltpu.CompilerParams(
             vmem_limit_bytes=sum(2 * math.prod(s) for s in outs) + 2 * 2**20
         ),
-        cost_estimate=pl.CostEstimate(
-            flops=0, transcendentals=0, bytes_accessed=sum(4 * math.prod(s) for s in outs)
-        ),
-    )(place, *pieces)
-
-
-def row_attn_at(ref, outs, shard, c):
+    )(place, *[value for _, value in pieces])
+
+
+def row_attn_at(ref, outs, shard, y, c):
     depth = outs[0].shape[0] // 8
     at = pl.multiple_of(shard * depth, depth)
     return [
@@ -409,27 +420,21 @@
     ]
 
 
-def halves_at(ref, outs, shard, c):
+def ffn_at(ref, outs, shard, y, c):
+    depth = ref.shape[0]
+    at = pl.multiple_of((y * 8 + shard) * depth, depth)
+    return [(ref, outs[0].at[pl.ds(at, depth)])]
+
+
+def col_attn_at(ref, outs, shard, y, c):
     depth, half = ref.shape[1], ref.shape[2]
-    at = pl.multiple_of(shard * depth, depth)
+    at = pl.multiple_of((shard * 2 + y) * depth, depth)
     moves = []
     slots = [(o, n) for o, out in enumerate(outs) for n in range(out.shape[1] // (2 * half))]
     for k, (o, n) in enumerate(slots):
         lane = pl.multiple_of(c * half + n * 2 * half, TILE)
         moves.append((ref.at[k], outs[o].at[pl.ds(at, depth), pl.ds(lane, half)]))
     return moves
-
-
-def all_halves(own_half, other_half, place, outs):
-    over_z, over_x = gather_pieces(own_half)
-    mine = over_z + over_x
-    plan = [(i, j, 0) for j in (0, 1) for i in range(4)]
-    theirs = [other_half] + [swap(piece, "c") for piece in mine[1:]]
-    plan = plan + [(i, j, 1) for (i, j, _) in plan]
-    pieces = mine + theirs
-    return placed_pieces(
-        pieces, plan, halves_at, outs, place, len(pieces) * own_half.shape[0]
-    )
 
 
 def contract(a, b, dims):
@@ -583,107 +588,270 @@
     )(info, tie, near, near, near, far, far, grad)
 
 
+def normed(value, gain, shift):
+    centred = value - jnp.mean(value, axis=-1, keepdims=True)
+    scale = lax.rsqrt(jnp.mean(centred * centred, axis=-1, keepdims=True) + eps_norm)
+    unit = centred * scale
+    return unit * gain + shift, unit, scale
+
+
+def normed_back(grad, unit, scale, gain):
+    inner = grad * gain
+    mean = jnp.mean(inner, axis=-1, keepdims=True)
+    along = jnp.mean(inner * unit, axis=-1, keepdims=True)
+    return scale * (inner - mean - unit * along)
+
+
 def column_masks(info_ref, rows, part):
     tokens = rows * part
-    first = lax.broadcasted_iota(jnp.int32, (tokens, tokens), 0)
-    second = lax.broadcasted_iota(jnp.int32, (tokens, tokens), 1)
-    same = first % part == second % part
-    return jnp.logical_and(same, second // part < info_ref[4])
-
-
-def col_fwd_kernel(info_ref, qkv_ref, o_ref):
-    rows, part, lanes = qkv_ref.shape
+    key = lax.broadcasted_iota(jnp.int32, (tokens, tokens), 0)
+    query = lax.broadcasted_iota(jnp.int32, (tokens, tokens), 1)
+    same = key % part == query % part
+    return jnp.logical_and(same, key // part < info_ref[4])
+
+
+def stacked(value, sides):
+    return jnp.concatenate([only(side, value) for side in sides], axis=0)
+
+
+def column_probs(query, key, keep, sides):
+    scores = contract(stacked(key, sides), query, LAST) * (1.0 / math.sqrt(DH))
+    tokens = query.shape[0]
+    probs = []
+    for n in (0, 1):
+        part = jnp.where(keep, scores[n * tokens : (n + 1) * tokens], masked_score)
+        expo = jnp.exp(part - jnp.max(part, axis=0, keepdims=True))
+        probs.append(expo / jnp.sum(expo, axis=0, keepdims=True))
+    return probs
+
+
+def col_fwd_kernel(
+    info_ref, x_ref, own_ref, other_ref, three_ref, col_ref, seven_ref, gain_ref,
+    mixed_one_ref, one_ref, normed_two_ref, qkv_ref, mixed_ref, resid_ref, normed_three_ref,
+):
+    bf16 = jnp.bfloat16
+    rows, cols, lanes = qkv_ref.shape
     width = lanes // 3
-    qkv = qkv_ref[...].reshape(rows * part, lanes)
+    part = 16
+    own, other = own_ref[...], other_ref[...]
+    flip = info_ref[2] == 0
+    mixed_one = jnp.concatenate(
+        [jnp.where(flip, own, other), jnp.where(flip, other, own)], axis=1
+    )
+    mixed_one_ref[...] = mixed_one
+    stream = (x_ref[...].astype(jnp.float32) + contract(mixed_one, three_ref[...], PLAIN)).astype(bf16)
+    one_ref[...] = stream
+    normed_two = normed(stream.astype(jnp.float32), gain_ref[2:3], gain_ref[3:4])[0].astype(bf16)
+    normed_two_ref[...] = normed_two
+    for n in range(3):
+        at = slice(n * width, (n + 1) * width)
+        found = contract(normed_two, col_ref[:, at], PLAIN).astype(bf16)
+        qkv_ref[:, :, at] = found.reshape(rows, cols, width)
     keep = column_masks(info_ref, rows, part)
     sides = head_lanes(TILE)
-    scale = 1.0 / math.sqrt(DH)
-    for at in range(0, width, TILE):
-        query = qkv[:, at : at + TILE]
-        key = qkv[:, width + at : width + at + TILE]
-        value = qkv[:, 2 * width + at : 2 * width + at + TILE]
-        mixed = []
-        for side in sides:
-            probs = softmax_of(contract(only(side, query), key, LAST) * scale, keep)
-            mixed.append(contract(probs.astype(jnp.bfloat16), value, PLAIN))
-        mixed = jnp.where(sides[0], mixed[0], mixed[1]).astype(jnp.bfloat16)
-        o_ref[:, :, at : at + TILE] = mixed.reshape(rows, part, TILE)
-
-
-def col_bwd_kernel(info_ref, qkv_ref, do_ref, d_ref):
+
+    def attend(b, carry):
+        at = pl.ds(pl.multiple_of(b * part, part), part)
+        def tile(n, t):
+            lane = n * width + t * TILE
+            return qkv_ref[:, at, lane : lane + TILE].reshape(rows * part, TILE)
+        tiles = range(width // TILE)
+        probs = [column_probs(tile(0, t), tile(1, t), keep, sides) for t in tiles]
+        for t in tiles:
+            low = jnp.concatenate(probs[t], axis=0).astype(bf16)
+            mixed = contract(low, stacked(tile(2, t), sides), FIRST).astype(bf16)
+            mixed_ref[:, at, t * TILE : (t + 1) * TILE] = mixed.reshape(rows, part, TILE)
+        return carry
+
+    lax.fori_loop(0, cols // part, attend, 0)
+    mixed = mixed_ref[...].reshape(rows * cols, width)
+    resid = one_ref[...].astype(jnp.float32) + contract(mixed, seven_ref[...], PLAIN)
+    resid_ref[...] = resid
+    normed_three_ref[...] = normed(resid, gain_ref[4:5], gain_ref[5:6])[0].astype(bf16)
+
+
+def col_bwd_kernel(
+    info_ref, up_ref, da_ref, da_got_ref, resid_ref, one_ref, qkv_ref, three_ref, col_ref, seven_ref,
+    gain_ref, branch_ref, dqkv_ref, stream_ref, own_ref, other_ref, norms_ref, do_ref,
+):
     bf16 = jnp.bfloat16
-    rows, part, lanes = qkv_ref.shape
+    f32 = jnp.float32
+    rows, cols, lanes = qkv_ref.shape
     width = lanes // 3
-    qkv = qkv_ref[...].reshape(rows * part, lanes)
-    out_grad = do_ref[...].reshape(rows * part, width)
+    part = 16
+    da = da_ref[...] + da_got_ref[...].astype(f32)
+    gain = gain_ref[4:5]
+    _, unit, scale = normed(resid_ref[...], gain, 0.0)
+    grad_three = up_ref[...].astype(f32) + normed_back(da, unit, scale, gain)
+    norms_ref[2:3] = jnp.sum(da * unit, axis=0, keepdims=True)
+    norms_ref[3:4] = jnp.sum(da, axis=0, keepdims=True)
+    branch = grad_three.astype(bf16)
+    branch_ref[...] = branch
+    do_ref[...] = contract(branch, seven_ref[...], LAST).astype(bf16).reshape(rows, cols, width)
     keep = column_masks(info_ref, rows, part)
     sides = head_lanes(TILE)
-    scale = 1.0 / math.sqrt(DH)
-    for at in range(0, width, TILE):
-        query = qkv[:, at : at + TILE]
-        key = qkv[:, width + at : width + at + TILE]
-        value = qkv[:, 2 * width + at : 2 * width + at + TILE]
-        out = out_grad[:, at : at + TILE]
-        found = []
-        for side in sides:
-            probs = softmax_of(contract(only(side, query), key, LAST) * scale, keep)
-            grads = contract(only(side, out), value, LAST)
-            delta = softmax_back(probs, grads).astype(bf16)
-            found.append(
-                (
-                    contract(delta, key, PLAIN) * scale,
-                    contract(delta, query, FIRST) * scale,
-                    contract(probs.astype(bf16), out, FIRST),
-                )
-            )
-        for n in range(3):
-            both = jnp.where(sides[0], found[0][n], found[1][n]).astype(bf16)
-            first = n * width + at
-            d_ref[:, :, first : first + TILE] = both.reshape(rows, part, TILE)
-
-
-def column_block(rows, part, lanes):
-    return pl.BlockSpec((rows, part, lanes), lambda b: (0, b, 0))
-
-
-def column_attention(info, qkv, part=16):
-    rows, cols, lanes = qkv.shape
+    ratio = 1.0 / math.sqrt(DH)
+
+    def attend(b, carry):
+        at = pl.ds(pl.multiple_of(b * part, part), part)
+        tokens = rows * part
+
+        def tile(n, t):
+            lane = n * width + t * TILE
+            return qkv_ref[:, at, lane : lane + TILE].reshape(tokens, TILE)
+
+        def out_tile(t):
+            return do_ref[:, at, t * TILE : (t + 1) * TILE].reshape(tokens, TILE)
+
+        def put(n, t, value):
+            lane = n * width + t * TILE
+            dqkv_ref[:, at, lane : lane + TILE] = value.astype(bf16).reshape(rows, part, TILE)
+
+        for t in range(width // TILE):
+            query, key, out = tile(0, t), tile(1, t), out_tile(t)
+            keys = stacked(key, sides)
+            probs = column_probs(query, key, keep, sides)
+            grads = contract(stacked(tile(2, t), sides), out, LAST)
+            deltas = []
+            for n, p in enumerate(probs):
+                g = grads[n * tokens : (n + 1) * tokens]
+                deltas.append((p * (g - jnp.sum(p * g, axis=0, keepdims=True))).astype(bf16))
+            put(0, t, contract(jnp.concatenate(deltas, axis=0), keys, FIRST) * ratio)
+            wide = jnp.concatenate(deltas, axis=1)
+            put(1, t, contract(wide, stacked(query, sides), PLAIN) * ratio)
+            wide = jnp.concatenate([p.astype(bf16) for p in probs], axis=1)
+            put(2, t, contract(wide, stacked(out, sides), PLAIN))
+        return carry
+
+    lax.fori_loop(0, cols // part, attend, 0)
+    grad_normed = contract(dqkv_ref[...].reshape(rows * cols, lanes), col_ref[...], LAST)
+    gain = gain_ref[2:3]
+    _, unit, scale = normed(one_ref[...].astype(f32), gain, 0.0)
+    norms_ref[0:1] = jnp.sum(grad_normed * unit, axis=0, keepdims=True)
+    norms_ref[1:2] = jnp.sum(grad_normed, axis=0, keepdims=True)
+    stream = (grad_three + normed_back(grad_normed, unit, scale, gain)).astype(bf16)
+    stream_ref[...] = stream
+    mixed = contract(stream, three_ref[...], LAST).astype(bf16)
+    half = width // 2
+    flip = info_ref[2] == 0
+    own_ref[...] = jnp.where(flip, mixed[:, :half], mixed[:, half:])
+    other_ref[...] = jnp.where(flip, mixed[:, half:], mixed[:, :half])
+
+
+def whole_call(kernel, info, args, outs, scratch=()):
+    inside = pl.BlockSpec(memory_space=pltpu.VMEM)
     return pl.pallas_call(
-        col_fwd_kernel,
-        grid=(cols // part,),
-        in_specs=[pl.BlockSpec(memory_space=pltpu.SMEM), column_block(rows, part, lanes)],
-        out_specs=column_block(rows, part, lanes // 3),
-        out_shape=jax.ShapeDtypeStruct((rows, cols, lanes // 3), jnp.bfloat16),
-        compiler_params=pltpu.CompilerParams(vmem_limit_bytes=32 * 2**20),
-    )(info, qkv)
-
-
-def column_attention_back(info, qkv, grad, part=16):
-    rows, cols, lanes = qkv.shape
+        kernel,
+        in_specs=[pl.BlockSpec(memory_space=pltpu.SMEM)] + [inside] * len(args),
+        out_specs=[inside] * len(outs),
+        out_shape=[jax.ShapeDtypeStruct(shape, kind) for shape, kind in outs],
+        scratch_shapes=list(scratch),
+        compiler_params=pltpu.CompilerParams(vmem_limit_bytes=56 * 2**20),
+    )(info, *args)
+
+
+def gelu_pair(u):
+    ratio = math.sqrt(2.0 / math.pi)
+    square = u * u
+    tanh = jnp.tanh(ratio * u * (1.0 + 0.044715 * square))
+    rise = 0.5 * (1.0 + tanh)
+    slope = (0.5 * ratio) * (1.0 - tanh * tanh) * (1.0 + (3.0 * 0.044715) * square)
+    return u * rise, rise + u * slope
+
+
+def ffn_kernel(
+    plan, place_ref, a_ref, a_got_ref, up_ref, up_got_ref, *refs
+):
+    bf16 = jnp.bfloat16
+    stacks, refs = refs[: len(plan)], refs[len(plan) :]
+    out_ref, out_other_ref, da_ref, da_other_ref, sent_ref, kept_ref = refs[:6]
+    w_ref, tokens_ref, turned_ref, out_sum, da_sum, sem = refs[6:]
+    step = pl.program_id(0)
+    count, width = a_ref.shape
+    chunk = sent_ref.shape[1]
+
+    @pl.when(step == 0)
+    def _():
+        copies = placing(plan, ffn_at, place_ref, stacks, [w_ref], sem)
+        for copy in copies:
+            copy.start()
+        for n, ref in enumerate((a_ref, a_got_ref, up_ref, up_got_ref)):
+            k, at = n // 2, slice((n % 2) * count, (n % 2 + 1) * count)
+            tokens_ref[k, at] = ref[...]
+            turned_ref[k, :, at] = ref[...].T
+        out_sum[...] = jnp.zeros_like(out_sum)
+        da_sum[...] = jnp.zeros_like(da_sum)
+        for copy in copies:
+            copy.wait()
+
+    lane = pl.ds(pl.multiple_of(step * chunk, chunk), chunk)
+    w_in = w_ref[:width, lane]
+    w_out = w_ref[width:, lane]
+    activs, grads = [], []
+    for n in (0, 1):
+        at = slice(n * count, (n + 1) * count)
+        activ, slope = gelu_pair(contract(tokens_ref[0, at], w_in, PLAIN))
+        activ = activ.astype(bf16)
+        grad = (contract(tokens_ref[1, at], w_out, PLAIN) * slope).astype(bf16)
+        out_sum[at] += contract(activ, w_out, LAST)
+        da_sum[at] += contract(grad, w_in, LAST)
+        activs.append(activ)
+        grads.append(grad)
+    in_terms = contract(turned_ref[0], jnp.concatenate(grads, axis=0), PLAIN).astype(bf16)
+    out_terms = contract(turned_ref[1], jnp.concatenate(activs, axis=0), PLAIN).astype(bf16)
+    first = place_ref[3] == 0
+    kept_ref[...] = jnp.where(first, in_terms, out_terms)
+    sent_ref[...] = jnp.where(first, out_terms, in_terms)
+
+    @pl.when(step == pl.num_programs(0) - 1)
+    def _():
+        out_ref[...] = out_sum[:count]
+        out_other_ref[...] = out_sum[count:].astype(bf16)
+        da_ref[...] = da_sum[:count]
+        da_other_ref[...] = da_sum[count:].astype(bf16)
+
+
+def feed_forward(place, normed_own, normed_got, up_own, up_got, pieces, chunk=512):
+    count, width = normed_own.shape
+    half = pieces[0][1].shape[-1]
+    anywhere = pl.BlockSpec(memory_space=pl.ANY)
+    inside = pl.BlockSpec(memory_space=pltpu.VMEM)
+    lanes = pl.BlockSpec((width, chunk), lambda n: (0, n))
+    f32, bf16 = jnp.float32, jnp.bfloat16
+    shapes = [((count, width), kind) for kind in (f32, bf16, f32, bf16)] + [((width, half), bf16)] * 2
     return pl.pallas_call(
-        col_bwd_kernel,
-        grid=(cols // part,),
-        in_specs=[
-            pl.BlockSpec(memory_space=pltpu.SMEM),
-            column_block(rows, part, lanes),
-            column_block(rows, part, lanes // 3),
+        partial(ffn_kernel, [step for step, _ in pieces]),
+        grid=(half // chunk,),
+        in_specs=[pl.BlockSpec(memory_space=pltpu.SMEM)] + [inside] * 4 + [anywhere] * len(pieces),
+        out_specs=[inside] * 4 + [lanes] * 2,
+        out_shape=[jax.ShapeDtypeStruct(shape, kind) for shape, kind in shapes],
+        scratch_shapes=[
+            pltpu.VMEM((2 * width, half), bf16),
+            pltpu.VMEM((2, 2 * count, width), bf16),
+            pltpu.VMEM((2, width, 2 * count), bf16),
+            pltpu.VMEM((2 * count, width), f32),
+            pltpu.VMEM((2 * count, width), f32),
+            pltpu.SemaphoreType.DMA((16,)),
         ],
-        out_specs=column_block(rows, part, lanes),
-        out_shape=jax.ShapeDtypeStruct((rows, cols, lanes), jnp.bfloat16),
-        compiler_params=pltpu.CompilerParams(vmem_limit_bytes=32 * 2**20),
-    )(info, qkv, grad)
-
-
-def summed_to_owner(terms, x):
-    bf16 = jnp.bfloat16
-    f32 = jnp.float32
-    depth = terms.shape[0] // 8
-    blocks = terms.reshape(4, 2, depth, *terms.shape[1:])
-    got = swap(pick(blocks, 1 - x, 1), "x")
-    column = (pick(blocks, x, 1).astype(f32) + got.astype(f32)).astype(bf16)
-    parts = lax.all_to_all(column, "z", 0, 0, tiled=True)
-    shard = jnp.sum(parts.astype(f32), axis=0).astype(bf16)
-    return (shard.astype(f32) + swap(shard, "y").astype(f32)).astype(bf16)
+        compiler_params=pltpu.CompilerParams(vmem_limit_bytes=56 * 2**20),
+    )(place, normed_own, normed_got, up_own, up_got, *[value for _, value in pieces])
+
+
+def added(a, b):
+    return (a.astype(jnp.float32) + b.astype(jnp.float32)).astype(jnp.bfloat16)
+
+
+def x_summed(blocks, x):
+    return added(pick(blocks, x, 1), swap(pick(blocks, 1 - x, 1), "x"))
+
+
+def z_summed(column, z):
+    shard = pick(column, z, 0).astype(jnp.float32)
+    for i in (1, 2, 3):
+        other = pick(column, lax.bitwise_xor(z, i), 0)
+        got = lax.ppermute(other, "z", [(k, k ^ i) for k in range(4)])
+        shard = shard + got.astype(jnp.float32)
+    return shard.astype(jnp.bfloat16)
 
 
 def paired_body(
@@ -706,7 +874,7 @@
 ):
     f32 = jnp.float32
     bf16 = jnp.bfloat16
-    z, x, c = (lax.axis_index(name) for name in ("z", "x", "c"))
+    z, x, y, c = (lax.axis_index(name) for name in ("z", "x", "y", "c"))
     width = tokens.shape[-1]
     hidden = in_weight.shape[1]
     depth = in_weight.shape[0]
@@ -718,8 +886,8 @@
     mine = jnp.where(z // 2 == c, counts, other_counts)
     mine = pick(mine, z % 2, 1)
     cols_live, rows_live = mine[0], mine[1]
-    place = jnp.stack([z, x, c]).astype(jnp.int32)
-    info = jnp.concatenate([place, mine])
+    place = jnp.stack([z, x, c, y]).astype(jnp.int32)
+    info = jnp.concatenate([place[:3], mine])
     tie = (lax.rsqrt(rows_live.astype(f32)) * (1.0 / math.sqrt(DH))).reshape(1)
 
     attn_low = attn_weight.astype(bf16)
@@ -728,11 +896,9 @@
     norm_row = jnp.pad(
         norm_param.astype(bf16).reshape(1, 6 * depth), ((0, 15), (0, 3 * half - 6 * depth))
     )
-    over_z, over_x = gather_pieces(jnp.concatenate([qkv_half, norm_row]))
-    plan = [(i, j, 0) for j in (0, 1) for i in range(4)]
+    row_z = gather_z(jnp.concatenate([qkv_half, norm_row]))
     w_row, norm_rows = placed_pieces(
-        over_z + over_x,
-        plan,
+        [((0, 0, 0), row_z), ((1, 0, 0), swap(row_z, "x"))],
         row_attn_at,
         [(width, 3 * half), (8, 16, 3 * half)],
         place,
@@ -740,59 +906,92 @@
     )
     norm_gain = norm_rows[:, 0, : 6 * depth].reshape(8, 6, depth)
     norm_gain = jnp.moveaxis(norm_gain, 0, 1).reshape(6, width).astype(f32)
-    w_three, w_col, w_seven = all_halves(
-        pick(halves[3:], c, 2),
-        pick(halves[3:], 1 - c, 2),
-        place,
-        [(width, width), (width, 3 * width), (width, width)],
-    )
-    ffn_low = jnp.stack([in_weight.astype(bf16), out_weight.astype(bf16).T])
-    ffn_halves = ffn_low.reshape(2, depth, 2, hidden_half)
-    w_in, w_out = all_halves(
-        pick(ffn_halves, c, 2),
-        pick(ffn_halves, 1 - c, 2),
-        place,
-        [(width, hidden), (width, hidden)],
-    )
+    col_quarter = pick(pick(halves[3:], c, 2).reshape(5, 2, depth // 2, half), y, 1)
+    col_z = gather_z(after(col_quarter, row_z))
+
+    ffn_low = [in_weight.astype(bf16), out_weight.astype(bf16).T]
+    ffn_low = [
+        jnp.where(c == 0, low[:, :hidden_half], low[:, hidden_half:]) for low in ffn_low
+    ]
+    ffn_z = gather_z(after(jnp.where(y == 0, *ffn_low), col_z))
 
     stream_zero = to_columns(tokens, c)
     rows, part, _ = stream_zero.shape
     count = rows * part
     resid_one = stream_zero.reshape(count, width).astype(f32)
     normed_one = layer_norm(resid_one, norm_gain[0], norm_gain[1]).astype(bf16)
-    near_normed = jnp.concatenate([normed_one, swap(normed_one, "c")])
+    col_z = after(col_z, normed_one)
+    w_three, w_col, w_seven = placed_pieces(
+        both_cores(spread(col_z)),
+        col_attn_at,
+        [(width, width), (width, 3 * width), (width, width)],
+        place,
+        8 * 4 * 5,
+    )
+    near_normed = after(jnp.concatenate([normed_one, swap(normed_one, "c")]), col_z)
     far_first = swap(normed_one, "x")
     far_normed = jnp.concatenate([far_first, swap(far_first, "c")])
     near = contract(near_normed, w_row, PLAIN).astype(bf16).reshape(2, rows, part, 3 * half)
     far = contract(far_normed, w_row[:, half:], PLAIN).astype(bf16)
     far = far.reshape(2, rows, part, 2 * half)
-    mixed_heads = row_attention(info, tie, near, far)
-    mixed_one = joined(
-        mixed_heads[0].reshape(count, half), swap(mixed_heads[1].reshape(count, half), "c"), c, 1
-    )
-    stream_one = (resid_one + contract(mixed_one, w_three, PLAIN)).astype(bf16)
-
-    resid_two = stream_one.astype(f32)
-    normed_two = layer_norm(resid_two, norm_gain[2], norm_gain[3]).astype(bf16)
-    qkv_two = contract(normed_two, w_col, PLAIN).astype(bf16).reshape(rows, part, 3 * width)
-    mixed_two = column_attention(info, qkv_two).reshape(count, width)
-    resid_three = resid_two + contract(mixed_two, w_seven, PLAIN)
-
-    normed_three = layer_norm(resid_three, norm_gain[4], norm_gain[5]).astype(bf16)
-    inner = contract(normed_three, w_in, PLAIN)
-    activ = jax.nn.gelu(inner, approximate=True).astype(bf16)
-    result = (resid_three + contract(activ, w_out, LAST)).astype(bf16)
-    block_out = to_rows(result.reshape(rows, part, width), c)
-
-    up = to_columns(cotangent, c)
+    ffn_pieces = spread(ffn_z)
+    mixed_heads = row_attention(info, tie, after(near, ffn_z), far).reshape(2, count, half)
+
+    whole_shape, wide_shape = ((count, width), bf16), ((rows, part, 3 * width), bf16)
+    stream_zero = stream_zero.reshape(count, width)
+    mixed_one, stream_one, normed_two, qkv_two, mixed_two, resid_three, normed_three = whole_call(
+        col_fwd_kernel,
+        info,
+        [
+            stream_zero,
+            mixed_heads[0],
+            swap(mixed_heads[1], "c"),
+            w_three,
+            w_col,
+            w_seven,
+            norm_gain,
+        ],
+        [whole_shape] * 3
+        + [wide_shape, ((rows, part, width), bf16), ((count, width), f32), whole_shape],
+    )
+    mixed_two = mixed_two.reshape(count, width)
+
+    up = to_columns(after(cotangent, mixed_heads), c)
     column = x * (2 * part) + c * part + jnp.arange(part, dtype=jnp.int32)
     live = jnp.logical_and(
         (jnp.arange(rows, dtype=jnp.int32) < rows_live)[:, None], (column < cols_live)[None, :]
     )
     up = jnp.where(live[..., None], up, jnp.zeros_like(up)).reshape(count, width)
-    grad_act = contract(up, w_out, PLAIN)
-    _, gelu_back = jax.vjp(partial(jax.nn.gelu, approximate=True), inner)
-    grad_inner = gelu_back(grad_act)[0].astype(bf16)
+    out_own, out_other, da_own, da_other, ffn_sent, ffn_kept = feed_forward(
+        place, normed_three, swap(normed_three, "c"), up, swap(up, "c"), ffn_pieces
+    )
+    da_got = swap(da_other, "c")
+    result = (resid_three + out_own + swap(out_other, "c").astype(f32)).astype(bf16)
+    block_out = to_rows(result.reshape(rows, part, width), c)
+    ffn_pair = added(ffn_kept, swap(ffn_sent, "y"))
+
+    branch_shape = ((count, width), bf16)
+    grad_branch_two, grad_qkv_two, grad_stream, grad_own, grad_other, col_norms = whole_call(
+        col_bwd_kernel,
+        info,
+        [
+            up,
+            da_own,
+            da_got,
+            resid_three,
+            stream_one,
+            qkv_two,
+            w_three,
+            w_col,
+            w_seven,
+            norm_gain,
+        ],
+        [branch_shape, wide_shape, branch_shape]
+        + [((count, half), bf16)] * 2
+        + [((4, width), f32)],
+        [pltpu.VMEM((rows, part, width), bf16)],
+    )
+    grad_qkv_two = grad_qkv_two.reshape(count, 3 * width)
 
     def lanes_of(value, which, groups):
         size = value.shape[1] // (2 * groups)
@@ -809,30 +1008,27 @@
         kept = [contract(a, lanes_of(b, c, g), FIRST) for a, b, g in sides]
         return [(k + v.astype(f32)).astype(bf16) for k, v in zip(kept, got)]
 
-    ffn_terms = over_cores([(normed_three, grad_inner, 1), (up, activ, 1)])
-    ffn_grad = summed_to_owner(jnp.concatenate(ffn_terms, axis=1), x)
-    grad_normed_three = contract(grad_inner, w_in, LAST)
-    _, norm_back_three = jax.vjp(layer_norm, resid_three, norm_gain[4], norm_gain[5])
-    part_three, gain_grad_three, shift_grad_three = norm_back_three(grad_normed_three)
-    grad_three = up.astype(f32) + part_three
-
-    grad_branch_two = grad_three.astype(bf16)
-    grad_mixed_two = contract(grad_branch_two, w_seven, LAST).astype(bf16)
-    grad_qkv_two = column_attention_back(
-        info, qkv_two, grad_mixed_two.reshape(rows, part, width)
-    ).reshape(count, 3 * width)
-    grad_normed_two = contract(grad_qkv_two, w_col, LAST)
-    _, norm_back_two = jax.vjp(layer_norm, resid_two, norm_gain[2], norm_gain[3])
-    part_two, gain_grad_two, shift_grad_two = norm_back_two(grad_normed_two)
-    grad_stream = (grad_three + part_two).astype(bf16)
-
-    grad_mixed_one = contract(grad_stream, w_three, LAST).astype(bf16)
-    grad_heads = jnp.stack(
-        [lanes_of(grad_mixed_one, c, 1), swap(lanes_of(grad_mixed_one, 1 - c, 1), "c")]
-    ).reshape(2, rows, part, half)
-    dq, dk, dv, dk_far, dv_far = row_attention_back(info, tie, near, far, grad_heads)
+    attn_terms = over_cores(
+        [
+            (mixed_one, grad_stream, 1),
+            (normed_two, grad_qkv_two, 3),
+            (mixed_two, grad_branch_two, 1),
+        ]
+    )
+    attn_terms = jnp.concatenate(attn_terms, axis=1).reshape(8, 2, depth // 2, 5 * half)
+    attn_pair_terms = added(pick(attn_terms, y, 1), swap(pick(attn_terms, 1 - y, 1), "y"))
+
+    grad_heads = jnp.stack([grad_own, swap(grad_other, "c")]).reshape(2, rows, part, half)
+    ffn_column = x_summed(ffn_pair.reshape(4, 2, depth, hidden_half), x)
+    dq, dk, dv, dk_far, dv_far = row_attention_back(
+        info, tie, near, far, after(grad_heads, ffn_pair)
+    )
     grad_near = jnp.concatenate([dq, dk, dv], axis=-1).reshape(2 * count, 3 * half)
     grad_far = jnp.concatenate([dk_far, dv_far], axis=-1).reshape(2 * count, 2 * half)
+    row_terms = contract(near_normed, grad_near, FIRST)
+    far_terms = contract(far_normed, grad_far, FIRST)
+    row_terms = jnp.concatenate([row_terms[:, :half], row_terms[:, half:] + far_terms], axis=1)
+    row_column = x_summed(row_terms.astype(bf16).reshape(4, 2, depth, 3 * half), x)
     far_part = contract(grad_far, w_row[:, half:], LAST).reshape(2, count, width)
     far_sum = far_part[0] + swap(far_part[1].astype(bf16), "c").astype(f32)
     far_got = swap(far_sum.astype(bf16), "x")
@@ -844,59 +1040,47 @@
     grad_input = (grad_stream.astype(f32) + part_one).astype(bf16)
     grad_tokens = to_rows(grad_input.reshape(rows, part, width), c).astype(f32)
 
-    attn_terms = over_cores(
-        [
-            (mixed_one, grad_stream, 1),
-            (normed_two, grad_qkv_two, 3),
-            (mixed_two, grad_branch_two, 1),
-        ]
-    )
-    attn_grad_b = summed_to_owner(jnp.concatenate(attn_terms, axis=1), x)
-    row_terms = contract(near_normed, grad_near, FIRST)
-    far_terms = contract(far_normed, grad_far, FIRST)
-    row_terms = jnp.concatenate([row_terms[:, :half], row_terms[:, half:] + far_terms], axis=1)
-    norm_stack = jnp.stack(
-        [
-            gain_grad_one,
-            shift_grad_one,
-            gain_grad_two,
-            shift_grad_two,
-            gain_grad_three,
-            shift_grad_three,
-        ]
-    )
-    norm_terms = jnp.moveaxis(norm_stack.reshape(6, 8, depth), 0, 1).reshape(8, 1, 6 * depth)
-    norm_terms = jnp.pad(norm_terms, ((0, 0), (0, 15), (0, 3 * half - 6 * depth)))
-    row_terms = jnp.concatenate(
-        [row_terms.reshape(8, depth, 3 * half), norm_terms], axis=1
-    ).astype(bf16)
-    row_grad = summed_to_owner(row_terms.reshape(8 * (depth + 16), 3 * half), x)
+    norm_stack = jnp.concatenate([jnp.stack([gain_grad_one, shift_grad_one]), col_norms])
+    norm_terms = jnp.moveaxis(norm_stack.reshape(6, 4, 2, depth), 0, 2).reshape(4, 2, 1, 6 * depth)
+    norm_terms = jnp.pad(norm_terms, ((0, 0), (0, 0), (0, 15), (0, 3 * half - 6 * depth)))
+    norm_column = x_summed(norm_terms.astype(bf16), x)
+    attn_column = x_summed(attn_pair_terms.reshape(4, 2, depth // 2, 5 * half), x)
+
+    ffn_own = z_summed(ffn_column, z)
+    attn_own = z_summed(attn_column, z)
+    row_own = z_summed(jnp.concatenate([row_column, norm_column], axis=1), z)
+    row_grad = added(row_own, swap(row_own, "y"))
+    ffn_grads = [ffn_own, swap(ffn_own, "y")]
+    attn_grad_b = joined(attn_own, swap(attn_own, "y"), y, 0)
 
     row_other = swap(row_grad, "c")
     attn_other = swap(attn_grad_b, "c")
-    ffn_other = swap(ffn_grad, "c")
+    ffn_whole = [joined(piece, swap(piece, "c"), c, 1) for piece in ffn_grads]
     norm_grad = row_grad[depth, : 6 * depth].astype(f32) + row_other[depth, : 6 * depth].astype(f32)
     norm_grad = norm_grad.reshape(6, depth)
+
     def whole(own, other, groups):
         size = own.shape[1] // groups
         return [
-            joined(own[:depth, n * size : (n + 1) * size], other[:depth, n * size : (n + 1) * size], c, 1)
+            joined(
+                own[:depth, n * size : (n + 1) * size], other[:depth, n * size : (n + 1) * size], c, 1
+            )
             for n in range(groups)
         ]
 
     attn_grad = jnp.stack(whole(row_grad, row_other, 3) + whole(attn_grad_b, attn_other, 5))
     attn_grad = attn_grad.astype(f32)
-    in_grad, out_grad = whole(ffn_grad, ffn_other, 2)
-    in_grad = in_grad.astype(f32)
-    out_grad = out_grad.astype(f32).T
-
-    squares = (
-        jnp.sum(attn_grad * attn_grad)
-        + jnp.sum(in_grad * in_grad)
-        + jnp.sum(out_grad * out_grad)
-        + jnp.sum(norm_grad * norm_grad)
-    )
-    grad_norm = jnp.sqrt(lax.psum(squares, ("z", "x")))
+    in_grad = jnp.where(y == 0, *ffn_whole).astype(f32)
+    out_grad = jnp.where(y == 0, *ffn_whole[::-1]).astype(f32).T
+
+    squares = sum(
+        jnp.sum(jnp.square(g.astype(f32))) for g in (row_grad[:depth], attn_grad_b, *ffn_grads)
+    )
+    squares = squares + swap(squares, "c") + jnp.sum(norm_grad * norm_grad)
+    squares = squares + swap(squares, "x")
+    squares = squares + lax.ppermute(squares, "z", [(k, k ^ 1) for k in range(4)])
+    squares = squares + lax.ppermute(squares, "z", [(k, k ^ 2) for k in range(4)])
+    grad_norm = jnp.sqrt(squares)
     factor = clip_bound / jnp.maximum(grad_norm, clip_bound)
     attn_first_new, attn_second_new, attn_weight_new = adam_update(
         attn_weight, attn_first, attn_second, attn_grad * factor, matrix_rate

time: 635 us -> 551 us (0.87)
  matrix products: 76.1 us -> 26.8 us
  waiting for transfers between devices: 239 us -> 196 us
  starting transfers between devices: 87.2 us -> 125 us
  blocking collectives: 19.3 us -> 0 us
  local copies, waits for them, and re-layouts: 54.8 us -> 38.7 us
  Pallas kernels: 62.6 us -> 75.3 us
  other arithmetic: 79.8 us -> 71.8 us
    dot_general x26 -> x12, matrix products: 76.1 us -> 26.8 us  [contract(): lax.dot_general(a, b, (dims, ((), ())), preferred_element_type=jnp.float32)]
    ppermute x53 -> x46, waiting for transfers between devices: 156 us -> 112 us  [swap(): return lax.ppermute(value, axis, PAIR)]
    ppermute x9 -> x20, starting transfers between devices: 19.7 us -> 60.8 us  [the longest x9 35.5 us: gather_z(): lax.ppermute(own, 'z', [(k, k ^ i) for k in range(4)])]
    ppermute x9 -> x20, waiting for transfers between devices: 49 us -> 83.8 us  [the longest x9 60.5 us: z_summed(): got = lax.ppermute(other, 'z', [(k, k ^ i) for k in range(4)])]
    all_to_all x3 -> x0, waiting for transfers between devices: 34.3 us -> none  [summed_to_owner(): parts = lax.all_to_all(column, 'z', 0, 0, tiled=True)]
    psum x1 -> x0, blocking collectives: 19.3 us -> none  [paired_body(): grad_norm = jnp.sqrt(lax.psum(squares, ('z', 'x')))]
    unnamed x256 -> x143, local copies, waits for them, and re-layouts: 31.6 us -> 14.9 us
    all_to_all x3 -> x0, starting transfers between devices: 13.2 us -> none  [summed_to_owner(): parts = lax.all_to_all(column, 'z', 0, 0, tiled=True)]
  transfers between devices with their start and end apart: 69 -> 70, of which waited for: 17 -> 22; matrix products, arithmetic and copies ran while one was open for 21% -> 22% of each run, Pallas kernels for 3% -> 9%
where the time goes in v3:
time: 551 us; the launch traced here: 544 us
  waiting for transfers between devices  196 us (36%)
  starting transfers between devices  125 us (23%)
  Pallas kernels  75.3 us (14%)
  other arithmetic  71.8 us (13%)
  local copies, waits for them, and re-layouts  38.7 us (7%)
  matrix products  26.8 us (5%)
  between operations  10 us (2%)
    ppermute x46, waiting for transfers between devices, swap(): return lax.ppermute(value, axis, PAIR)  112 us
    ppermute x9, waiting for transfers between devices, z_summed(): got = lax.ppermute(other, 'z', [(k, k ^ i) for k in range(4)])  60.5 us
    ppermute x9, starting transfers between devices, gather_z(): lax.ppermute(own, 'z', [(k, k ^ i) for k in range(4)])  35.5 us
    pallas_call x2, Pallas kernels, whole_call(): pl.pallas_call(kernel, in_specs=[pl.BlockSpec(memory_space=pltpu.SMEM)] +...  31.8 us
    ppermute x46, starting transfers between devices, swap(): return lax.ppermute(value, axis, PAIR)  30.4 us
    dot_general x12, matrix products, contract(): lax.dot_general(a, b, (dims, ((), ())), preferred_element_type=jnp.float32)  26.8 us
    pallas_call x1, Pallas kernels, feed_forward(): pl.pallas_call(partial(ffn_kernel, [step for step, _ in pieces]), grid=(h...  24.2 us
    ppermute x9, waiting for transfers between devices, gather_z(): lax.ppermute(own, 'z', [(k, k ^ i) for k in range(4)])  22.2 us
  transfers between devices with their start and end apart: 70, of which 22 were waited for; matrix products, arithmetic and copies ran while one was open for 22% of the time, Pallas kernels for 9%

profile of v3, /device:TPU:0, one launch (start us, length us, event | category | flops | bytes accessed | tf_op | source)
XLA Modules:
  0.0 543.9 jit_solution(16343427031178647820)
XLA Ops:
  16.5 6.0 %all-to-all-start = ((bf16[8,64,768]{2,1,0:T(8,128)(2,1)}), bf16[8,64,768]{2,1,0:T(8,128)(2,1)}, u32[]{:S(2)}, u32[]{:S(2)}) async-start(bf16[8,64,768]{2,1,0:T(8,128)(2,1)} %bitcast.9), calls=%async_computation | async-start | bytes 1572864 | tf_op jit(solution)/shard_map/all_to_all | solution.py:349
  22.6 6.2 %collective-permute-done.3 = bf16[112,1152]{1,0:T(8,128)(2,1)} collective-permute-done((bf16[112,1152]{1,0:T(8,128)(2,1)}, bf16[112,1152]{1,0:T(8,128)(2,1)}, u32[]{:S(2)}, u32[]{:S(2)}) %collective-permute-start.3) | collective-permute-done | bytes 258080 | tf_op jit(solution)/shard_map/ppermute | solution.py:366
  38.7 12.5 %collective-permute-start.7 = (bf16[5,48,384]{2,1,0:T(8,128)(2,1)S(1)}, bf16[5,48,384]{2,1,0:T(8,128)(2,1)S(1)}, u32[]{:S(2)}, u32[]{:S(2)}) collective-permute-start(bf16[5,48,384]{2,1,0:T(8,128)(2,1)S(1)} %dynamic-slice_bitcast_fusion.17), channel_id=1, source_target_pairs={{0,8},{8,0},{16,24},{24,16},{1,9},{9,1},{17,25},{25,17},{2,10},{10... | collective-permute-start | bytes 552968 | tf_op jit(solution)/shard_map/ppermute | solution.py:366
  70.2 9.5 %collective-permute-start.10 = (bf16[96,1536]{1,0:T(8,128)(2,1)S(1)}, bf16[96,1536]{1,0:T(8,128)(2,1)S(1)}, u32[]{:S(2)}, u32[]{:S(2)}) collective-permute-start(bf16[96,1536]{1,0:T(8,128)(2,1)S(1)} %fusion.60), channel_id=1, source_target_pairs={{0,8},{8,0},{16,24},{24,16},{1,9},{9,1},{17,25},{25,17},{2,10},{10... | collective-permute-start | bytes 884744 | tf_op jit(solution)/shard_map/ppermute | solution.py:366
  92.0 6.4 %all-to-all-start.1 = ((bf16[8,64,768]{2,1,0:T(8,128)(2,1)}), bf16[8,64,768]{2,1,0:T(8,128)(2,1)}, u32[]{:S(2)}, u32[]{:S(2)}) async-start(bf16[8,64,768]{2,1,0:T(8,128)(2,1)} %bitcast.40), calls=%async_computation.1 | async-start | bytes 1572864 | tf_op jit(solution)/shard_map/all_to_all | solution.py:349
  98.6 16.0 %collective-permute-done.11 = bf16[96,1536]{1,0:T(8,128)(2,1)} collective-permute-done((bf16[96,1536]{1,0:T(8,128)(2,1)S(1)}, bf16[96,1536]{1,0:T(8,128)(2,1)}, u32[]{:S(2)}, u32[]{:S(2)}) %collective-permute-start.11) | collective-permute-done | bytes 294944 | tf_op jit(solution)/shard_map/ppermute | solution.py:366
  122.4 13.9 %collective-permute-done.17.refs_2_ = bf16[4,5,48,384]{3,2,1,0:T(8,128)(2,1)} collective-permute-done((bf16[4,5,48,384]{3,2,1,0:T(8,128)(2,1)S(1)}, bf16[4,5,48,384]{3,2,1,0:T(8,128)(2,1)}, u32[]{:S(2)}, u32[]{:S(2)}) %collective-permute-start.17) | collective-permute-done | bytes 737312 | tf_op jit(solution)/shard_map/ppermute | solution.py:319
  136.3 10.2 %collective-permute-done.18.refs_3_ = bf16[4,5,48,384]{3,2,1,0:T(8,128)(2,1)} collective-permute-done((bf16[4,5,48,384]{3,2,1,0:T(8,128)(2,1)}, bf16[4,5,48,384]{3,2,1,0:T(8,128)(2,1)}, u32[]{:S(2)}, u32[]{:S(2)}) %collective-permute-start.18) | collective-permute-done | bytes 737312 | tf_op jit(solution)/shard_map/ppermute | solution.py:319
  170.2 11.8 %shard_map.298 = (bf16[512,768]{1,0:T(8,128)(2,1)}, bf16[512,768]{1,0:T(8,128)(2,1)}, bf16[512,768]{1,0:T(8,128)(2,1)}, bf16[8,64,2304]{2,1,0:T(8,128)(2,1)}, bf...) custom-call(s32[5]{0:T(128)} %copy-done.9, bf16[512,768]{1,0:T(8,128)(2,1)} %bitcast.10.x_ref, ...), custom_call_target="tpu_custom_call" | custom-call | tf_op jit(solution)/shard_map/pallas_call | solution.py:743
  182.5 24.3 %collective-permute-done.28.refs_3_ = bf16[4,96,1536]{2,1,0:T(8,128)(2,1)} collective-permute-done((bf16[4,96,1536]{2,1,0:T(8,128)(2,1)}, bf16[4,96,1536]{2,1,0:T(8,128)(2,1)}, u32[]{:S(2)}, u32[]{:S(2)}) %collective-permute-start.28) | collective-permute-done | bytes 1179680 | tf_op jit(solution)/shard_map/ppermute | solution.py:319
  207.7 24.2 %shard_map.299 = (f32[512,768]{1,0:T(8,128)}, bf16[512,768]{1,0:T(8,128)(2,1)}, f32[512,768]{1,0:T(8,128)}, bf16[512,768]{1,0:T(8,128)(2,1)}, bf16[768,1536]{1,0:T(8,128)(2,1)}, /*index=5*/bf16[768,1536]{1,0:T(8,128)(2,1)}) custom-call(s32[4]{0:T(128)} %copy-done.11, bf16[512,768]{1,0:T(8,128)(2,1)} %get-tuple-element.64.a_ref, bf16[512,768]{1,0:T(8,128)(2,1)} %copy-done.38, ...), custom_call_target="tpu_custom_call" | custom-call | tf_op jit(solution)/shard_map/pallas_call | solution.py:822
  235.0 19.9 %shard_map.300 = (bf16[512,768]{1,0:T(8,128)(2,1)}, bf16[8,64,2304]{2,1,0:T(8,128)(2,1)}, bf16[512,768]{1,0:T(8,128)(2,1)}, bf16[512,384]{1,0:T(8,128)(2,1)}, bf...) custom-call(s32[5]{0:T(128)} %copy-done.9, bf16[512,768]{1,0:T(8,128)(2,1)} %bitcast.229, f32[512,768]{1,0:T(8,128)} %get-tuple-element.67.da_ref, ...), custom_call_target="tpu_custom_call" | custom-call | tf_op jit(solution)/shard_map/pallas_call | solution.py:743
  259.2 14.5 %all-to-all-start.2 = ((bf16[8,64,768]{2,1,0:T(8,128)(2,1)}), bf16[8,64,768]{2,1,0:T(8,128)(2,1)}, u32[]{:S(2)}, u32[]{:S(2)}) async-start(bf16[8,64,768]{2,1,0:T(8,128)(2,1)} %bitcast.42), calls=%async_computation.2 | async-start | bytes 1572864 | tf_op jit(solution)/shard_map/all_to_all | solution.py:354
  298.9 7.7 %shard_map.301 = (bf16[2,8,64,384]{3,2,1,0:T(8,128)(2,1)S(1)}, bf16[2,8,64,384]{3,2,1,0:T(8,128)(2,1)S(1)}, bf16[2,8,64,384]{3,2,1,0:T(8,128)(2,1)S(1)}, bf16[2,...) custom-call(s32[5]{0:T(128)S(1)} %copy-done.10, f32[1]{0:T(128)} %bitcast.12.tie_ref, ...), custom_call_target="tpu_custom_call" | custom-call | tf_op jit(solution)/shard_map/pallas_call | solution.py:578
  328.4 37.3 %collective-permute-done.53 = bf16[4,96,1536]{2,1,0:T(8,128)(2,1)S(1)} collective-permute-done((bf16[4,96,1536]{2,1,0:T(8,128)(2,1)S(1)}, bf16[4,96,1536]{2,1,0:T(8,128)(2,1)S(1)}, u32[]{:S(2)}, u32[]{:S(2)}) %collective-permute-start.53) | collective-permute-done | bytes 1179680 | tf_op jit(solution)/shard_map/ppermute | solution.py:319
  371.6 7.5 %collective-permute-done.54 = bf16[96,1536]{1,0:T(8,128)(2,1)S(1)} collective-permute-done((bf16[96,1536]{1,0:T(8,128)(2,1)S(1)}, bf16[96,1536]{1,0:T(8,128)(2,1)S(1)}, u32[]{:S(2)}, u32[]{:S(2)}) %collective-permute-start.54) | collective-permute-done | bytes 294944 | tf_op jit(solution)/shard_map/ppermute | solution.py:852
  380.6 10.7 %collective-permute-done.55 = bf16[96,1536]{1,0:T(8,128)(2,1)S(1)} collective-permute-done((bf16[96,1536]{1,0:T(8,128)(2,1)S(1)}, bf16[96,1536]{1,0:T(8,128)(2,1)S(1)}, u32[]{:S(2)}, u32[]{:S(2)}) %collective-permute-start.55) | collective-permute-done | bytes 294944 | tf_op jit(solution)/shard_map/ppermute | solution.py:852
  403.8 7.0 %all-to-all-start.3 = ((bf16[8,64,768]{2,1,0:T(8,128)(2,1)}), bf16[8,64,768]{2,1,0:T(8,128)(2,1)}, u32[]{:S(2)}, u32[]{:S(2)}) async-start(bf16[8,64,768]{2,1,0:T(8,128)(2,1)} %bitcast.236), calls=%async_computation.3 | async-start | bytes 1572864 | tf_op jit(solution)/shard_map/all_to_all | solution.py:354
  419.7 13.3 %collective-permute-done.40 = bf16[112,1152]{1,0:T(8,128)(2,1)S(1)} collective-permute-done((bf16[112,1152]{1,0:T(8,128)(2,1)S(1)}, bf16[112,1152]{1,0:T(8,128)(2,1)S(1)}, u32[]{:S(2)}, u32[]{:S(2)}) %collective-permute-start.40) | collective-permute-done | bytes 258080 | tf_op jit(solution)/shard_map/ppermute | solution.py:852
  433.0 16.2 %collective-permute-done.41 = bf16[112,1152]{1,0:T(8,128)(2,1)S(1)} collective-permute-done((bf16[112,1152]{1,0:T(8,128)(2,1)S(1)}, bf16[112,1152]{1,0:T(8,128)(2,1)S(1)}, u32[]{:S(2)}, u32[]{:S(2)}) %collective-permute-start.41) | collective-permute-done | bytes 258080 | tf_op jit(solution)/shard_map/ppermute | solution.py:852
  457.5 9.7 %collective-permute-done.48 = bf16[4,48,1920]{2,1,0:T(8,128)(2,1)S(1)} collective-permute-done((bf16[4,48,1920]{2,1,0:T(8,128)(2,1)S(1)}, bf16[4,48,1920]{2,1,0:T(8,128)(2,1)S(1)}, u32[]{:S(2)}, u32[]{:S(2)}) %collective-permute-start.48) | collective-permute-done | bytes 737312 | tf_op jit(solution)/shard_map/ppermute | solution.py:319
  467.5 6.2 %collective-permute-start.49 = (bf16[48,1920]{1,0:T(8,128)(2,1)S(1)}, bf16[48,1920]{1,0:T(8,128)(2,1)S(1)}, u32[]{:S(2)}, u32[]{:S(2)}) collective-permute-start(bf16[48,1920]{1,0:T(8,128)(2,1)S(1)} %get-tuple-element.138), channel_id=1, source_target_pairs={{0,8},{8,0},{16,24},{24,16},{1,9},{9,1},{17,25},{25,17},{2,10},{10... | collective-permute-start | bytes 552968 | tf_op jit(solution)/shard_map/ppermute | solution.py:852
  479.5 9.5 %collective-permute-done.50 = bf16[48,1920]{1,0:T(8,128)(2,1)S(1)} collective-permute-done((bf16[48,1920]{1,0:T(8,128)(2,1)S(1)}, bf16[48,1920]{1,0:T(8,128)(2,1)S(1)}, u32[]{:S(2)}, u32[]{:S(2)}) %collective-permute-start.50) | collective-permute-done | bytes 184352 | tf_op jit(solution)/shard_map/ppermute | solution.py:852
  534.0 6.9 %fusion.90 = (bf16[8,96,768]{2,1,0:T(8,128)(2,1)}, f32[8,96,768]{2,1,0:T(8,128)}, f32[8,96,768]{2,1,0:T(8,128)}, f32[8,96,768]{2,1,0:T(8,128)}) fusion(f32[8,96,768]{2,1,0:T(8,128)S(1)} %copy-done.17, f32[]{:T(128)S(6)} %div.78, bf16[8,96,768]{2,1,0:T(8,128)(2,1)} %fusion.78, f32[8,96,768]{2,1,0:T(8,128)S(1)} %copy-done.28, f32[8,96,768]{2,1,0:T(8,128)} %param.24), kind=kLoop, calls=%fused_computation.248 | loop fusion | flops 10027008 | bytes 16515076 | tf_op jit(solution)/shard_map/convert_element_type | solution.py:1104
  (399 shorter events, 226.2 us)
Async XLA Ops:
  15.5 67.0 %collective-permute-start.24 = (bf16[2,2,64,768]{3,2,1,0:T(8,128)(2,1)}, bf16[2,2,64,768]{3,2,1,0:T(8,128)(2,1)}, u32[]{:S(2)}, u32[]{:S(2)}) collective-permute-start(bf16[2,2,64,768]{3,2,1,0:T(8,128)(2,1)} %get-tuple-element.133), channel_id=1, source_target_pairs={{0,1},{1,0},{2,3},{3,2},{4,5},{5,4},{6,7},{7,6},{8,9},{9,8},{10,11... | collective-permute-start | bytes 1179656 | tf_op jit(solution)/shard_map/ppermute | solution.py:319
  16.5 47.0 %all-to-all-start = ((bf16[8,64,768]{2,1,0:T(8,128)(2,1)}), bf16[8,64,768]{2,1,0:T(8,128)(2,1)}, u32[]{:S(2)}, u32[]{:S(2)}) async-start(bf16[8,64,768]{2,1,0:T(8,128)(2,1)} %bitcast.9), calls=%async_computation | async-start | bytes 1572864 | tf_op jit(solution)/shard_map/all_to_all | solution.py:349
  79.9 38.4 %collective-permute-start.6 = (bf16[512,768]{1,0:T(8,128)(2,1)S(1)}, bf16[512,768]{1,0:T(8,128)(2,1)S(1)}, u32[]{:S(2)}, u32[]{:S(2)}) collective-permute-start(bf16[512,768]{1,0:T(8,128)(2,1)S(1)} %add_convert_fusion.3), channel_id=1, source_target_pairs={{0,1},{1,0},{2,3},{3,2},{4,5},{5,4},{6,7},{7,6},{8,9},{9,8},{10,11... | collective-permute-start | bytes 2359304 | tf_op jit(solution)/shard_map/ppermute | solution.py:319
  80.0 38.3 %collective-permute-start.16 = (bf16[4,5,48,384]{3,2,1,0:T(8,128)(2,1)S(1)}, bf16[4,5,48,384]{3,2,1,0:T(8,128)(2,1)}, u32[]{:S(2)}, u32[]{:S(2)}) collective-permute-start(bf16[4,5,48,384]{3,2,1,0:T(8,128)(2,1)S(1)} %pad_maximum_fusion.7.refs_0_), channel_id=1, source_target_pairs={{0,4},{4,0},{1,5},{5,1},{2,6},{6,2},{3,7},{7,3},{8,12},{12,8},{9,1... | collective-permute-start | bytes 2211848 | tf_op jit(solution)/shard_map/ppermute | solution.py:319
  82.5 32.0 %collective-permute-start.11 = (bf16[96,1536]{1,0:T(8,128)(2,1)S(1)}, bf16[96,1536]{1,0:T(8,128)(2,1)}, u32[]{:S(2)}, u32[]{:S(2)}) collective-permute-start(bf16[96,1536]{1,0:T(8,128)(2,1)S(1)} %fusion.60), channel_id=1, source_target_pairs={{0,16},{8,24},{16,0},{24,8},{1,17},{9,25},{17,1},{25,9},{2,18},{10... | collective-permute-start | bytes 884744 | tf_op jit(solution)/shard_map/ppermute | solution.py:366
  92.0 67.2 %all-to-all-start.1 = ((bf16[8,64,768]{2,1,0:T(8,128)(2,1)}), bf16[8,64,768]{2,1,0:T(8,128)(2,1)}, u32[]{:S(2)}, u32[]{:S(2)}) async-start(bf16[8,64,768]{2,1,0:T(8,128)(2,1)} %bitcast.40), calls=%async_computation.1 | async-start | bytes 1572864 | tf_op jit(solution)/shard_map/all_to_all | solution.py:349
  98.5 48.0 %collective-permute-start.14 = (bf16[512,768]{1,0:T(8,128)(2,1)}, bf16[512,768]{1,0:T(8,128)(2,1)S(1)}, u32[]{:S(2)}, u32[]{:S(2)}) collective-permute-start(bf16[512,768]{1,0:T(8,128)(2,1)} %collective-permute-done.13), channel_id=1, source_target_pairs={{0,1},{1,0},{2,3},{3,2},{4,5},{5,4},{6,7},{7,6},{8,9},{9,8},{10,11... | collective-permute-start | bytes 2359304 | tf_op jit(solution)/shard_map/ppermute | solution.py:319
  116.8 36.6 %collective-permute-start.26 = (bf16[4,96,1536]{2,1,0:T(8,128)(2,1)}, bf16[4,96,1536]{2,1,0:T(8,128)(2,1)}, u32[]{:S(2)}, u32[]{:S(2)}) collective-permute-start(bf16[4,96,1536]{2,1,0:T(8,128)(2,1)} %pad_maximum_fusion.4.refs_0_), channel_id=1, source_target_pairs={{0,4},{4,0},{1,5},{5,1},{2,6},{6,2},{3,7},{7,3},{8,12},{12,8},{9,1... | collective-permute-start | bytes 3538952 | tf_op jit(solution)/shard_map/ppermute | solution.py:319
  118.3 36.6 %collective-permute-start.19 = (bf16[4,5,48,384]{3,2,1,0:T(8,128)(2,1)S(1)}, bf16[4,5,48,384]{3,2,1,0:T(8,128)(2,1)S(1)}, u32[]{:S(2)}, u32[]{:S(2)}) collective-permute-start(bf16[4,5,48,384]{3,2,1,0:T(8,128)(2,1)S(1)} %pad_maximum_fusion.7.refs_0_), channel_id=1, source_target_pairs={{0,1},{1,0},{2,3},{3,2},{4,5},{5,4},{6,7},{7,6},{8,9},{9,8},{10,11... | collective-permute-start | bytes 2211848 | tf_op jit(solution)/shard_map/ppermute | solution.py:319
  155.8 51.1 %collective-permute-start.28 = (bf16[4,96,1536]{2,1,0:T(8,128)(2,1)}, bf16[4,96,1536]{2,1,0:T(8,128)(2,1)}, u32[]{:S(2)}, u32[]{:S(2)}) collective-permute-start(bf16[4,96,1536]{2,1,0:T(8,128)(2,1)} %collective-permute-done.26.refs_1_), channel_id=1, source_target_pairs={{0,2},{2,0},{1,3},{3,1},{4,6},{6,4},{5,7},{7,5},{8,10},{10,8},{9,1... | collective-permute-start | bytes 3538952 | tf_op jit(solution)/shard_map/ppermute | solution.py:319
  232.5 63.2 %collective-permute-start.33 = (bf16[768,1536]{1,0:T(8,128)(2,1)}, bf16[768,1536]{1,0:T(8,128)(2,1)}, u32[]{:S(2)}, u32[]{:S(2)}) collective-permute-start(bf16[768,1536]{1,0:T(8,128)(2,1)} %get-tuple-element.75), channel_id=1, source_target_pairs={{0,2},{2,0},{1,3},{3,1},{4,6},{6,4},{5,7},{7,5},{8,10},{10,8},{9,1... | collective-permute-start | bytes 7077896 | tf_op jit(solution)/shard_map/ppermute | solution.py:319
  259.2 35.2 %all-to-all-start.2 = ((bf16[8,64,768]{2,1,0:T(8,128)(2,1)}), bf16[8,64,768]{2,1,0:T(8,128)(2,1)}, u32[]{:S(2)}, u32[]{:S(2)}) async-start(bf16[8,64,768]{2,1,0:T(8,128)(2,1)} %bitcast.42), calls=%async_computation.2 | async-start | bytes 1572864 | tf_op jit(solution)/shard_map/all_to_all | solution.py:354
  285.0 34.8 %collective-permute-start.45 = (bf16[768,1152]{1,0:T(8,128)(2,1)}, bf16[768,1152]{1,0:T(8,128)(2,1)}, u32[]{:S(2)}, u32[]{:S(2)}) collective-permute-start(bf16[768,1152]{1,0:T(8,128)(2,1)} %convolution_convert_fusion.1), channel_id=1, source_target_pairs={{0,1},{1,0},{2,3},{3,2},{4,5},{5,4},{6,7},{7,6},{8,9},{9,8},{10,11... | collective-permute-start | bytes 5308424 | tf_op jit(solution)/shard_map/ppermute | solution.py:319
  310.4 83.3 %collective-permute-start.34 = (bf16[512,768]{1,0:T(8,128)(2,1)S(1)}, bf16[512,768]{1,0:T(8,128)(2,1)S(1)}, u32[]{:S(2)}, u32[]{:S(2)}) collective-permute-start(bf16[512,768]{1,0:T(8,128)(2,1)S(1)} %slice.375), channel_id=1, source_target_pairs={{0,1},{1,0},{2,3},{3,2},{4,5},{5,4},{6,7},{7,6},{8,9},{9,8},{10,11... | collective-permute-start | bytes 2359304 | tf_op jit(solution)/shard_map/ppermute | solution.py:319
  317.8 52.4 %collective-permute-start.38 = (bf16[4,96,1152]{2,1,0:T(8,128)(2,1)S(1)}, bf16[4,96,1152]{2,1,0:T(8,128)(2,1)S(1)}, u32[]{:S(2)}, u32[]{:S(2)}) collective-permute-start(bf16[4,96,1152]{2,1,0:T(8,128)(2,1)S(1)} %fusion.30), channel_id=1, source_target_pairs={{0,4},{4,0},{1,5},{5,1},{2,6},{6,2},{3,7},{7,3},{8,12},{12,8},{9,1... | collective-permute-start | bytes 2654216 | tf_op jit(solution)/shard_map/ppermute | solution.py:319
  319.8 45.9 %collective-permute-start.53 = (bf16[4,96,1536]{2,1,0:T(8,128)(2,1)S(1)}, bf16[4,96,1536]{2,1,0:T(8,128)(2,1)S(1)}, u32[]{:S(2)}, u32[]{:S(2)}) collective-permute-start(bf16[4,96,1536]{2,1,0:T(8,128)(2,1)S(1)} %dynamic-slice_bitcast_fusion.1), channel_id=1, source_target_pairs={{0,4},{4,0},{1,5},{5,1},{2,6},{6,2},{3,7},{7,3},{8,12},{12,8},{9,1... | collective-permute-start | bytes 3538952 | tf_op jit(solution)/shard_map/ppermute | solution.py:319
  326.6 67.1 %collective-permute-start.36 = (bf16[512,768]{1,0:T(8,128)(2,1)S(1)}, bf16[512,768]{1,0:T(8,128)(2,1)S(1)}, u32[]{:S(2)}, u32[]{:S(2)}) collective-permute-start(bf16[512,768]{1,0:T(8,128)(2,1)S(1)} %fusion.8), channel_id=1, source_target_pairs={{0,4},{4,0},{1,5},{5,1},{2,6},{6,2},{3,7},{7,3},{8,12},{12,8},{9,1... | collective-permute-start | bytes 2359304 | tf_op jit(solution)/shard_map/ppermute | solution.py:319
  379.1 38.6 %collective-permute-start.47 = (bf16[8,48,1920]{2,1,0:T(8,128)(2,1)}, bf16[8,48,1920]{2,1,0:T(8,128)(2,1)}, u32[]{:S(2)}, u32[]{:S(2)}) collective-permute-start(bf16[8,48,1920]{2,1,0:T(8,128)(2,1)} %dynamic-slice_bitcast_fusion), channel_id=1, source_target_pairs={{0,2},{2,0},{1,3},{3,1},{4,6},{6,4},{5,7},{7,5},{8,10},{10,8},{9,1... | collective-permute-start | bytes 4423688 | tf_op jit(solution)/shard_map/ppermute | solution.py:319
  392.1 59.2 %collective-permute-start.57 = (bf16[96,1536]{1,0:T(8,128)(2,1)S(1)}, bf16[96,1536]{1,0:T(8,128)(2,1)S(1)}, u32[]{:S(2)}, u32[]{:S(2)}) collective-permute-start(bf16[96,1536]{1,0:T(8,128)(2,1)S(1)} %get-tuple-element.109), channel_id=1, source_target_pairs={{0,2},{2,0},{1,3},{3,1},{4,6},{6,4},{5,7},{7,5},{8,10},{10,8},{9,1... | collective-permute-start | bytes 884744 | tf_op jit(solution)/shard_map/ppermute | solution.py:319
  393.6 123.8 %collective-permute-start.64 = (bf16[96,1536]{1,0:T(8,128)(2,1)S(1)}, bf16[96,1536]{1,0:T(8,128)(2,1)}, u32[]{:S(2)}, u32[]{:S(2)}) collective-permute-start(bf16[96,1536]{1,0:T(8,128)(2,1)S(1)} %get-tuple-element.109), channel_id=1, source_target_pairs={{0,1},{1,0},{2,3},{3,2},{4,5},{5,4},{6,7},{7,6},{8,9},{9,8},{10,11... | collective-permute-start | bytes 884744 | tf_op jit(solution)/shard_map/ppermute | solution.py:319
  403.8 124.2 %all-to-all-start.3 = ((bf16[8,64,768]{2,1,0:T(8,128)(2,1)}), bf16[8,64,768]{2,1,0:T(8,128)(2,1)}, u32[]{:S(2)}, u32[]{:S(2)}) async-start(bf16[8,64,768]{2,1,0:T(8,128)(2,1)} %bitcast.236), calls=%async_computation.3 | async-start | bytes 1572864 | tf_op jit(solution)/shard_map/all_to_all | solution.py:354
  415.3 33.9 %collective-permute-start.41 = (bf16[112,1152]{1,0:T(8,128)(2,1)S(1)}, bf16[112,1152]{1,0:T(8,128)(2,1)S(1)}, u32[]{:S(2)}, u32[]{:S(2)}) collective-permute-start(bf16[112,1152]{1,0:T(8,128)(2,1)S(1)} %get-tuple-element.126), channel_id=1, source_target_pairs={{0,16},{8,24},{16,0},{24,8},{1,17},{9,25},{17,1},{25,9},{2,18},{10... | collective-permute-start | bytes 774152 | tf_op jit(solution)/shard_map/ppermute | solution.py:852
  417.7 31.5 %collective-permute-start.42 = (bf16[112,1152]{1,0:T(8,128)(2,1)S(1)}, bf16[112,1152]{1,0:T(8,128)(2,1)S(1)}, u32[]{:S(2)}, u32[]{:S(2)}) collective-permute-start(bf16[112,1152]{1,0:T(8,128)(2,1)S(1)} %get-tuple-element.127), channel_id=1, source_target_pairs={{0,24},{8,16},{16,8},{24,0},{1,25},{9,17},{17,9},{25,1},{2,26},{10... | collective-permute-start | bytes 774152 | tf_op jit(solution)/shard_map/ppermute | solution.py:852
  451.3 66.2 %collective-permute-start.65 = (bf16[96,1536]{1,0:T(8,128)(2,1)S(1)}, bf16[96,1536]{1,0:T(8,128)(2,1)S(1)}, u32[]{:S(2)}, u32[]{:S(2)}) collective-permute-start(bf16[96,1536]{1,0:T(8,128)(2,1)S(1)} %collective-permute-done.57), channel_id=1, source_target_pairs={{0,1},{1,0},{2,3},{3,2},{4,5},{5,4},{6,7},{7,6},{8,9},{9,8},{10,11... | collective-permute-start | bytes 884744 | tf_op jit(solution)/shard_map/ppermute | solution.py:319
  (116 other events, 1432.8 us)

commit v4 on v3

--- a/solution.py
+++ b/solution.py
@@ -339,14 +339,13 @@
     )
 
 
-def to_columns(value, c):
+def merge_cores(value, c):
     prot, _, cols, width = value.shape
     part = cols // 4
     split = value.reshape(prot, 2, 2, part, width)
     got = swap(pick(split, 1 - c, 2), "c")
     both = merge(pick(split, c, 2), got, c, 0)
-    both = both.reshape(8, part, width)
-    return lax.all_to_all(both, ("z", "x"), 0, 0, tiled=True)
+    return both.reshape(8, part, width)
 
 
 def to_rows(value, c):
@@ -358,13 +357,12 @@
     return both.reshape(2, 1, 4 * part, width)
 
 
-def after(value, *earlier):
-    return lax.optimization_barrier((value, *earlier))[0]
+def together(*values):
+    return lax.optimization_barrier(values)
 
 
 def gather_z(own):
-    others = [lax.ppermute(own, "z", [(k, k ^ i) for k in range(4)]) for i in (1, 2, 3)]
-    return jnp.stack([own] + others)
+    return [own] + [lax.ppermute(own, "z", [(k, k ^ i) for k in range(4)]) for i in (1, 2, 3)]
 
 
 def spread(over_z):
@@ -412,11 +410,11 @@
 
 
 def row_attn_at(ref, outs, shard, y, c):
-    depth = outs[0].shape[0] // 8
-    at = pl.multiple_of(shard * depth, depth)
+    depth = outs[0].shape[0] // 16
+    at = pl.multiple_of((shard * 2 + y) * depth, depth)
     return [
         (ref.at[pl.ds(0, depth)], outs[0].at[pl.ds(at, depth)]),
-        (ref.at[pl.ds(depth, 16)], outs[1].at[shard]),
+        (ref.at[pl.ds(depth, 16)], outs[1].at[shard * 2 + y]),
     ]
 
 
@@ -506,45 +504,87 @@
 
 
 def row_bwd_kernel(
-    info_ref, tie_ref, q_ref, k_ref, v_ref, kf_ref, vf_ref, do_ref,
-    dq_ref, dk_ref, dv_ref, dkf_ref, dvf_ref,
+    info_ref, tie_ref, near_ref, far_ref, own_ref, got_ref, w_ref, near_tokens_ref, far_tokens_ref,
+    near_part_ref, near_theirs_ref, far_part_ref, far_theirs_ref, sent_ref, kept_ref,
+    do_ref, d_near_ref, d_far_ref,
 ):
     bf16 = jnp.bfloat16
-    blocks, rows, part, lanes = q_ref.shape
+    blocks, rows, part, lanes = near_ref.shape
+    half = lanes // 3
     near = blocks * part
-    sides = head_lanes(2 * lanes)
+    sides = head_lanes(2 * TILE)
     keep = column_keep(info_ref, near, near, part)
     tie = tie_ref[0]
-    scores = [jnp.zeros((near, 2 * near), jnp.float32) for _ in sides]
-    grads = [jnp.zeros((near, 2 * near), jnp.float32) for _ in sides]
-    for row in range(0, rows, 2):
-        query = live_pair(row_pair(q_ref, row), row, info_ref)
-        key = jnp.concatenate([row_pair(k_ref, row), row_pair(kf_ref, row)], axis=0)
-        value = jnp.concatenate([row_pair(v_ref, row), row_pair(vf_ref, row)], axis=0)
-        out = row_pair(do_ref, row)
-        for n, side in enumerate(sides):
-            scores[n] = scores[n] + contract(only(side, query), key, LAST)
-            grads[n] = grads[n] + contract(only(side, out), value, LAST)
-    probs = [softmax_of(s * tie, keep) for s in scores]
-    lows = [p.astype(bf16) for p in probs]
-    deltas = [softmax_back(p, g).astype(bf16) for p, g in zip(probs, grads)]
-    for row in range(0, rows, 2):
-        query = live_pair(row_pair(q_ref, row), row, info_ref)
-        key = jnp.concatenate([row_pair(k_ref, row), row_pair(kf_ref, row)], axis=0)
-        out = row_pair(do_ref, row)
-        dq = [contract(d, key, PLAIN) for d in deltas]
-        dk = [contract(d, query, FIRST) for d in deltas]
-        dv = [contract(p, out, FIRST) for p in lows]
-        dq = live_pair(jnp.where(sides[0], dq[0], dq[1]) * tie, row, info_ref).astype(bf16)
-        dk = (jnp.where(sides[0], dk[0], dk[1]) * tie).astype(bf16)
-        dv = jnp.where(sides[0], dv[0], dv[1]).astype(bf16)
-        for n in (0, 1):
-            at = slice(n * lanes, (n + 1) * lanes)
-            dq_ref[:, row + n] = dq[:, at].reshape(blocks, part, lanes)
-            dk_ref[:, row + n] = dk[:near, at].reshape(blocks, part, lanes)
-            dv_ref[:, row + n] = dv[:near, at].reshape(blocks, part, lanes)
-            dkf_ref[:, row + n] = dk[near:, at].reshape(blocks, part, lanes)
-            dvf_ref[:, row + n] = dv[near:, at].reshape(blocks, part, lanes)
+    do_ref[0] = own_ref[...].reshape(rows, part, half)
+    do_ref[1] = got_ref[...].reshape(rows, part, half)
+
+    for lane in range(0, half, TILE):
+
+        def pair(ref, row, first):
+            at = slice(first + lane, first + lane + TILE)
+            found = [ref[:, row + n, :, at].reshape(near, TILE) for n in (0, 1)]
+            return jnp.concatenate(found, axis=1)
+
+        def both(row, first):
+            return jnp.concatenate(
+                [pair(near_ref, row, first), pair(far_ref, row, first - half)], axis=0
+            )
+
+        scores = [jnp.zeros((near, 2 * near), jnp.float32) for _ in sides]
+        grads = [jnp.zeros((near, 2 * near), jnp.float32) for _ in sides]
+        for row in range(0, rows, 2):
+            query = live_pair(pair(near_ref, row, 0), row, info_ref)
+            key, value = both(row, half), both(row, 2 * half)
+            out = pair(do_ref, row, 0)
+            for n, side in enumerate(sides):
+                scores[n] = scores[n] + contract(only(side, query), key, LAST)
+                grads[n] = grads[n] + contract(only(side, out), value, LAST)
+        probs = [softmax_of(s * tie, keep) for s in scores]
+        lows = [p.astype(bf16) for p in probs]
+        deltas = [softmax_back(p, g).astype(bf16) for p, g in zip(probs, grads)]
+        low_turned = [p.T for p in lows]
+        delta_turned = [d.T for d in deltas]
+        for row in range(0, rows, 2):
+            query = live_pair(pair(near_ref, row, 0), row, info_ref)
+            key, out = both(row, half), pair(do_ref, row, 0)
+            dq = [contract(d, key, PLAIN) for d in deltas]
+            dk = [contract(d, query, PLAIN) for d in delta_turned]
+            dv = [contract(p, out, PLAIN) for p in low_turned]
+            dq = live_pair(jnp.where(sides[0], dq[0], dq[1]) * tie, row, info_ref).astype(bf16)
+            dk = (jnp.where(sides[0], dk[0], dk[1]) * tie).astype(bf16)
+            dv = jnp.where(sides[0], dv[0], dv[1]).astype(bf16)
+
+            def put(ref, first, value):
+                for n in (0, 1):
+                    piece = value[:, n * TILE : (n + 1) * TILE].reshape(blocks, part, TILE)
+                    ref[:, row + n, :, first + lane : first + lane + TILE] = piece
+
+            put(d_near_ref, 0, dq)
+            put(d_near_ref, half, dk[:near])
+            put(d_near_ref, 2 * half, dv[:near])
+            put(d_far_ref, 0, dk[near:])
+            put(d_far_ref, half, dv[near:])
+
+    count = rows * part
+    d_far = d_far_ref[...].reshape(blocks * count, 2 * half)
+    far_weights = w_ref[:, half:]
+    far_part_ref[...] = contract(d_far[:count], far_weights, LAST)
+    far_theirs_ref[...] = contract(d_far[count:], far_weights, LAST).astype(bf16)
+    d_near = d_near_ref[...].reshape(blocks * count, lanes)
+    near_part_ref[...] = contract(d_near[:count], w_ref[...], LAST)
+    near_theirs_ref[...] = contract(d_near[count:], w_ref[...], LAST).astype(bf16)
+    near_turned = near_tokens_ref[...].T
+    far_turned = far_tokens_ref[...].T
+    zs, depth = kept_ref.shape[0], kept_ref.shape[1]
+    first = info_ref[1] == 0
+    for n in range(3):
+        at = slice(n * half, (n + 1) * half)
+        terms = contract(near_turned, d_near[:, at], PLAIN)
+        if n > 0:
+            terms = terms + contract(far_turned, d_far[:, (n - 1) * half : n * half], PLAIN)
+        terms = terms.astype(bf16).reshape(zs, 2, depth, half)
+        kept_ref[:, :, at] = jnp.where(first, terms[:, 0], terms[:, 1])
+        sent_ref[:, :, at] = jnp.where(first, terms[:, 1], terms[:, 0])
 
 
 def lane_block(shape, first):
@@ -569,23 +609,27 @@
     )(info, tie, near, near, near, far, far)
 
 
-def row_attention_back(info, tie, near, far, grad):
+def row_attention_back(info, tie, near, far, own, got, weights, near_tokens, far_tokens):
     blocks, rows, part, lanes = near.shape
-    tiles = lanes // 3 // TILE
-    shape = near.shape
+    count, width = rows * part, weights.shape[0]
+    half = lanes // 3
+    f32, bf16 = jnp.float32, jnp.bfloat16
     small = pl.BlockSpec(memory_space=pltpu.SMEM)
-    result = jax.ShapeDtypeStruct((blocks, rows, part, lanes // 3), jnp.bfloat16)
+    inside = pl.BlockSpec(memory_space=pltpu.VMEM)
+    shapes = [((count, width), kind) for kind in (f32, bf16) * 2]
+    shapes = shapes + [((4, width // 8, lanes), bf16)] * 2
     return pl.pallas_call(
         row_bwd_kernel,
-        grid=(tiles,),
-        in_specs=[small, small]
-        + [lane_block(shape, n * tiles) for n in range(3)]
-        + [lane_block(shape, n * tiles) for n in range(2)]
-        + [lane_block(shape, 0)],
-        out_specs=[lane_block(shape, 0)] * 5,
-        out_shape=[result] * 5,
-        compiler_params=pltpu.CompilerParams(vmem_limit_bytes=32 * 2**20),
-    )(info, tie, near, near, near, far, far, grad)
+        in_specs=[small, small] + [inside] * 7,
+        out_specs=[inside] * 6,
+        out_shape=[jax.ShapeDtypeStruct(shape, kind) for shape, kind in shapes],
+        scratch_shapes=[
+            pltpu.VMEM((blocks, rows, part, half), bf16),
+            pltpu.VMEM((blocks, rows, part, lanes), bf16),
+            pltpu.VMEM((blocks, rows, part, 2 * half), bf16),
+        ],
+        compiler_params=pltpu.CompilerParams(vmem_limit_bytes=56 * 2**20),
+    )(info, tie, near, far, own, got, weights, near_tokens, far_tokens)
 
 
 def normed(value, gain, shift):
@@ -627,7 +671,7 @@
 
 def col_fwd_kernel(
     info_ref, x_ref, own_ref, other_ref, three_ref, col_ref, seven_ref, gain_ref,
-    mixed_one_ref, one_ref, normed_two_ref, qkv_ref, mixed_ref, resid_ref, normed_three_ref,
+    acts_ref, one_ref, qkv_ref, resid_ref, normed_three_ref, mixed_ref,
 ):
     bf16 = jnp.bfloat16
     rows, cols, lanes = qkv_ref.shape
@@ -638,11 +682,11 @@
     mixed_one = jnp.concatenate(
         [jnp.where(flip, own, other), jnp.where(flip, other, own)], axis=1
     )
-    mixed_one_ref[...] = mixed_one
+    acts_ref[:, :width] = mixed_one
     stream = (x_ref[...].astype(jnp.float32) + contract(mixed_one, three_ref[...], PLAIN)).astype(bf16)
     one_ref[...] = stream
     normed_two = normed(stream.astype(jnp.float32), gain_ref[2:3], gain_ref[3:4])[0].astype(bf16)
-    normed_two_ref[...] = normed_two
+    acts_ref[:, width : 2 * width] = normed_two
     for n in range(3):
         at = slice(n * width, (n + 1) * width)
         found = contract(normed_two, col_ref[:, at], PLAIN).astype(bf16)
@@ -665,6 +709,7 @@
 
     lax.fori_loop(0, cols // part, attend, 0)
     mixed = mixed_ref[...].reshape(rows * cols, width)
+    acts_ref[:, 2 * width :] = mixed
     resid = one_ref[...].astype(jnp.float32) + contract(mixed, seven_ref[...], PLAIN)
     resid_ref[...] = resid
     normed_three_ref[...] = normed(resid, gain_ref[4:5], gain_ref[5:6])[0].astype(bf16)
@@ -672,7 +717,7 @@
 
 def col_bwd_kernel(
     info_ref, up_ref, da_ref, da_got_ref, resid_ref, one_ref, qkv_ref, three_ref, col_ref, seven_ref,
-    gain_ref, branch_ref, dqkv_ref, stream_ref, own_ref, other_ref, norms_ref, do_ref,
+    gain_ref, stream_ref, own_ref, other_ref, mine_ref, theirs_ref, norms_ref, dqkv_ref, do_ref,
 ):
     bf16 = jnp.bfloat16
     f32 = jnp.float32
@@ -686,7 +731,15 @@
     norms_ref[2:3] = jnp.sum(da * unit, axis=0, keepdims=True)
     norms_ref[3:4] = jnp.sum(da, axis=0, keepdims=True)
     branch = grad_three.astype(bf16)
-    branch_ref[...] = branch
+    half = width // 2
+    flip = info_ref[2] == 0
+
+    def put_halves(first, value):
+        at = slice(first, first + half)
+        mine_ref[:, at] = jnp.where(flip, value[:, :half], value[:, half:])
+        theirs_ref[:, at] = jnp.where(flip, value[:, half:], value[:, :half])
+
+    put_halves(4 * half, branch)
     do_ref[...] = contract(branch, seven_ref[...], LAST).astype(bf16).reshape(rows, cols, width)
     keep = column_masks(info_ref, rows, part)
     sides = head_lanes(TILE)
@@ -724,18 +777,38 @@
         return carry
 
     lax.fori_loop(0, cols // part, attend, 0)
-    grad_normed = contract(dqkv_ref[...].reshape(rows * cols, lanes), col_ref[...], LAST)
+    dqkv = dqkv_ref[...].reshape(rows * cols, lanes)
+    for n in range(3):
+        put_halves((n + 1) * half, dqkv[:, n * width : (n + 1) * width])
+    grad_normed = contract(dqkv, col_ref[...], LAST)
     gain = gain_ref[2:3]
     _, unit, scale = normed(one_ref[...].astype(f32), gain, 0.0)
     norms_ref[0:1] = jnp.sum(grad_normed * unit, axis=0, keepdims=True)
     norms_ref[1:2] = jnp.sum(grad_normed, axis=0, keepdims=True)
     stream = (grad_three + normed_back(grad_normed, unit, scale, gain)).astype(bf16)
     stream_ref[...] = stream
+    put_halves(0, stream)
     mixed = contract(stream, three_ref[...], LAST).astype(bf16)
-    half = width // 2
-    flip = info_ref[2] == 0
     own_ref[...] = jnp.where(flip, mixed[:, :half], mixed[:, half:])
     other_ref[...] = jnp.where(flip, mixed[:, half:], mixed[:, :half])
+
+
+def attn_terms_kernel(place_ref, acts_ref, got_ref, mine_ref, theirs_ref, sent_ref, kept_ref):
+    width = acts_ref.shape[1] // 3
+    half = width // 2
+    depth = sent_ref.shape[1]
+    turned = [
+        jnp.concatenate([ref[:, n * width : (n + 1) * width].T for ref in (acts_ref, got_ref)], axis=1)
+        for n in range(3)
+    ]
+    first = place_ref[3] == 0
+    for n, m in enumerate((0, 1, 1, 1, 2)):
+        at = slice(n * half, (n + 1) * half)
+        grads = jnp.concatenate([mine_ref[:, at], theirs_ref[:, at]], axis=0)
+        terms = contract(turned[m], grads, PLAIN).astype(jnp.bfloat16)
+        terms = terms.reshape(sent_ref.shape[0], 2, depth, half)
+        kept_ref[:, :, at] = jnp.where(first, terms[:, 0], terms[:, 1])
+        sent_ref[:, :, at] = jnp.where(first, terms[:, 1], terms[:, 0])
 
 
 def whole_call(kernel, info, args, outs, scratch=()):
@@ -839,10 +912,6 @@
 
 def added(a, b):
     return (a.astype(jnp.float32) + b.astype(jnp.float32)).astype(jnp.bfloat16)
-
-
-def x_summed(blocks, x):
-    return added(pick(blocks, x, 1), swap(pick(blocks, 1 - x, 1), "x"))
 
 
 def z_summed(column, z):
@@ -890,56 +959,64 @@
     info = jnp.concatenate([place[:3], mine])
     tie = (lax.rsqrt(rows_live.astype(f32)) * (1.0 / math.sqrt(DH))).reshape(1)
 
+    tokens_here = merge_cores(tokens, c)
+
     attn_low = attn_weight.astype(bf16)
     halves = attn_low.reshape(8, depth, 2, half)
-    qkv_half = jnp.moveaxis(pick(halves[:3], c, 2), 0, 1).reshape(depth, 3 * half)
+    row_half = jnp.moveaxis(pick(halves[:3], c, 2), 0, 1).reshape(2, depth // 2, 3 * half)
     norm_row = jnp.pad(
         norm_param.astype(bf16).reshape(1, 6 * depth), ((0, 15), (0, 3 * half - 6 * depth))
     )
-    row_z = gather_z(jnp.concatenate([qkv_half, norm_row]))
-    w_row, norm_rows = placed_pieces(
-        [((0, 0, 0), row_z), ((1, 0, 0), swap(row_z, "x"))],
-        row_attn_at,
-        [(width, 3 * half), (8, 16, 3 * half)],
-        place,
-        16,
-    )
-    norm_gain = norm_rows[:, 0, : 6 * depth].reshape(8, 6, depth)
-    norm_gain = jnp.moveaxis(norm_gain, 0, 1).reshape(6, width).astype(f32)
+    row_quarter = jnp.concatenate([pick(row_half, y, 0), norm_row])
     col_quarter = pick(pick(halves[3:], c, 2).reshape(5, 2, depth // 2, half), y, 1)
-    col_z = gather_z(after(col_quarter, row_z))
-
     ffn_low = [in_weight.astype(bf16), out_weight.astype(bf16).T]
     ffn_low = [
         jnp.where(c == 0, low[:, :hidden_half], low[:, hidden_half:]) for low in ffn_low
     ]
-    ffn_z = gather_z(after(jnp.where(y == 0, *ffn_low), col_z))
-
-    stream_zero = to_columns(tokens, c)
+    ffn_quarter = jnp.where(y == 0, *ffn_low)
+    tokens_here, row_quarter, col_quarter, ffn_quarter = together(
+        tokens_here, row_quarter, col_quarter, ffn_quarter
+    )
+
+    stream_zero = lax.all_to_all(tokens_here, ("z", "x"), 0, 0, tiled=True)
+    *row_z, col_quarter = together(*gather_z(row_quarter), col_quarter)
+    w_row, norm_rows = placed_pieces(
+        spread(jnp.stack(row_z)),
+        row_attn_at,
+        [(width, 3 * half), (16, 16, 3 * half)],
+        place,
+        32,
+    )
+    norm_gain = norm_rows.reshape(8, 2, 16, 3 * half)[:, 0, 0, : 6 * depth].reshape(8, 6, depth)
+    norm_gain = jnp.moveaxis(norm_gain, 0, 1).reshape(6, width).astype(f32)
     rows, part, _ = stream_zero.shape
     count = rows * part
-    resid_one = stream_zero.reshape(count, width).astype(f32)
+    stream_zero = stream_zero.reshape(count, width)
+    resid_one = stream_zero.astype(f32)
     normed_one = layer_norm(resid_one, norm_gain[0], norm_gain[1]).astype(bf16)
-    col_z = after(col_z, normed_one)
+    *col_z, normed_one, ffn_quarter = together(*gather_z(col_quarter), normed_one, ffn_quarter)
+    near_normed = jnp.concatenate([normed_one, swap(normed_one, "c")])
+    far_first = swap(normed_one, "x")
+    col_pieces = spread(jnp.stack(col_z))
+    near = contract(near_normed, w_row, PLAIN).astype(bf16).reshape(2, rows, part, 3 * half)
+    ffn_z = gather_z(ffn_quarter)
+    far_normed = jnp.concatenate([far_first, swap(far_first, "c")])
+    far = contract(far_normed, w_row[:, half:], PLAIN).astype(bf16)
+    far, *early = together(far.reshape(2, rows, part, 2 * half), *[v for _, v in col_pieces[:3]])
+    col_pieces = [(step, v) for (step, _), v in zip(col_pieces[:3], early)] + col_pieces[3:]
+    mixed_heads = row_attention(info, tie, near, far).reshape(2, count, half)
+    mixed_heads, cotangent, *ffn_z = together(mixed_heads, cotangent, *ffn_z)
+    ffn_pieces = spread(jnp.stack(ffn_z))
     w_three, w_col, w_seven = placed_pieces(
-        both_cores(spread(col_z)),
+        both_cores(col_pieces),
         col_attn_at,
         [(width, width), (width, 3 * width), (width, width)],
         place,
         8 * 4 * 5,
     )
-    near_normed = after(jnp.concatenate([normed_one, swap(normed_one, "c")]), col_z)
-    far_first = swap(normed_one, "x")
-    far_normed = jnp.concatenate([far_first, swap(far_first, "c")])
-    near = contract(near_normed, w_row, PLAIN).astype(bf16).reshape(2, rows, part, 3 * half)
-    far = contract(far_normed, w_row[:, half:], PLAIN).astype(bf16)
-    far = far.reshape(2, rows, part, 2 * half)
-    ffn_pieces = spread(ffn_z)
-    mixed_heads = row_attention(info, tie, after(near, ffn_z), far).reshape(2, count, half)
 
     whole_shape, wide_shape = ((count, width), bf16), ((rows, part, 3 * width), bf16)
-    stream_zero = stream_zero.reshape(count, width)
-    mixed_one, stream_one, normed_two, qkv_two, mixed_two, resid_three, normed_three = whole_call(
+    acts, stream_one, qkv_two, resid_three, normed_three = whole_call(
         col_fwd_kernel,
         info,
         [
@@ -951,12 +1028,11 @@
             w_seven,
             norm_gain,
         ],
-        [whole_shape] * 3
-        + [wide_shape, ((rows, part, width), bf16), ((count, width), f32), whole_shape],
-    )
-    mixed_two = mixed_two.reshape(count, width)
-
-    up = to_columns(after(cotangent, mixed_heads), c)
+        [((count, 3 * width), bf16), whole_shape, wide_shape, ((count, width), f32), whole_shape],
+        [pltpu.VMEM((rows, part, width), bf16)],
+    )
+
+    up = lax.all_to_all(merge_cores(cotangent, c), ("z", "x"), 0, 0, tiled=True)
     column = x * (2 * part) + c * part + jnp.arange(part, dtype=jnp.int32)
     live = jnp.logical_and(
         (jnp.arange(rows, dtype=jnp.int32) < rows_live)[:, None], (column < cols_live)[None, :]
@@ -967,11 +1043,10 @@
     )
     da_got = swap(da_other, "c")
     result = (resid_three + out_own + swap(out_other, "c").astype(f32)).astype(bf16)
-    block_out = to_rows(result.reshape(rows, part, width), c)
-    ffn_pair = added(ffn_kept, swap(ffn_sent, "y"))
-
-    branch_shape = ((count, width), bf16)
-    grad_branch_two, grad_qkv_two, grad_stream, grad_own, grad_other, col_norms = whole_call(
+    ffn_got = swap(ffn_sent, "y")
+
+    acts_got = swap(acts, "c")
+    grad_stream, grad_own, grad_other, attn_mine, attn_theirs, col_norms = whole_call(
         col_bwd_kernel,
         info,
         [
@@ -986,78 +1061,65 @@
             w_seven,
             norm_gain,
         ],
-        [branch_shape, wide_shape, branch_shape]
+        [whole_shape]
         + [((count, half), bf16)] * 2
+        + [((count, 5 * half), bf16)] * 2
         + [((4, width), f32)],
-        [pltpu.VMEM((rows, part, width), bf16)],
-    )
-    grad_qkv_two = grad_qkv_two.reshape(count, 3 * width)
-
-    def lanes_of(value, which, groups):
-        size = value.shape[1] // (2 * groups)
-        first, second = (
-            [value[:, (2 * n + k) * size : (2 * n + k + 1) * size] for n in range(groups)]
-            for k in (0, 1)
-        )
-        chosen = [jnp.where(which == 0, a, b) for a, b in zip(first, second)]
-        return chosen[0] if groups == 1 else jnp.concatenate(chosen, axis=1)
-
-    def over_cores(sides):
-        sent = [contract(a, lanes_of(b, 1 - c, g), FIRST).astype(bf16) for a, b, g in sides]
-        got = [swap(value, "c") for value in sent]
-        kept = [contract(a, lanes_of(b, c, g), FIRST) for a, b, g in sides]
-        return [(k + v.astype(f32)).astype(bf16) for k, v in zip(kept, got)]
-
-    attn_terms = over_cores(
-        [
-            (mixed_one, grad_stream, 1),
-            (normed_two, grad_qkv_two, 3),
-            (mixed_two, grad_branch_two, 1),
-        ]
-    )
-    attn_terms = jnp.concatenate(attn_terms, axis=1).reshape(8, 2, depth // 2, 5 * half)
-    attn_pair_terms = added(pick(attn_terms, y, 1), swap(pick(attn_terms, 1 - y, 1), "y"))
-
-    grad_heads = jnp.stack([grad_own, swap(grad_other, "c")]).reshape(2, rows, part, half)
-    ffn_column = x_summed(ffn_pair.reshape(4, 2, depth, hidden_half), x)
-    dq, dk, dv, dk_far, dv_far = row_attention_back(
-        info, tie, near, far, after(grad_heads, ffn_pair)
-    )
-    grad_near = jnp.concatenate([dq, dk, dv], axis=-1).reshape(2 * count, 3 * half)
-    grad_far = jnp.concatenate([dk_far, dv_far], axis=-1).reshape(2 * count, 2 * half)
-    row_terms = contract(near_normed, grad_near, FIRST)
-    far_terms = contract(far_normed, grad_far, FIRST)
-    row_terms = jnp.concatenate([row_terms[:, :half], row_terms[:, half:] + far_terms], axis=1)
-    row_column = x_summed(row_terms.astype(bf16).reshape(4, 2, depth, 3 * half), x)
-    far_part = contract(grad_far, w_row[:, half:], LAST).reshape(2, count, width)
-    far_sum = far_part[0] + swap(far_part[1].astype(bf16), "c").astype(f32)
-    far_got = swap(far_sum.astype(bf16), "x")
-    near_part = contract(grad_near, w_row, LAST).reshape(2, count, width)
-    near_got = swap(near_part[1].astype(bf16), "c")
-    grad_normed_one = near_part[0] + near_got.astype(f32) + far_got.astype(f32)
+        [pltpu.VMEM((rows, part, 3 * width), bf16), pltpu.VMEM((rows, part, width), bf16)],
+    )
+    attn_sent, attn_kept = whole_call(
+        attn_terms_kernel,
+        place,
+        [acts, acts_got, attn_mine, swap(attn_theirs, "c")],
+        [((8, depth // 2, 5 * half), bf16)] * 2,
+    )
+    ffn_pair = added(ffn_kept, ffn_got).reshape(4, 2, depth, hidden_half)
+
+    ffn_pair, attn_sent, attn_kept, grad_own = together(ffn_pair, attn_sent, attn_kept, grad_own)
+    attn_got = swap(attn_sent, "y")
+    ffn_column = added(pick(ffn_pair, x, 1), swap(pick(ffn_pair, 1 - x, 1), "x"))
+    near_part, near_theirs, far_part, far_theirs, row_sent, row_kept = row_attention_back(
+        info, tie, near, far, grad_own, swap(grad_other, "c"), w_row, near_normed, far_normed
+    )
+    ffn_column, row_sent, far_theirs, near_theirs = together(
+        ffn_column, row_sent, far_theirs, near_theirs
+    )
+    row_column = added(row_kept, swap(row_sent, "x"))
+    far_sum = added(far_part, swap(far_theirs, "c"))
+    far_got = swap(far_sum, "x")
+    near_got = swap(near_theirs, "c")
+    attn_pair_terms = added(attn_kept, attn_got).reshape(4, 2, depth // 2, 5 * half)
+    ffn_own = z_summed(ffn_column, z)
+    row_column, attn_pair_terms, far_got, ffn_own = together(
+        row_column, attn_pair_terms, far_got, ffn_own
+    )
+    row_own = z_summed(row_column, z)
+    grad_normed_one = near_part + near_got.astype(f32) + far_got.astype(f32)
     _, norm_back_one = jax.vjp(layer_norm, resid_one, norm_gain[0], norm_gain[1])
     part_one, gain_grad_one, shift_grad_one = norm_back_one(grad_normed_one)
     grad_input = (grad_stream.astype(f32) + part_one).astype(bf16)
-    grad_tokens = to_rows(grad_input.reshape(rows, part, width), c).astype(f32)
+    both_out = jnp.concatenate([result, grad_input], axis=1).reshape(rows, part, 2 * width)
+    both_out = to_rows(both_out, c)
+    block_out, grad_tokens = both_out[..., :width], both_out[..., width:].astype(f32)
 
     norm_stack = jnp.concatenate([jnp.stack([gain_grad_one, shift_grad_one]), col_norms])
     norm_terms = jnp.moveaxis(norm_stack.reshape(6, 4, 2, depth), 0, 2).reshape(4, 2, 1, 6 * depth)
-    norm_terms = jnp.pad(norm_terms, ((0, 0), (0, 0), (0, 15), (0, 3 * half - 6 * depth)))
-    norm_column = x_summed(norm_terms.astype(bf16), x)
-    attn_column = x_summed(attn_pair_terms.reshape(4, 2, depth // 2, 5 * half), x)
-
-    ffn_own = z_summed(ffn_column, z)
+    norm_terms = jnp.pad(norm_terms, ((0, 0), (0, 0), (0, 15), (0, 5 * half - 6 * depth)))
+    attn_blocks = jnp.concatenate([attn_pair_terms, norm_terms.astype(bf16)], axis=2)
+    attn_column = added(pick(attn_blocks, x, 1), swap(pick(attn_blocks, 1 - x, 1), "x"))
+    attn_column, row_own = together(attn_column, row_own)
     attn_own = z_summed(attn_column, z)
-    row_own = z_summed(jnp.concatenate([row_column, norm_column], axis=1), z)
     row_grad = added(row_own, swap(row_own, "y"))
+    attn_y = swap(attn_own, "y")
+    attn_grad_b = joined(attn_own[: depth // 2], attn_y[: depth // 2], y, 0)
+    norm_grad = added(attn_own[depth // 2 :], attn_y[depth // 2 :])
     ffn_grads = [ffn_own, swap(ffn_own, "y")]
-    attn_grad_b = joined(attn_own, swap(attn_own, "y"), y, 0)
 
     row_other = swap(row_grad, "c")
-    attn_other = swap(attn_grad_b, "c")
+    attn_other = swap(jnp.concatenate([attn_grad_b, norm_grad]), "c")
+    norm_grad = norm_grad[0, : 6 * depth].astype(f32) + attn_other[depth, : 6 * depth].astype(f32)
+    norm_grad = norm_grad.reshape(6, depth)
     ffn_whole = [joined(piece, swap(piece, "c"), c, 1) for piece in ffn_grads]
-    norm_grad = row_grad[depth, : 6 * depth].astype(f32) + row_other[depth, : 6 * depth].astype(f32)
-    norm_grad = norm_grad.reshape(6, depth)
 
     def whole(own, other, groups):
         size = own.shape[1] // groups
@@ -1074,13 +1136,12 @@
     out_grad = jnp.where(y == 0, *ffn_whole[::-1]).astype(f32).T
 
     squares = sum(
-        jnp.sum(jnp.square(g.astype(f32))) for g in (row_grad[:depth], attn_grad_b, *ffn_grads)
+        jnp.sum(jnp.square(g.astype(f32))) for g in (row_grad, attn_grad_b, *ffn_grads)
     )
     squares = squares + swap(squares, "c") + jnp.sum(norm_grad * norm_grad)
     squares = squares + swap(squares, "x")
-    squares = squares + lax.ppermute(squares, "z", [(k, k ^ 1) for k in range(4)])
-    squares = squares + lax.ppermute(squares, "z", [(k, k ^ 2) for k in range(4)])
-    grad_norm = jnp.sqrt(squares)
+    squares = gather_z(squares)
+    grad_norm = jnp.sqrt((squares[0] + squares[1]) + (squares[2] + squares[3]))
     factor = clip_bound / jnp.maximum(grad_norm, clip_bound)
     attn_first_new, attn_second_new, attn_weight_new = adam_update(
         attn_weight, attn_first, attn_second, attn_grad * factor, matrix_rate

time: 551 us -> 509 us (0.924)
  matrix products: 26.8 us -> 3.62 us
  Pallas kernels: 75.3 us -> 96.7 us
  starting transfers between devices: 125 us -> 104 us
  local copies, waits for them, and re-layouts: 38.7 us -> 27.6 us
  waiting for transfers between devices: 196 us -> 185 us
    ppermute x9, waiting for transfers between devices: 60.5 us -> 32.8 us  [z_summed(): got = lax.ppermute(other, 'z', [(k, k ^ i) for k in range(4)])]
    ppermute x46 -> x45, waiting for transfers between devices: 112 us -> 135 us  [swap(): return lax.ppermute(value, axis, PAIR)]
    dot_general x12 -> x2, matrix products: 26.8 us -> 3.62 us  [contract(): lax.dot_general(a, b, (dims, ((), ())), preferred_element_type=jnp.float32)]
    all_to_all x2 -> x1, starting transfers between devices: 21.6 us -> 5.9 us  [to_rows(): got = lax.all_to_all(value, ('z', 'x'), 0, 0, tiled=True)]
    pallas_call x2 -> x3, Pallas kernels: 31.8 us -> 42.3 us  [whole_call(): pl.pallas_call(kernel, in_specs=[pl.BlockSpec(memory_space=pltpu.SMEM)] +...]
    pallas_call x1, Pallas kernels: 7.7 us -> 17.4 us  [row_attention_back(): pl.pallas_call(row_bwd_kernel, in_specs=[small, small] + [inside] * 7, ou...]
    ppermute x2 -> x0, starting transfers between devices: 7.57 us -> none  [the longest x1 4 us: paired_body(): lax.ppermute(squares, 'z', [(k, k ^ 1) for k in range(4)])]
    ppermute x9 -> x12, waiting for transfers between devices: 22.2 us -> 16.4 us  [gather_z(): lax.ppermute(own, 'z', [(k, k ^ i) for k in range(4)])]
  transfers between devices with their start and end apart: 70 -> 69, of which waited for: 22 -> 26; matrix products, arithmetic and copies ran while one was open for 22% -> 17% of each run, Pallas kernels for 9% -> 13%
where the time goes in v4:
time: 509 us; the launch traced here: 499 us
  waiting for transfers between devices  185 us (36%)
  starting transfers between devices  104 us (20%)
  Pallas kernels  96.7 us (19%)
  other arithmetic  72.2 us (14%)
  local copies, waits for them, and re-layouts  27.6 us (5%)
  between operations  10.7 us (2%)
    ppermute x45, waiting for transfers between devices, swap(): return lax.ppermute(value, axis, PAIR)  135 us
    pallas_call x3, Pallas kernels, whole_call(): pl.pallas_call(kernel, in_specs=[pl.BlockSpec(memory_space=pltpu.SMEM)] +...  42.3 us
    ppermute x45, starting transfers between devices, swap(): return lax.ppermute(value, axis, PAIR)  33.8 us
    ppermute x9, waiting for transfers between devices, z_summed(): got = lax.ppermute(other, 'z', [(k, k ^ i) for k in range(4)])  32.8 us
    ppermute x12, starting transfers between devices, gather_z(): lax.ppermute(own, 'z', [(k, k ^ i) for k in range(4)])  30.3 us
    pallas_call x1, Pallas kernels, feed_forward(): pl.pallas_call(partial(ffn_kernel, [step for step, _ in pieces]), grid=(h...  24.3 us
    ppermute x9, starting transfers between devices, z_summed(): got = lax.ppermute(other, 'z', [(k, k ^ i) for k in range(4)])  18.9 us
    pallas_call x1, Pallas kernels, row_attention_back(): pl.pallas_call(row_bwd_kernel, in_specs=[small, small] + [inside] * 7, ou...  17.4 us
  transfers between devices with their start and end apart: 69, of which 26 were waited for; matrix products, arithmetic and copies ran while one was open for 17% of the time, Pallas kernels for 13%

profile of v4, /device:TPU:0, one launch (start us, length us, event | category | flops | bytes accessed | tf_op | source)
XLA Modules:
  0.0 499.3 jit_solution(1592136626678787611)
XLA Ops:
  21.6 6.7 %collective-permute-done.3 = bf16[64,1152]{1,0:T(8,128)(2,1)S(1)} collective-permute-done((bf16[64,1152]{1,0:T(8,128)(2,1)S(1)}, bf16[64,1152]{1,0:T(8,128)(2,1)S(1)}, u32[]{:S(2)}, u32[]{:S(2)}) %collective-permute-start.3) | collective-permute-done | bytes 147488 | tf_op jit(solution)/shard_map/ppermute | solution.py:365
  29.9 5.3 %all-to-all-start = ((bf16[8,64,768]{2,1,0:T(8,128)(2,1)}), bf16[8,64,768]{2,1,0:T(8,128)(2,1)}, u32[]{:S(2)}, u32[]{:S(2)}) async-start(bf16[8,64,768]{2,1,0:T(8,128)(2,1)} %bitcast.9), calls=%async_computation | async-start | bytes 1572864 | tf_op jit(solution)/shard_map/all_to_all | solution.py:981
  36.7 12.1 %collective-permute-done.8.refs_1_ = bf16[4,64,1152]{2,1,0:T(8,128)(2,1)S(1)} collective-permute-done((bf16[4,64,1152]{2,1,0:T(8,128)(2,1)S(1)}, bf16[4,64,1152]{2,1,0:T(8,128)(2,1)S(1)}, u32[]{:S(2)}, u32[]{:S(2)}) %collective-permute-start.8) | collective-permute-done | bytes 589856 | tf_op jit(solution)/shard_map/ppermute | solution.py:319
  79.0 14.0 %collective-permute-done.12 = bf16[512,768]{1,0:T(8,128)(2,1)S(1)} collective-permute-done((bf16[512,768]{1,0:T(8,128)(2,1)S(1)}, bf16[512,768]{1,0:T(8,128)(2,1)S(1)}, u32[]{:S(2)}, u32[]{:S(2)}) %collective-permute-start.12) | collective-permute-done | bytes 786464 | tf_op jit(solution)/shard_map/ppermute | solution.py:319
  100.2 4.8 collective-permute-done.14.refs_1_
  123.7 9.5 %all-to-all-start.1 = ((bf16[8,64,768]{2,1,0:T(8,128)(2,1)}), bf16[8,64,768]{2,1,0:T(8,128)(2,1)}, u32[]{:S(2)}, u32[]{:S(2)}) async-start(bf16[8,64,768]{2,1,0:T(8,128)(2,1)} %bitcast.38), calls=%async_computation.1 | async-start | bytes 1572864 | tf_op jit(solution)/shard_map/all_to_all | solution.py:1035
  139.1 17.0 %collective-permute-done.28.refs_1_ = bf16[4,96,1536]{2,1,0:T(8,128)(2,1)} collective-permute-done((bf16[4,96,1536]{2,1,0:T(8,128)(2,1)}, bf16[4,96,1536]{2,1,0:T(8,128)(2,1)}, u32[]{:S(2)}, u32[]{:S(2)}) %collective-permute-start.28) | collective-permute-done | bytes 1179680 | tf_op jit(solution)/shard_map/ppermute | solution.py:319
  167.3 12.4 %shard_map.298 = (bf16[512,2304]{1,0:T(8,128)(2,1)}, bf16[512,768]{1,0:T(8,128)(2,1)}, bf16[8,64,2304]{2,1,0:T(8,128)(2,1)}, f32[512,768]{1,0:T(8,128)}, bf16[512,768]{1,0:T(8,128)(2,1)}) custom-call(s32[5]{0:T(128)} %copy-done.12, bf16[512,768]{1,0:T(8,128)(2,1)} %bitcast.14.x_ref, bf16[512,384]{1,0:T(8,128)(2,1)} %get-tuple-element.198.own_ref, ...), custom_call_target="tpu_custom_call" | custom-call | tf_op jit(solution)/shard_map/pallas_call | solution.py:816
  182.2 9.1 %collective-permute-done.30.refs_3_ = bf16[4,96,1536]{2,1,0:T(8,128)(2,1)} collective-permute-done((bf16[4,96,1536]{2,1,0:T(8,128)(2,1)}, bf16[4,96,1536]{2,1,0:T(8,128)(2,1)}, u32[]{:S(2)}, u32[]{:S(2)}) %collective-permute-start.30) | collective-permute-done | bytes 1179680 | tf_op jit(solution)/shard_map/ppermute | solution.py:319
  192.2 24.3 %shard_map.299 = (f32[512,768]{1,0:T(8,128)}, bf16[512,768]{1,0:T(8,128)(2,1)}, f32[512,768]{1,0:T(8,128)}, bf16[512,768]{1,0:T(8,128)(2,1)}, bf16[768,1536]{1,0:T(8,128)(2,1)}, /*index=5*/bf16[768,1536]{1,0:T(8,128)(2,1)}) custom-call(s32[4]{0:T(128)} %copy-done.11, bf16[512,768]{1,0:T(8,128)(2,1)} %get-tuple-element.113.a_ref, ...), custom_call_target="tpu_custom_call" | custom-call | tf_op jit(solution)/shard_map/pallas_call | solution.py:895
  222.6 20.5 %shard_map.300 = (bf16[512,768]{1,0:T(8,128)(2,1)}, bf16[512,384]{1,0:T(8,128)(2,1)}, bf16[512,384]{1,0:T(8,128)(2,1)}, bf16[512,1920]{1,0:T(8,128)(2,1)}, bf16[512,1920]{1,0:T(8,128)(2,1)}, /*index=5*/f32[4,768]{1,0:T(4,128)}) custom-call(s32[5]{0:T(128)} %copy-done.12, bf16[512,768]{1,0:T(8,128)(2,1)} %bitcast.172, f32[512,768]{1,0:T(8,128)} %get-tuple-element.121.da_ref, ...), custom_call_target="tpu_custom_call" | custom-call | tf_op jit(solution)/shard_map/pallas_call | solution.py:816
  243.2 26.1 %collective-permute-done.33 = bf16[768,1536]{1,0:T(8,128)(2,1)S(1)} collective-permute-done((bf16[768,1536]{1,0:T(8,128)(2,1)}, bf16[768,1536]{1,0:T(8,128)(2,1)S(1)}, u32[]{:S(2)}, u32[]{:S(2)}) %collective-permute-start.33) | collective-permute-done | bytes 2359328 | tf_op jit(solution)/shard_map/ppermute | solution.py:319
  273.7 9.4 %shard_map.301 = (bf16[8,48,1920]{2,1,0:T(8,128)(2,1)}, bf16[8,48,1920]{2,1,0:T(8,128)(2,1)}) custom-call(s32[4]{0:T(128)} %copy-done.11, bf16[512,2304]{1,0:T(8,128)(2,1)} %get-tuple-element.128.acts_ref, bf16[512,2304]{1,0:T(8,128)(2,1)} %collective-permute-done.34.got_ref, bf16[512,1920]{1,0:T(8,128)(2,1)} %get-tuple-element.129.mine_ref, ...), custom_call_target="tpu_custom_call" | custom-call | tf_op jit(solution)/shard_map/pallas_call | solution.py:816
  291.3 17.4 %shard_map.302 = (f32[512,768]{1,0:T(8,128)}, bf16[512,768]{1,0:T(8,128)(2,1)}, f32[512,768]{1,0:T(8,128)}, bf16[512,768]{1,0:T(8,128)(2,1)}, bf16[4,96,1152]{2,...) custom-call(s32[5]{0:T(128)} %copy-done.12, f32[1]{0:T(128)} %bitcast.16.tie_ref, bf16[2,8,64,1152]{3,2,1,0:T(8,128)(2,1)} %bitcast.162, ...), custom_call_target="tpu_custom_call" | custom-call | tf_op jit(solution)/shard_map/pallas_call | solution.py:621
  318.9 5.1 %collective-permute-done.43 = bf16[96,1536]{1,0:T(8,128)(2,1)S(1)} collective-permute-done((bf16[96,1536]{1,0:T(8,128)(2,1)S(1)}, bf16[96,1536]{1,0:T(8,128)(2,1)S(1)}, u32[]{:S(2)}, u32[]{:S(2)}) %collective-permute-start.43) | collective-permute-done | bytes 294944 | tf_op jit(solution)/shard_map/ppermute | solution.py:921
  324.5 12.6 %collective-permute-done.44 = bf16[96,1536]{1,0:T(8,128)(2,1)S(1)} collective-permute-done((bf16[96,1536]{1,0:T(8,128)(2,1)S(1)}, bf16[96,1536]{1,0:T(8,128)(2,1)S(1)}, u32[]{:S(2)}, u32[]{:S(2)}) %collective-permute-start.44) | collective-permute-done | bytes 294944 | tf_op jit(solution)/shard_map/ppermute | solution.py:921
  344.2 15.4 %collective-permute-done.42 = bf16[512,768]{1,0:T(8,128)(2,1)S(1)} collective-permute-done((bf16[512,768]{1,0:T(8,128)(2,1)S(1)}, bf16[512,768]{1,0:T(8,128)(2,1)S(1)}, u32[]{:S(2)}, u32[]{:S(2)}) %collective-permute-start.42) | collective-permute-done | bytes 786464 | tf_op jit(solution)/shard_map/ppermute | solution.py:319
  360.4 5.2 %collective-permute-start.49 = (bf16[96,1152]{1,0:T(8,128)(2,1)}, bf16[96,1152]{1,0:T(8,128)(2,1)}, u32[]{:S(2)}, u32[]{:S(2)}) collective-permute-start(bf16[96,1152]{1,0:T(8,128)(2,1)} %get-tuple-element.196), channel_id=1, source_target_pairs={{0,16},{8,24},{16,0},{24,8},{1,17},{9,25},{17,1},{25,9},{2,18},{10... | collective-permute-start | bytes 663560 | tf_op jit(solution)/shard_map/ppermute | solution.py:921
  378.0 5.9 %all-to-all-start.2 = ((bf16[8,64,1536]{2,1,0:T(8,128)(2,1)}), bf16[8,64,1536]{2,1,0:T(8,128)(2,1)S(1)}, u32[]{:S(2)}, u32[]{:S(2)}) async-start(bf16[8,64,1536]{2,1,0:T(8,128)(2,1)} %bitcast.174), calls=%async_computation.2 | async-start | bytes 3145728 | tf_op jit(solution)/shard_map/all_to_all | solution.py:353
  389.3 18.3 %collective-permute-done.47 = bf16[4,64,1920]{2,1,0:T(8,128)(2,1)} collective-permute-done((bf16[4,64,1920]{2,1,0:T(8,128)(2,1)}, bf16[4,64,1920]{2,1,0:T(8,128)(2,1)}, u32[]{:S(2)}, u32[]{:S(2)}) %collective-permute-start.47) | collective-permute-done | bytes 983072 | tf_op jit(solution)/shard_map/ppermute | solution.py:319
  409.2 5.0 %collective-permute-start.53 = (bf16[64,1920]{1,0:T(8,128)(2,1)S(1)}, bf16[64,1920]{1,0:T(8,128)(2,1)S(1)}, u32[]{:S(2)}, u32[]{:S(2)}) collective-permute-start(bf16[64,1920]{1,0:T(8,128)(2,1)S(1)} %get-tuple-element.193), channel_id=1, source_target_pairs={{0,16},{8,24},{16,0},{24,8},{1,17},{9,25},{17,1},{25,9},{2,18},{10... | collective-permute-start | bytes 737288 | tf_op jit(solution)/shard_map/ppermute | solution.py:921
  420.7 14.2 %collective-permute-done.53 = bf16[64,1920]{1,0:T(8,128)(2,1)S(1)} collective-permute-done((bf16[64,1920]{1,0:T(8,128)(2,1)S(1)}, bf16[64,1920]{1,0:T(8,128)(2,1)S(1)}, u32[]{:S(2)}, u32[]{:S(2)}) %collective-permute-start.53) | collective-permute-done | bytes 245792 | tf_op jit(solution)/shard_map/ppermute | solution.py:921
  476.7 5.4 %fusion.35 = (bf16[3072,96]{0,1:T(8,128)(2,1)}, f32[3072,96]{0,1:T(8,128)}, f32[3072,96]{0,1:T(8,128)}, f32[3072,96]{0,1:T(8,128)}) fusion(f32[3072,96]{0,1:T(8,128)S(1)} %copy-done.17, f32[]{:T(128)S(6)} %div.78, bf16[96,1536]{1,0:T(8,128)(2,1)} %fusion.13, bf16[96,1536]{1,0:T(8,128)(2,1)} %collective-permute-done.64, ...), kind=kLoop, calls=%fused_computation.168 | loop fusion | flops 10616832 | bytes 8847366 | tf_op jit(solution)/shard_map/convert_element_type | solution.py:1173
  488.3 7.6 %fusion.39 = (bf16[8,96,768]{2,1,0:T(8,128)(2,1)}, f32[8,96,768]{2,1,0:T(8,128)}, f32[8,96,768]{2,1,0:T(8,128)}, f32[8,96,768]{2,1,0:T(8,128)}) fusion(f32[8,96,768]{2,1,0:T(8,128)S(1)} %copy-done.13, f32[]{:T(128)S(6)} %div.78, bf16[8,96,768]{2,1,0:T(8,128)(2,1)} %fusion.30, f32[8,96,768]{2,1,0:T(8,128)} %param.25, f32[8,96,768]{2,1,0:T(8,128)} %param.24), kind=kLoop, calls=%fused_computation.170 | loop fusion | flops 10027008 | bytes 16515076 | tf_op jit(solution)/shard_map/convert_element_type | solution.py:1165
  (351 shorter events, 205.1 us)
Async XLA Ops:
  29.9 38.0 %all-to-all-start = ((bf16[8,64,768]{2,1,0:T(8,128)(2,1)}), bf16[8,64,768]{2,1,0:T(8,128)(2,1)}, u32[]{:S(2)}, u32[]{:S(2)}) async-start(bf16[8,64,768]{2,1,0:T(8,128)(2,1)} %bitcast.9), calls=%async_computation | async-start | bytes 1572864 | tf_op jit(solution)/shard_map/all_to_all | solution.py:981
  77.1 28.0 %collective-permute-start.14 = (bf16[4,5,48,384]{3,2,1,0:T(8,128)(2,1)S(1)}, bf16[4,5,48,384]{3,2,1,0:T(8,128)(2,1)}, u32[]{:S(2)}, u32[]{:S(2)}) collective-permute-start(bf16[4,5,48,384]{3,2,1,0:T(8,128)(2,1)S(1)} %pad_maximum_fusion.2.refs_0_), channel_id=1, source_target_pairs={{0,4},{4,0},{1,5},{5,1},{2,6},{6,2},{3,7},{7,3},{8,12},{12,8},{9,1... | collective-permute-start | bytes 2211848 | tf_op jit(solution)/shard_map/ppermute | solution.py:319
  77.5 34.3 %collective-permute-start.15 = (bf16[4,5,48,384]{3,2,1,0:T(8,128)(2,1)S(1)}, bf16[4,5,48,384]{3,2,1,0:T(8,128)(2,1)S(1)}, u32[]{:S(2)}, u32[]{:S(2)}) collective-permute-start(bf16[4,5,48,384]{3,2,1,0:T(8,128)(2,1)S(1)} %pad_maximum_fusion.2.refs_0_), channel_id=1, source_target_pairs={{0,2},{2,0},{1,3},{3,1},{4,6},{6,4},{5,7},{7,5},{8,10},{10,8},{9,1... | collective-permute-start | bytes 2211848 | tf_op jit(solution)/shard_map/ppermute | solution.py:319
  120.7 35.5 %collective-permute-start.28 = (bf16[4,96,1536]{2,1,0:T(8,128)(2,1)}, bf16[4,96,1536]{2,1,0:T(8,128)(2,1)}, u32[]{:S(2)}, u32[]{:S(2)}) collective-permute-start(bf16[4,96,1536]{2,1,0:T(8,128)(2,1)} %pad_maximum_fusion.1.refs_0_), channel_id=1, source_target_pairs={{0,4},{4,0},{1,5},{5,1},{2,6},{6,2},{3,7},{7,3},{8,12},{12,8},{9,1... | collective-permute-start | bytes 3538952 | tf_op jit(solution)/shard_map/ppermute | solution.py:319
  123.7 56.0 %all-to-all-start.1 = ((bf16[8,64,768]{2,1,0:T(8,128)(2,1)}), bf16[8,64,768]{2,1,0:T(8,128)(2,1)}, u32[]{:S(2)}, u32[]{:S(2)}) async-start(bf16[8,64,768]{2,1,0:T(8,128)(2,1)} %bitcast.38), calls=%async_computation.1 | async-start | bytes 1572864 | tf_op jit(solution)/shard_map/all_to_all | solution.py:1035
  133.9 24.6 %collective-permute-start.22 = (bf16[4,5,48,384]{3,2,1,0:T(8,128)(2,1)}, bf16[4,5,48,384]{3,2,1,0:T(8,128)(2,1)}, u32[]{:S(2)}, u32[]{:S(2)}) collective-permute-start(bf16[4,5,48,384]{3,2,1,0:T(8,128)(2,1)} %collective-permute-done.14.refs_1_), channel_id=1, source_target_pairs={{0,1},{1,0},{2,3},{3,2},{4,5},{5,4},{6,7},{7,6},{8,9},{9,8},{10,11... | collective-permute-start | bytes 2211848 | tf_op jit(solution)/shard_map/ppermute | solution.py:319
  133.9 24.5 %collective-permute-start.23 = (bf16[4,5,48,384]{3,2,1,0:T(8,128)(2,1)S(1)}, bf16[4,5,48,384]{3,2,1,0:T(8,128)(2,1)}, u32[]{:S(2)}, u32[]{:S(2)}) collective-permute-start(bf16[4,5,48,384]{3,2,1,0:T(8,128)(2,1)S(1)} %copy-done.10), channel_id=1, source_target_pairs={{0,1},{1,0},{2,3},{3,2},{4,5},{5,4},{6,7},{7,6},{8,9},{9,8},{10,11... | collective-permute-start | bytes 2211848 | tf_op jit(solution)/shard_map/ppermute | solution.py:319
  135.9 30.6 %collective-permute-start.19 = (bf16[512,384]{1,0:T(8,128)(2,1)}, bf16[512,384]{1,0:T(8,128)(2,1)S(1)}, u32[]{:S(2)}, u32[]{:S(2)}) collective-permute-start(bf16[512,384]{1,0:T(8,128)(2,1)} %get-tuple-element.197), channel_id=1, source_target_pairs={{0,1},{1,0},{2,3},{3,2},{4,5},{5,4},{6,7},{7,6},{8,9},{9,8},{10,11... | collective-permute-start | bytes 1179656 | tf_op jit(solution)/shard_map/ppermute | solution.py:319
  137.6 44.0 %collective-permute-start.29 = (bf16[4,96,1536]{2,1,0:T(8,128)(2,1)}, bf16[4,96,1536]{2,1,0:T(8,128)(2,1)}, u32[]{:S(2)}, u32[]{:S(2)}) collective-permute-start(bf16[4,96,1536]{2,1,0:T(8,128)(2,1)} %pad_maximum_fusion.1.refs_0_), channel_id=1, source_target_pairs={{0,2},{2,0},{1,3},{3,1},{4,6},{6,4},{5,7},{7,5},{8,10},{10,8},{9,1... | collective-permute-start | bytes 3538952 | tf_op jit(solution)/shard_map/ppermute | solution.py:319
  156.2 35.2 %collective-permute-start.30 = (bf16[4,96,1536]{2,1,0:T(8,128)(2,1)}, bf16[4,96,1536]{2,1,0:T(8,128)(2,1)}, u32[]{:S(2)}, u32[]{:S(2)}) collective-permute-start(bf16[4,96,1536]{2,1,0:T(8,128)(2,1)} %collective-permute-done.28.refs_1_), channel_id=1, source_target_pairs={{0,2},{2,0},{1,3},{3,1},{4,6},{6,4},{5,7},{7,5},{8,10},{10,8},{9,1... | collective-permute-start | bytes 3538952 | tf_op jit(solution)/shard_map/ppermute | solution.py:319
  216.5 52.8 %collective-permute-start.33 = (bf16[768,1536]{1,0:T(8,128)(2,1)}, bf16[768,1536]{1,0:T(8,128)(2,1)S(1)}, u32[]{:S(2)}, u32[]{:S(2)}) collective-permute-start(bf16[768,1536]{1,0:T(8,128)(2,1)} %get-tuple-element.127), channel_id=1, source_target_pairs={{0,2},{2,0},{1,3},{3,1},{4,6},{6,4},{5,7},{7,5},{8,10},{10,8},{9,1... | collective-permute-start | bytes 7077896 | tf_op jit(solution)/shard_map/ppermute | solution.py:319
  218.1 55.6 %collective-permute-start.34 = (bf16[512,2304]{1,0:T(8,128)(2,1)}, bf16[512,2304]{1,0:T(8,128)(2,1)}, u32[]{:S(2)}, u32[]{:S(2)}) collective-permute-start(bf16[512,2304]{1,0:T(8,128)(2,1)} %get-tuple-element.128.acts_ref), channel_id=1, source_target_pairs={{0,1},{1,0},{2,3},{3,2},{4,5},{5,4},{6,7},{7,6},{8,9},{9,8},{10,11... | collective-permute-start | bytes 7077896 | tf_op jit(solution)/shard_map/ppermute | solution.py:319
  243.0 30.7 %collective-permute-start.35 = (bf16[512,1920]{1,0:T(8,128)(2,1)}, bf16[512,1920]{1,0:T(8,128)(2,1)}, u32[]{:S(2)}, u32[]{:S(2)}) collective-permute-start(bf16[512,1920]{1,0:T(8,128)(2,1)} %get-tuple-element.130), channel_id=1, source_target_pairs={{0,1},{1,0},{2,3},{3,2},{4,5},{5,4},{6,7},{7,6},{8,9},{9,8},{10,11... | collective-permute-start | bytes 5898248 | tf_op jit(solution)/shard_map/ppermute | solution.py:319
  283.2 26.8 %collective-permute-start.37 = (bf16[4,96,1536]{2,1,0:T(8,128)(2,1)S(1)}, bf16[4,96,1536]{2,1,0:T(8,128)(2,1)}, u32[]{:S(2)}, u32[]{:S(2)}) collective-permute-start(bf16[4,96,1536]{2,1,0:T(8,128)(2,1)S(1)} %dynamic-slice_bitcast_fusion), channel_id=1, source_target_pairs={{0,4},{4,0},{1,5},{5,1},{2,6},{6,2},{3,7},{7,3},{8,12},{12,8},{9,1... | collective-permute-start | bytes 3538952 | tf_op jit(solution)/shard_map/ppermute | solution.py:319
  285.3 31.0 %collective-permute-start.31 = (bf16[512,768]{1,0:T(8,128)(2,1)}, bf16[512,768]{1,0:T(8,128)(2,1)}, u32[]{:S(2)}, u32[]{:S(2)}) collective-permute-start(bf16[512,768]{1,0:T(8,128)(2,1)} %get-tuple-element.120), channel_id=1, source_target_pairs={{0,1},{1,0},{2,3},{3,2},{4,5},{5,4},{6,7},{7,6},{8,9},{9,8},{10,11... | collective-permute-start | bytes 2359304 | tf_op jit(solution)/shard_map/ppermute | solution.py:319
  289.8 49.3 %collective-permute-start.40 = (bf16[8,48,1920]{2,1,0:T(8,128)(2,1)}, bf16[8,48,1920]{2,1,0:T(8,128)(2,1)S(1)}, u32[]{:S(2)}, u32[]{:S(2)}) collective-permute-start(bf16[8,48,1920]{2,1,0:T(8,128)(2,1)} %get-tuple-element.145), channel_id=1, source_target_pairs={{0,2},{2,0},{1,3},{3,1},{4,6},{6,4},{5,7},{7,5},{8,10},{10,8},{9,1... | collective-permute-start | bytes 4423688 | tf_op jit(solution)/shard_map/ppermute | solution.py:319
  337.1 28.5 %collective-permute-start.38 = (bf16[512,768]{1,0:T(8,128)(2,1)S(1)}, bf16[512,768]{1,0:T(8,128)(2,1)S(1)}, u32[]{:S(2)}, u32[]{:S(2)}) collective-permute-start(bf16[512,768]{1,0:T(8,128)(2,1)S(1)} %copy-done.53), channel_id=1, source_target_pairs={{0,1},{1,0},{2,3},{3,2},{4,5},{5,4},{6,7},{7,6},{8,9},{9,8},{10,11... | collective-permute-start | bytes 2359304 | tf_op jit(solution)/shard_map/ppermute | solution.py:319
  360.4 25.2 %collective-permute-start.48 = (bf16[96,1152]{1,0:T(8,128)(2,1)}, bf16[96,1152]{1,0:T(8,128)(2,1)}, u32[]{:S(2)}, u32[]{:S(2)}) collective-permute-start(bf16[96,1152]{1,0:T(8,128)(2,1)} %get-tuple-element.194), channel_id=1, source_target_pairs={{0,8},{8,0},{16,24},{24,16},{1,9},{9,1},{17,25},{25,17},{2,10},{10... | collective-permute-start | bytes 663560 | tf_op jit(solution)/shard_map/ppermute | solution.py:921
  360.4 25.2 %collective-permute-start.49 = (bf16[96,1152]{1,0:T(8,128)(2,1)}, bf16[96,1152]{1,0:T(8,128)(2,1)}, u32[]{:S(2)}, u32[]{:S(2)}) collective-permute-start(bf16[96,1152]{1,0:T(8,128)(2,1)} %get-tuple-element.196), channel_id=1, source_target_pairs={{0,16},{8,24},{16,0},{24,8},{1,17},{9,25},{17,1},{25,9},{2,18},{10... | collective-permute-start | bytes 663560 | tf_op jit(solution)/shard_map/ppermute | solution.py:921
  372.9 34.6 %collective-permute-start.47 = (bf16[4,64,1920]{2,1,0:T(8,128)(2,1)}, bf16[4,64,1920]{2,1,0:T(8,128)(2,1)}, u32[]{:S(2)}, u32[]{:S(2)}) collective-permute-start(bf16[4,64,1920]{2,1,0:T(8,128)(2,1)} %dynamic-slice_bitcast_fusion.1), channel_id=1, source_target_pairs={{0,4},{4,0},{1,5},{5,1},{2,6},{6,2},{3,7},{7,3},{8,12},{12,8},{9,1... | collective-permute-start | bytes 2949128 | tf_op jit(solution)/shard_map/ppermute | solution.py:319
  378.0 108.6 %all-to-all-start.2 = ((bf16[8,64,1536]{2,1,0:T(8,128)(2,1)}), bf16[8,64,1536]{2,1,0:T(8,128)(2,1)S(1)}, u32[]{:S(2)}, u32[]{:S(2)}) async-start(bf16[8,64,1536]{2,1,0:T(8,128)(2,1)} %bitcast.174), calls=%async_computation.2 | async-start | bytes 3145728 | tf_op jit(solution)/shard_map/all_to_all | solution.py:353
  385.6 91.1 %collective-permute-start.64 = (bf16[96,1536]{1,0:T(8,128)(2,1)}, bf16[96,1536]{1,0:T(8,128)(2,1)}, u32[]{:S(2)}, u32[]{:S(2)}) collective-permute-start(bf16[96,1536]{1,0:T(8,128)(2,1)} %fusion.13), channel_id=1, source_target_pairs={{0,1},{1,0},{2,3},{3,2},{4,5},{5,4},{6,7},{7,6},{8,9},{9,8},{10,11... | collective-permute-start | bytes 884744 | tf_op jit(solution)/shard_map/ppermute | solution.py:319
  387.0 89.7 %collective-permute-start.65 = (bf16[96,1536]{1,0:T(8,128)(2,1)}, bf16[96,1536]{1,0:T(8,128)(2,1)}, u32[]{:S(2)}, u32[]{:S(2)}) collective-permute-start(bf16[96,1536]{1,0:T(8,128)(2,1)} %collective-permute-done.56), channel_id=1, source_target_pairs={{0,1},{1,0},{2,3},{3,2},{4,5},{5,4},{6,7},{7,6},{8,9},{9,8},{10,11... | collective-permute-start | bytes 884744 | tf_op jit(solution)/shard_map/ppermute | solution.py:319
  409.2 25.6 %collective-permute-start.53 = (bf16[64,1920]{1,0:T(8,128)(2,1)S(1)}, bf16[64,1920]{1,0:T(8,128)(2,1)S(1)}, u32[]{:S(2)}, u32[]{:S(2)}) collective-permute-start(bf16[64,1920]{1,0:T(8,128)(2,1)S(1)} %get-tuple-element.193), channel_id=1, source_target_pairs={{0,16},{8,24},{16,0},{24,8},{1,17},{9,25},{17,1},{25,9},{2,18},{10... | collective-permute-start | bytes 737288 | tf_op jit(solution)/shard_map/ppermute | solution.py:921
  (100 other events, 1133.2 us)

commit v5 on v4

--- a/solution.py
+++ b/solution.py
@@ -348,9 +348,12 @@
     return both.reshape(8, part, width)
 
 
-def to_rows(value, c):
-    rows, part, width = value.shape
-    got = lax.all_to_all(value, ("z", "x"), 0, 0, tiled=True)
+def to_blocks(value):
+    return lax.all_to_all(value, ("z", "x"), 0, 0, tiled=True)
+
+
+def to_rows(got, c):
+    _, part, width = got.shape
     got = got.reshape(2, 2, 2, part, width)
     other = swap(pick(got, 1 - c, 0), "c")
     both = merge(pick(got, c, 0), other, c, 2)
@@ -375,12 +378,12 @@
     return half + [((j, m, 1), swap(value, "c")) for (j, m, _), value in half]
 
 
-def placing(plan, outs_at, place_ref, stacks, outs, sem):
+def placing(plan, outs_at, place_ref, stacks, outs, sem, steps=True):
     copies = []
     for stack, (j, m, k) in zip(stacks, plan):
         x, y, c = (lax.bitwise_xor(place_ref[n], step) for n, step in ((1, j), (3, m), (2, k)))
         for i in range(4):
-            shard = lax.bitwise_xor(place_ref[0], i) * 2 + x
+            shard = (lax.bitwise_xor(place_ref[0], i) if steps else i) * 2 + x
             for source, target in outs_at(stack.at[i], outs, shard, y, c):
                 copies.append(pltpu.make_async_copy(source, target, sem.at[len(copies)]))
     return copies
@@ -412,10 +415,7 @@
 def row_attn_at(ref, outs, shard, y, c):
     depth = outs[0].shape[0] // 16
     at = pl.multiple_of((shard * 2 + y) * depth, depth)
-    return [
-        (ref.at[pl.ds(0, depth)], outs[0].at[pl.ds(at, depth)]),
-        (ref.at[pl.ds(depth, 16)], outs[1].at[shard * 2 + y]),
-    ]
+    return [(ref, outs[0].at[pl.ds(at, depth)])]
 
 
 def ffn_at(ref, outs, shard, y, c):
@@ -469,44 +469,97 @@
     return column < info_ref[3]
 
 
-def row_pair(ref, row):
-    blocks, _, part, lanes = ref.shape
-    return jnp.concatenate(
-        [ref[:, row + n].reshape(blocks * part, lanes) for n in (0, 1)], axis=1
-    )
-
-
 def live_pair(value, row, info_ref):
     lane = lax.broadcasted_iota(jnp.int32, (1, value.shape[1]), 1) // TILE + row
     return only(lane < info_ref[4], value)
 
 
-def row_fwd_kernel(info_ref, tie_ref, q_ref, k_ref, v_ref, kf_ref, vf_ref, o_ref):
-    blocks, rows, part, lanes = q_ref.shape
+def head_pair(ref, row, lane):
+    blocks, _, part, _ = ref.shape
+    found = [ref[:, row + n, :, lane : lane + TILE].reshape(blocks * part, TILE) for n in (0, 1)]
+    return jnp.concatenate(found, axis=1)
+
+
+def row_fwd_kernel(token_plan, weight_plan, place_ref, info_ref, tie_ref, *refs):
+    bf16 = jnp.bfloat16
+    f32 = jnp.float32
+    tokens, refs = refs[: len(token_plan)], refs[len(token_plan) :]
+    stacks, refs = refs[: len(weight_plan)], refs[len(weight_plan) :]
+    own_ref, near_tokens_ref, far_tokens_ref, w_ref, gain_ref, near_ref, far_ref, o_ref = refs[:8]
+    all_ref, norm_ref, token_sem, weight_sem = refs[8:]
+    blocks, rows, part, lanes = near_ref.shape
+    half = lanes // 3
+    count = rows * part
     near = blocks * part
-    sides = head_lanes(2 * lanes)
+    copies = []
+    for stack, (j, k) in zip(tokens, token_plan):
+        x = lax.bitwise_xor(place_ref[1], j)
+        for i in range(4):
+            row = lax.bitwise_xor(place_ref[0], i) * 2 + x
+            moves = [(stack.at[i, pl.ds(0, 2 * part)], all_ref.at[k, row])]
+            if k == 0:
+                moves.append((stack.at[i, pl.ds(2 * part, 16)], norm_ref.at[j * 4 + i]))
+            for source, target in moves:
+                copies.append(pltpu.make_async_copy(source, target, token_sem.at[len(copies)]))
+    weights = placing(weight_plan, row_attn_at, place_ref, stacks, [w_ref], weight_sem)
+    for copy in copies + weights:
+        copy.start()
+    for copy in copies:
+        copy.wait()
+    gains = jnp.sum(norm_ref[...].astype(f32), axis=0)
+    gain_ref[...] = gains
+    x = info_ref[1]
+    for ref, side in ((near_tokens_ref, x), (far_tokens_ref, 1 - x)):
+        at = pl.ds(pl.multiple_of(side * part, part), part)
+        for k in range(blocks):
+            value = all_ref[k, :, at, :].reshape(count, -1)
+            if k == 0:
+                @pl.when(side == x)
+                def _():
+                    own_ref[...] = value
+            found = normed(value.astype(f32), gains[0:1], gains[1:2])[0]
+            ref[k * count : (k + 1) * count] = found.astype(bf16)
+    for copy in weights:
+        copy.wait()
+    for n in range(3):
+        at = slice(n * half, (n + 1) * half)
+        found = contract(near_tokens_ref[...], w_ref[:, at], PLAIN).astype(bf16)
+        near_ref[:, :, :, at] = found.reshape(blocks, rows, part, half)
+        if n > 0:
+            found = contract(far_tokens_ref[...], w_ref[:, at], PLAIN).astype(bf16)
+            far_ref[:, :, :, (n - 1) * half : n * half] = found.reshape(blocks, rows, part, half)
+    sides = head_lanes(2 * TILE)
     keep = column_keep(info_ref, near, near, part)
     tie = tie_ref[0]
-    scores = [jnp.zeros((near, 2 * near), jnp.float32) for _ in sides]
-    for row in range(0, rows, 2):
-        query = live_pair(row_pair(q_ref, row), row, info_ref)
-        key = jnp.concatenate([row_pair(k_ref, row), row_pair(kf_ref, row)], axis=0)
-        for n, side in enumerate(sides):
-            scores[n] = scores[n] + contract(only(side, query), key, LAST)
-    probs = [softmax_of(s * tie, keep).astype(jnp.bfloat16) for s in scores]
-    for row in range(0, rows, 2):
-        value = jnp.concatenate([row_pair(v_ref, row), row_pair(vf_ref, row)], axis=0)
-        mixed = jnp.where(
-            sides[0], contract(probs[0], value, PLAIN), contract(probs[1], value, PLAIN)
-        ).astype(jnp.bfloat16)
-        for n in (0, 1):
-            o_ref[:, row + n] = mixed[:, n * lanes : (n + 1) * lanes].reshape(blocks, part, lanes)
+    for lane in range(0, half, TILE):
+        scores = [jnp.zeros((near, 2 * near), f32) for _ in sides]
+        for row in range(0, rows, 2):
+            query = live_pair(head_pair(near_ref, row, lane), row, info_ref)
+            key = jnp.concatenate(
+                [head_pair(near_ref, row, half + lane), head_pair(far_ref, row, lane)], axis=0
+            )
+            for n, side in enumerate(sides):
+                scores[n] = scores[n] + contract(only(side, query), key, LAST)
+        probs = [softmax_of(s * tie, keep).astype(bf16) for s in scores]
+        for row in range(0, rows, 2):
+            value = jnp.concatenate(
+                [head_pair(near_ref, row, 2 * half + lane), head_pair(far_ref, row, half + lane)],
+                axis=0,
+            )
+            mixed = jnp.where(
+                sides[0], contract(probs[0], value, PLAIN), contract(probs[1], value, PLAIN)
+            ).astype(bf16)
+            for n in (0, 1):
+                o_ref[:, row + n, :, lane : lane + TILE] = mixed[:, n * TILE : (n + 1) * TILE].reshape(
+                    blocks, part, TILE
+                )
 
 
 def row_bwd_kernel(
     info_ref, tie_ref, near_ref, far_ref, own_ref, got_ref, w_ref, near_tokens_ref, far_tokens_ref,
+    y_kept_ref, y_got_ref, x_kept_ref, x_got_ref,
     near_part_ref, near_theirs_ref, far_part_ref, far_theirs_ref, sent_ref, kept_ref,
-    do_ref, d_near_ref, d_far_ref,
+    to_x_ref, with_x_ref, to_y_ref, with_y_ref, do_ref, d_near_ref, d_far_ref,
 ):
     bf16 = jnp.bfloat16
     blocks, rows, part, lanes = near_ref.shape
@@ -577,6 +630,13 @@
     far_turned = far_tokens_ref[...].T
     zs, depth = kept_ref.shape[0], kept_ref.shape[1]
     first = info_ref[1] == 0
+    first_y = info_ref[5] == 0
+    summed = added(y_kept_ref[...], y_got_ref[...]).reshape(zs, 2, depth, -1)
+    with_x_ref[...] = jnp.where(first, summed[:, 0], summed[:, 1])
+    to_x_ref[...] = jnp.where(first, summed[:, 1], summed[:, 0])
+    summed = added(x_kept_ref[...], x_got_ref[...])
+    with_y_ref[...] = jnp.where(first_y, summed[:, 0], summed[:, 1])
+    to_y_ref[...] = jnp.where(first_y, summed[:, 1], summed[:, 0])
     for n in range(3):
         at = slice(n * half, (n + 1) * half)
         terms = contract(near_turned, d_near[:, at], PLAIN)
@@ -587,29 +647,40 @@
         sent_ref[:, :, at] = jnp.where(first, terms[:, 1], terms[:, 0])
 
 
-def lane_block(shape, first):
-    blocks, rows, part, _ = shape
-    return pl.BlockSpec((blocks, rows, part, TILE), lambda t: (0, 0, 0, first + t))
-
-
-def row_attention(info, tie, near, far):
-    blocks, rows, part, lanes = near.shape
-    tiles = lanes // 3 // TILE
-    shape = near.shape
+def row_attention(place, info, tie, tokens, weights, rows, half):
+    f32, bf16 = jnp.float32, jnp.bfloat16
+    zs, deep, width = tokens[0][1].shape
+    part = (deep - 16) // 2
+    count = rows * part
     small = pl.BlockSpec(memory_space=pltpu.SMEM)
+    anywhere = pl.BlockSpec(memory_space=pl.ANY)
+    inside = pl.BlockSpec(memory_space=pltpu.VMEM)
+    shapes = [
+        ((count, width), bf16),
+        ((2 * count, width), bf16),
+        ((2 * count, width), bf16),
+        ((width, 3 * half), bf16),
+        ((16, width), f32),
+        ((2, rows, part, 3 * half), bf16),
+        ((2, rows, part, 2 * half), bf16),
+        ((2, rows, part, half), bf16),
+    ]
     return pl.pallas_call(
-        row_fwd_kernel,
-        grid=(tiles,),
-        in_specs=[small, small]
-        + [lane_block(shape, n * tiles) for n in range(3)]
-        + [lane_block(shape, n * tiles) for n in range(2)],
-        out_specs=lane_block(shape, 0),
-        out_shape=jax.ShapeDtypeStruct((blocks, rows, part, lanes // 3), jnp.bfloat16),
-        compiler_params=pltpu.CompilerParams(vmem_limit_bytes=32 * 2**20),
-    )(info, tie, near, near, near, far, far)
-
-
-def row_attention_back(info, tie, near, far, own, got, weights, near_tokens, far_tokens):
+        partial(row_fwd_kernel, [step for step, _ in tokens], [step for step, _ in weights]),
+        in_specs=[small] * 3 + [anywhere] * (len(tokens) + len(weights)),
+        out_specs=[inside] * len(shapes),
+        out_shape=[jax.ShapeDtypeStruct(shape, kind) for shape, kind in shapes],
+        scratch_shapes=[
+            pltpu.VMEM((2, rows, 2 * part, width), bf16),
+            pltpu.VMEM((8, 16, width), bf16),
+            pltpu.SemaphoreType.DMA((24,)),
+            pltpu.SemaphoreType.DMA((16,)),
+        ],
+        compiler_params=pltpu.CompilerParams(vmem_limit_bytes=56 * 2**20),
+    )(place, info, tie, *[v for _, v in tokens], *[v for _, v in weights])
+
+
+def row_attention_back(info, tie, near, far, own, got, weights, near_tokens, far_tokens, *ffn_terms):
     blocks, rows, part, lanes = near.shape
     count, width = rows * part, weights.shape[0]
     half = lanes // 3
@@ -618,10 +689,11 @@
     inside = pl.BlockSpec(memory_space=pltpu.VMEM)
     shapes = [((count, width), kind) for kind in (f32, bf16) * 2]
     shapes = shapes + [((4, width // 8, lanes), bf16)] * 2
+    shapes = shapes + [((4, width // 8, ffn_terms[0].shape[1]), bf16)] * 4
     return pl.pallas_call(
         row_bwd_kernel,
-        in_specs=[small, small] + [inside] * 7,
-        out_specs=[inside] * 6,
+        in_specs=[small, small] + [inside] * 11,
+        out_specs=[inside] * 10,
         out_shape=[jax.ShapeDtypeStruct(shape, kind) for shape, kind in shapes],
         scratch_shapes=[
             pltpu.VMEM((blocks, rows, part, half), bf16),
@@ -629,7 +701,7 @@
             pltpu.VMEM((blocks, rows, part, 2 * half), bf16),
         ],
         compiler_params=pltpu.CompilerParams(vmem_limit_bytes=56 * 2**20),
-    )(info, tie, near, far, own, got, weights, near_tokens, far_tokens)
+    )(info, tie, near, far, own, got, weights, near_tokens, far_tokens, *ffn_terms)
 
 
 def normed(value, gain, shift):
@@ -669,10 +741,13 @@
     return probs
 
 
-def col_fwd_kernel(
-    info_ref, x_ref, own_ref, other_ref, three_ref, col_ref, seven_ref, gain_ref,
-    acts_ref, one_ref, qkv_ref, resid_ref, normed_three_ref, mixed_ref,
-):
+def col_fwd_kernel(plan, info_ref, place_ref, *refs):
+    stacks, refs = refs[: len(plan)], refs[len(plan) :]
+    x_ref, own_ref, other_ref, gain_ref, acts_ref, one_ref, qkv_ref = refs[:7]
+    resid_ref, normed_three_ref, mixed_ref, three_ref, col_ref, seven_ref, sem = refs[7:]
+    copies = placing(plan, col_attn_at, place_ref, stacks, [three_ref, col_ref, seven_ref], sem)
+    for copy in copies:
+        copy.start()
     bf16 = jnp.bfloat16
     rows, cols, lanes = qkv_ref.shape
     width = lanes // 3
@@ -683,6 +758,8 @@
         [jnp.where(flip, own, other), jnp.where(flip, other, own)], axis=1
     )
     acts_ref[:, :width] = mixed_one
+    for copy in copies:
+        copy.wait()
     stream = (x_ref[...].astype(jnp.float32) + contract(mixed_one, three_ref[...], PLAIN)).astype(bf16)
     one_ref[...] = stream
     normed_two = normed(stream.astype(jnp.float32), gain_ref[2:3], gain_ref[3:4])[0].astype(bf16)
@@ -715,15 +792,20 @@
     normed_three_ref[...] = normed(resid, gain_ref[4:5], gain_ref[5:6])[0].astype(bf16)
 
 
-def col_bwd_kernel(
-    info_ref, up_ref, da_ref, da_got_ref, resid_ref, one_ref, qkv_ref, three_ref, col_ref, seven_ref,
-    gain_ref, stream_ref, own_ref, other_ref, mine_ref, theirs_ref, norms_ref, dqkv_ref, do_ref,
-):
+def col_bwd_kernel(plan, info_ref, place_ref, *refs):
+    stacks, refs = refs[: len(plan)], refs[len(plan) :]
+    up_ref, da_ref, da_got_ref, out_ref, out_got_ref, resid_ref, one_ref, qkv_ref, gain_ref = refs[:9]
+    result_ref, stream_ref, own_ref, other_ref, mine_ref, theirs_ref, norms_ref = refs[9:16]
+    dqkv_ref, do_ref, three_ref, col_ref, seven_ref, sem = refs[16:]
+    copies = placing(plan, col_attn_at, place_ref, stacks, [three_ref, col_ref, seven_ref], sem)
+    for copy in copies:
+        copy.start()
     bf16 = jnp.bfloat16
     f32 = jnp.float32
     rows, cols, lanes = qkv_ref.shape
     width = lanes // 3
     part = 16
+    result_ref[...] = (resid_ref[...] + out_ref[...] + out_got_ref[...].astype(f32)).astype(bf16)
     da = da_ref[...] + da_got_ref[...].astype(f32)
     gain = gain_ref[4:5]
     _, unit, scale = normed(resid_ref[...], gain, 0.0)
@@ -740,6 +822,8 @@
         theirs_ref[:, at] = jnp.where(flip, value[:, half:], value[:, :half])
 
     put_halves(4 * half, branch)
+    for copy in copies:
+        copy.wait()
     do_ref[...] = contract(branch, seven_ref[...], LAST).astype(bf16).reshape(rows, cols, width)
     keep = column_masks(info_ref, rows, part)
     sides = head_lanes(TILE)
@@ -811,6 +895,54 @@
         sent_ref[:, :, at] = jnp.where(first, terms[:, 1], terms[:, 0])
 
 
+def column_call(kernel, info, place, pieces, args, outs, scratch):
+    width = args[-1].shape[1]
+    bf16 = jnp.bfloat16
+    small = pl.BlockSpec(memory_space=pltpu.SMEM)
+    inside = pl.BlockSpec(memory_space=pltpu.VMEM)
+    anywhere = pl.BlockSpec(memory_space=pl.ANY)
+    return pl.pallas_call(
+        partial(kernel, [step for step, _ in pieces]),
+        in_specs=[small] * 2 + [anywhere] * len(pieces) + [inside] * len(args),
+        out_specs=[inside] * len(outs),
+        out_shape=[jax.ShapeDtypeStruct(shape, kind) for shape, kind in outs],
+        scratch_shapes=[
+            *scratch,
+            pltpu.VMEM((width, width), bf16),
+            pltpu.VMEM((width, 3 * width), bf16),
+            pltpu.VMEM((width, width), bf16),
+            pltpu.SemaphoreType.DMA((20 * len(pieces),)),
+        ],
+        compiler_params=pltpu.CompilerParams(vmem_limit_bytes=56 * 2**20),
+    )(info, place, *[value for _, value in pieces], *args)
+
+
+def adam_kernel(place_ref, factor_ref, own_ref, other_ref, w_ref, first_ref, second_ref, *outs):
+    half = w_ref.shape[2] // 2
+    at = pl.ds(pl.multiple_of(pl.program_id(0) * half, TILE), half)
+    own, other = own_ref[:, at], other_ref[:, at]
+    low = place_ref[2] == 0
+    grad = jnp.concatenate([jnp.where(low, own, other), jnp.where(low, other, own)], axis=1)
+    grad = grad.astype(jnp.float32) * factor_ref[0]
+    first, second, weight = adam_update(w_ref[0], first_ref[0], second_ref[0], grad, matrix_rate)
+    for ref, value in zip(outs, (first, second, weight, weight.astype(jnp.bfloat16))):
+        ref[0] = value
+
+
+def attn_adam(place, factor, own, other, weight, first, second):
+    small = pl.BlockSpec(memory_space=pltpu.SMEM)
+    inside = pl.BlockSpec(memory_space=pltpu.VMEM)
+    block = pl.BlockSpec((1, *weight.shape[1:]), lambda m: (m, 0, 0))
+    kinds = [jnp.float32] * 3 + [jnp.bfloat16]
+    return pl.pallas_call(
+        adam_kernel,
+        grid=(weight.shape[0],),
+        in_specs=[small, small, inside, inside] + [block] * 3,
+        out_specs=[block] * 4,
+        out_shape=[jax.ShapeDtypeStruct(weight.shape, kind) for kind in kinds],
+    )(place, factor.reshape(1), own, other, weight, first, second)
+
+
 def whole_call(kernel, info, args, outs, scratch=()):
     inside = pl.BlockSpec(memory_space=pltpu.VMEM)
     return pl.pallas_call(
@@ -837,15 +969,17 @@
 ):
     bf16 = jnp.bfloat16
     stacks, refs = refs[: len(plan)], refs[len(plan) :]
-    out_ref, out_other_ref, da_ref, da_other_ref, sent_ref, kept_ref = refs[:6]
-    w_ref, tokens_ref, turned_ref, out_sum, da_sum, sem = refs[6:]
+    out_ref, out_other_ref, da_ref, da_other_ref = refs[:4]
+    y_sent_ref, y_kept_ref, x_sent_ref, x_kept_ref = refs[4:8]
+    w_ref, tokens_ref, turned_ref, out_sum, da_sum, sem = refs[8:]
     step = pl.program_id(0)
     count, width = a_ref.shape
-    chunk = sent_ref.shape[1]
+    chunk = x_sent_ref.shape[3]
+    last = pl.num_programs(0) - 1
 
     @pl.when(step == 0)
     def _():
-        copies = placing(plan, ffn_at, place_ref, stacks, [w_ref], sem)
+        copies = placing(plan, ffn_at, place_ref, stacks, [w_ref], sem, steps=False)
         for copy in copies:
             copy.start()
         for n, ref in enumerate((a_ref, a_got_ref, up_ref, up_got_ref)):
@@ -872,11 +1006,23 @@
         grads.append(grad)
     in_terms = contract(turned_ref[0], jnp.concatenate(grads, axis=0), PLAIN).astype(bf16)
     out_terms = contract(turned_ref[1], jnp.concatenate(activs, axis=0), PLAIN).astype(bf16)
-    first = place_ref[3] == 0
-    kept_ref[...] = jnp.where(first, in_terms, out_terms)
-    sent_ref[...] = jnp.where(first, out_terms, in_terms)
-
-    @pl.when(step == pl.num_programs(0) - 1)
+
+    @pl.when(step < last)
+    def _():
+        first = place_ref[3] == 0
+        y_kept_ref[...] = jnp.where(first, in_terms, out_terms)
+        y_sent_ref[...] = jnp.where(first, out_terms, in_terms)
+
+    @pl.when(step == last)
+    def _():
+        first = place_ref[1] == 0
+        zs, _, depth, _ = x_sent_ref.shape
+        for n, terms in enumerate((in_terms, out_terms)):
+            terms = terms.reshape(zs, 2, depth, chunk)
+            x_kept_ref[:, n] = jnp.where(first, terms[:, 0], terms[:, 1])
+            x_sent_ref[:, n] = jnp.where(first, terms[:, 1], terms[:, 0])
+
+    @pl.when(step == last)
     def _():
         out_ref[...] = out_sum[:count]
         out_other_ref[...] = out_sum[count:].astype(bf16)
@@ -884,19 +1030,21 @@
         da_other_ref[...] = da_sum[count:].astype(bf16)
 
 
-def feed_forward(place, normed_own, normed_got, up_own, up_got, pieces, chunk=512):
+def feed_forward(place, normed_own, normed_got, up_own, up_got, pieces, chunk=768):
     count, width = normed_own.shape
     half = pieces[0][1].shape[-1]
     anywhere = pl.BlockSpec(memory_space=pl.ANY)
     inside = pl.BlockSpec(memory_space=pltpu.VMEM)
-    lanes = pl.BlockSpec((width, chunk), lambda n: (0, n))
+    steps = half // chunk
+    lanes = pl.BlockSpec((width, chunk), lambda n: (0, jnp.minimum(n, steps - 2)))
     f32, bf16 = jnp.float32, jnp.bfloat16
-    shapes = [((count, width), kind) for kind in (f32, bf16, f32, bf16)] + [((width, half), bf16)] * 2
+    shapes = [((count, width), kind) for kind in (f32, bf16, f32, bf16)]
+    shapes = shapes + [((width, half - chunk), bf16)] * 2 + [((4, 2, width // 8, chunk), bf16)] * 2
     return pl.pallas_call(
         partial(ffn_kernel, [step for step, _ in pieces]),
-        grid=(half // chunk,),
+        grid=(steps,),
         in_specs=[pl.BlockSpec(memory_space=pltpu.SMEM)] + [inside] * 4 + [anywhere] * len(pieces),
-        out_specs=[inside] * 4 + [lanes] * 2,
+        out_specs=[inside] * 4 + [lanes] * 2 + [inside] * 2,
         out_shape=[jax.ShapeDtypeStruct(shape, kind) for shape, kind in shapes],
         scratch_shapes=[
             pltpu.VMEM((2 * width, half), bf16),
@@ -956,182 +1104,185 @@
     mine = pick(mine, z % 2, 1)
     cols_live, rows_live = mine[0], mine[1]
     place = jnp.stack([z, x, c, y]).astype(jnp.int32)
-    info = jnp.concatenate([place[:3], mine])
+    info = jnp.concatenate([place[:3], mine, place[3:]])
     tie = (lax.rsqrt(rows_live.astype(f32)) * (1.0 / math.sqrt(DH))).reshape(1)
-
-    tokens_here = merge_cores(tokens, c)
 
     attn_low = attn_weight.astype(bf16)
     halves = attn_low.reshape(8, depth, 2, half)
     row_half = jnp.moveaxis(pick(halves[:3], c, 2), 0, 1).reshape(2, depth // 2, 3 * half)
-    norm_row = jnp.pad(
-        norm_param.astype(bf16).reshape(1, 6 * depth), ((0, 15), (0, 3 * half - 6 * depth))
-    )
-    row_quarter = jnp.concatenate([pick(row_half, y, 0), norm_row])
+    row_quarter = pick(row_half, y, 0)
     col_quarter = pick(pick(halves[3:], c, 2).reshape(5, 2, depth // 2, half), y, 1)
+    row_z = gather_z(row_quarter)
     ffn_low = [in_weight.astype(bf16), out_weight.astype(bf16).T]
     ffn_low = [
         jnp.where(c == 0, low[:, :hidden_half], low[:, hidden_half:]) for low in ffn_low
     ]
     ffn_quarter = jnp.where(y == 0, *ffn_low)
-    tokens_here, row_quarter, col_quarter, ffn_quarter = together(
-        tokens_here, row_quarter, col_quarter, ffn_quarter
-    )
-
-    stream_zero = lax.all_to_all(tokens_here, ("z", "x"), 0, 0, tiled=True)
-    *row_z, col_quarter = together(*gather_z(row_quarter), col_quarter)
-    w_row, norm_rows = placed_pieces(
-        spread(jnp.stack(row_z)),
-        row_attn_at,
-        [(width, 3 * half), (16, 16, 3 * half)],
+
+    lanes = jnp.arange(width, dtype=jnp.int32) // depth
+    norm_low = jnp.tile(norm_param.astype(bf16), (1, width // depth))
+    norm_rows = jnp.where(lanes[None] == z * 2 + x, norm_low, jnp.zeros_like(norm_low))
+    norm_rows = jnp.pad(norm_rows, ((0, 10), (0, 0)))
+    part = tokens.shape[2] // 4
+    tokens_here = merge_cores(tokens, c).reshape(4, 2 * part, width)
+    parts = [
+        jnp.concatenate([pick(tokens_here, lax.bitwise_xor(z, i), 0), norm_rows]) for i in range(4)
+    ]
+    parts = [parts[0]] + [
+        lax.ppermute(parts[i], "z", [(k, k ^ i) for k in range(4)]) for i in (1, 2, 3)
+    ]
+    row_pieces = spread(jnp.stack(row_z))
+    row_x, row_y, *parts, col_quarter = together(
+        row_pieces[1][1], row_pieces[2][1], *parts, col_quarter
+    )
+    row_pieces = [
+        row_pieces[0],
+        ((1, 0, 0), row_x),
+        ((0, 1, 0), row_y),
+        row_pieces[3],
+    ]
+    tokens_z = jnp.stack(parts)
+    col_z = gather_z(col_quarter)
+    tokens_x, row_last, ffn_quarter, *col_z = together(
+        swap(tokens_z, "x"), row_pieces[3][1], ffn_quarter, *col_z
+    )
+    row_pieces[3] = (row_pieces[3][0], row_last)
+    col_pieces = spread(jnp.stack(col_z))
+    ffn_z = lax.all_to_all(
+        jnp.broadcast_to(ffn_quarter, (4, *ffn_quarter.shape)), "z", 0, 0, tiled=True
+    )
+    tokens_far = swap(tokens_x, "c")
+    tokens_far, col_x, col_y, ffn_z, up = together(
+        tokens_far, col_pieces[1][1], col_pieces[2][1], ffn_z, merge_cores(cotangent, c)
+    )
+    up = lax.all_to_all(up, ("z", "x"), 0, 0, tiled=True)
+    col_pieces[1] = (col_pieces[1][0], col_x)
+
+    rows = 8
+    count = rows * part
+    stream_zero, near_normed, far_normed, w_row, norm_gain, near, far, mixed_heads = row_attention(
         place,
-        32,
-    )
-    norm_gain = norm_rows.reshape(8, 2, 16, 3 * half)[:, 0, 0, : 6 * depth].reshape(8, 6, depth)
-    norm_gain = jnp.moveaxis(norm_gain, 0, 1).reshape(6, width).astype(f32)
-    rows, part, _ = stream_zero.shape
-    count = rows * part
-    stream_zero = stream_zero.reshape(count, width)
+        info,
+        tie,
+        [((0, 0), tokens_z), ((1, 0), tokens_x), ((0, 1), swap(tokens_z, "c")), ((1, 1), tokens_far)],
+        row_pieces,
+        rows,
+        half,
+    )
     resid_one = stream_zero.astype(f32)
-    normed_one = layer_norm(resid_one, norm_gain[0], norm_gain[1]).astype(bf16)
-    *col_z, normed_one, ffn_quarter = together(*gather_z(col_quarter), normed_one, ffn_quarter)
-    near_normed = jnp.concatenate([normed_one, swap(normed_one, "c")])
-    far_first = swap(normed_one, "x")
-    col_pieces = spread(jnp.stack(col_z))
-    near = contract(near_normed, w_row, PLAIN).astype(bf16).reshape(2, rows, part, 3 * half)
-    ffn_z = gather_z(ffn_quarter)
-    far_normed = jnp.concatenate([far_first, swap(far_first, "c")])
-    far = contract(far_normed, w_row[:, half:], PLAIN).astype(bf16)
-    far, *early = together(far.reshape(2, rows, part, 2 * half), *[v for _, v in col_pieces[:3]])
-    col_pieces = [(step, v) for (step, _), v in zip(col_pieces[:3], early)] + col_pieces[3:]
-    mixed_heads = row_attention(info, tie, near, far).reshape(2, count, half)
-    mixed_heads, cotangent, *ffn_z = together(mixed_heads, cotangent, *ffn_z)
-    ffn_pieces = spread(jnp.stack(ffn_z))
-    w_three, w_col, w_seven = placed_pieces(
-        both_cores(col_pieces),
-        col_attn_at,
-        [(width, width), (width, 3 * width), (width, width)],
-        place,
-        8 * 4 * 5,
-    )
+    mixed_heads = mixed_heads.reshape(2, count, half)
+    ffn_pieces = spread(ffn_z)
+    col_quarters = [col_pieces[0][1], col_x, col_y]
+    mixed_heads, up, last, ffn_x, ffn_y, *col_others = together(
+        mixed_heads, up, swap(col_x, "y"), ffn_pieces[1][1], ffn_pieces[2][1],
+        *[swap(value, "c") for value in col_quarters],
+    )
+    ffn_pieces[1:] = [
+        (ffn_pieces[1][0], ffn_x),
+        (ffn_pieces[2][0], ffn_y),
+        (ffn_pieces[3][0], swap(ffn_x, "y")),
+    ]
+    steps = [(j, m) for m in (0, 1) for j in (0, 1)]
+    col_pieces = [((*step, 0), v) for step, v in zip(steps, [*col_quarters, last])]
+    col_others = [*col_others, swap(last, "c")]
+    col_pieces = col_pieces + [((*step, 1), v) for step, v in zip(steps, col_others)]
 
     whole_shape, wide_shape = ((count, width), bf16), ((rows, part, 3 * width), bf16)
-    acts, stream_one, qkv_two, resid_three, normed_three = whole_call(
+    acts, stream_one, qkv_two, resid_three, normed_three = column_call(
         col_fwd_kernel,
         info,
-        [
-            stream_zero,
-            mixed_heads[0],
-            swap(mixed_heads[1], "c"),
-            w_three,
-            w_col,
-            w_seven,
-            norm_gain,
-        ],
+        place,
+        col_pieces,
+        [stream_zero, mixed_heads[0], swap(mixed_heads[1], "c"), norm_gain],
         [((count, 3 * width), bf16), whole_shape, wide_shape, ((count, width), f32), whole_shape],
         [pltpu.VMEM((rows, part, width), bf16)],
     )
 
-    up = lax.all_to_all(merge_cores(cotangent, c), ("z", "x"), 0, 0, tiled=True)
     column = x * (2 * part) + c * part + jnp.arange(part, dtype=jnp.int32)
     live = jnp.logical_and(
         (jnp.arange(rows, dtype=jnp.int32) < rows_live)[:, None], (column < cols_live)[None, :]
     )
     up = jnp.where(live[..., None], up, jnp.zeros_like(up)).reshape(count, width)
-    out_own, out_other, da_own, da_other, ffn_sent, ffn_kept = feed_forward(
+    out_own, out_other, da_own, da_other, *ffn_terms = feed_forward(
         place, normed_three, swap(normed_three, "c"), up, swap(up, "c"), ffn_pieces
     )
     da_got = swap(da_other, "c")
-    result = (resid_three + out_own + swap(out_other, "c").astype(f32)).astype(bf16)
-    ffn_got = swap(ffn_sent, "y")
+    out_got = swap(out_other, "c")
+    y_sent, y_kept, x_sent, x_kept = ffn_terms
+    y_got, x_got = swap(y_sent, "y"), swap(x_sent, "x")
 
     acts_got = swap(acts, "c")
-    grad_stream, grad_own, grad_other, attn_mine, attn_theirs, col_norms = whole_call(
+    result, grad_stream, grad_own, grad_other, attn_mine, attn_theirs, col_norms = column_call(
         col_bwd_kernel,
         info,
-        [
-            up,
-            da_own,
-            da_got,
-            resid_three,
-            stream_one,
-            qkv_two,
-            w_three,
-            w_col,
-            w_seven,
-            norm_gain,
-        ],
-        [whole_shape]
+        place,
+        col_pieces,
+        [up, da_own, da_got, out_own, out_got, resid_three, stream_one, qkv_two, norm_gain],
+        [whole_shape] * 2
         + [((count, half), bf16)] * 2
         + [((count, 5 * half), bf16)] * 2
         + [((4, width), f32)],
         [pltpu.VMEM((rows, part, 3 * width), bf16), pltpu.VMEM((rows, part, width), bf16)],
     )
+
+    result, x_got, y_got = together(result, x_got, y_got)
+    block_out = to_blocks(result.reshape(rows, part, width))
+    (
+        near_part, near_theirs, far_part, far_theirs, row_sent, row_kept,
+        ffn_to_x, ffn_x, ffn_to_y, ffn_y,
+    ) = row_attention_back(
+        info, tie, near, far, grad_own, swap(grad_other, "c"), w_row, near_normed, far_normed,
+        y_kept, y_got, x_kept, x_got,
+    )
+    row_sent, far_theirs, near_theirs, attn_theirs, block_out, ffn_to_x, ffn_to_y = together(
+        row_sent, far_theirs, near_theirs, attn_theirs, block_out, ffn_to_x, ffn_to_y
+    )
+    ffn_x_got, ffn_y_got = swap(ffn_to_x, "x"), swap(ffn_to_y, "y")
+    row_got = swap(row_sent, "x")
+    far_sum = added(far_part, swap(far_theirs, "c"))
+    far_got = swap(far_sum, "x")
+    near_got = swap(near_theirs, "c")
     attn_sent, attn_kept = whole_call(
         attn_terms_kernel,
         place,
         [acts, acts_got, attn_mine, swap(attn_theirs, "c")],
         [((8, depth // 2, 5 * half), bf16)] * 2,
     )
-    ffn_pair = added(ffn_kept, ffn_got).reshape(4, 2, depth, hidden_half)
-
-    ffn_pair, attn_sent, attn_kept, grad_own = together(ffn_pair, attn_sent, attn_kept, grad_own)
     attn_got = swap(attn_sent, "y")
-    ffn_column = added(pick(ffn_pair, x, 1), swap(pick(ffn_pair, 1 - x, 1), "x"))
-    near_part, near_theirs, far_part, far_theirs, row_sent, row_kept = row_attention_back(
-        info, tie, near, far, grad_own, swap(grad_other, "c"), w_row, near_normed, far_normed
-    )
-    ffn_column, row_sent, far_theirs, near_theirs = together(
-        ffn_column, row_sent, far_theirs, near_theirs
-    )
-    row_column = added(row_kept, swap(row_sent, "x"))
-    far_sum = added(far_part, swap(far_theirs, "c"))
-    far_got = swap(far_sum, "x")
-    near_got = swap(near_theirs, "c")
+    attn_kept, ffn_y_got, ffn_x_got = together(attn_kept, ffn_y_got, ffn_x_got)
+    ffn_column = jnp.concatenate([added(ffn_x, ffn_x_got), added(ffn_y, ffn_y_got)], axis=2)
+    ffn_own = z_summed(ffn_column, z)
+    row_column, ffn_own = together(added(row_kept, row_got), ffn_own)
+    row_own = z_summed(row_column, z)
+    far_got, attn_got, block_out = together(far_got, attn_got, block_out)
+    block_out = to_rows(block_out, c)
     attn_pair_terms = added(attn_kept, attn_got).reshape(4, 2, depth // 2, 5 * half)
-    ffn_own = z_summed(ffn_column, z)
-    row_column, attn_pair_terms, far_got, ffn_own = together(
-        row_column, attn_pair_terms, far_got, ffn_own
-    )
-    row_own = z_summed(row_column, z)
     grad_normed_one = near_part + near_got.astype(f32) + far_got.astype(f32)
     _, norm_back_one = jax.vjp(layer_norm, resid_one, norm_gain[0], norm_gain[1])
     part_one, gain_grad_one, shift_grad_one = norm_back_one(grad_normed_one)
     grad_input = (grad_stream.astype(f32) + part_one).astype(bf16)
-    both_out = jnp.concatenate([result, grad_input], axis=1).reshape(rows, part, 2 * width)
-    both_out = to_rows(both_out, c)
-    block_out, grad_tokens = both_out[..., :width], both_out[..., width:].astype(f32)
+    grad_tokens = to_blocks(grad_input.reshape(rows, part, width))
 
     norm_stack = jnp.concatenate([jnp.stack([gain_grad_one, shift_grad_one]), col_norms])
-    norm_terms = jnp.moveaxis(norm_stack.reshape(6, 4, 2, depth), 0, 2).reshape(4, 2, 1, 6 * depth)
-    norm_terms = jnp.pad(norm_terms, ((0, 0), (0, 0), (0, 15), (0, 5 * half - 6 * depth)))
-    attn_blocks = jnp.concatenate([attn_pair_terms, norm_terms.astype(bf16)], axis=2)
+    norm_terms = jnp.moveaxis(norm_stack.reshape(6, 4, 2, depth), 0, 2).reshape(4, 2, depth // 2, 12)
+    norm_terms = jnp.pad(norm_terms.astype(bf16), ((0, 0), (0, 0), (0, 0), (0, TILE - 12)))
+    attn_blocks = jnp.concatenate([attn_pair_terms, norm_terms], axis=3)
     attn_column = added(pick(attn_blocks, x, 1), swap(pick(attn_blocks, 1 - x, 1), "x"))
-    attn_column, row_own = together(attn_column, row_own)
+    attn_column, row_own, grad_tokens = together(attn_column, row_own, grad_tokens)
     attn_own = z_summed(attn_column, z)
+    grad_tokens = to_rows(grad_tokens, c).astype(f32)
     row_grad = added(row_own, swap(row_own, "y"))
     attn_y = swap(attn_own, "y")
-    attn_grad_b = joined(attn_own[: depth // 2], attn_y[: depth // 2], y, 0)
-    norm_grad = added(attn_own[depth // 2 :], attn_y[depth // 2 :])
+    attn_grad_b = joined(attn_own[:, : 5 * half], attn_y[:, : 5 * half], y, 0)
+    norm_grad = added(attn_own[:, 5 * half :], attn_y[:, 5 * half :])
     ffn_grads = [ffn_own, swap(ffn_own, "y")]
 
     row_other = swap(row_grad, "c")
-    attn_other = swap(jnp.concatenate([attn_grad_b, norm_grad]), "c")
-    norm_grad = norm_grad[0, : 6 * depth].astype(f32) + attn_other[depth, : 6 * depth].astype(f32)
-    norm_grad = norm_grad.reshape(6, depth)
+    attn_other = swap(attn_grad_b, "c")
+    norm_grad = norm_grad.astype(f32) + swap(norm_grad, "c").astype(f32)
+    norm_grad = norm_grad[:, :12].reshape(6, depth)
     ffn_whole = [joined(piece, swap(piece, "c"), c, 1) for piece in ffn_grads]
 
-    def whole(own, other, groups):
-        size = own.shape[1] // groups
-        return [
-            joined(
-                own[:depth, n * size : (n + 1) * size], other[:depth, n * size : (n + 1) * size], c, 1
-            )
-            for n in range(groups)
-        ]
-
-    attn_grad = jnp.stack(whole(row_grad, row_other, 3) + whole(attn_grad_b, attn_other, 5))
-    attn_grad = attn_grad.astype(f32)
     in_grad = jnp.where(y == 0, *ffn_whole).astype(f32)
     out_grad = jnp.where(y == 0, *ffn_whole[::-1]).astype(f32).T
 
@@ -1139,12 +1290,18 @@
         jnp.sum(jnp.square(g.astype(f32))) for g in (row_grad, attn_grad_b, *ffn_grads)
     )
     squares = squares + swap(squares, "c") + jnp.sum(norm_grad * norm_grad)
-    squares = squares + swap(squares, "x")
-    squares = gather_z(squares)
-    grad_norm = jnp.sqrt((squares[0] + squares[1]) + (squares[2] + squares[3]))
+    squares = jnp.broadcast_to(squares, (8, 8, TILE))
+    squares = lax.all_to_all(squares, ("z", "x"), 0, 0, tiled=True)
+    grad_norm = jnp.sqrt(jnp.sum(squares[:, 0, 0]))
     factor = clip_bound / jnp.maximum(grad_norm, clip_bound)
-    attn_first_new, attn_second_new, attn_weight_new = adam_update(
-        attn_weight, attn_first, attn_second, attn_grad * factor, matrix_rate
+    attn_first_new, attn_second_new, attn_weight_new, attn_copy = attn_adam(
+        place,
+        factor,
+        jnp.concatenate([row_grad, attn_grad_b], axis=1),
+        jnp.concatenate([row_other, attn_other], axis=1),
+        attn_weight,
+        attn_first,
+        attn_second,
     )
     in_first_new, in_second_new, in_weight_new = adam_update(
         in_weight, in_first, in_second, in_grad * factor, matrix_rate
@@ -1162,7 +1319,7 @@
         attn_first_new,
         attn_second_new,
         attn_weight_new,
-        attn_weight_new.astype(bf16),
+        attn_copy,
         in_first_new,
         in_second_new,
         in_weight_new,

time: 509 us -> 452 us (0.89)
  waiting for transfers between devices: 185 us -> 156 us
  other arithmetic: 72.2 us -> 48 us
  Pallas kernels: 96.7 us -> 115 us
  starting transfers between devices: 104 us -> 92.5 us
    pallas_call x5 -> x6, Pallas kernels: 54.4 us -> 106 us  [the longest x2 37.2 us: column_call(): pl.pallas_call(partial(kernel, [step for step, _ in pieces]), in_specs=[s...]
    ppermute x45 -> x48, waiting for transfers between devices: 135 us -> 89.3 us  [swap(): return lax.ppermute(value, axis, PAIR)]
    pallas_call x3 -> x1, Pallas kernels: 42.3 us -> 9.48 us  [whole_call(): pl.pallas_call(kernel, in_specs=[pl.BlockSpec(memory_space=pltpu.SMEM)] +...]
    ppermute x12 -> x6, starting transfers between devices: 30.3 us -> 11.2 us  [gather_z(): lax.ppermute(own, 'z', [(k, k ^ i) for k in range(4)])]
    ppermute x0 -> x3, waiting for transfers between devices: none -> 13.1 us  [paired_body(): lax.ppermute(parts[i], 'z', [(k, k ^ i) for k in range(4)])]
    convert_element_type x6 -> x3, other arithmetic: 13.2 us -> 1.28 us  [the longest x1 1.25 us: paired_body(): grad_tokens = to_rows(grad_tokens, c).astype(f32)]
    all_to_all x3 -> x5, waiting for transfers between devices: 0.01 us -> 10.7 us  [the longest x1 6.56 us: paired_body(): lax.all_to_all(jnp.broadcast_to(ffn_quarter, (4, *ffn_quarter.shape)), 'z...]
    ppermute x9, waiting for transfers between devices: 32.8 us -> 24.3 us  [z_summed(): got = lax.ppermute(other, 'z', [(k, k ^ i) for k in range(4)])]
  transfers between devices with their start and end apart: 69 -> 71, of which waited for: 26 -> 26; matrix products, arithmetic and copies ran while one was open for 17% -> 13% of each run, Pallas kernels for 13% -> 18%
where the time goes in v5:
time: 452 us; the launch traced here: 444 us
  waiting for transfers between devices  156 us (35%)
  Pallas kernels  115 us (25%)
  starting transfers between devices  92.5 us (20%)
  other arithmetic  48 us (11%)
  local copies, waits for them, and re-layouts  24.6 us (5%)
  between operations  8.39 us (2%)
    ppermute x48, waiting for transfers between devices, swap(): return lax.ppermute(value, axis, PAIR)  89.3 us
    pallas_call x2, Pallas kernels, column_call(): pl.pallas_call(partial(kernel, [step for step, _ in pieces]), in_specs=[s...  37.2 us
    ppermute x48, starting transfers between devices, swap(): return lax.ppermute(value, axis, PAIR)  32.6 us
    pallas_call x1, Pallas kernels, feed_forward(): pl.pallas_call(partial(ffn_kernel, [step for step, _ in pieces]), grid=(s...  25.2 us
    ppermute x9, waiting for transfers between devices, z_summed(): got = lax.ppermute(other, 'z', [(k, k ^ i) for k in range(4)])  24.3 us
    pallas_call x1, Pallas kernels, row_attention_back(): pl.pallas_call(row_bwd_kernel, in_specs=[small, small] + [inside] * 11, o...  20.4 us
    ppermute x9, starting transfers between devices, z_summed(): got = lax.ppermute(other, 'z', [(k, k ^ i) for k in range(4)])  20.1 us
    ppermute x6, waiting for transfers between devices, gather_z(): lax.ppermute(own, 'z', [(k, k ^ i) for k in range(4)])  18.4 us
  transfers between devices with their start and end apart: 71, of which 26 were waited for; matrix products, arithmetic and copies ran while one was open for 13% of the time, Pallas kernels for 18%

profile of v5, /device:TPU:0, one launch (start us, length us, event | category | flops | bytes accessed | tf_op | source)
XLA Modules:
  0.0 444.4 jit_solution(7696421447563666447)
XLA Ops:
  11.2 6.8 %collective-permute-done.2 = bf16[48,1152]{1,0:T(8,128)(2,1)S(1)} collective-permute-done((bf16[48,1152]{1,0:T(8,128)(2,1)S(1)}, bf16[48,1152]{1,0:T(8,128)(2,1)S(1)}, u32[]{:S(2)}, u32[]{:S(2)}) %collective-permute-start.2) | collective-permute-done | bytes 110624 | tf_op jit(solution)/shard_map/ppermute | solution.py:368
  32.0 11.4 %collective-permute-done.8 = bf16[144,768]{1,0:T(8,128)(2,1)S(1)} collective-permute-done((bf16[144,768]{1,0:T(8,128)(2,1)S(1)}, bf16[144,768]{1,0:T(8,128)(2,1)S(1)}, u32[]{:S(2)}, u32[]{:S(2)}) %collective-permute-start.8) | collective-permute-done | bytes 221216 | tf_op jit(solution)/shard_map/ppermute | solution.py:1132
  53.6 9.2 %collective-permute-done.13 = bf16[5,48,384]{2,1,0:T(8,128)(2,1)S(1)} collective-permute-done((bf16[5,48,384]{2,1,0:T(8,128)(2,1)S(1)}, bf16[5,48,384]{2,1,0:T(8,128)(2,1)S(1)}, u32[]{:S(2)}, u32[]{:S(2)}) %collective-permute-start.13) | collective-permute-done | bytes 184352 | tf_op jit(solution)/shard_map/ppermute | solution.py:368
  65.4 5.7 %all-to-all-start = ((bf16[4,96,1536]{2,1,0:T(8,128)(2,1)}), bf16[4,96,1536]{2,1,0:T(8,128)(2,1)}, u32[]{:S(2)}, u32[]{:S(2)}) async-start(bf16[4,96,1536]{2,1,0:T(8,128)(2,1)} %broadcast_in_dim.42), calls=%async_computation | async-start | bytes 2359296 | tf_op jit(solution)/shard_map/all_to_all | solution.py:1151
  78.0 13.2 %collective-permute-done.17.refs_1_ = bf16[4,5,48,384]{3,2,1,0:T(8,128)(2,1)S(1)} collective-permute-done((bf16[4,5,48,384]{3,2,1,0:T(8,128)(2,1)S(1)}, bf16[4,5,48,384]{3,2,1,0:T(8,128)(2,1)S(1)}, u32[]{:S(2)}, u32[]{:S(2)}) %collective-permute-start.17) | collective-permute-done | bytes 737312 | tf_op jit(solution)/shard_map/ppermute | solution.py:319
  93.0 6.6 %all-to-all-done.refs_0_ = bf16[4,96,1536]{2,1,0:T(8,128)(2,1)} async-done(((bf16[4,96,1536]{2,1,0:T(8,128)(2,1)}), bf16[4,96,1536]{2,1,0:T(8,128)(2,1)}, u32[]{:S(2)}, u32[]{:S(2)}) %all-to-all-start) | async-done | bytes 1179680 | tf_op jit(solution)/shard_map/all_to_all | solution.py:1151
  113.5 13.3 %shard_map.295 = (bf16[512,768]{1,0:T(8,128)(2,1)}, bf16[1024,768]{1,0:T(8,128)(2,1)}, bf16[1024,768]{1,0:T(8,128)(2,1)}, bf16[768,1152]{1,0:T(8,128)(2,1)}, f32...) custom-call(s32[4]{0:T(128)} %pad_add_fusion.1.place_ref, ...), custom_call_target="tpu_custom_call" | custom-call | tf_op jit(solution)/shard_map/pallas_call | solution.py:668
  126.8 21.9 %collective-permute-done.20.refs_3_ = bf16[4,5,48,384]{3,2,1,0:T(8,128)(2,1)} collective-permute-done((bf16[4,5,48,384]{3,2,1,0:T(8,128)(2,1)}, bf16[4,5,48,384]{3,2,1,0:T(8,128)(2,1)}, u32[]{:S(2)}, u32[]{:S(2)}) %collective-permute-start.20) | collective-permute-done | bytes 737312 | tf_op jit(solution)/shard_map/ppermute | solution.py:319
  155.4 14.3 %shard_map.296 = (bf16[512,2304]{1,0:T(8,128)(2,1)}, bf16[512,768]{1,0:T(8,128)(2,1)}, bf16[8,64,2304]{2,1,0:T(8,128)(2,1)}, f32[512,768]{1,0:T(8,128)}, bf16[512,768]{1,0:T(8,128)(2,1)}) custom-call(s32[6]{0:T(128)} %concatenate.58.info_ref, s32[4]{0:T(128)} %pad_add_fusion.1.place_ref, bf16[4,5,48,384]{3,2,1,0:T(8,128)(2,1)} %copy-done.2, ...), custom_call_target="tpu_custom_call" | custom-call | tf_op jit(solution)/shard_map/pallas_call | solution.py:904
  170.2 9.4 %collective-permute-done.30.refs_3_ = bf16[4,96,1536]{2,1,0:T(8,128)(2,1)S(1)} collective-permute-done((bf16[4,96,1536]{2,1,0:T(8,128)(2,1)}, bf16[4,96,1536]{2,1,0:T(8,128)(2,1)S(1)}, u32[]{:S(2)}, u32[]{:S(2)}) %collective-permute-start.30) | collective-permute-done | bytes 1179680 | tf_op jit(solution)/shard_map/ppermute | solution.py:319
  181.5 25.2 %shard_map.297 = (f32[512,768]{1,0:T(8,128)}, bf16[512,768]{1,0:T(8,128)(2,1)}, f32[512,768]{1,0:T(8,128)}, bf16[512,768]{1,0:T(8,128)(2,1)}, bf16[768,768]{1,0:...) custom-call(s32[4]{0:T(128)} %pad_add_fusion.1.place_ref, ...), custom_call_target="tpu_custom_call" | custom-call | tf_op jit(solution)/shard_map/pallas_call | solution.py:1043
  213.2 22.9 %shard_map.298 = (bf16[512,768]{1,0:T(8,128)(2,1)}, bf16[512,768]{1,0:T(8,128)(2,1)}, bf16[512,384]{1,0:T(8,128)(2,1)}, bf16[512,384]{1,0:T(8,128)(2,1)}, bf16[5...) custom-call(s32[6]{0:T(128)} %concatenate.58.info_ref, s32[4]{0:T(128)} %pad_add_fusion.1.place_ref, ...), custom_call_target="tpu_custom_call" | custom-call | tf_op jit(solution)/shard_map/pallas_call | solution.py:904
  236.1 5.9 %all-to-all-start.2 = ((bf16[8,64,768]{2,1,0:T(8,128)(2,1)}), bf16[8,64,768]{2,1,0:T(8,128)(2,1)}, u32[]{:S(2)}, u32[]{:S(2)}) async-start(bf16[8,64,768]{2,1,0:T(8,128)(2,1)} %bitcast.132), calls=%async_computation.2 | async-start | bytes 1572864 | tf_op jit(solution)/shard_map/all_to_all | solution.py:352
  247.5 20.4 %shard_map.299 = (f32[512,768]{1,0:T(8,128)}, bf16[512,768]{1,0:T(8,128)(2,1)}, f32[512,768]{1,0:T(8,128)}, bf16[512,768]{1,0:T(8,128)(2,1)}, bf16[4,96,1152]{2,...) custom-call(s32[6]{0:T(128)} %concatenate.58.info_ref, ...), custom_call_target="tpu_custom_call" | custom-call | tf_op jit(solution)/shard_map/pallas_call | solution.py:693
  272.9 9.5 %shard_map.300 = (bf16[8,48,1920]{2,1,0:T(8,128)(2,1)}, bf16[8,48,1920]{2,1,0:T(8,128)(2,1)}) custom-call(s32[4]{0:T(128)} %pad_add_fusion.1.place_ref, bf16[512,2304]{1,0:T(8,128)(2,1)} %get-tuple-element.171.acts_ref, bf16[512,2304]{1,0:T(8,128)(2,1)} %collective-permute-done.38.got_ref, bf16[512,1920]{1,0:T(8,128)(2,1)} %get-tuple-element.172.mine_ref, ...), custom_call_target="tpu_custom_call" | custom-call | tf_op jit(solution)/shard_map/pallas_call | solution.py:948
  292.1 12.2 %collective-permute-done.46 = bf16[4,96,1152]{2,1,0:T(8,128)(2,1)} collective-permute-done((bf16[4,96,1152]{2,1,0:T(8,128)(2,1)}, bf16[4,96,1152]{2,1,0:T(8,128)(2,1)}, u32[]{:S(2)}, u32[]{:S(2)}) %collective-permute-start.46) | collective-permute-done | bytes 884768 | tf_op jit(solution)/shard_map/ppermute | solution.py:319
  310.2 16.1 %collective-permute-done.48 = bf16[96,1536]{1,0:T(8,128)(2,1)S(1)} collective-permute-done((bf16[96,1536]{1,0:T(8,128)(2,1)S(1)}, bf16[96,1536]{1,0:T(8,128)(2,1)S(1)}, u32[]{:S(2)}, u32[]{:S(2)}) %collective-permute-start.48) | collective-permute-done | bytes 294944 | tf_op jit(solution)/shard_map/ppermute | solution.py:1069
  327.4 5.9 %collective-permute-start.50 = (bf16[96,1152]{1,0:T(8,128)(2,1)}, bf16[96,1152]{1,0:T(8,128)(2,1)}, u32[]{:S(2)}, u32[]{:S(2)}) collective-permute-start(bf16[96,1152]{1,0:T(8,128)(2,1)} %get-tuple-element.228), channel_id=1, source_target_pairs={{0,8},{8,0},{16,24},{24,16},{1,9},{9,1},{17,25},{25,17},{2,10},{10... | collective-permute-start | bytes 663560 | tf_op jit(solution)/shard_map/ppermute | solution.py:1069
  341.0 4.5 %all-to-all-start.3 = ((bf16[8,64,768]{2,1,0:T(8,128)(2,1)}), bf16[8,64,768]{2,1,0:T(8,128)(2,1)}, u32[]{:S(2)}, u32[]{:S(2)}) async-start(bf16[8,64,768]{2,1,0:T(8,128)(2,1)} %bitcast.126), calls=%async_computation.3 | async-start | bytes 1572864 | tf_op jit(solution)/shard_map/all_to_all | solution.py:352
  363.0 10.5 %collective-permute-done.45 = bf16[4,48,2048]{2,1,0:T(8,128)(2,1)S(1)} collective-permute-done((bf16[4,48,2048]{2,1,0:T(8,128)(2,1)S(1)}, bf16[4,48,2048]{2,1,0:T(8,128)(2,1)S(1)}, u32[]{:S(2)}, u32[]{:S(2)}) %collective-permute-start.45) | collective-permute-done | bytes 786464 | tf_op jit(solution)/shard_map/ppermute | solution.py:319
  384.2 8.2 %collective-permute-done.56 = bf16[48,2048]{1,0:T(8,128)(2,1)S(1)} collective-permute-done((bf16[48,2048]{1,0:T(8,128)(2,1)S(1)}, bf16[48,2048]{1,0:T(8,128)(2,1)S(1)}, u32[]{:S(2)}, u32[]{:S(2)}) %collective-permute-start.56) | collective-permute-done | bytes 196640 | tf_op jit(solution)/shard_map/ppermute | solution.py:1069
  395.4 4.4 collective-permute-done.58
  421.5 5.2 %fusion.45 = (bf16[3072,96]{0,1:T(8,128)(2,1)}, f32[3072,96]{0,1:T(8,128)}, f32[3072,96]{0,1:T(8,128)}, f32[3072,96]{0,1:T(8,128)}) fusion(f32[3072,96]{0,1:T(8,128)S(1)} %copy-done.3, f32[]{:T(128)} %div.75, bf16[96,1536]{1,0:T(8,128)(2,1)S(1)} %fusion.15, bf16[96,1536]{1,0:T(8,128)(2,1)} %collective-permute-done.64, ...), kind=kLoop, calls=%fused_computation.150 | loop fusion | flops 10616832 | bytes 8847366 | tf_op jit(solution)/shard_map/convert_element_type | solution.py:1330
  433.6 9.4 %shard_map.301 = (f32[8,96,768]{2,1,0:T(8,128)}, f32[8,96,768]{2,1,0:T(8,128)}, f32[8,96,768]{2,1,0:T(8,128)}, bf16[8,96,768]{2,1,0:T(8,128)(2,1)}) custom-call(s32[4]{0:T(128)} %pad_add_fusion.1.place_ref, f32[1]{0:T(128)} %bitcast.71.factor_ref, bf16[96,3072]{1,0:T(8,128)(2,1)} %pad_maximum_fusion.2.own_ref, bf16[96,3072]{1,0:T(8,128)(2,1)} %pad_maximum_fusion.3.other_ref, ...), custom_call_target="tpu_custom_call" | custom-call | tf_op jit(solution)/shard_map/pallas_call | solution.py:937
  (315 shorter events, 163.9 us)
Async XLA Ops:
  65.4 34.2 %all-to-all-start = ((bf16[4,96,1536]{2,1,0:T(8,128)(2,1)}), bf16[4,96,1536]{2,1,0:T(8,128)(2,1)}, u32[]{:S(2)}, u32[]{:S(2)}) async-start(bf16[4,96,1536]{2,1,0:T(8,128)(2,1)} %broadcast_in_dim.42), calls=%async_computation | async-start | bytes 2359296 | tf_op jit(solution)/shard_map/all_to_all | solution.py:1151
  75.2 33.7 %collective-permute-start.15 = (bf16[4,144,768]{2,1,0:T(8,128)(2,1)}, bf16[4,144,768]{2,1,0:T(8,128)(2,1)}, u32[]{:S(2)}, u32[]{:S(2)}) collective-permute-start(bf16[4,144,768]{2,1,0:T(8,128)(2,1)} %pad_maximum_fusion.refs_0_), channel_id=1, source_target_pairs={{0,1},{1,0},{2,3},{3,2},{4,5},{5,4},{6,7},{7,6},{8,9},{9,8},{10,11... | collective-permute-start | bytes 2654216 | tf_op jit(solution)/shard_map/ppermute | solution.py:319
  76.9 32.0 %collective-permute-start.23 = (bf16[4,5,48,384]{3,2,1,0:T(8,128)(2,1)S(1)}, bf16[4,5,48,384]{3,2,1,0:T(8,128)(2,1)}, u32[]{:S(2)}, u32[]{:S(2)}) collective-permute-start(bf16[4,5,48,384]{3,2,1,0:T(8,128)(2,1)S(1)} %pad_maximum_fusion.1.refs_0_), channel_id=1, source_target_pairs={{0,1},{1,0},{2,3},{3,2},{4,5},{5,4},{6,7},{7,6},{8,9},{9,8},{10,11... | collective-permute-start | bytes 2211848 | tf_op jit(solution)/shard_map/ppermute | solution.py:319
  99.5 49.2 %all-to-all-start.1 = ((bf16[8,64,768]{2,1,0:T(8,128)(2,1)}), bf16[8,64,768]{2,1,0:T(8,128)(2,1)}, u32[]{:S(2)}, u32[]{:S(2)}) async-start(bf16[8,64,768]{2,1,0:T(8,128)(2,1)} %bitcast.124), calls=%async_computation.1 | async-start | bytes 1572864 | tf_op jit(solution)/shard_map/all_to_all | solution.py:1158
  103.8 45.0 %collective-permute-start.21 = (bf16[4,96,1536]{2,1,0:T(8,128)(2,1)}, bf16[4,96,1536]{2,1,0:T(8,128)(2,1)}, u32[]{:S(2)}, u32[]{:S(2)}) collective-permute-start(bf16[4,96,1536]{2,1,0:T(8,128)(2,1)} %all-to-all-done.refs_0_), channel_id=1, source_target_pairs={{0,4},{4,0},{1,5},{5,1},{2,6},{6,2},{3,7},{7,3},{8,12},{12,8},{9,1... | collective-permute-start | bytes 3538952 | tf_op jit(solution)/shard_map/ppermute | solution.py:319
  105.6 43.1 %collective-permute-start.22 = (bf16[4,96,1536]{2,1,0:T(8,128)(2,1)}, bf16[4,96,1536]{2,1,0:T(8,128)(2,1)}, u32[]{:S(2)}, u32[]{:S(2)}) collective-permute-start(bf16[4,96,1536]{2,1,0:T(8,128)(2,1)} %all-to-all-done.refs_0_), channel_id=1, source_target_pairs={{0,2},{2,0},{1,3},{3,1},{4,6},{6,4},{5,7},{7,5},{8,10},{10,8},{9,1... | collective-permute-start | bytes 3538952 | tf_op jit(solution)/shard_map/ppermute | solution.py:319
  108.3 40.4 %collective-permute-start.20 = (bf16[4,5,48,384]{3,2,1,0:T(8,128)(2,1)}, bf16[4,5,48,384]{3,2,1,0:T(8,128)(2,1)}, u32[]{:S(2)}, u32[]{:S(2)}) collective-permute-start(bf16[4,5,48,384]{3,2,1,0:T(8,128)(2,1)} %copy-done.6), channel_id=1, source_target_pairs={{0,2},{2,0},{1,3},{3,1},{4,6},{6,4},{5,7},{7,5},{8,10},{10,8},{9,1... | collective-permute-start | bytes 2211848 | tf_op jit(solution)/shard_map/ppermute | solution.py:319
  108.9 39.8 %collective-permute-start.24 = (bf16[4,5,48,384]{3,2,1,0:T(8,128)(2,1)}, bf16[4,5,48,384]{3,2,1,0:T(8,128)(2,1)}, u32[]{:S(2)}, u32[]{:S(2)}) collective-permute-start(bf16[4,5,48,384]{3,2,1,0:T(8,128)(2,1)} %copy-done.6), channel_id=1, source_target_pairs={{0,1},{1,0},{2,3},{3,2},{4,5},{5,4},{6,7},{7,6},{8,9},{9,8},{10,11... | collective-permute-start | bytes 2211848 | tf_op jit(solution)/shard_map/ppermute | solution.py:319
  108.9 39.8 %collective-permute-start.25 = (bf16[4,5,48,384]{3,2,1,0:T(8,128)(2,1)}, bf16[4,5,48,384]{3,2,1,0:T(8,128)(2,1)S(1)}, u32[]{:S(2)}, u32[]{:S(2)}) collective-permute-start(bf16[4,5,48,384]{3,2,1,0:T(8,128)(2,1)} %copy-done.7), channel_id=1, source_target_pairs={{0,1},{1,0},{2,3},{3,2},{4,5},{5,4},{6,7},{7,6},{8,9},{9,8},{10,11... | collective-permute-start | bytes 2211848 | tf_op jit(solution)/shard_map/ppermute | solution.py:319
  151.3 28.3 %collective-permute-start.30 = (bf16[4,96,1536]{2,1,0:T(8,128)(2,1)}, bf16[4,96,1536]{2,1,0:T(8,128)(2,1)S(1)}, u32[]{:S(2)}, u32[]{:S(2)}) collective-permute-start(bf16[4,96,1536]{2,1,0:T(8,128)(2,1)} %collective-permute-done.21.refs_1_), channel_id=1, source_target_pairs={{0,2},{2,0},{1,3},{3,1},{4,6},{6,4},{5,7},{7,5},{8,10},{10,8},{9,1... | collective-permute-start | bytes 3538952 | tf_op jit(solution)/shard_map/ppermute | solution.py:319
  206.6 29.5 %collective-permute-start.34 = (bf16[4,2,96,768]{3,2,1,0:T(8,128)(2,1)}, bf16[4,2,96,768]{3,2,1,0:T(8,128)(2,1)}, u32[]{:S(2)}, u32[]{:S(2)}) collective-permute-start(bf16[4,2,96,768]{3,2,1,0:T(8,128)(2,1)} %get-tuple-element.157), channel_id=1, source_target_pairs={{0,4},{4,0},{1,5},{5,1},{2,6},{6,2},{3,7},{7,3},{8,12},{12,8},{9,1... | collective-permute-start | bytes 3538952 | tf_op jit(solution)/shard_map/ppermute | solution.py:319
  207.2 28.9 %collective-permute-start.35 = (bf16[768,768]{1,0:T(8,128)(2,1)}, bf16[768,768]{1,0:T(8,128)(2,1)}, u32[]{:S(2)}, u32[]{:S(2)}) collective-permute-start(bf16[768,768]{1,0:T(8,128)(2,1)} %get-tuple-element.158), channel_id=1, source_target_pairs={{0,2},{2,0},{1,3},{3,1},{4,6},{6,4},{5,7},{7,5},{8,10},{10,8},{9,1... | collective-permute-start | bytes 3538952 | tf_op jit(solution)/shard_map/ppermute | solution.py:319
  236.1 31.8 %all-to-all-start.2 = ((bf16[8,64,768]{2,1,0:T(8,128)(2,1)}), bf16[8,64,768]{2,1,0:T(8,128)(2,1)}, u32[]{:S(2)}, u32[]{:S(2)}) async-start(bf16[8,64,768]{2,1,0:T(8,128)(2,1)} %bitcast.132), calls=%async_computation.2 | async-start | bytes 1572864 | tf_op jit(solution)/shard_map/all_to_all | solution.py:352
  242.0 29.2 %collective-permute-start.38 = (bf16[512,2304]{1,0:T(8,128)(2,1)}, bf16[512,2304]{1,0:T(8,128)(2,1)}, u32[]{:S(2)}, u32[]{:S(2)}) collective-permute-start(bf16[512,2304]{1,0:T(8,128)(2,1)} %get-tuple-element.171.acts_ref), channel_id=1, source_target_pairs={{0,1},{1,0},{2,3},{3,2},{4,5},{5,4},{6,7},{7,6},{8,9},{9,8},{10,11... | collective-permute-start | bytes 7077896 | tf_op jit(solution)/shard_map/ppermute | solution.py:319
  271.2 33.1 %collective-permute-start.46 = (bf16[4,96,1152]{2,1,0:T(8,128)(2,1)}, bf16[4,96,1152]{2,1,0:T(8,128)(2,1)}, u32[]{:S(2)}, u32[]{:S(2)}) collective-permute-start(bf16[4,96,1152]{2,1,0:T(8,128)(2,1)} %get-tuple-element.187), channel_id=1, source_target_pairs={{0,4},{4,0},{1,5},{5,1},{2,6},{6,2},{3,7},{7,3},{8,12},{12,8},{9,1... | collective-permute-start | bytes 2654216 | tf_op jit(solution)/shard_map/ppermute | solution.py:319
  272.3 64.1 %collective-permute-start.44 = (bf16[512,768]{1,0:T(8,128)(2,1)}, bf16[512,768]{1,0:T(8,128)(2,1)S(1)}, u32[]{:S(2)}, u32[]{:S(2)}) collective-permute-start(bf16[512,768]{1,0:T(8,128)(2,1)} %get-tuple-element.183), channel_id=1, source_target_pairs={{0,1},{1,0},{2,3},{3,2},{4,5},{5,4},{6,7},{7,6},{8,9},{9,8},{10,11... | collective-permute-start | bytes 2359304 | tf_op jit(solution)/shard_map/ppermute | solution.py:319
  284.1 52.4 %collective-permute-start.40 = (bf16[8,48,1920]{2,1,0:T(8,128)(2,1)}, bf16[8,48,1920]{2,1,0:T(8,128)(2,1)S(1)}, u32[]{:S(2)}, u32[]{:S(2)}) collective-permute-start(bf16[8,48,1920]{2,1,0:T(8,128)(2,1)} %get-tuple-element.174), channel_id=1, source_target_pairs={{0,2},{2,0},{1,3},{3,1},{4,6},{6,4},{5,7},{7,5},{8,10},{10,8},{9,1... | collective-permute-start | bytes 4423688 | tf_op jit(solution)/shard_map/ppermute | solution.py:319
  290.6 44.4 %collective-permute-start.37 = (bf16[512,768]{1,0:T(8,128)(2,1)S(1)}, bf16[512,768]{1,0:T(8,128)(2,1)S(1)}, u32[]{:S(2)}, u32[]{:S(2)}) collective-permute-start(bf16[512,768]{1,0:T(8,128)(2,1)S(1)} %add_convert_fusion.3), channel_id=1, source_target_pairs={{0,4},{4,0},{1,5},{5,1},{2,6},{6,2},{3,7},{7,3},{8,12},{12,8},{9,1... | collective-permute-start | bytes 2359304 | tf_op jit(solution)/shard_map/ppermute | solution.py:319
  327.4 25.3 %collective-permute-start.50 = (bf16[96,1152]{1,0:T(8,128)(2,1)}, bf16[96,1152]{1,0:T(8,128)(2,1)}, u32[]{:S(2)}, u32[]{:S(2)}) collective-permute-start(bf16[96,1152]{1,0:T(8,128)(2,1)} %get-tuple-element.228), channel_id=1, source_target_pairs={{0,8},{8,0},{16,24},{24,16},{1,9},{9,1},{17,25},{25,17},{2,10},{10... | collective-permute-start | bytes 663560 | tf_op jit(solution)/shard_map/ppermute | solution.py:1069
  341.0 32.8 %all-to-all-start.3 = ((bf16[8,64,768]{2,1,0:T(8,128)(2,1)}), bf16[8,64,768]{2,1,0:T(8,128)(2,1)}, u32[]{:S(2)}, u32[]{:S(2)}) async-start(bf16[8,64,768]{2,1,0:T(8,128)(2,1)} %bitcast.126), calls=%async_computation.3 | async-start | bytes 1572864 | tf_op jit(solution)/shard_map/all_to_all | solution.py:352
  348.3 25.2 %collective-permute-start.45 = (bf16[4,48,2048]{2,1,0:T(8,128)(2,1)S(1)}, bf16[4,48,2048]{2,1,0:T(8,128)(2,1)S(1)}, u32[]{:S(2)}, u32[]{:S(2)}) collective-permute-start(bf16[4,48,2048]{2,1,0:T(8,128)(2,1)S(1)} %dynamic-slice_bitcast_fusion), channel_id=1, source_target_pairs={{0,4},{4,0},{1,5},{5,1},{2,6},{6,2},{3,7},{7,3},{8,12},{12,8},{9,1... | collective-permute-start | bytes 2359304 | tf_op jit(solution)/shard_map/ppermute | solution.py:319
  352.6 68.8 %collective-permute-start.64 = (bf16[96,1536]{1,0:T(8,128)(2,1)S(1)}, bf16[96,1536]{1,0:T(8,128)(2,1)}, u32[]{:S(2)}, u32[]{:S(2)}) collective-permute-start(bf16[96,1536]{1,0:T(8,128)(2,1)S(1)} %fusion.15), channel_id=1, source_target_pairs={{0,1},{1,0},{2,3},{3,2},{4,5},{5,4},{6,7},{7,6},{8,9},{9,8},{10,11... | collective-permute-start | bytes 884744 | tf_op jit(solution)/shard_map/ppermute | solution.py:319
  358.7 62.7 %collective-permute-start.65 = (bf16[96,1536]{1,0:T(8,128)(2,1)}, bf16[96,1536]{1,0:T(8,128)(2,1)}, u32[]{:S(2)}, u32[]{:S(2)}) collective-permute-start(bf16[96,1536]{1,0:T(8,128)(2,1)} %collective-permute-done.59), channel_id=1, source_target_pairs={{0,1},{1,0},{2,3},{3,2},{4,5},{5,4},{6,7},{7,6},{8,9},{9,8},{10,11... | collective-permute-start | bytes 884744 | tf_op jit(solution)/shard_map/ppermute | solution.py:319
  406.6 25.2 %collective-permute-start.62 = (bf16[96,1152]{1,0:T(8,128)(2,1)}, bf16[96,1152]{1,0:T(8,128)(2,1)}, u32[]{:S(2)}, u32[]{:S(2)}) collective-permute-start(bf16[96,1152]{1,0:T(8,128)(2,1)} %get-tuple-element.221), channel_id=1, source_target_pairs={{0,1},{1,0},{2,3},{3,2},{4,5},{5,4},{6,7},{7,6},{8,9},{9,8},{10,11... | collective-permute-start | bytes 663560 | tf_op jit(solution)/shard_map/ppermute | solution.py:319
  (96 other events, 969.6 us)

commit v6 on v5

--- a/solution.py
+++ b/solution.py
@@ -370,46 +370,33 @@
 
 def spread(over_z):
     over_x = swap(over_z, "x")
-    quarter = [((0, 0, 0), over_z), ((1, 0, 0), over_x)]
-    return quarter + [((j, 1, 0), swap(value, "y")) for (j, _, _), value in quarter]
-
-
-def both_cores(half):
-    return half + [((j, m, 1), swap(value, "c")) for (j, m, _), value in half]
+    quarter = [((0, 0, 0), over_z, 0), ((1, 0, 0), over_x, 0)]
+    return quarter + [((j, 1, 0), swap(value, "y"), 0) for (j, _, _), value, _ in quarter]
+
+
+def across(over_x, over_y):
+    half = over_x.shape[0] // 2
+    return swap(over_x[:half], "y"), swap(over_y[half:], "x")
+
+
+def across_pieces(by_y, by_x):
+    return [((1, 1, 0), by_y, 0), ((1, 1, 0), by_x, by_y.shape[0])]
+
+
+def plan_of(pieces):
+    return [(step, first) for step, _, first in pieces]
 
 
 def placing(plan, outs_at, place_ref, stacks, outs, sem, steps=True):
     copies = []
-    for stack, (j, m, k) in zip(stacks, plan):
+    for stack, ((j, m, k), first) in zip(stacks, plan):
         x, y, c = (lax.bitwise_xor(place_ref[n], step) for n, step in ((1, j), (3, m), (2, k)))
-        for i in range(4):
-            shard = (lax.bitwise_xor(place_ref[0], i) if steps else i) * 2 + x
+        for i in range(stack.shape[0]):
+            z = first + i
+            shard = (lax.bitwise_xor(place_ref[0], z) if steps else z) * 2 + x
             for source, target in outs_at(stack.at[i], outs, shard, y, c):
                 copies.append(pltpu.make_async_copy(source, target, sem.at[len(copies)]))
     return copies
-
-
-def place_kernel(plan, outs_at, place_ref, *refs):
-    stacks = refs[: len(plan)]
-    copies = placing(plan, outs_at, place_ref, stacks, refs[len(plan) : -1], refs[-1])
-    for copy in copies:
-        copy.start()
-    for copy in copies:
-        copy.wait()
-
-
-def placed_pieces(pieces, outs_at, outs, place, count):
-    anywhere = pl.BlockSpec(memory_space=pl.ANY)
-    return pl.pallas_call(
-        partial(place_kernel, [step for step, _ in pieces], outs_at),
-        in_specs=[pl.BlockSpec(memory_space=pltpu.SMEM)] + [anywhere] * len(pieces),
-        out_specs=[pl.BlockSpec(memory_space=pltpu.VMEM)] * len(outs),
-        out_shape=[jax.ShapeDtypeStruct(shape, jnp.bfloat16) for shape in outs],
-        scratch_shapes=[pltpu.SemaphoreType.DMA((count,))],
-        compiler_params=pltpu.CompilerParams(
-            vmem_limit_bytes=sum(2 * math.prod(s) for s in outs) + 2 * 2**20
-        ),
-    )(place, *[value for _, value in pieces])
 
 
 def row_attn_at(ref, outs, shard, y, c):
@@ -666,7 +653,7 @@
         ((2, rows, part, half), bf16),
     ]
     return pl.pallas_call(
-        partial(row_fwd_kernel, [step for step, _ in tokens], [step for step, _ in weights]),
+        partial(row_fwd_kernel, [step for step, _ in tokens], plan_of(weights)),
         in_specs=[small] * 3 + [anywhere] * (len(tokens) + len(weights)),
         out_specs=[inside] * len(shapes),
         out_shape=[jax.ShapeDtypeStruct(shape, kind) for shape, kind in shapes],
@@ -677,7 +664,8 @@
             pltpu.SemaphoreType.DMA((16,)),
         ],
         compiler_params=pltpu.CompilerParams(vmem_limit_bytes=56 * 2**20),
-    )(place, info, tie, *[v for _, v in tokens], *[v for _, v in weights])
+        cost_estimate=pl.CostEstimate(flops=7 * 10**9, bytes_accessed=10**7, transcendentals=10**6),
+    )(place, info, tie, *[v for _, v in tokens], *[v for _, v, _ in weights])
 
 
 def row_attention_back(info, tie, near, far, own, got, weights, near_tokens, far_tokens, *ffn_terms):
@@ -877,6 +865,42 @@
     other_ref[...] = jnp.where(flip, mixed[:, half:], mixed[:, :half])
 
 
+def tokens_back_kernel(
+    info_ref, near_ref, near_got_ref, far_got_ref, x_ref, stream_ref, gain_ref, norms_ref,
+    blocks_ref,
+):
+    f32 = jnp.float32
+    grad = near_ref[...] + near_got_ref[...].astype(f32) + far_got_ref[...].astype(f32)
+    gain = gain_ref[0:1]
+    _, unit, scale = normed(x_ref[...].astype(f32), gain, 0.0)
+    found = stream_ref[...].astype(f32) + normed_back(grad, unit, scale, gain)
+    rows, deep, width = blocks_ref.shape
+    part = deep - 16
+    blocks_ref[:, :part] = found.astype(jnp.bfloat16).reshape(rows, part, width)
+    sums = [
+        jnp.sum(grad * unit, axis=0, keepdims=True),
+        jnp.sum(grad, axis=0, keepdims=True),
+        norms_ref[...],
+        jnp.zeros((2, width), f32),
+    ]
+    sums = jnp.concatenate(sums, axis=0)
+    depth = width // 8
+    lane = lax.broadcasted_iota(jnp.int32, (width, TILE), 0)
+    place = lax.broadcasted_iota(jnp.int32, (width, TILE), 1)
+    for shard in range(8):
+        chosen = jnp.logical_and(lane == shard * depth + place, place < depth)
+        found = lax.dot_general(
+            sums,
+            chosen.astype(f32),
+            (PLAIN, ((), ())),
+            precision=lax.Precision.HIGHEST,
+            preferred_element_type=f32,
+        )
+        found = jnp.concatenate([found, jnp.zeros((8, TILE), f32)], axis=0)
+        blocks_ref[shard, part:, :TILE] = found.astype(jnp.bfloat16)
+        blocks_ref[shard, part:, TILE:] = jnp.zeros((16, width - TILE), jnp.bfloat16)
+
+
 def attn_terms_kernel(place_ref, acts_ref, got_ref, mine_ref, theirs_ref, sent_ref, kept_ref):
     width = acts_ref.shape[1] // 3
     half = width // 2
@@ -902,7 +926,7 @@
     inside = pl.BlockSpec(memory_space=pltpu.VMEM)
     anywhere = pl.BlockSpec(memory_space=pl.ANY)
     return pl.pallas_call(
-        partial(kernel, [step for step, _ in pieces]),
+        partial(kernel, plan_of(pieces)),
         in_specs=[small] * 2 + [anywhere] * len(pieces) + [inside] * len(args),
         out_specs=[inside] * len(outs),
         out_shape=[jax.ShapeDtypeStruct(shape, kind) for shape, kind in outs],
@@ -911,35 +935,38 @@
             pltpu.VMEM((width, width), bf16),
             pltpu.VMEM((width, 3 * width), bf16),
             pltpu.VMEM((width, width), bf16),
-            pltpu.SemaphoreType.DMA((20 * len(pieces),)),
+            pltpu.SemaphoreType.DMA((160,)),
         ],
         compiler_params=pltpu.CompilerParams(vmem_limit_bytes=56 * 2**20),
-    )(info, place, *[value for _, value in pieces], *args)
+    )(info, place, *[value for _, value, _ in pieces], *args)
 
 
 def adam_kernel(place_ref, factor_ref, own_ref, other_ref, w_ref, first_ref, second_ref, *outs):
-    half = w_ref.shape[2] // 2
-    at = pl.ds(pl.multiple_of(pl.program_id(0) * half, TILE), half)
-    own, other = own_ref[:, at], other_ref[:, at]
+    count, _, width = w_ref.shape
+    half = width // 2
     low = place_ref[2] == 0
-    grad = jnp.concatenate([jnp.where(low, own, other), jnp.where(low, other, own)], axis=1)
-    grad = grad.astype(jnp.float32) * factor_ref[0]
-    first, second, weight = adam_update(w_ref[0], first_ref[0], second_ref[0], grad, matrix_rate)
-    for ref, value in zip(outs, (first, second, weight, weight.astype(jnp.bfloat16))):
-        ref[0] = value
+    for n in range(count):
+        at = pl.ds(pl.multiple_of((pl.program_id(0) * count + n) * half, TILE), half)
+        own, other = own_ref[:, at], other_ref[:, at]
+        grad = jnp.concatenate([jnp.where(low, own, other), jnp.where(low, other, own)], axis=1)
+        grad = grad.astype(jnp.float32) * factor_ref[0]
+        first, second, weight = adam_update(w_ref[n], first_ref[n], second_ref[n], grad, matrix_rate)
+        for ref, value in zip(outs, (first, second, weight, weight.astype(jnp.bfloat16))):
+            ref[n] = value
 
 
 def attn_adam(place, factor, own, other, weight, first, second):
     small = pl.BlockSpec(memory_space=pltpu.SMEM)
     inside = pl.BlockSpec(memory_space=pltpu.VMEM)
-    block = pl.BlockSpec((1, *weight.shape[1:]), lambda m: (m, 0, 0))
+    block = pl.BlockSpec((4, *weight.shape[1:]), lambda m: (m, 0, 0))
     kinds = [jnp.float32] * 3 + [jnp.bfloat16]
     return pl.pallas_call(
         adam_kernel,
-        grid=(weight.shape[0],),
+        grid=(weight.shape[0] // 4,),
         in_specs=[small, small, inside, inside] + [block] * 3,
         out_specs=[block] * 4,
         out_shape=[jax.ShapeDtypeStruct(weight.shape, kind) for kind in kinds],
+        compiler_params=pltpu.CompilerParams(vmem_limit_bytes=40 * 2**20),
     )(place, factor.reshape(1), own, other, weight, first, second)
 
 
@@ -1041,7 +1068,7 @@
     shapes = [((count, width), kind) for kind in (f32, bf16, f32, bf16)]
     shapes = shapes + [((width, half - chunk), bf16)] * 2 + [((4, 2, width // 8, chunk), bf16)] * 2
     return pl.pallas_call(
-        partial(ffn_kernel, [step for step, _ in pieces]),
+        partial(ffn_kernel, plan_of(pieces)),
         grid=(steps,),
         in_specs=[pl.BlockSpec(memory_space=pltpu.SMEM)] + [inside] * 4 + [anywhere] * len(pieces),
         out_specs=[inside] * 4 + [lanes] * 2 + [inside] * 2,
@@ -1055,7 +1082,7 @@
             pltpu.SemaphoreType.DMA((16,)),
         ],
         compiler_params=pltpu.CompilerParams(vmem_limit_bytes=56 * 2**20),
-    )(place, normed_own, normed_got, up_own, up_got, *[value for _, value in pieces])
+    )(place, normed_own, normed_got, up_own, up_got, *[value for _, value, _ in pieces])
 
 
 def added(a, b):
@@ -1135,28 +1162,29 @@
     row_x, row_y, *parts, col_quarter = together(
         row_pieces[1][1], row_pieces[2][1], *parts, col_quarter
     )
-    row_pieces = [
-        row_pieces[0],
-        ((1, 0, 0), row_x),
-        ((0, 1, 0), row_y),
-        row_pieces[3],
-    ]
     tokens_z = jnp.stack(parts)
+    up = merge_cores(cotangent, c).reshape(4, 2, part, width)
+    up = joined(pick(up, x, 1)[:, None], swap(pick(up, 1 - x, 1), "x")[:, None], x, 1)
     col_z = gather_z(col_quarter)
-    tokens_x, row_last, ffn_quarter, *col_z = together(
-        swap(tokens_z, "x"), row_pieces[3][1], ffn_quarter, *col_z
-    )
-    row_pieces[3] = (row_pieces[3][0], row_last)
-    col_pieces = spread(jnp.stack(col_z))
+    tokens_x, row_last, ffn_quarter, up, *col_z = together(
+        swap(tokens_z, "x"), swap(row_x, "y"), ffn_quarter, up, *col_z
+    )
+    steps = [(0, 0, 0), (1, 0, 0), (0, 1, 0), (1, 1, 0)]
+    row_stacks = [row_pieces[0][1], row_x, row_y, row_last]
+    row_pieces = [(step, value, 0) for step, value in zip(steps, row_stacks)]
+    col_z = jnp.stack(col_z)
     ffn_z = lax.all_to_all(
         jnp.broadcast_to(ffn_quarter, (4, *ffn_quarter.shape)), "z", 0, 0, tiled=True
     )
-    tokens_far = swap(tokens_x, "c")
-    tokens_far, col_x, col_y, ffn_z, up = together(
-        tokens_far, col_pieces[1][1], col_pieces[2][1], ffn_z, merge_cores(cotangent, c)
-    )
-    up = lax.all_to_all(up, ("z", "x"), 0, 0, tiled=True)
-    col_pieces[1] = (col_pieces[1][0], col_x)
+    col_x = swap(col_z, "x")
+    col_last = swap(col_x, "y")
+    col_x, col_y, ffn_z = together(col_x, swap(col_z, "y"), ffn_z)
+    tokens_far, col_last = together(swap(tokens_x, "c"), col_last)
+    ffn_x, ffn_y = swap(ffn_z, "x"), swap(ffn_z, "y")
+    ups = [pick(up, z, 0)] + [
+        lax.ppermute(pick(up, lax.bitwise_xor(z, i), 0), "z", [(k, k ^ i) for k in range(4)])
+        for i in (1, 2, 3)
+    ]
 
     rows = 8
     count = rows * part
@@ -1169,23 +1197,19 @@
         rows,
         half,
     )
-    resid_one = stream_zero.astype(f32)
     mixed_heads = mixed_heads.reshape(2, count, half)
-    ffn_pieces = spread(ffn_z)
-    col_quarters = [col_pieces[0][1], col_x, col_y]
-    mixed_heads, up, last, ffn_x, ffn_y, *col_others = together(
-        mixed_heads, up, swap(col_x, "y"), ffn_pieces[1][1], ffn_pieces[2][1],
-        *[swap(value, "c") for value in col_quarters],
-    )
-    ffn_pieces[1:] = [
-        (ffn_pieces[1][0], ffn_x),
-        (ffn_pieces[2][0], ffn_y),
-        (ffn_pieces[3][0], swap(ffn_x, "y")),
-    ]
-    steps = [(j, m) for m in (0, 1) for j in (0, 1)]
-    col_pieces = [((*step, 0), v) for step, v in zip(steps, [*col_quarters, last])]
-    col_others = [*col_others, swap(last, "c")]
-    col_pieces = col_pieces + [((*step, 1), v) for step, v in zip(steps, col_others)]
+    col_stacks = [col_z, col_x, col_y]
+    mixed_heads, ffn_x, ffn_y, *rest = together(
+        mixed_heads, ffn_x, ffn_y, *ups, *[swap(value, "c") for value in col_stacks]
+    )
+    ups, col_others = rest[:4], rest[4:]
+    ups = [jnp.where(z % 2 == 0, a, b) for a, b in zip(ups, (ups[1], ups[0], ups[3], ups[2]))]
+    ups = [jnp.where(z < 2, a, b) for a, b in zip(ups, ups[2:] + ups[:2])]
+    up = jnp.concatenate(ups)
+    col_stacks, col_others = [*col_stacks, col_last], [*col_others, swap(col_last, "c")]
+    col_pieces = [(step, v, 0) for step, v in zip(steps, col_stacks)]
+    col_pieces = col_pieces + [((j, m, 1), v, 0) for (j, m, _), v in zip(steps, col_others)]
+    ffn_pieces = [(step, v, 0) for step, v in zip(steps, [ffn_z, ffn_x, ffn_y])]
 
     whole_shape, wide_shape = ((count, width), bf16), ((rows, part, 3 * width), bf16)
     acts, stream_one, qkv_two, resid_three, normed_three = column_call(
@@ -1197,6 +1221,8 @@
         [((count, 3 * width), bf16), whole_shape, wide_shape, ((count, width), f32), whole_shape],
         [pltpu.VMEM((rows, part, width), bf16)],
     )
+    normed_three, *ffn_across = together(normed_three, *across(ffn_x, ffn_y))
+    ffn_pieces = ffn_pieces + across_pieces(*ffn_across)
 
     column = x * (2 * part) + c * part + jnp.arange(part, dtype=jnp.int32)
     live = jnp.logical_and(
@@ -1251,47 +1277,48 @@
     attn_got = swap(attn_sent, "y")
     attn_kept, ffn_y_got, ffn_x_got = together(attn_kept, ffn_y_got, ffn_x_got)
     ffn_column = jnp.concatenate([added(ffn_x, ffn_x_got), added(ffn_y, ffn_y_got)], axis=2)
-    ffn_own = z_summed(ffn_column, z)
-    row_column, ffn_own = together(added(row_kept, row_got), ffn_own)
-    row_own = z_summed(row_column, z)
-    far_got, attn_got, block_out = together(far_got, attn_got, block_out)
+    ffn_own = lax.all_to_all(ffn_column, "z", 0, 0, tiled=True)
+    ffn_own = jnp.sum(ffn_own.astype(f32), axis=0).astype(bf16)
+    ffn_own, row_got, block_out = together(ffn_own, row_got, block_out)
+    row_own = z_summed(added(row_kept, row_got), z)
+    attn_pair_terms = added(attn_kept, attn_got).reshape(4, 2, depth // 2, 5 * half)
+    attn_column = pick(attn_pair_terms, x, 1)
+    attn_x_got = swap(pick(attn_pair_terms, 1 - x, 1), "x")
+    blocks = whole_call(
+        tokens_back_kernel,
+        info,
+        [near_part, near_got, far_got, stream_zero, grad_stream, norm_gain, col_norms],
+        [((rows, part + 16, width), bf16)],
+    )[0]
+    blocks, row_own = together(blocks, row_own)
+    blocks = to_blocks(blocks)
+    grad_tokens = to_rows(blocks[:, :part], c).astype(f32)
+    norm_grad = jnp.sum(blocks[:, part : part + 8, :TILE].astype(f32), axis=0)
     block_out = to_rows(block_out, c)
-    attn_pair_terms = added(attn_kept, attn_got).reshape(4, 2, depth // 2, 5 * half)
-    grad_normed_one = near_part + near_got.astype(f32) + far_got.astype(f32)
-    _, norm_back_one = jax.vjp(layer_norm, resid_one, norm_gain[0], norm_gain[1])
-    part_one, gain_grad_one, shift_grad_one = norm_back_one(grad_normed_one)
-    grad_input = (grad_stream.astype(f32) + part_one).astype(bf16)
-    grad_tokens = to_blocks(grad_input.reshape(rows, part, width))
-
-    norm_stack = jnp.concatenate([jnp.stack([gain_grad_one, shift_grad_one]), col_norms])
-    norm_terms = jnp.moveaxis(norm_stack.reshape(6, 4, 2, depth), 0, 2).reshape(4, 2, depth // 2, 12)
-    norm_terms = jnp.pad(norm_terms.astype(bf16), ((0, 0), (0, 0), (0, 0), (0, TILE - 12)))
-    attn_blocks = jnp.concatenate([attn_pair_terms, norm_terms], axis=3)
-    attn_column = added(pick(attn_blocks, x, 1), swap(pick(attn_blocks, 1 - x, 1), "x"))
-    attn_column, row_own, grad_tokens = together(attn_column, row_own, grad_tokens)
+    attn_column = added(attn_column, attn_x_got)
+    norm_parts = [norm_grad] + [
+        lax.ppermute(norm_grad, ("y", "c"), [(k, k ^ i) for k in range(4)]) for i in (1, 2, 3)
+    ]
+    norm_grad = (norm_parts[0] + norm_parts[1]) + (norm_parts[2] + norm_parts[3])
+    norm_grad = norm_grad[:6, :depth]
     attn_own = z_summed(attn_column, z)
-    grad_tokens = to_rows(grad_tokens, c).astype(f32)
     row_grad = added(row_own, swap(row_own, "y"))
-    attn_y = swap(attn_own, "y")
-    attn_grad_b = joined(attn_own[:, : 5 * half], attn_y[:, : 5 * half], y, 0)
-    norm_grad = added(attn_own[:, 5 * half :], attn_y[:, 5 * half :])
+    attn_grad_b = joined(attn_own, swap(attn_own, "y"), y, 0)
     ffn_grads = [ffn_own, swap(ffn_own, "y")]
 
     row_other = swap(row_grad, "c")
     attn_other = swap(attn_grad_b, "c")
-    norm_grad = norm_grad.astype(f32) + swap(norm_grad, "c").astype(f32)
-    norm_grad = norm_grad[:, :12].reshape(6, depth)
     ffn_whole = [joined(piece, swap(piece, "c"), c, 1) for piece in ffn_grads]
 
     in_grad = jnp.where(y == 0, *ffn_whole).astype(f32)
     out_grad = jnp.where(y == 0, *ffn_whole[::-1]).astype(f32).T
 
-    squares = sum(
-        jnp.sum(jnp.square(g.astype(f32))) for g in (row_grad, attn_grad_b, *ffn_grads)
-    )
-    squares = squares + swap(squares, "c") + jnp.sum(norm_grad * norm_grad)
-    squares = jnp.broadcast_to(squares, (8, 8, TILE))
-    squares = lax.all_to_all(squares, ("z", "x"), 0, 0, tiled=True)
+    attn_own, block_out = together(attn_own, block_out)
+    squares = sum(jnp.sum(jnp.square(g.astype(f32))) for g in (attn_own, ffn_own))
+    squares = squares + 0.5 * jnp.sum(jnp.square(row_grad.astype(f32)))
+    squares = squares + 0.25 * jnp.sum(norm_grad * norm_grad)
+    squares = jnp.broadcast_to(squares, (32, 8, TILE))
+    squares = lax.all_to_all(squares, ("z", "x", "y", "c"), 0, 0, tiled=True)
     grad_norm = jnp.sqrt(jnp.sum(squares[:, 0, 0]))
     factor = clip_bound / jnp.maximum(grad_norm, clip_bound)
     attn_first_new, attn_second_new, attn_weight_new, attn_copy = attn_adam(

time: 452 us -> 419 us (0.927)
  starting transfers between devices: 92.5 us -> 78.5 us
  waiting for transfers between devices: 156 us -> 144 us
  other arithmetic: 48 us -> 41.6 us
    ppermute x48, waiting for transfers between devices: 89.3 us -> 51.7 us  [swap(): return lax.ppermute(value, axis, PAIR)]
    ppermute x0 -> x6, waiting for transfers between devices: none -> 13.2 us  [the longest x3 11.4 us: paired_body(): lax.ppermute(pick(up, lax.bitwise_xor(z, i), 0), 'z', [(k, k ^ i) for k i...]
    ppermute x9 -> x6, waiting for transfers between devices: 24.3 us -> 36.9 us  [z_summed(): got = lax.ppermute(other, 'z', [(k, k ^ i) for k in range(4)])]
    ppermute x9 -> x6, starting transfers between devices: 20.1 us -> 8.24 us  [z_summed(): got = lax.ppermute(other, 'z', [(k, k ^ i) for k in range(4)])]
    ppermute x0 -> x6, starting transfers between devices: none -> 5.89 us  [the longest x3 3.77 us: paired_body(): lax.ppermute(pick(up, lax.bitwise_xor(z, i), 0), 'z', [(k, k ^ i) for k i...]
    pallas_call x1 -> x2, Pallas kernels: 9.48 us -> 15.3 us  [whole_call(): pl.pallas_call(kernel, in_specs=[pl.BlockSpec(memory_space=pltpu.SMEM)] +...]
    all_to_all x1, waiting for transfers between devices: 6.56 us -> 12 us  [paired_body(): lax.all_to_all(jnp.broadcast_to(ffn_quarter, (4, *ffn_quarter.shape)), 'z...]
    pallas_call x5, Pallas kernels: 85.1 us -> 80.4 us  [the longest x2 37.2 us: column_call(): pl.pallas_call(partial(kernel, plan_of(pieces)), in_specs=[small] * 2 + [...]
  transfers between devices with their start and end apart: 71 -> 74, of which waited for: 26 -> 32; matrix products, arithmetic and copies ran while one was open for 13% -> 13% of each run, Pallas kernels for 18% -> 22%
where the time goes in v6:
time: 419 us; the launch traced here: 411 us
  waiting for transfers between devices  144 us (34%)
  Pallas kernels  116 us (28%)
  starting transfers between devices  78.5 us (19%)
  other arithmetic  41.6 us (10%)
  local copies, waits for them, and re-layouts  24 us (6%)
  between operations  7.02 us (2%)
    ppermute x48, waiting for transfers between devices, swap(): return lax.ppermute(value, axis, PAIR)  51.7 us
    pallas_call x2, Pallas kernels, column_call(): pl.pallas_call(partial(kernel, plan_of(pieces)), in_specs=[small] * 2 + [...  37.2 us
    ppermute x6, waiting for transfers between devices, z_summed(): got = lax.ppermute(other, 'z', [(k, k ^ i) for k in range(4)])  36.9 us
    ppermute x48, starting transfers between devices, swap(): return lax.ppermute(value, axis, PAIR)  28.7 us
    pallas_call x1, Pallas kernels, feed_forward(): pl.pallas_call(partial(ffn_kernel, plan_of(pieces)), grid=(steps,), in_sp...  25.2 us
    pallas_call x1, Pallas kernels, row_attention_back(): pl.pallas_call(row_bwd_kernel, in_specs=[small, small] + [inside] * 11, o...  20.3 us
    pallas_call x2, Pallas kernels, whole_call(): pl.pallas_call(kernel, in_specs=[pl.BlockSpec(memory_space=pltpu.SMEM)] +...  15.3 us
    ppermute x6, waiting for transfers between devices, gather_z(): lax.ppermute(own, 'z', [(k, k ^ i) for k in range(4)])  13.8 us
  transfers between devices with their start and end apart: 74, of which 32 were waited for; matrix products, arithmetic and copies ran while one was open for 13% of the time, Pallas kernels for 22%

profile of v6, /device:TPU:0, one launch (start us, length us, event | category | flops | bytes accessed | tf_op | source)
XLA Modules:
  0.0 411.0 jit_solution(478820071185252541)
XLA Ops:
  4.3 5.0 %collective-permute-start.3 = (bf16[48,1152]{1,0:T(8,128)(2,1)}, bf16[48,1152]{1,0:T(8,128)(2,1)}, u32[]{:S(2)}, u32[]{:S(2)}) collective-permute-start(bf16[48,1152]{1,0:T(8,128)(2,1)} %fusion.27), channel_id=1, source_target_pairs={{0,24},{8,16},{16,8},{24,0},{1,25},{9,17},{17,9},{25,1},{2,26},{10... | collective-permute-start | bytes 331784 | tf_op jit(solution)/shard_map/ppermute | solution.py:368
  14.5 4.4 %collective-permute-done.2 = bf16[48,1152]{1,0:T(8,128)(2,1)} collective-permute-done((bf16[48,1152]{1,0:T(8,128)(2,1)}, bf16[48,1152]{1,0:T(8,128)(2,1)}, u32[]{:S(2)}, u32[]{:S(2)}) %collective-permute-start.2) | collective-permute-done | bytes 110624 | tf_op jit(solution)/shard_map/ppermute | solution.py:368
  34.7 4.7 %collective-permute-done.7 = bf16[144,768]{1,0:T(8,128)(2,1)S(1)} collective-permute-done((bf16[144,768]{1,0:T(8,128)(2,1)S(1)}, bf16[144,768]{1,0:T(8,128)(2,1)S(1)}, u32[]{:S(2)}, u32[]{:S(2)}) %collective-permute-start.7) | collective-permute-done | bytes 221216 | tf_op jit(solution)/shard_map/ppermute | solution.py:1159
  39.5 4.8 %collective-permute-done.8 = bf16[144,768]{1,0:T(8,128)(2,1)S(1)} collective-permute-done((bf16[144,768]{1,0:T(8,128)(2,1)S(1)}, bf16[144,768]{1,0:T(8,128)(2,1)S(1)}, u32[]{:S(2)}, u32[]{:S(2)}) %collective-permute-start.8) | collective-permute-done | bytes 221216 | tf_op jit(solution)/shard_map/ppermute | solution.py:1159
  56.2 6.3 %collective-permute-done.15 = bf16[5,48,384]{2,1,0:T(8,128)(2,1)} collective-permute-done((bf16[5,48,384]{2,1,0:T(8,128)(2,1)S(1)}, bf16[5,48,384]{2,1,0:T(8,128)(2,1)}, u32[]{:S(2)}, u32[]{:S(2)}) %collective-permute-start.15) | collective-permute-done | bytes 184352 | tf_op jit(solution)/shard_map/ppermute | solution.py:368
  77.4 9.1 %collective-permute-done.17.refs_1_ = bf16[4,5,48,384]{3,2,1,0:T(8,128)(2,1)S(1)} collective-permute-done((bf16[4,5,48,384]{3,2,1,0:T(8,128)(2,1)S(1)}, bf16[4,5,48,384]{3,2,1,0:T(8,128)(2,1)S(1)}, u32[]{:S(2)}, u32[]{:S(2)}) %collective-permute-start.17) | collective-permute-done | bytes 737312 | tf_op jit(solution)/shard_map/ppermute | solution.py:319
  91.4 12.0 %all-to-all-done.refs_0_ = bf16[4,96,1536]{2,1,0:T(8,128)(2,1)} async-done(((bf16[4,96,1536]{2,1,0:T(8,128)(2,1)}), bf16[4,96,1536]{2,1,0:T(8,128)(2,1)}, u32[]{:S(2)}, u32[]{:S(2)}) %all-to-all-start) | async-done | bytes 1179680 | tf_op jit(solution)/shard_map/all_to_all | solution.py:1176
  105.3 7.4 %collective-permute-done.25 = bf16[2,64,768]{2,1,0:T(8,128)(2,1)} collective-permute-done((bf16[2,64,768]{2,1,0:T(8,128)(2,1)}, bf16[2,64,768]{2,1,0:T(8,128)(2,1)}, u32[]{:S(2)}, u32[]{:S(2)}) %collective-permute-start.25) | collective-permute-done | bytes 196640 | tf_op jit(solution)/shard_map/ppermute | solution.py:1185
  120.2 13.3 %shard_map.295 = (bf16[512,768]{1,0:T(8,128)(2,1)}, bf16[1024,768]{1,0:T(8,128)(2,1)}, bf16[1024,768]{1,0:T(8,128)(2,1)}, bf16[768,1152]{1,0:T(8,128)(2,1)}, f32...) custom-call(s32[4]{0:T(128)} %pad_add_fusion.1.place_ref, ...), custom_call_target="tpu_custom_call" | custom-call | flops 7000000000 | bytes 10000000 | tf_op jit(solution)/shard_map/pallas_call | solution.py:655
  142.1 14.3 %shard_map.296 = (bf16[512,2304]{1,0:T(8,128)(2,1)}, bf16[512,768]{1,0:T(8,128)(2,1)}, bf16[8,64,2304]{2,1,0:T(8,128)(2,1)}, f32[512,768]{1,0:T(8,128)}, bf16[512,768]{1,0:T(8,128)(2,1)}) custom-call(s32[6]{0:T(128)} %concatenate.55.info_ref, s32[4]{0:T(128)} %pad_add_fusion.1.place_ref, bf16[4,5,48,384]{3,2,1,0:T(8,128)(2,1)} %copy-done.5, ...), custom_call_target="tpu_custom_call" | custom-call | tf_op jit(solution)/shard_map/pallas_call | solution.py:928
  160.0 25.2 %shard_map.297 = (f32[512,768]{1,0:T(8,128)}, bf16[512,768]{1,0:T(8,128)(2,1)}, f32[512,768]{1,0:T(8,128)}, bf16[512,768]{1,0:T(8,128)(2,1)}, bf16[768,768]{1,0:...) custom-call(s32[4]{0:T(128)} %pad_add_fusion.1.place_ref, ...), custom_call_target="tpu_custom_call" | custom-call | tf_op jit(solution)/shard_map/pallas_call | solution.py:1070
  192.7 22.9 %shard_map.298 = (bf16[512,768]{1,0:T(8,128)(2,1)}, bf16[512,768]{1,0:T(8,128)(2,1)}, bf16[512,384]{1,0:T(8,128)(2,1)}, bf16[512,384]{1,0:T(8,128)(2,1)}, bf16[5...) custom-call(s32[6]{0:T(128)} %concatenate.55.info_ref, s32[4]{0:T(128)} %pad_add_fusion.1.place_ref, ...), custom_call_target="tpu_custom_call" | custom-call | tf_op jit(solution)/shard_map/pallas_call | solution.py:928
  222.4 20.3 %shard_map.299 = (f32[512,768]{1,0:T(8,128)}, bf16[512,768]{1,0:T(8,128)(2,1)}, f32[512,768]{1,0:T(8,128)}, bf16[512,768]{1,0:T(8,128)(2,1)}, bf16[4,96,1152]{2,...) custom-call(s32[6]{0:T(128)} %concatenate.55.info_ref, ...), custom_call_target="tpu_custom_call" | custom-call | tf_op jit(solution)/shard_map/pallas_call | solution.py:681
  248.3 9.7 %shard_map.300 = (bf16[8,48,1920]{2,1,0:T(8,128)(2,1)}, bf16[8,48,1920]{2,1,0:T(8,128)(2,1)}) custom-call(s32[4]{0:T(128)} %pad_add_fusion.1.place_ref, bf16[512,2304]{1,0:T(8,128)(2,1)} %get-tuple-element.142.acts_ref, bf16[512,2304]{1,0:T(8,128)(2,1)} %collective-permute-done.32.got_ref, bf16[512,1920]{1,0:T(8,128)(2,1)} %get-tuple-element.160.mine_ref, ...), custom_call_target="tpu_custom_call" | custom-call | tf_op jit(solution)/shard_map/pallas_call | solution.py:975
  262.2 4.9 %all-to-all-start.2 = ((bf16[4,96,1536]{2,1,0:T(8,128)(2,1)}), bf16[4,96,1536]{2,1,0:T(8,128)(2,1)}, u32[]{:S(2)}, u32[]{:S(2)}) async-start(bf16[4,96,1536]{2,1,0:T(8,128)(2,1)} %pad_maximum_fusion), calls=%async_computation.2 | async-start | bytes 2359296 | tf_op jit(solution)/shard_map/all_to_all | solution.py:1280
  270.2 23.3 %collective-permute-done.45 = bf16[8,48,1920]{2,1,0:T(8,128)(2,1)} collective-permute-done((bf16[8,48,1920]{2,1,0:T(8,128)(2,1)}, bf16[8,48,1920]{2,1,0:T(8,128)(2,1)}, u32[]{:S(2)}, u32[]{:S(2)}) %collective-permute-start.45) | collective-permute-done | bytes 1474592 | tf_op jit(solution)/shard_map/ppermute | solution.py:319
  306.8 5.6 %shard_map.301 = bf16[8,80,768]{2,1,0:T(8,128)(2,1)} custom-call(s32[6]{0:T(128)} %concatenate.55.info_ref, f32[512,768]{1,0:T(8,128)} %get-tuple-element.196.near_ref, bf16[512,768]{1,0:T(8,128)(2,1)} %collective-permute-done.52.near_got_ref, bf16[512,768]{1,0:T(8,128)(2,1)} %collective-permute-done.54.far_got_ref, ...), custom_call_target="tpu_custom_call" | custom-call | tf_op jit(solution)/shard_map/pallas_call | solution.py:975
  315.2 7.1 %collective-permute-done.56 = bf16[96,1152]{1,0:T(8,128)(2,1)S(1)} collective-permute-done((bf16[96,1152]{1,0:T(8,128)(2,1)S(1)}, bf16[96,1152]{1,0:T(8,128)(2,1)S(1)}, u32[]{:S(2)}, u32[]{:S(2)}) %collective-permute-start.56) | collective-permute-done | bytes 221216 | tf_op jit(solution)/shard_map/ppermute | solution.py:1096
  338.0 10.5 %collective-permute-done.47 = bf16[48,1920]{1,0:T(8,128)(2,1)S(1)} collective-permute-done((bf16[48,1920]{1,0:T(8,128)(2,1)S(1)}, bf16[48,1920]{1,0:T(8,128)(2,1)S(1)}, u32[]{:S(2)}, u32[]{:S(2)}) %collective-permute-start.47) | collective-permute-done | bytes 184352 | tf_op jit(solution)/shard_map/ppermute | solution.py:1096
  348.5 6.9 %collective-permute-done.49 = bf16[48,1920]{1,0:T(8,128)(2,1)S(1)} collective-permute-done((bf16[48,1920]{1,0:T(8,128)(2,1)S(1)}, bf16[48,1920]{1,0:T(8,128)(2,1)S(1)}, u32[]{:S(2)}, u32[]{:S(2)}) %collective-permute-start.49) | collective-permute-done | bytes 184352 | tf_op jit(solution)/shard_map/ppermute | solution.py:1096
  355.5 10.3 %collective-permute-done.48 = bf16[48,1920]{1,0:T(8,128)(2,1)S(1)} collective-permute-done((bf16[48,1920]{1,0:T(8,128)(2,1)S(1)}, bf16[48,1920]{1,0:T(8,128)(2,1)S(1)}, u32[]{:S(2)}, u32[]{:S(2)}) %collective-permute-start.48) | collective-permute-done | bytes 184352 | tf_op jit(solution)/shard_map/ppermute | solution.py:1096
  386.1 4.8 %all-to-all-done.4 = f32[32,8,128]{2,1,0:T(8,128)S(1)} async-done(((f32[32,8,128]{2,1,0:T(8,128)}), f32[32,8,128]{2,1,0:T(8,128)S(1)}, u32[]{:S(2)}, u32[]{:S(2)}) %all-to-all-start.4) | async-done | bytes 131104 | tf_op jit(solution)/shard_map/all_to_all | solution.py:1321
  392.4 5.0 %fusion.23 = (bf16[96,3072]{1,0:T(8,128)(2,1)}, f32[96,3072]{1,0:T(8,128)}, f32[96,3072]{1,0:T(8,128)}, f32[96,3072]{1,0:T(8,128)}) fusion(f32[96,3072]{1,0:T(8,128)S(1)} %copy-done.6, f32[]{:T(128)} %div.52, bf16[96,1536]{1,0:T(8,128)(2,1)} %collective-permute-done.67, bf16[96,1536]{1,0:T(8,128)(2,1)} %collective-permute-done.68, ...), kind=kLoop, calls=%fused_computation.121 | loop fusion | flops 10616832 | bytes 8847366 | tf_op jit(solution)/shard_map/convert_element_type | solution.py:1353
  401.8 4.7 %shard_map.302 = (f32[8,96,768]{2,1,0:T(8,128)}, f32[8,96,768]{2,1,0:T(8,128)}, f32[8,96,768]{2,1,0:T(8,128)}, bf16[8,96,768]{2,1,0:T(8,128)(2,1)}) custom-call(s32[4]{0:T(128)S(1)} %copy-done.3, f32[1]{0:T(128)} %bitcast.71.factor_ref, bf16[96,3072]{1,0:T(8,128)(2,1)S(1)} %pad_maximum_fusion.4.own_ref, bf16[96,3072]{1,0:T(8,128)(2,1)S(1)} %pad_maximum_fusion.5.other_ref, ...), custom_call_target="tpu_custom_call" | custom-call | tf_op jit(solution)/shard_map/pallas_call | solution.py:963
  (305 shorter events, 161.2 us)
Async XLA Ops:
  65.7 37.6 %all-to-all-start = ((bf16[4,96,1536]{2,1,0:T(8,128)(2,1)}), bf16[4,96,1536]{2,1,0:T(8,128)(2,1)}, u32[]{:S(2)}, u32[]{:S(2)}) async-start(bf16[4,96,1536]{2,1,0:T(8,128)(2,1)} %broadcast_in_dim.39), calls=%async_computation | async-start | bytes 2359296 | tf_op jit(solution)/shard_map/all_to_all | solution.py:1176
  72.0 31.4 %collective-permute-start.21 = (bf16[4,144,768]{2,1,0:T(8,128)(2,1)}, bf16[4,144,768]{2,1,0:T(8,128)(2,1)}, u32[]{:S(2)}, u32[]{:S(2)}) collective-permute-start(bf16[4,144,768]{2,1,0:T(8,128)(2,1)} %pad_maximum_fusion.1.refs_0_), channel_id=1, source_target_pairs={{0,1},{1,0},{2,3},{3,2},{4,5},{5,4},{6,7},{7,6},{8,9},{9,8},{10,11... | collective-permute-start | bytes 2654216 | tf_op jit(solution)/shard_map/ppermute | solution.py:319
  72.5 46.3 %collective-permute-start.19 = (bf16[4,144,768]{2,1,0:T(8,128)(2,1)}, bf16[4,144,768]{2,1,0:T(8,128)(2,1)}, u32[]{:S(2)}, u32[]{:S(2)}) collective-permute-start(bf16[4,144,768]{2,1,0:T(8,128)(2,1)} %collective-permute-done.10.refs_1_), channel_id=1, source_target_pairs={{0,1},{1,0},{2,3},{3,2},{4,5},{5,4},{6,7},{7,6},{8,9},{9,8},{10,11... | collective-permute-start | bytes 2654216 | tf_op jit(solution)/shard_map/ppermute | solution.py:319
  73.6 30.3 %collective-permute-start.26 = (bf16[2,64,768]{2,1,0:T(8,128)(2,1)}, bf16[2,64,768]{2,1,0:T(8,128)(2,1)}, u32[]{:S(2)}, u32[]{:S(2)}) collective-permute-start(bf16[2,64,768]{2,1,0:T(8,128)(2,1)} %get-tuple-element.240), channel_id=1, source_target_pairs={{0,24},{8,16},{16,8},{24,0},{1,25},{9,17},{17,9},{25,1},{2,26},{10... | collective-permute-start | bytes 589832 | tf_op jit(solution)/shard_map/ppermute | solution.py:1185
  86.4 32.8 %collective-permute-start.20 = (bf16[4,5,48,384]{3,2,1,0:T(8,128)(2,1)S(1)}, bf16[4,5,48,384]{3,2,1,0:T(8,128)(2,1)S(1)}, u32[]{:S(2)}, u32[]{:S(2)}) collective-permute-start(bf16[4,5,48,384]{3,2,1,0:T(8,128)(2,1)S(1)} %collective-permute-done.17.refs_1_), channel_id=1, source_target_pairs={{0,2},{2,0},{1,3},{3,1},{4,6},{6,4},{5,7},{7,5},{8,10},{10,8},{9,1... | collective-permute-start | bytes 2211848 | tf_op jit(solution)/shard_map/ppermute | solution.py:319
  103.4 30.7 %collective-permute-start.23 = (bf16[4,96,1536]{2,1,0:T(8,128)(2,1)}, bf16[4,96,1536]{2,1,0:T(8,128)(2,1)}, u32[]{:S(2)}, u32[]{:S(2)}) collective-permute-start(bf16[4,96,1536]{2,1,0:T(8,128)(2,1)} %all-to-all-done.refs_0_), channel_id=1, source_target_pairs={{0,2},{2,0},{1,3},{3,1},{4,6},{6,4},{5,7},{7,5},{8,10},{10,8},{9,1... | collective-permute-start | bytes 3538952 | tf_op jit(solution)/shard_map/ppermute | solution.py:319
  103.9 30.1 %collective-permute-start.22 = (bf16[4,96,1536]{2,1,0:T(8,128)(2,1)}, bf16[4,96,1536]{2,1,0:T(8,128)(2,1)}, u32[]{:S(2)}, u32[]{:S(2)}) collective-permute-start(bf16[4,96,1536]{2,1,0:T(8,128)(2,1)} %all-to-all-done.refs_0_), channel_id=1, source_target_pairs={{0,4},{4,0},{1,5},{5,1},{2,6},{6,2},{3,7},{7,3},{8,12},{12,8},{9,1... | collective-permute-start | bytes 3538952 | tf_op jit(solution)/shard_map/ppermute | solution.py:319
  185.2 30.4 %collective-permute-start.40 = (bf16[4,2,96,768]{3,2,1,0:T(8,128)(2,1)}, bf16[4,2,96,768]{3,2,1,0:T(8,128)(2,1)S(1)}, u32[]{:S(2)}, u32[]{:S(2)}) collective-permute-start(bf16[4,2,96,768]{3,2,1,0:T(8,128)(2,1)} %get-tuple-element.170), channel_id=1, source_target_pairs={{0,4},{4,0},{1,5},{5,1},{2,6},{6,2},{3,7},{7,3},{8,12},{12,8},{9,1... | collective-permute-start | bytes 3538952 | tf_op jit(solution)/shard_map/ppermute | solution.py:319
  186.7 28.9 %collective-permute-start.41 = (bf16[768,768]{1,0:T(8,128)(2,1)}, bf16[768,768]{1,0:T(8,128)(2,1)}, u32[]{:S(2)}, u32[]{:S(2)}) collective-permute-start(bf16[768,768]{1,0:T(8,128)(2,1)} %get-tuple-element.171), channel_id=1, source_target_pairs={{0,2},{2,0},{1,3},{3,1},{4,6},{6,4},{5,7},{7,5},{8,10},{10,8},{9,1... | collective-permute-start | bytes 3538952 | tf_op jit(solution)/shard_map/ppermute | solution.py:319
  215.6 27.1 %all-to-all-start.1 = ((bf16[8,64,768]{2,1,0:T(8,128)(2,1)}), bf16[8,64,768]{2,1,0:T(8,128)(2,1)S(1)}, u32[]{:S(2)}, u32[]{:S(2)}) async-start(bf16[8,64,768]{2,1,0:T(8,128)(2,1)} %bitcast.133), calls=%async_computation.1 | async-start | bytes 1572864 | tf_op jit(solution)/shard_map/all_to_all | solution.py:352
  220.0 25.8 %collective-permute-start.32 = (bf16[512,2304]{1,0:T(8,128)(2,1)}, bf16[512,2304]{1,0:T(8,128)(2,1)}, u32[]{:S(2)}, u32[]{:S(2)}) collective-permute-start(bf16[512,2304]{1,0:T(8,128)(2,1)} %get-tuple-element.142.acts_ref), channel_id=1, source_target_pairs={{0,1},{1,0},{2,3},{3,2},{4,5},{5,4},{6,7},{7,6},{8,9},{9,8},{10,11... | collective-permute-start | bytes 7077896 | tf_op jit(solution)/shard_map/ppermute | solution.py:319
  245.7 22.9 %collective-permute-start.53 = (bf16[512,768]{1,0:T(8,128)(2,1)}, bf16[512,768]{1,0:T(8,128)(2,1)S(1)}, u32[]{:S(2)}, u32[]{:S(2)}) collective-permute-start(bf16[512,768]{1,0:T(8,128)(2,1)} %get-tuple-element.199), channel_id=1, source_target_pairs={{0,1},{1,0},{2,3},{3,2},{4,5},{5,4},{6,7},{7,6},{8,9},{9,8},{10,11... | collective-permute-start | bytes 2359304 | tf_op jit(solution)/shard_map/ppermute | solution.py:319
  259.5 34.1 %collective-permute-start.45 = (bf16[8,48,1920]{2,1,0:T(8,128)(2,1)}, bf16[8,48,1920]{2,1,0:T(8,128)(2,1)}, u32[]{:S(2)}, u32[]{:S(2)}) collective-permute-start(bf16[8,48,1920]{2,1,0:T(8,128)(2,1)} %get-tuple-element.187), channel_id=1, source_target_pairs={{0,2},{2,0},{1,3},{3,1},{4,6},{6,4},{5,7},{7,5},{8,10},{10,8},{9,1... | collective-permute-start | bytes 4423688 | tf_op jit(solution)/shard_map/ppermute | solution.py:319
  262.2 35.5 %all-to-all-start.2 = ((bf16[4,96,1536]{2,1,0:T(8,128)(2,1)}), bf16[4,96,1536]{2,1,0:T(8,128)(2,1)}, u32[]{:S(2)}, u32[]{:S(2)}) async-start(bf16[4,96,1536]{2,1,0:T(8,128)(2,1)} %pad_maximum_fusion), calls=%async_computation.2 | async-start | bytes 2359296 | tf_op jit(solution)/shard_map/all_to_all | solution.py:1280
  267.2 37.6 %collective-permute-start.52 = (bf16[512,768]{1,0:T(8,128)(2,1)}, bf16[512,768]{1,0:T(8,128)(2,1)}, u32[]{:S(2)}, u32[]{:S(2)}) collective-permute-start(bf16[512,768]{1,0:T(8,128)(2,1)} %get-tuple-element.197), channel_id=1, source_target_pairs={{0,1},{1,0},{2,3},{3,2},{4,5},{5,4},{6,7},{7,6},{8,9},{9,8},{10,11... | collective-permute-start | bytes 2359304 | tf_op jit(solution)/shard_map/ppermute | solution.py:319
  267.2 32.0 %collective-permute-start.50 = (bf16[4,96,1152]{2,1,0:T(8,128)(2,1)}, bf16[4,96,1152]{2,1,0:T(8,128)(2,1)}, u32[]{:S(2)}, u32[]{:S(2)}) collective-permute-start(bf16[4,96,1152]{2,1,0:T(8,128)(2,1)} %get-tuple-element.192), channel_id=1, source_target_pairs={{0,4},{4,0},{1,5},{5,1},{2,6},{6,2},{3,7},{7,3},{8,12},{12,8},{9,1... | collective-permute-start | bytes 2654216 | tf_op jit(solution)/shard_map/ppermute | solution.py:319
  269.7 37.1 %collective-permute-start.54 = (bf16[512,768]{1,0:T(8,128)(2,1)}, bf16[512,768]{1,0:T(8,128)(2,1)}, u32[]{:S(2)}, u32[]{:S(2)}) collective-permute-start(bf16[512,768]{1,0:T(8,128)(2,1)} %add_convert_fusion.2), channel_id=1, source_target_pairs={{0,4},{4,0},{1,5},{5,1},{2,6},{6,2},{3,7},{7,3},{8,12},{12,8},{9,1... | collective-permute-start | bytes 2359304 | tf_op jit(solution)/shard_map/ppermute | solution.py:319
  296.3 31.2 %collective-permute-start.46 = (bf16[4,48,1920]{2,1,0:T(8,128)(2,1)}, bf16[4,48,1920]{2,1,0:T(8,128)(2,1)}, u32[]{:S(2)}, u32[]{:S(2)}) collective-permute-start(bf16[4,48,1920]{2,1,0:T(8,128)(2,1)} %dynamic-slice_bitcast_fusion), channel_id=1, source_target_pairs={{0,4},{4,0},{1,5},{5,1},{2,6},{6,2},{3,7},{7,3},{8,12},{12,8},{9,1... | collective-permute-start | bytes 2211848 | tf_op jit(solution)/shard_map/ppermute | solution.py:319
  313.2 22.0 %collective-permute-start.51 = (bf16[2,2,64,768]{3,2,1,0:T(8,128)(2,1)}, bf16[2,2,64,768]{3,2,1,0:T(8,128)(2,1)}, u32[]{:S(2)}, u32[]{:S(2)}) collective-permute-start(bf16[2,2,64,768]{3,2,1,0:T(8,128)(2,1)} %get-tuple-element.233), channel_id=1, source_target_pairs={{0,1},{1,0},{2,3},{3,2},{4,5},{5,4},{6,7},{7,6},{8,9},{9,8},{10,11... | collective-permute-start | bytes 1179656 | tf_op jit(solution)/shard_map/ppermute | solution.py:319
  323.2 48.4 %all-to-all-start.3 = ((bf16[8,80,768]{2,1,0:T(8,128)(2,1)}), bf16[8,80,768]{2,1,0:T(8,128)(2,1)}, u32[]{:S(2)}, u32[]{:S(2)}) async-start(bf16[8,80,768]{2,1,0:T(8,128)(2,1)} %shard_map.301), calls=%async_computation.3 | async-start | bytes 1966080 | tf_op jit(solution)/shard_map/all_to_all | solution.py:352
  330.8 24.7 %collective-permute-start.49 = (bf16[48,1920]{1,0:T(8,128)(2,1)S(1)}, bf16[48,1920]{1,0:T(8,128)(2,1)S(1)}, u32[]{:S(2)}, u32[]{:S(2)}) collective-permute-start(bf16[48,1920]{1,0:T(8,128)(2,1)S(1)} %get-tuple-element.255), channel_id=1, source_target_pairs={{0,24},{8,16},{16,8},{24,0},{1,25},{9,17},{17,9},{25,1},{2,26},{10... | collective-permute-start | bytes 552968 | tf_op jit(solution)/shard_map/ppermute | solution.py:1096
  333.1 32.6 %collective-permute-start.48 = (bf16[48,1920]{1,0:T(8,128)(2,1)S(1)}, bf16[48,1920]{1,0:T(8,128)(2,1)S(1)}, u32[]{:S(2)}, u32[]{:S(2)}) collective-permute-start(bf16[48,1920]{1,0:T(8,128)(2,1)S(1)} %get-tuple-element.256), channel_id=1, source_target_pairs={{0,16},{8,24},{16,0},{24,8},{1,17},{9,25},{17,1},{25,9},{2,18},{10... | collective-permute-start | bytes 552968 | tf_op jit(solution)/shard_map/ppermute | solution.py:1096
  333.9 40.6 %collective-permute-start.67 = (bf16[96,1536]{1,0:T(8,128)(2,1)S(1)}, bf16[96,1536]{1,0:T(8,128)(2,1)}, u32[]{:S(2)}, u32[]{:S(2)}) collective-permute-start(bf16[96,1536]{1,0:T(8,128)(2,1)S(1)} %reduce_sum.66), channel_id=1, source_target_pairs={{0,2},{2,0},{1,3},{3,1},{4,6},{6,4},{5,7},{7,5},{8,10},{10,8},{9,1... | collective-permute-start | bytes 884744 | tf_op jit(solution)/shard_map/ppermute | solution.py:319
  335.2 32.0 %collective-permute-start.59 = (bf16[96,1152]{1,0:T(8,128)(2,1)S(1)}, bf16[96,1152]{1,0:T(8,128)(2,1)S(1)}, u32[]{:S(2)}, u32[]{:S(2)}) collective-permute-start(bf16[96,1152]{1,0:T(8,128)(2,1)S(1)} %copy-done.20), channel_id=1, source_target_pairs={{0,2},{2,0},{1,3},{3,1},{4,6},{6,4},{5,7},{7,5},{8,10},{10,8},{9,1... | collective-permute-start | bytes 663560 | tf_op jit(solution)/shard_map/ppermute | solution.py:319
  (94 other events, 993.6 us)

commit v7 on v6

--- a/solution.py
+++ b/solution.py
@@ -542,11 +542,37 @@
                 )
 
 
+def next_sums_kernel(
+    place_ref, y_kept_ref, y_got_ref, x_kept_ref, x_got_ref, to_x_ref, with_x_ref, to_y_ref, with_y_ref
+):
+    _, depth, lanes = to_x_ref.shape
+    first, first_y = place_ref[1] == 0, place_ref[3] == 0
+    summed = added(y_kept_ref[...], y_got_ref[...]).reshape(2, depth, lanes)
+    with_x_ref[0] = jnp.where(first, summed[0], summed[1])
+    to_x_ref[0] = jnp.where(first, summed[1], summed[0])
+    summed = added(x_kept_ref[0], x_got_ref[0])
+    with_y_ref[0] = jnp.where(first_y, summed[0], summed[1])
+    to_y_ref[0] = jnp.where(first_y, summed[1], summed[0])
+
+
+def next_sums(place, y_kept, y_got, x_kept, x_got):
+    zs, _, depth, lanes = x_kept.shape
+    by_rows = pl.BlockSpec((2 * depth, lanes), lambda n: (n, 0))
+    by_z = pl.BlockSpec((1, 2, depth, lanes), lambda n: (n, 0, 0, 0))
+    return pl.pallas_call(
+        next_sums_kernel,
+        grid=(zs,),
+        in_specs=[pl.BlockSpec(memory_space=pltpu.SMEM), by_rows, by_rows, by_z, by_z],
+        out_specs=[pl.BlockSpec((1, depth, lanes), lambda n: (n, 0, 0))] * 4,
+        out_shape=[jax.ShapeDtypeStruct((zs, depth, lanes), jnp.bfloat16)] * 4,
+        compiler_params=pltpu.CompilerParams(vmem_limit_bytes=56 * 2**20),
+    )(place, y_kept, y_got, x_kept, x_got)
+
+
 def row_bwd_kernel(
     info_ref, tie_ref, near_ref, far_ref, own_ref, got_ref, w_ref, near_tokens_ref, far_tokens_ref,
-    y_kept_ref, y_got_ref, x_kept_ref, x_got_ref,
     near_part_ref, near_theirs_ref, far_part_ref, far_theirs_ref, sent_ref, kept_ref,
-    to_x_ref, with_x_ref, to_y_ref, with_y_ref, do_ref, d_near_ref, d_far_ref,
+    do_ref, d_near_ref, d_far_ref,
 ):
     bf16 = jnp.bfloat16
     blocks, rows, part, lanes = near_ref.shape
@@ -617,13 +643,6 @@
     far_turned = far_tokens_ref[...].T
     zs, depth = kept_ref.shape[0], kept_ref.shape[1]
     first = info_ref[1] == 0
-    first_y = info_ref[5] == 0
-    summed = added(y_kept_ref[...], y_got_ref[...]).reshape(zs, 2, depth, -1)
-    with_x_ref[...] = jnp.where(first, summed[:, 0], summed[:, 1])
-    to_x_ref[...] = jnp.where(first, summed[:, 1], summed[:, 0])
-    summed = added(x_kept_ref[...], x_got_ref[...])
-    with_y_ref[...] = jnp.where(first_y, summed[:, 0], summed[:, 1])
-    to_y_ref[...] = jnp.where(first_y, summed[:, 1], summed[:, 0])
     for n in range(3):
         at = slice(n * half, (n + 1) * half)
         terms = contract(near_turned, d_near[:, at], PLAIN)
@@ -668,7 +687,7 @@
     )(place, info, tie, *[v for _, v in tokens], *[v for _, v, _ in weights])
 
 
-def row_attention_back(info, tie, near, far, own, got, weights, near_tokens, far_tokens, *ffn_terms):
+def row_attention_back(info, tie, near, far, own, got, weights, near_tokens, far_tokens):
     blocks, rows, part, lanes = near.shape
     count, width = rows * part, weights.shape[0]
     half = lanes // 3
@@ -677,11 +696,10 @@
     inside = pl.BlockSpec(memory_space=pltpu.VMEM)
     shapes = [((count, width), kind) for kind in (f32, bf16) * 2]
     shapes = shapes + [((4, width // 8, lanes), bf16)] * 2
-    shapes = shapes + [((4, width // 8, ffn_terms[0].shape[1]), bf16)] * 4
     return pl.pallas_call(
         row_bwd_kernel,
-        in_specs=[small, small] + [inside] * 11,
-        out_specs=[inside] * 10,
+        in_specs=[small, small] + [inside] * 7,
+        out_specs=[inside] * 6,
         out_shape=[jax.ShapeDtypeStruct(shape, kind) for shape, kind in shapes],
         scratch_shapes=[
             pltpu.VMEM((blocks, rows, part, half), bf16),
@@ -689,7 +707,7 @@
             pltpu.VMEM((blocks, rows, part, 2 * half), bf16),
         ],
         compiler_params=pltpu.CompilerParams(vmem_limit_bytes=56 * 2**20),
-    )(info, tie, near, far, own, got, weights, near_tokens, far_tokens, *ffn_terms)
+    )(info, tie, near, far, own, got, weights, near_tokens, far_tokens)
 
 
 def normed(value, gain, shift):
@@ -966,8 +984,48 @@
         in_specs=[small, small, inside, inside] + [block] * 3,
         out_specs=[block] * 4,
         out_shape=[jax.ShapeDtypeStruct(weight.shape, kind) for kind in kinds],
-        compiler_params=pltpu.CompilerParams(vmem_limit_bytes=40 * 2**20),
+        compiler_params=pltpu.CompilerParams(vmem_limit_bytes=58 * 2**20),
     )(place, factor.reshape(1), own, other, weight, first, second)
+
+
+def ffn_adam_kernel(place_ref, factor_ref, *refs):
+    pieces, refs = refs[:4], refs[4:]
+    low, even = place_ref[2] == 0, place_ref[3] == 0
+    factor = factor_ref[0]
+    depth = pieces[0].shape[0]
+    part = depth // 2
+    half = pl.program_id(0)
+
+    def by_matrix(first, second):
+        return jnp.where(even, first, second), jnp.where(even, second, first)
+
+    def put(grad, ins, outs):
+        values = adam_update(*[ref[...] for ref in ins], grad * factor, matrix_rate)
+        for ref, value in zip(outs, (*values, values[2].astype(jnp.bfloat16))):
+            ref[...] = value
+
+    rows = pl.ds(pl.multiple_of(half * part, 16), part)
+    owns = by_matrix(pieces[0][rows], pieces[1][rows])
+    others = by_matrix(pieces[2][rows], pieces[3][rows])
+    for n, (own, other) in enumerate(zip(owns, others)):
+        grad = jnp.concatenate([jnp.where(low, own, other), jnp.where(low, other, own)], axis=1)
+        put(grad.astype(jnp.float32), refs[3 * n : 3 * n + 3], refs[6 + 4 * n : 10 + 4 * n])
+
+
+def ffn_adam(place, factor, pieces, ins, outs):
+    small = pl.BlockSpec(memory_space=pltpu.SMEM)
+    inside = pl.BlockSpec(memory_space=pltpu.VMEM)
+    depth, hidden = ins[0].shape
+    block = pl.BlockSpec((depth // 2, hidden), lambda n: (n, 0))
+    kinds = [jnp.float32] * 3 + [jnp.bfloat16]
+    return pl.pallas_call(
+        ffn_adam_kernel,
+        grid=(2,),
+        in_specs=[small, small] + [inside] * 4 + [block] * 6,
+        out_specs=[block] * 8,
+        out_shape=[jax.ShapeDtypeStruct((depth, hidden), kind) for kind in kinds * 2],
+        compiler_params=pltpu.CompilerParams(vmem_limit_bytes=58 * 2**20),
+    )(place, factor.reshape(1), *pieces, *ins, *[value.T for value in outs])
 
 
 def whole_call(kernel, info, args, outs, scratch=()):
@@ -991,91 +1049,73 @@
     return u * rise, rise + u * slope
 
 
-def ffn_kernel(
-    plan, place_ref, a_ref, a_got_ref, up_ref, up_got_ref, *refs
-):
+def ffn_kernel(plan, place_ref, a_ref, a_got_ref, up_ref, up_got_ref, *refs):
     bf16 = jnp.bfloat16
     stacks, refs = refs[: len(plan)], refs[len(plan) :]
     out_ref, out_other_ref, da_ref, da_other_ref = refs[:4]
     y_sent_ref, y_kept_ref, x_sent_ref, x_kept_ref = refs[4:8]
-    w_ref, tokens_ref, turned_ref, out_sum, da_sum, sem = refs[8:]
-    step = pl.program_id(0)
+    w_ref, turned_ref, out_sum, da_sum, sem = refs[8:]
     count, width = a_ref.shape
-    chunk = x_sent_ref.shape[3]
-    last = pl.num_programs(0) - 1
-
-    @pl.when(step == 0)
-    def _():
-        copies = placing(plan, ffn_at, place_ref, stacks, [w_ref], sem, steps=False)
-        for copy in copies:
-            copy.start()
-        for n, ref in enumerate((a_ref, a_got_ref, up_ref, up_got_ref)):
-            k, at = n // 2, slice((n % 2) * count, (n % 2 + 1) * count)
-            tokens_ref[k, at] = ref[...]
-            turned_ref[k, :, at] = ref[...].T
-        out_sum[...] = jnp.zeros_like(out_sum)
-        da_sum[...] = jnp.zeros_like(da_sum)
-        for copy in copies:
-            copy.wait()
-
-    lane = pl.ds(pl.multiple_of(step * chunk, chunk), chunk)
-    w_in = w_ref[:width, lane]
-    w_out = w_ref[width:, lane]
-    activs, grads = [], []
-    for n in (0, 1):
-        at = slice(n * count, (n + 1) * count)
-        activ, slope = gelu_pair(contract(tokens_ref[0, at], w_in, PLAIN))
-        activ = activ.astype(bf16)
-        grad = (contract(tokens_ref[1, at], w_out, PLAIN) * slope).astype(bf16)
-        out_sum[at] += contract(activ, w_out, LAST)
-        da_sum[at] += contract(grad, w_in, LAST)
-        activs.append(activ)
-        grads.append(grad)
-    in_terms = contract(turned_ref[0], jnp.concatenate(grads, axis=0), PLAIN).astype(bf16)
-    out_terms = contract(turned_ref[1], jnp.concatenate(activs, axis=0), PLAIN).astype(bf16)
-
-    @pl.when(step < last)
-    def _():
-        first = place_ref[3] == 0
-        y_kept_ref[...] = jnp.where(first, in_terms, out_terms)
-        y_sent_ref[...] = jnp.where(first, out_terms, in_terms)
-
-    @pl.when(step == last)
-    def _():
-        first = place_ref[1] == 0
-        zs, _, depth, _ = x_sent_ref.shape
-        for n, terms in enumerate((in_terms, out_terms)):
-            terms = terms.reshape(zs, 2, depth, chunk)
-            x_kept_ref[:, n] = jnp.where(first, terms[:, 0], terms[:, 1])
-            x_sent_ref[:, n] = jnp.where(first, terms[:, 1], terms[:, 0])
-
-    @pl.when(step == last)
-    def _():
-        out_ref[...] = out_sum[:count]
-        out_other_ref[...] = out_sum[count:].astype(bf16)
-        da_ref[...] = da_sum[:count]
-        da_other_ref[...] = da_sum[count:].astype(bf16)
-
-
-def feed_forward(place, normed_own, normed_got, up_own, up_got, pieces, chunk=768):
+    chunk = w_ref.shape[1] // 2
+    copies = placing(plan, ffn_at, place_ref, stacks, [w_ref], sem, steps=False)
+    for copy in copies:
+        copy.start()
+    for n, ref in enumerate((a_ref, a_got_ref, up_ref, up_got_ref)):
+        turned_ref[n // 2, :, (n % 2) * count : (n % 2 + 1) * count] = ref[...].T
+    for copy in copies:
+        copy.wait()
+    for step in (0, 1):
+        lane = slice(step * chunk, (step + 1) * chunk)
+        w_in = w_ref[:width, lane]
+        w_out = w_ref[width:, lane]
+        activs, grads = [], []
+        for n, (tokens, ups) in enumerate(((a_ref, up_ref), (a_got_ref, up_got_ref))):
+            at = slice(n * count, (n + 1) * count)
+            activ, slope = gelu_pair(contract(tokens[...], w_in, PLAIN))
+            activ = activ.astype(bf16)
+            grad = (contract(ups[...], w_out, PLAIN) * slope).astype(bf16)
+            out, da = contract(activ, w_out, LAST), contract(grad, w_in, LAST)
+            if step == 0:
+                out_sum[at] = out
+                da_sum[at] = da
+            elif n == 0:
+                out_ref[...] = out_sum[at] + out
+                da_ref[...] = da_sum[at] + da
+            else:
+                out_other_ref[...] = (out_sum[at] + out).astype(bf16)
+                da_other_ref[...] = (da_sum[at] + da).astype(bf16)
+            activs.append(activ)
+            grads.append(grad)
+        in_terms = contract(turned_ref[0], jnp.concatenate(grads, axis=0), PLAIN).astype(bf16)
+        out_terms = contract(turned_ref[1], jnp.concatenate(activs, axis=0), PLAIN).astype(bf16)
+        if step == 0:
+            first = place_ref[3] == 0
+            y_kept_ref[...] = jnp.where(first, in_terms, out_terms)
+            y_sent_ref[...] = jnp.where(first, out_terms, in_terms)
+        else:
+            first = place_ref[1] == 0
+            zs, _, depth, _ = x_sent_ref.shape
+            for n, terms in enumerate((in_terms, out_terms)):
+                terms = terms.reshape(zs, 2, depth, chunk)
+                x_kept_ref[:, n] = jnp.where(first, terms[:, 0], terms[:, 1])
+                x_sent_ref[:, n] = jnp.where(first, terms[:, 1], terms[:, 0])
+
+
+def feed_forward(place, normed_own, normed_got, up_own, up_got, pieces):
     count, width = normed_own.shape
     half = pieces[0][1].shape[-1]
     anywhere = pl.BlockSpec(memory_space=pl.ANY)
     inside = pl.BlockSpec(memory_space=pltpu.VMEM)
-    steps = half // chunk
-    lanes = pl.BlockSpec((width, chunk), lambda n: (0, jnp.minimum(n, steps - 2)))
     f32, bf16 = jnp.float32, jnp.bfloat16
     shapes = [((count, width), kind) for kind in (f32, bf16, f32, bf16)]
-    shapes = shapes + [((width, half - chunk), bf16)] * 2 + [((4, 2, width // 8, chunk), bf16)] * 2
+    shapes = shapes + [((width, half // 2), bf16)] * 2 + [((4, 2, width // 8, half // 2), bf16)] * 2
     return pl.pallas_call(
         partial(ffn_kernel, plan_of(pieces)),
-        grid=(steps,),
         in_specs=[pl.BlockSpec(memory_space=pltpu.SMEM)] + [inside] * 4 + [anywhere] * len(pieces),
-        out_specs=[inside] * 4 + [lanes] * 2 + [inside] * 2,
+        out_specs=[inside] * 8,
         out_shape=[jax.ShapeDtypeStruct(shape, kind) for shape, kind in shapes],
         scratch_shapes=[
             pltpu.VMEM((2 * width, half), bf16),
-            pltpu.VMEM((2, 2 * count, width), bf16),
             pltpu.VMEM((2, width, 2 * count), bf16),
             pltpu.VMEM((2 * count, width), f32),
             pltpu.VMEM((2 * count, width), f32),
@@ -1178,7 +1218,7 @@
     )
     col_x = swap(col_z, "x")
     col_last = swap(col_x, "y")
-    col_x, col_y, ffn_z = together(col_x, swap(col_z, "y"), ffn_z)
+    col_x, col_y, ffn_z, up = together(col_x, swap(col_z, "y"), ffn_z, up)
     tokens_far, col_last = together(swap(tokens_x, "c"), col_last)
     ffn_x, ffn_y = swap(ffn_z, "x"), swap(ffn_z, "y")
     ups = [pick(up, z, 0)] + [
@@ -1253,17 +1293,16 @@
 
     result, x_got, y_got = together(result, x_got, y_got)
     block_out = to_blocks(result.reshape(rows, part, width))
+    ffn_to_x, ffn_x, ffn_to_y, ffn_y = next_sums(place, y_kept, y_got, x_kept, x_got)
+    near_part, near_theirs, far_part, far_theirs, row_sent, row_kept = row_attention_back(
+        info, tie, near, far, grad_own, swap(grad_other, "c"), w_row, near_normed, far_normed
+    )
     (
-        near_part, near_theirs, far_part, far_theirs, row_sent, row_kept,
-        ffn_to_x, ffn_x, ffn_to_y, ffn_y,
-    ) = row_attention_back(
-        info, tie, near, far, grad_own, swap(grad_other, "c"), w_row, near_normed, far_normed,
-        y_kept, y_got, x_kept, x_got,
-    )
-    row_sent, far_theirs, near_theirs, attn_theirs, block_out, ffn_to_x, ffn_to_y = together(
-        row_sent, far_theirs, near_theirs, attn_theirs, block_out, ffn_to_x, ffn_to_y
-    )
-    ffn_x_got, ffn_y_got = swap(ffn_to_x, "x"), swap(ffn_to_y, "y")
+        row_sent, far_theirs, near_theirs, attn_theirs, block_out, ffn_x_got, ffn_y_got
+    ) = together(
+        row_sent, far_theirs, near_theirs, attn_theirs, block_out,
+        swap(ffn_to_x, "x"), swap(ffn_to_y, "y"),
+    )
     row_got = swap(row_sent, "x")
     far_sum = added(far_part, swap(far_theirs, "c"))
     far_got = swap(far_sum, "x")
@@ -1274,10 +1313,10 @@
         [acts, acts_got, attn_mine, swap(attn_theirs, "c")],
         [((8, depth // 2, 5 * half), bf16)] * 2,
     )
-    attn_got = swap(attn_sent, "y")
-    attn_kept, ffn_y_got, ffn_x_got = together(attn_kept, ffn_y_got, ffn_x_got)
     ffn_column = jnp.concatenate([added(ffn_x, ffn_x_got), added(ffn_y, ffn_y_got)], axis=2)
     ffn_own = lax.all_to_all(ffn_column, "z", 0, 0, tiled=True)
+    attn_sent, attn_kept, ffn_own, row_got = together(attn_sent, attn_kept, ffn_own, row_got)
+    attn_got = swap(attn_sent, "y")
     ffn_own = jnp.sum(ffn_own.astype(f32), axis=0).astype(bf16)
     ffn_own, row_got, block_out = together(ffn_own, row_got, block_out)
     row_own = z_summed(added(row_kept, row_got), z)
@@ -1308,10 +1347,7 @@
 
     row_other = swap(row_grad, "c")
     attn_other = swap(attn_grad_b, "c")
-    ffn_whole = [joined(piece, swap(piece, "c"), c, 1) for piece in ffn_grads]
-
-    in_grad = jnp.where(y == 0, *ffn_whole).astype(f32)
-    out_grad = jnp.where(y == 0, *ffn_whole[::-1]).astype(f32).T
+    ffn_others = [swap(piece, "c") for piece in ffn_grads]
 
     attn_own, block_out = together(attn_own, block_out)
     squares = sum(jnp.sum(jnp.square(g.astype(f32))) for g in (attn_own, ffn_own))
@@ -1330,12 +1366,14 @@
         attn_first,
         attn_second,
     )
-    in_first_new, in_second_new, in_weight_new = adam_update(
-        in_weight, in_first, in_second, in_grad * factor, matrix_rate
-    )
-    out_first_new, out_second_new, out_weight_new = adam_update(
-        out_weight, out_first, out_second, out_grad * factor, matrix_rate
-    )
+    in_first_new, in_second_new, in_weight_new, in_copy, *turned = ffn_adam(
+        place,
+        factor,
+        [*ffn_grads, *ffn_others],
+        (in_weight, in_first, in_second),
+        (out_weight, out_first, out_second),
+    )
+    out_first_new, out_second_new, out_weight_new, out_copy = [value.T for value in turned]
     norm_first_new, norm_second_new, norm_new = adam_update(
         norm_param, norm_first, norm_second, norm_grad * factor, norm_rate
     )
@@ -1350,11 +1388,11 @@
         in_first_new,
         in_second_new,
         in_weight_new,
-        in_weight_new.astype(bf16),
+        in_copy,
         out_first_new,
         out_second_new,
         out_weight_new,
-        out_weight_new.astype(bf16),
+        out_copy,
         norm_first_new,
         norm_second_new,
         norm_new,

time: 419 us -> 403 us (0.962)
  other arithmetic: 41.6 us -> 31.3 us
  Pallas kernels: 116 us -> 124 us
  starting transfers between devices: 78.5 us -> 71.2 us
    ppermute x6, waiting for transfers between devices: 36.9 us -> 24.4 us  [z_summed(): got = lax.ppermute(other, 'z', [(k, k ^ i) for k in range(4)])]
    ppermute x48, waiting for transfers between devices: 51.7 us -> 61.7 us  [swap(): return lax.ppermute(value, axis, PAIR)]
    convert_element_type x2 -> x0, other arithmetic: 9.29 us -> none  [the longest x1 4.99 us: paired_body(): in_weight_new.astype(bf16)]
    all_to_all x1, waiting for transfers between devices: 12 us -> 5 us  [paired_body(): lax.all_to_all(jnp.broadcast_to(ffn_quarter, (4, *ffn_quarter.shape)), 'z...]
    all_to_all x1, waiting for transfers between devices: 0.01 us -> 6.12 us  [paired_body(): ffn_own = lax.all_to_all(ffn_column, 'z', 0, 0, tiled=True)]
    pallas_call x2 -> x4, Pallas kernels: 45.5 us -> 51.3 us  [the longest x1 22.2 us: feed_forward(): pl.pallas_call(partial(ffn_kernel, plan_of(pieces)), in_specs=[pl.BlockSp...]
    all_to_all x2, waiting for transfers between devices: 0.01 us -> 4.32 us  [to_blocks(): return lax.all_to_all(value, ('z', 'x'), 0, 0, tiled=True)]
    ppermute x48, starting transfers between devices: 28.7 us -> 24.4 us  [swap(): return lax.ppermute(value, axis, PAIR)]
  transfers between devices with their start and end apart: 74 -> 74, of which waited for: 32 -> 35; matrix products, arithmetic and copies ran while one was open for 13% -> 11% of each run, Pallas kernels for 22% -> 24%
where the time goes in v7:
time: 403 us; the launch traced here: 396 us
  waiting for transfers between devices  141 us (35%)
  Pallas kernels  124 us (31%)
  starting transfers between devices  71.2 us (18%)
  other arithmetic  31.3 us (8%)
  local copies, waits for them, and re-layouts  21.4 us (5%)
  between operations  7.24 us (2%)
    ppermute x48, waiting for transfers between devices, swap(): return lax.ppermute(value, axis, PAIR)  61.7 us
    pallas_call x2, Pallas kernels, column_call(): pl.pallas_call(partial(kernel, plan_of(pieces)), in_specs=[small] * 2 + [...  37.1 us
    ppermute x48, starting transfers between devices, swap(): return lax.ppermute(value, axis, PAIR)  24.4 us
    ppermute x6, waiting for transfers between devices, z_summed(): got = lax.ppermute(other, 'z', [(k, k ^ i) for k in range(4)])  24.4 us
    pallas_call x1, Pallas kernels, feed_forward(): pl.pallas_call(partial(ffn_kernel, plan_of(pieces)), in_specs=[pl.BlockSp...  22.2 us
    pallas_call x1, Pallas kernels, row_attention_back(): pl.pallas_call(row_bwd_kernel, in_specs=[small, small] + [inside] * 7, ou...  17.3 us
    pallas_call x2, Pallas kernels, whole_call(): pl.pallas_call(kernel, in_specs=[pl.BlockSpec(memory_space=pltpu.SMEM)] +...  15 us
    pallas_call x1, Pallas kernels, row_attention(): pl.pallas_call(partial(row_fwd_kernel, [step for step, _ in tokens], plan...  13.4 us
  transfers between devices with their start and end apart: 74, of which 35 were waited for; matrix products, arithmetic and copies ran while one was open for 11% of the time, Pallas kernels for 24%

profile of v7, /device:TPU:0, one launch (start us, length us, event | category | flops | bytes accessed | tf_op | source)
XLA Modules:
  0.0 395.5 jit_solution(4327602868621133434)
XLA Ops:
  4.3 5.0 %collective-permute-start.3 = (bf16[48,1152]{1,0:T(8,128)(2,1)}, bf16[48,1152]{1,0:T(8,128)(2,1)}, u32[]{:S(2)}, u32[]{:S(2)}) collective-permute-start(bf16[48,1152]{1,0:T(8,128)(2,1)} %fusion.21), channel_id=1, source_target_pairs={{0,24},{8,16},{16,8},{24,0},{1,25},{9,17},{17,9},{25,1},{2,26},{10... | collective-permute-start | bytes 331784 | tf_op jit(solution)/shard_map/ppermute | solution.py:368
  34.7 4.7 %collective-permute-done.7 = bf16[144,768]{1,0:T(8,128)(2,1)S(1)} collective-permute-done((bf16[144,768]{1,0:T(8,128)(2,1)S(1)}, bf16[144,768]{1,0:T(8,128)(2,1)S(1)}, u32[]{:S(2)}, u32[]{:S(2)}) %collective-permute-start.7) | collective-permute-done | bytes 221216 | tf_op jit(solution)/shard_map/ppermute | solution.py:1199
  39.5 5.2 %collective-permute-done.8 = bf16[144,768]{1,0:T(8,128)(2,1)S(1)} collective-permute-done((bf16[144,768]{1,0:T(8,128)(2,1)S(1)}, bf16[144,768]{1,0:T(8,128)(2,1)S(1)}, u32[]{:S(2)}, u32[]{:S(2)}) %collective-permute-start.8) | collective-permute-done | bytes 221216 | tf_op jit(solution)/shard_map/ppermute | solution.py:1199
  56.0 5.9 %collective-permute-done.15 = bf16[5,48,384]{2,1,0:T(8,128)(2,1)S(1)} collective-permute-done((bf16[5,48,384]{2,1,0:T(8,128)(2,1)S(1)}, bf16[5,48,384]{2,1,0:T(8,128)(2,1)S(1)}, u32[]{:S(2)}, u32[]{:S(2)}) %collective-permute-start.15) | collective-permute-done | bytes 184352 | tf_op jit(solution)/shard_map/ppermute | solution.py:368
  73.9 12.4 %collective-permute-done.17.refs_1_ = bf16[4,5,48,384]{3,2,1,0:T(8,128)(2,1)S(1)} collective-permute-done((bf16[4,5,48,384]{3,2,1,0:T(8,128)(2,1)S(1)}, bf16[4,5,48,384]{3,2,1,0:T(8,128)(2,1)S(1)}, u32[]{:S(2)}, u32[]{:S(2)}) %collective-permute-start.17) | collective-permute-done | bytes 737312 | tf_op jit(solution)/shard_map/ppermute | solution.py:319
  90.7 5.0 %all-to-all-done.refs_0_ = bf16[4,96,1536]{2,1,0:T(8,128)(2,1)S(1)} async-done(((bf16[4,96,1536]{2,1,0:T(8,128)(2,1)}), bf16[4,96,1536]{2,1,0:T(8,128)(2,1)S(1)}, u32[]{:S(2)}, u32[]{:S(2)}) %all-to-all-start) | async-done | bytes 1179680 | tf_op jit(solution)/shard_map/all_to_all | solution.py:1216
  108.9 6.4 %collective-permute-done.25 = bf16[2,64,768]{2,1,0:T(8,128)(2,1)} collective-permute-done((bf16[2,64,768]{2,1,0:T(8,128)(2,1)}, bf16[2,64,768]{2,1,0:T(8,128)(2,1)}, u32[]{:S(2)}, u32[]{:S(2)}) %collective-permute-start.25) | collective-permute-done | bytes 196640 | tf_op jit(solution)/shard_map/ppermute | solution.py:1225
  115.3 13.4 %shard_map.295 = (bf16[512,768]{1,0:T(8,128)(2,1)}, bf16[1024,768]{1,0:T(8,128)(2,1)}, bf16[1024,768]{1,0:T(8,128)(2,1)}, bf16[768,1152]{1,0:T(8,128)(2,1)}, f32...) custom-call(s32[4]{0:T(128)} %pad_add_fusion.1.place_ref, ...), custom_call_target="tpu_custom_call" | custom-call | flops 7000000000 | bytes 10000000 | tf_op jit(solution)/shard_map/pallas_call | solution.py:674
  140.3 14.3 %shard_map.296 = (bf16[512,2304]{1,0:T(8,128)(2,1)}, bf16[512,768]{1,0:T(8,128)(2,1)}, bf16[8,64,2304]{2,1,0:T(8,128)(2,1)}, f32[512,768]{1,0:T(8,128)}, bf16[512,768]{1,0:T(8,128)(2,1)}) custom-call(s32[6]{0:T(128)} %concatenate.43.info_ref, s32[4]{0:T(128)} %pad_add_fusion.1.place_ref, bf16[4,5,48,384]{3,2,1,0:T(8,128)(2,1)} %copy-done.1, ...), custom_call_target="tpu_custom_call" | custom-call | tf_op jit(solution)/shard_map/pallas_call | solution.py:946
  158.2 22.2 %shard_map.297 = (f32[512,768]{1,0:T(8,128)}, bf16[512,768]{1,0:T(8,128)(2,1)}, f32[512,768]{1,0:T(8,128)}, bf16[512,768]{1,0:T(8,128)(2,1)}, bf16[768,768]{1,0:...) custom-call(s32[4]{0:T(128)} %pad_add_fusion.1.place_ref, ...), custom_call_target="tpu_custom_call" | custom-call | tf_op jit(solution)/shard_map/pallas_call | solution.py:1112
  187.1 22.8 %shard_map.298 = (bf16[512,768]{1,0:T(8,128)(2,1)}, bf16[512,768]{1,0:T(8,128)(2,1)}, bf16[512,384]{1,0:T(8,128)(2,1)}, bf16[512,384]{1,0:T(8,128)(2,1)}, bf16[5...) custom-call(s32[6]{0:T(128)} %concatenate.43.info_ref, s32[4]{0:T(128)} %pad_add_fusion.1.place_ref, ...), custom_call_target="tpu_custom_call" | custom-call | tf_op jit(solution)/shard_map/pallas_call | solution.py:946
  209.9 6.3 %all-to-all-start.1 = ((bf16[8,64,768]{2,1,0:T(8,128)(2,1)}), bf16[8,64,768]{2,1,0:T(8,128)(2,1)S(1)}, u32[]{:S(2)}, u32[]{:S(2)}) async-start(bf16[8,64,768]{2,1,0:T(8,128)(2,1)} %bitcast.138), calls=%async_computation.1 | async-start | bytes 1572864 | tf_op jit(solution)/shard_map/all_to_all | solution.py:352
  226.5 17.3 %shard_map.299 = (f32[512,768]{1,0:T(8,128)}, bf16[512,768]{1,0:T(8,128)(2,1)}, f32[512,768]{1,0:T(8,128)}, bf16[512,768]{1,0:T(8,128)(2,1)}, bf16[4,96,1152]{2,...) custom-call(s32[6]{0:T(128)} %concatenate.43.info_ref, f32[1]{0:T(128)} %bitcast.39.tie_ref, ...), custom_call_target="tpu_custom_call" | custom-call | tf_op jit(solution)/shard_map/pallas_call | solution.py:699
  245.4 4.9 %all-to-all-start.2 = ((bf16[4,96,1536]{2,1,0:T(8,128)(2,1)}), bf16[4,96,1536]{2,1,0:T(8,128)(2,1)S(1)}, u32[]{:S(2)}, u32[]{:S(2)}) async-start(bf16[4,96,1536]{2,1,0:T(8,128)(2,1)} %pad_maximum_fusion), calls=%async_computation.2 | async-start | bytes 2359296 | tf_op jit(solution)/shard_map/all_to_all | solution.py:1317
  255.8 9.5 %shard_map.301 = (bf16[8,48,1920]{2,1,0:T(8,128)(2,1)}, bf16[8,48,1920]{2,1,0:T(8,128)(2,1)}) custom-call(s32[4]{0:T(128)} %pad_add_fusion.1.place_ref, bf16[512,2304]{1,0:T(8,128)(2,1)} %get-tuple-element.153.acts_ref, bf16[512,2304]{1,0:T(8,128)(2,1)} %collective-permute-done.32.got_ref, bf16[512,1920]{1,0:T(8,128)(2,1)} %get-tuple-element.171.mine_ref, ...), custom_call_target="tpu_custom_call" | custom-call | tf_op jit(solution)/shard_map/pallas_call | solution.py:1033
  265.3 8.0 %collective-permute-done.45 = bf16[4,96,1152]{2,1,0:T(8,128)(2,1)} collective-permute-done((bf16[4,96,1152]{2,1,0:T(8,128)(2,1)}, bf16[4,96,1152]{2,1,0:T(8,128)(2,1)}, u32[]{:S(2)}, u32[]{:S(2)}) %collective-permute-start.45) | collective-permute-done | bytes 884768 | tf_op jit(solution)/shard_map/ppermute | solution.py:319
  273.3 6.1 %all-to-all-done.2 = bf16[4,96,1536]{2,1,0:T(8,128)(2,1)S(1)} async-done(((bf16[4,96,1536]{2,1,0:T(8,128)(2,1)}), bf16[4,96,1536]{2,1,0:T(8,128)(2,1)S(1)}, u32[]{:S(2)}, u32[]{:S(2)}) %all-to-all-start.2) | async-done | bytes 1179680 | tf_op jit(solution)/shard_map/all_to_all | solution.py:1317
  289.7 5.5 %shard_map.302 = bf16[8,80,768]{2,1,0:T(8,128)(2,1)} custom-call(s32[6]{0:T(128)} %concatenate.43.info_ref, f32[512,768]{1,0:T(8,128)} %get-tuple-element.208.near_ref, bf16[512,768]{1,0:T(8,128)(2,1)} %collective-permute-done.52.near_got_ref, bf16[512,768]{1,0:T(8,128)(2,1)} %collective-permute-done.54.far_got_ref, ...), custom_call_target="tpu_custom_call" | custom-call | tf_op jit(solution)/shard_map/pallas_call | solution.py:1033
  295.2 8.9 %collective-permute-done.56 = bf16[96,1152]{1,0:T(8,128)(2,1)S(1)} collective-permute-done((bf16[96,1152]{1,0:T(8,128)(2,1)S(1)}, bf16[96,1152]{1,0:T(8,128)(2,1)S(1)}, u32[]{:S(2)}, u32[]{:S(2)}) %collective-permute-start.56) | collective-permute-done | bytes 221216 | tf_op jit(solution)/shard_map/ppermute | solution.py:1136
  346.5 5.6 %collective-permute-done.50 = bf16[48,1920]{1,0:T(8,128)(2,1)S(1)} collective-permute-done((bf16[48,1920]{1,0:T(8,128)(2,1)S(1)}, bf16[48,1920]{1,0:T(8,128)(2,1)S(1)}, u32[]{:S(2)}, u32[]{:S(2)}) %collective-permute-start.50) | collective-permute-done | bytes 184352 | tf_op jit(solution)/shard_map/ppermute | solution.py:1136
  352.1 7.5 %collective-permute-done.49 = bf16[48,1920]{1,0:T(8,128)(2,1)S(1)} collective-permute-done((bf16[48,1920]{1,0:T(8,128)(2,1)S(1)}, bf16[48,1920]{1,0:T(8,128)(2,1)S(1)}, u32[]{:S(2)}, u32[]{:S(2)}) %collective-permute-start.49) | collective-permute-done | bytes 184352 | tf_op jit(solution)/shard_map/ppermute | solution.py:1136
  370.0 6.8 %all-to-all-done.4 = f32[32,8,128]{2,1,0:T(8,128)S(1)} async-done(((f32[32,8,128]{2,1,0:T(8,128)}), f32[32,8,128]{2,1,0:T(8,128)S(1)}, u32[]{:S(2)}, u32[]{:S(2)}) %all-to-all-start.4) | async-done | bytes 131104 | tf_op jit(solution)/shard_map/all_to_all | solution.py:1357
  378.2 7.3 %shard_map.304 = (f32[96,3072]{1,0:T(8,128)}, f32[96,3072]{1,0:T(8,128)}, f32[96,3072]{1,0:T(8,128)}, bf16[96,3072]{1,0:T(8,128)(2,1)}, f32[96,3072]{1,0:T(8,128...) custom-call(s32[4]{0:T(128)} %pad_add_fusion.1.place_ref, f32[1]{0:T(128)} %bitcast.71.factor_ref, ...), custom_call_target="tpu_custom_call" | custom-call | tf_op jit(solution)/shard_map/pallas_call | solution.py:1021
  387.1 6.8 %shard_map.303 = (f32[8,96,768]{2,1,0:T(8,128)}, f32[8,96,768]{2,1,0:T(8,128)}, f32[8,96,768]{2,1,0:T(8,128)}, bf16[8,96,768]{2,1,0:T(8,128)(2,1)}) custom-call(s32[4]{0:T(128)} %pad_add_fusion.1.place_ref, f32[1]{0:T(128)} %bitcast.71.factor_ref, bf16[96,3072]{1,0:T(8,128)(2,1)} %pad_maximum_fusion.4.own_ref, bf16[96,3072]{1,0:T(8,128)(2,1)} %pad_maximum_fusion.5.other_ref, ...), custom_call_target="tpu_custom_call" | custom-call | tf_op jit(solution)/shard_map/pallas_call | solution.py:981
  (297 shorter events, 170.2 us)
Async XLA Ops:
  65.7 30.0 %all-to-all-start = ((bf16[4,96,1536]{2,1,0:T(8,128)(2,1)}), bf16[4,96,1536]{2,1,0:T(8,128)(2,1)S(1)}, u32[]{:S(2)}, u32[]{:S(2)}) async-start(bf16[4,96,1536]{2,1,0:T(8,128)(2,1)} %broadcast_in_dim.39), calls=%async_computation | async-start | bytes 2359296 | tf_op jit(solution)/shard_map/all_to_all | solution.py:1216
  71.3 24.9 %collective-permute-start.21 = (bf16[4,144,768]{2,1,0:T(8,128)(2,1)}, bf16[4,144,768]{2,1,0:T(8,128)(2,1)}, u32[]{:S(2)}, u32[]{:S(2)}) collective-permute-start(bf16[4,144,768]{2,1,0:T(8,128)(2,1)} %pad_maximum_fusion.1.refs_0_), channel_id=1, source_target_pairs={{0,1},{1,0},{2,3},{3,2},{4,5},{5,4},{6,7},{7,6},{8,9},{9,8},{10,11... | collective-permute-start | bytes 2654216 | tf_op jit(solution)/shard_map/ppermute | solution.py:319
  71.8 29.3 %collective-permute-start.19 = (bf16[4,144,768]{2,1,0:T(8,128)(2,1)}, bf16[4,144,768]{2,1,0:T(8,128)(2,1)}, u32[]{:S(2)}, u32[]{:S(2)}) collective-permute-start(bf16[4,144,768]{2,1,0:T(8,128)(2,1)} %collective-permute-done.10.refs_1_), channel_id=1, source_target_pairs={{0,1},{1,0},{2,3},{3,2},{4,5},{5,4},{6,7},{7,6},{8,9},{9,8},{10,11... | collective-permute-start | bytes 2654216 | tf_op jit(solution)/shard_map/ppermute | solution.py:319
  73.7 24.7 %collective-permute-start.27 = (bf16[4,5,48,384]{3,2,1,0:T(8,128)(2,1)S(1)}, bf16[4,5,48,384]{3,2,1,0:T(8,128)(2,1)}, u32[]{:S(2)}, u32[]{:S(2)}) collective-permute-start(bf16[4,5,48,384]{3,2,1,0:T(8,128)(2,1)S(1)} %pad_maximum_fusion.3.refs_0_), channel_id=1, source_target_pairs={{0,1},{1,0},{2,3},{3,2},{4,5},{5,4},{6,7},{7,6},{8,9},{9,8},{10,11... | collective-permute-start | bytes 2211848 | tf_op jit(solution)/shard_map/ppermute | solution.py:319
  95.7 35.7 %collective-permute-start.23 = (bf16[4,96,1536]{2,1,0:T(8,128)(2,1)S(1)}, bf16[4,96,1536]{2,1,0:T(8,128)(2,1)}, u32[]{:S(2)}, u32[]{:S(2)}) collective-permute-start(bf16[4,96,1536]{2,1,0:T(8,128)(2,1)S(1)} %all-to-all-done.refs_0_), channel_id=1, source_target_pairs={{0,2},{2,0},{1,3},{3,1},{4,6},{6,4},{5,7},{7,5},{8,10},{10,8},{9,1... | collective-permute-start | bytes 3538952 | tf_op jit(solution)/shard_map/ppermute | solution.py:319
  96.2 35.2 %collective-permute-start.22 = (bf16[4,96,1536]{2,1,0:T(8,128)(2,1)S(1)}, bf16[4,96,1536]{2,1,0:T(8,128)(2,1)}, u32[]{:S(2)}, u32[]{:S(2)}) collective-permute-start(bf16[4,96,1536]{2,1,0:T(8,128)(2,1)S(1)} %all-to-all-done.refs_0_), channel_id=1, source_target_pairs={{0,4},{4,0},{1,5},{5,1},{2,6},{6,2},{3,7},{7,3},{8,12},{12,8},{9,1... | collective-permute-start | bytes 3538952 | tf_op jit(solution)/shard_map/ppermute | solution.py:319
  106.5 22.2 %collective-permute-start.28 = (bf16[4,5,48,384]{3,2,1,0:T(8,128)(2,1)S(1)}, bf16[4,5,48,384]{3,2,1,0:T(8,128)(2,1)S(1)}, u32[]{:S(2)}, u32[]{:S(2)}) collective-permute-start(bf16[4,5,48,384]{3,2,1,0:T(8,128)(2,1)S(1)} %collective-permute-done.17.refs_1_), channel_id=1, source_target_pairs={{0,1},{1,0},{2,3},{3,2},{4,5},{5,4},{6,7},{7,6},{8,9},{9,8},{10,11... | collective-permute-start | bytes 2211848 | tf_op jit(solution)/shard_map/ppermute | solution.py:319
  108.1 20.7 %collective-permute-start.29 = (bf16[4,5,48,384]{3,2,1,0:T(8,128)(2,1)}, bf16[4,5,48,384]{3,2,1,0:T(8,128)(2,1)}, u32[]{:S(2)}, u32[]{:S(2)}) collective-permute-start(bf16[4,5,48,384]{3,2,1,0:T(8,128)(2,1)} %collective-permute-done.18.refs_2_), channel_id=1, source_target_pairs={{0,1},{1,0},{2,3},{3,2},{4,5},{5,4},{6,7},{7,6},{8,9},{9,8},{10,11... | collective-permute-start | bytes 2211848 | tf_op jit(solution)/shard_map/ppermute | solution.py:319
  180.4 29.5 %collective-permute-start.40 = (bf16[4,2,96,768]{3,2,1,0:T(8,128)(2,1)}, bf16[4,2,96,768]{3,2,1,0:T(8,128)(2,1)S(1)}, u32[]{:S(2)}, u32[]{:S(2)}) collective-permute-start(bf16[4,2,96,768]{3,2,1,0:T(8,128)(2,1)} %get-tuple-element.184), channel_id=1, source_target_pairs={{0,4},{4,0},{1,5},{5,1},{2,6},{6,2},{3,7},{7,3},{8,12},{12,8},{9,1... | collective-permute-start | bytes 3538952 | tf_op jit(solution)/shard_map/ppermute | solution.py:319
  181.0 28.9 %collective-permute-start.41 = (bf16[768,768]{1,0:T(8,128)(2,1)}, bf16[768,768]{1,0:T(8,128)(2,1)S(1)}, u32[]{:S(2)}, u32[]{:S(2)}) collective-permute-start(bf16[768,768]{1,0:T(8,128)(2,1)} %get-tuple-element.185), channel_id=1, source_target_pairs={{0,2},{2,0},{1,3},{3,1},{4,6},{6,4},{5,7},{7,5},{8,10},{10,8},{9,1... | collective-permute-start | bytes 3538952 | tf_op jit(solution)/shard_map/ppermute | solution.py:319
  209.9 33.9 %all-to-all-start.1 = ((bf16[8,64,768]{2,1,0:T(8,128)(2,1)}), bf16[8,64,768]{2,1,0:T(8,128)(2,1)S(1)}, u32[]{:S(2)}, u32[]{:S(2)}) async-start(bf16[8,64,768]{2,1,0:T(8,128)(2,1)} %bitcast.138), calls=%async_computation.1 | async-start | bytes 1572864 | tf_op jit(solution)/shard_map/all_to_all | solution.py:352
  220.7 23.1 %collective-permute-start.42 = (bf16[4,96,768]{2,1,0:T(8,128)(2,1)}, bf16[4,96,768]{2,1,0:T(8,128)(2,1)S(1)}, u32[]{:S(2)}, u32[]{:S(2)}) collective-permute-start(bf16[4,96,768]{2,1,0:T(8,128)(2,1)} %get-tuple-element.191), channel_id=1, source_target_pairs={{0,4},{4,0},{1,5},{5,1},{2,6},{6,2},{3,7},{7,3},{8,12},{12,8},{9,1... | collective-permute-start | bytes 1769480 | tf_op jit(solution)/shard_map/ppermute | solution.py:319
  222.7 21.1 %collective-permute-start.43 = (bf16[4,96,768]{2,1,0:T(8,128)(2,1)}, bf16[4,96,768]{2,1,0:T(8,128)(2,1)S(1)}, u32[]{:S(2)}, u32[]{:S(2)}) collective-permute-start(bf16[4,96,768]{2,1,0:T(8,128)(2,1)} %get-tuple-element.192), channel_id=1, source_target_pairs={{0,2},{2,0},{1,3},{3,1},{4,6},{6,4},{5,7},{7,5},{8,10},{10,8},{9,1... | collective-permute-start | bytes 1769480 | tf_op jit(solution)/shard_map/ppermute | solution.py:319
  223.5 32.3 %collective-permute-start.32 = (bf16[512,2304]{1,0:T(8,128)(2,1)}, bf16[512,2304]{1,0:T(8,128)(2,1)}, u32[]{:S(2)}, u32[]{:S(2)}) collective-permute-start(bf16[512,2304]{1,0:T(8,128)(2,1)} %get-tuple-element.153.acts_ref), channel_id=1, source_target_pairs={{0,1},{1,0},{2,3},{3,2},{4,5},{5,4},{6,7},{7,6},{8,9},{9,8},{10,11... | collective-permute-start | bytes 7077896 | tf_op jit(solution)/shard_map/ppermute | solution.py:319
  245.4 34.0 %all-to-all-start.2 = ((bf16[4,96,1536]{2,1,0:T(8,128)(2,1)}), bf16[4,96,1536]{2,1,0:T(8,128)(2,1)S(1)}, u32[]{:S(2)}, u32[]{:S(2)}) async-start(bf16[4,96,1536]{2,1,0:T(8,128)(2,1)} %pad_maximum_fusion), calls=%async_computation.2 | async-start | bytes 2359296 | tf_op jit(solution)/shard_map/all_to_all | solution.py:1317
  250.5 22.8 %collective-permute-start.45 = (bf16[4,96,1152]{2,1,0:T(8,128)(2,1)}, bf16[4,96,1152]{2,1,0:T(8,128)(2,1)}, u32[]{:S(2)}, u32[]{:S(2)}) collective-permute-start(bf16[4,96,1152]{2,1,0:T(8,128)(2,1)} %get-tuple-element.200), channel_id=1, source_target_pairs={{0,4},{4,0},{1,5},{5,1},{2,6},{6,2},{3,7},{7,3},{8,12},{12,8},{9,1... | collective-permute-start | bytes 2654216 | tf_op jit(solution)/shard_map/ppermute | solution.py:319
  251.1 32.9 %collective-permute-start.52 = (bf16[512,768]{1,0:T(8,128)(2,1)}, bf16[512,768]{1,0:T(8,128)(2,1)}, u32[]{:S(2)}, u32[]{:S(2)}) collective-permute-start(bf16[512,768]{1,0:T(8,128)(2,1)} %get-tuple-element.209), channel_id=1, source_target_pairs={{0,1},{1,0},{2,3},{3,2},{4,5},{5,4},{6,7},{7,6},{8,9},{9,8},{10,11... | collective-permute-start | bytes 2359304 | tf_op jit(solution)/shard_map/ppermute | solution.py:319
  255.2 34.5 %collective-permute-start.54 = (bf16[512,768]{1,0:T(8,128)(2,1)}, bf16[512,768]{1,0:T(8,128)(2,1)}, u32[]{:S(2)}, u32[]{:S(2)}) collective-permute-start(bf16[512,768]{1,0:T(8,128)(2,1)} %add_convert_fusion.2), channel_id=1, source_target_pairs={{0,4},{4,0},{1,5},{5,1},{2,6},{6,2},{3,7},{7,3},{8,12},{12,8},{9,1... | collective-permute-start | bytes 2359304 | tf_op jit(solution)/shard_map/ppermute | solution.py:319
  279.6 35.4 %collective-permute-start.46 = (bf16[8,48,1920]{2,1,0:T(8,128)(2,1)}, bf16[8,48,1920]{2,1,0:T(8,128)(2,1)}, u32[]{:S(2)}, u32[]{:S(2)}) collective-permute-start(bf16[8,48,1920]{2,1,0:T(8,128)(2,1)} %get-tuple-element.202), channel_id=1, source_target_pairs={{0,2},{2,0},{1,3},{3,1},{4,6},{6,4},{5,7},{7,5},{8,10},{10,8},{9,1... | collective-permute-start | bytes 4423688 | tf_op jit(solution)/shard_map/ppermute | solution.py:319
  305.0 26.7 %all-to-all-start.3 = ((bf16[8,80,768]{2,1,0:T(8,128)(2,1)}), bf16[8,80,768]{2,1,0:T(8,128)(2,1)S(1)}, u32[]{:S(2)}, u32[]{:S(2)}) async-start(bf16[8,80,768]{2,1,0:T(8,128)(2,1)} %shard_map.302), calls=%async_computation.3 | async-start | bytes 1966080 | tf_op jit(solution)/shard_map/all_to_all | solution.py:352
  308.5 69.6 %collective-permute-start.67 = (bf16[96,1536]{1,0:T(8,128)(2,1)S(1)}, bf16[96,1536]{1,0:T(8,128)(2,1)}, u32[]{:S(2)}, u32[]{:S(2)}) collective-permute-start(bf16[96,1536]{1,0:T(8,128)(2,1)S(1)} %reduce_sum.66.refs_0_), channel_id=1, source_target_pairs={{0,1},{1,0},{2,3},{3,2},{4,5},{5,4},{6,7},{7,6},{8,9},{9,8},{10,11... | collective-permute-start | bytes 884744 | tf_op jit(solution)/shard_map/ppermute | solution.py:319
  317.7 20.3 %collective-permute-start.47 = (bf16[4,48,1920]{2,1,0:T(8,128)(2,1)}, bf16[4,48,1920]{2,1,0:T(8,128)(2,1)}, u32[]{:S(2)}, u32[]{:S(2)}) collective-permute-start(bf16[4,48,1920]{2,1,0:T(8,128)(2,1)} %dynamic-slice_bitcast_fusion), channel_id=1, source_target_pairs={{0,4},{4,0},{1,5},{5,1},{2,6},{6,2},{3,7},{7,3},{8,12},{12,8},{9,1... | collective-permute-start | bytes 2211848 | tf_op jit(solution)/shard_map/ppermute | solution.py:319
  321.3 56.9 %collective-permute-start.68 = (bf16[96,1536]{1,0:T(8,128)(2,1)}, bf16[96,1536]{1,0:T(8,128)(2,1)}, u32[]{:S(2)}, u32[]{:S(2)}) collective-permute-start(bf16[96,1536]{1,0:T(8,128)(2,1)} %collective-permute-done.66.refs_1_), channel_id=1, source_target_pairs={{0,1},{1,0},{2,3},{3,2},{4,5},{5,4},{6,7},{7,6},{8,9},{9,8},{10,11... | collective-permute-start | bytes 884744 | tf_op jit(solution)/shard_map/ppermute | solution.py:319
  346.5 39.7 %collective-permute-start.64 = (bf16[96,1152]{1,0:T(8,128)(2,1)S(1)}, bf16[96,1152]{1,0:T(8,128)(2,1)S(1)}, u32[]{:S(2)}, u32[]{:S(2)}) collective-permute-start(bf16[96,1152]{1,0:T(8,128)(2,1)S(1)} %copy-done.12), channel_id=1, source_target_pairs={{0,1},{1,0},{2,3},{3,2},{4,5},{5,4},{6,7},{7,6},{8,9},{9,8},{10,11... | collective-permute-start | bytes 663560 | tf_op jit(solution)/shard_map/ppermute | solution.py:319
  (90 other events, 974.1 us)

commit v8 on v7

--- a/solution.py
+++ b/solution.py
@@ -440,6 +440,24 @@
 def head_lanes(lanes):
     side = lax.broadcasted_iota(jnp.int32, (1, lanes), 1) % TILE < DH
     return (side, jnp.logical_not(side))
+
+
+def lasting(microseconds):
+    return pl.CostEstimate(
+        flops=int(microseconds * 0.58e9), bytes_accessed=0, transcendentals=0
+    )
+
+
+def moved(pairs, sem, first=0):
+    copies = [pltpu.make_async_copy(a, b, sem.at[first + n]) for n, (a, b) in enumerate(pairs)]
+    for copy in copies:
+        copy.start()
+    return copies
+
+
+def wait_all(copies):
+    for copy in copies:
+        copy.wait()
 
 
 def only(keep, value):
@@ -565,15 +583,20 @@
         in_specs=[pl.BlockSpec(memory_space=pltpu.SMEM), by_rows, by_rows, by_z, by_z],
         out_specs=[pl.BlockSpec((1, depth, lanes), lambda n: (n, 0, 0))] * 4,
         out_shape=[jax.ShapeDtypeStruct((zs, depth, lanes), jnp.bfloat16)] * 4,
+        cost_estimate=lasting(4),
         compiler_params=pltpu.CompilerParams(vmem_limit_bytes=56 * 2**20),
     )(place, y_kept, y_got, x_kept, x_got)
 
 
 def row_bwd_kernel(
-    info_ref, tie_ref, near_ref, far_ref, own_ref, got_ref, w_ref, near_tokens_ref, far_tokens_ref,
-    near_part_ref, near_theirs_ref, far_part_ref, far_theirs_ref, sent_ref, kept_ref,
-    do_ref, d_near_ref, d_far_ref,
+    info_ref, tie_ref, near_ref, far_ref, own_ref, got_ref, w_any, near_any, far_any,
+    near_part_any, near_theirs_any, far_part_any, far_theirs_any, sent_ref, kept_ref,
+    do_ref, d_near_ref, d_far_ref, w_ref, near_tokens_ref, far_tokens_ref,
+    near_part_ref, near_theirs_ref, far_part_ref, far_theirs_ref, sem,
 ):
+    arriving = moved(
+        [(w_any, w_ref), (near_any, near_tokens_ref), (far_any, far_tokens_ref)], sem
+    )
     bf16 = jnp.bfloat16
     blocks, rows, part, lanes = near_ref.shape
     half = lanes // 3
@@ -632,6 +655,7 @@
             put(d_far_ref, half, dv[near:])
 
     count = rows * part
+    wait_all(arriving)
     d_far = d_far_ref[...].reshape(blocks * count, 2 * half)
     far_weights = w_ref[:, half:]
     far_part_ref[...] = contract(d_far[:count], far_weights, LAST)
@@ -639,6 +663,16 @@
     d_near = d_near_ref[...].reshape(blocks * count, lanes)
     near_part_ref[...] = contract(d_near[:count], w_ref[...], LAST)
     near_theirs_ref[...] = contract(d_near[count:], w_ref[...], LAST).astype(bf16)
+    leaving = moved(
+        [
+            (far_theirs_ref, far_theirs_any),
+            (near_theirs_ref, near_theirs_any),
+            (far_part_ref, far_part_any),
+            (near_part_ref, near_part_any),
+        ],
+        sem,
+        3,
+    )
     near_turned = near_tokens_ref[...].T
     far_turned = far_tokens_ref[...].T
     zs, depth = kept_ref.shape[0], kept_ref.shape[1]
@@ -651,6 +685,7 @@
         terms = terms.astype(bf16).reshape(zs, 2, depth, half)
         kept_ref[:, :, at] = jnp.where(first, terms[:, 0], terms[:, 1])
         sent_ref[:, :, at] = jnp.where(first, terms[:, 1], terms[:, 0])
+    wait_all(leaving)
 
 
 def row_attention(place, info, tie, tokens, weights, rows, half):
@@ -683,7 +718,7 @@
             pltpu.SemaphoreType.DMA((16,)),
         ],
         compiler_params=pltpu.CompilerParams(vmem_limit_bytes=56 * 2**20),
-        cost_estimate=pl.CostEstimate(flops=7 * 10**9, bytes_accessed=10**7, transcendentals=10**6),
+        cost_estimate=lasting(13),
     )(place, info, tie, *[v for _, v in tokens], *[v for _, v, _ in weights])
 
 
@@ -693,19 +728,26 @@
     half = lanes // 3
     f32, bf16 = jnp.float32, jnp.bfloat16
     small = pl.BlockSpec(memory_space=pltpu.SMEM)
+    anywhere = pl.BlockSpec(memory_space=pl.ANY)
     inside = pl.BlockSpec(memory_space=pltpu.VMEM)
     shapes = [((count, width), kind) for kind in (f32, bf16) * 2]
     shapes = shapes + [((4, width // 8, lanes), bf16)] * 2
     return pl.pallas_call(
         row_bwd_kernel,
-        in_specs=[small, small] + [inside] * 7,
-        out_specs=[inside] * 6,
+        in_specs=[small, small] + [inside] * 4 + [anywhere] * 3,
+        out_specs=[anywhere] * 4 + [inside] * 2,
         out_shape=[jax.ShapeDtypeStruct(shape, kind) for shape, kind in shapes],
         scratch_shapes=[
             pltpu.VMEM((blocks, rows, part, half), bf16),
             pltpu.VMEM((blocks, rows, part, lanes), bf16),
             pltpu.VMEM((blocks, rows, part, 2 * half), bf16),
+            pltpu.VMEM(weights.shape, bf16),
+            pltpu.VMEM(near_tokens.shape, bf16),
+            pltpu.VMEM(far_tokens.shape, bf16),
+            *[pltpu.VMEM(shape, kind) for shape, kind in shapes[:4]],
+            pltpu.SemaphoreType.DMA((7,)),
         ],
+        cost_estimate=lasting(16),
         compiler_params=pltpu.CompilerParams(vmem_limit_bytes=56 * 2**20),
     )(info, tie, near, far, own, got, weights, near_tokens, far_tokens)
 
@@ -800,9 +842,9 @@
 
 def col_bwd_kernel(plan, info_ref, place_ref, *refs):
     stacks, refs = refs[: len(plan)], refs[len(plan) :]
-    up_ref, da_ref, da_got_ref, out_ref, out_got_ref, resid_ref, one_ref, qkv_ref, gain_ref = refs[:9]
-    result_ref, stream_ref, own_ref, other_ref, mine_ref, theirs_ref, norms_ref = refs[9:16]
-    dqkv_ref, do_ref, three_ref, col_ref, seven_ref, sem = refs[16:]
+    up_ref, da_ref, out_ref, got_ref, resid_ref, one_ref, qkv_ref, gain_ref = refs[:8]
+    result_ref, stream_ref, own_ref, other_ref, mine_ref, theirs_ref, norms_ref = refs[8:15]
+    dqkv_ref, do_ref, three_ref, col_ref, seven_ref, sem = refs[15:]
     copies = placing(plan, col_attn_at, place_ref, stacks, [three_ref, col_ref, seven_ref], sem)
     for copy in copies:
         copy.start()
@@ -811,8 +853,8 @@
     rows, cols, lanes = qkv_ref.shape
     width = lanes // 3
     part = 16
-    result_ref[...] = (resid_ref[...] + out_ref[...] + out_got_ref[...].astype(f32)).astype(bf16)
-    da = da_ref[...] + da_got_ref[...].astype(f32)
+    result_ref[...] = (resid_ref[...] + out_ref[...] + got_ref[0].astype(f32)).astype(bf16)
+    da = da_ref[...] + got_ref[1].astype(f32)
     gain = gain_ref[4:5]
     _, unit, scale = normed(resid_ref[...], gain, 0.0)
     grad_three = up_ref[...].astype(f32) + normed_back(da, unit, scale, gain)
@@ -937,7 +979,7 @@
         sent_ref[:, :, at] = jnp.where(first, terms[:, 1], terms[:, 0])
 
 
-def column_call(kernel, info, place, pieces, args, outs, scratch):
+def column_call(kernel, info, place, pieces, args, outs, scratch, time):
     width = args[-1].shape[1]
     bf16 = jnp.bfloat16
     small = pl.BlockSpec(memory_space=pltpu.SMEM)
@@ -955,25 +997,55 @@
             pltpu.VMEM((width, width), bf16),
             pltpu.SemaphoreType.DMA((160,)),
         ],
+        cost_estimate=lasting(time),
         compiler_params=pltpu.CompilerParams(vmem_limit_bytes=56 * 2**20),
     )(info, place, *[value for _, value, _ in pieces], *args)
 
 
-def adam_kernel(place_ref, factor_ref, own_ref, other_ref, w_ref, first_ref, second_ref, *outs):
+def last_sums_kernel(place_ref, own_ref, *refs):
+    f32 = jnp.float32
+    got, (before_ref, sum_ref, squares_ref) = refs[:3], refs[3:]
+    total = own_ref[...].astype(f32)
+    for ref in got:
+        total = total + ref[...].astype(f32)
+    low = total.astype(jnp.bfloat16)
+    sum_ref[...] = low
+    low = low.astype(f32)
+    squares = jnp.sum(low * low, axis=1, keepdims=True)
+    squares = jnp.sum(squares, axis=0, keepdims=True) + before_ref[0:1, 0:1]
+    squares_ref[...] = jnp.broadcast_to(squares[None], squares_ref.shape)
+
+
+def clip_factor(squares_ref):
+    total = jnp.sum(squares_ref[:, 0:1, 0:1], axis=0)
+    return clip_bound / jnp.maximum(jnp.sqrt(total), clip_bound)
+
+
+def adam_kernel(
+    place_ref, squares_ref, row_ref, row_other_ref, col_ref, col_other_ref, w_ref, first_ref, second_ref, *outs
+):
     count, _, width = w_ref.shape
     half = width // 2
     low = place_ref[2] == 0
+    early = pl.program_id(0) == 0
+    factor = clip_factor(squares_ref)
     for n in range(count):
-        at = pl.ds(pl.multiple_of((pl.program_id(0) * count + n) * half, TILE), half)
-        own, other = own_ref[:, at], other_ref[:, at]
+        at = slice((n + 1) * half, (n + 2) * half)
+        own, other = col_ref[:, at], col_other_ref[:, at]
+        if n < 3:
+            at = slice(n * half, (n + 1) * half)
+            sooner, sooner_other = row_ref[:, at], row_other_ref[:, at]
+        else:
+            sooner, sooner_other = col_ref[:, :half], col_other_ref[:, :half]
+        own, other = jnp.where(early, sooner, own), jnp.where(early, sooner_other, other)
         grad = jnp.concatenate([jnp.where(low, own, other), jnp.where(low, other, own)], axis=1)
-        grad = grad.astype(jnp.float32) * factor_ref[0]
+        grad = grad.astype(jnp.float32) * factor
         first, second, weight = adam_update(w_ref[n], first_ref[n], second_ref[n], grad, matrix_rate)
         for ref, value in zip(outs, (first, second, weight, weight.astype(jnp.bfloat16))):
             ref[n] = value
 
 
-def attn_adam(place, factor, own, other, weight, first, second):
+def attn_adam(place, squares, grads, weight, first, second):
     small = pl.BlockSpec(memory_space=pltpu.SMEM)
     inside = pl.BlockSpec(memory_space=pltpu.VMEM)
     block = pl.BlockSpec((4, *weight.shape[1:]), lambda m: (m, 0, 0))
@@ -981,17 +1053,17 @@
     return pl.pallas_call(
         adam_kernel,
         grid=(weight.shape[0] // 4,),
-        in_specs=[small, small, inside, inside] + [block] * 3,
+        in_specs=[small] + [inside] * 5 + [block] * 3,
         out_specs=[block] * 4,
         out_shape=[jax.ShapeDtypeStruct(weight.shape, kind) for kind in kinds],
-        compiler_params=pltpu.CompilerParams(vmem_limit_bytes=58 * 2**20),
-    )(place, factor.reshape(1), own, other, weight, first, second)
-
-
-def ffn_adam_kernel(place_ref, factor_ref, *refs):
+        compiler_params=pltpu.CompilerParams(vmem_limit_bytes=40 * 2**20),
+    )(place, squares, *grads, weight, first, second)
+
+
+def ffn_adam_kernel(place_ref, squares_ref, *refs):
     pieces, refs = refs[:4], refs[4:]
     low, even = place_ref[2] == 0, place_ref[3] == 0
-    factor = factor_ref[0]
+    factor = clip_factor(squares_ref)
     depth = pieces[0].shape[0]
     part = depth // 2
     half = pl.program_id(0)
@@ -1012,7 +1084,7 @@
         put(grad.astype(jnp.float32), refs[3 * n : 3 * n + 3], refs[6 + 4 * n : 10 + 4 * n])
 
 
-def ffn_adam(place, factor, pieces, ins, outs):
+def ffn_adam(place, squares, pieces, ins, outs):
     small = pl.BlockSpec(memory_space=pltpu.SMEM)
     inside = pl.BlockSpec(memory_space=pltpu.VMEM)
     depth, hidden = ins[0].shape
@@ -1021,21 +1093,21 @@
     return pl.pallas_call(
         ffn_adam_kernel,
         grid=(2,),
-        in_specs=[small, small] + [inside] * 4 + [block] * 6,
+        in_specs=[small] + [inside] * 5 + [block] * 6,
         out_specs=[block] * 8,
         out_shape=[jax.ShapeDtypeStruct((depth, hidden), kind) for kind in kinds * 2],
         compiler_params=pltpu.CompilerParams(vmem_limit_bytes=58 * 2**20),
-    )(place, factor.reshape(1), *pieces, *ins, *[value.T for value in outs])
-
-
-def whole_call(kernel, info, args, outs, scratch=()):
+    )(place, squares, *pieces, *ins, *[value.T for value in outs])
+
+
+def whole_call(kernel, info, args, outs, time):
     inside = pl.BlockSpec(memory_space=pltpu.VMEM)
     return pl.pallas_call(
         kernel,
         in_specs=[pl.BlockSpec(memory_space=pltpu.SMEM)] + [inside] * len(args),
         out_specs=[inside] * len(outs),
         out_shape=[jax.ShapeDtypeStruct(shape, kind) for shape, kind in outs],
-        scratch_shapes=list(scratch),
+        cost_estimate=lasting(time),
         compiler_params=pltpu.CompilerParams(vmem_limit_bytes=56 * 2**20),
     )(info, *args)
 
@@ -1052,9 +1124,9 @@
 def ffn_kernel(plan, place_ref, a_ref, a_got_ref, up_ref, up_got_ref, *refs):
     bf16 = jnp.bfloat16
     stacks, refs = refs[: len(plan)], refs[len(plan) :]
-    out_ref, out_other_ref, da_ref, da_other_ref = refs[:4]
-    y_sent_ref, y_kept_ref, x_sent_ref, x_kept_ref = refs[4:8]
-    w_ref, turned_ref, out_sum, da_sum, sem = refs[8:]
+    out_ref, da_ref, others_ref = refs[:3]
+    y_sent_ref, y_kept_ref, x_sent_ref, x_kept_ref = refs[3:7]
+    w_ref, turned_ref, out_sum, da_sum, sem = refs[7:]
     count, width = a_ref.shape
     chunk = w_ref.shape[1] // 2
     copies = placing(plan, ffn_at, place_ref, stacks, [w_ref], sem, steps=False)
@@ -1082,8 +1154,8 @@
                 out_ref[...] = out_sum[at] + out
                 da_ref[...] = da_sum[at] + da
             else:
-                out_other_ref[...] = (out_sum[at] + out).astype(bf16)
-                da_other_ref[...] = (da_sum[at] + da).astype(bf16)
+                others_ref[0] = (out_sum[at] + out).astype(bf16)
+                others_ref[1] = (da_sum[at] + da).astype(bf16)
             activs.append(activ)
             grads.append(grad)
         in_terms = contract(turned_ref[0], jnp.concatenate(grads, axis=0), PLAIN).astype(bf16)
@@ -1107,12 +1179,12 @@
     anywhere = pl.BlockSpec(memory_space=pl.ANY)
     inside = pl.BlockSpec(memory_space=pltpu.VMEM)
     f32, bf16 = jnp.float32, jnp.bfloat16
-    shapes = [((count, width), kind) for kind in (f32, bf16, f32, bf16)]
+    shapes = [((count, width), f32)] * 2 + [((2, count, width), bf16)]
     shapes = shapes + [((width, half // 2), bf16)] * 2 + [((4, 2, width // 8, half // 2), bf16)] * 2
     return pl.pallas_call(
         partial(ffn_kernel, plan_of(pieces)),
         in_specs=[pl.BlockSpec(memory_space=pltpu.SMEM)] + [inside] * 4 + [anywhere] * len(pieces),
-        out_specs=[inside] * 8,
+        out_specs=[inside] * 7,
         out_shape=[jax.ShapeDtypeStruct(shape, kind) for shape, kind in shapes],
         scratch_shapes=[
             pltpu.VMEM((2 * width, half), bf16),
@@ -1121,6 +1193,7 @@
             pltpu.VMEM((2 * count, width), f32),
             pltpu.SemaphoreType.DMA((16,)),
         ],
+        cost_estimate=lasting(22),
         compiler_params=pltpu.CompilerParams(vmem_limit_bytes=56 * 2**20),
     )(place, normed_own, normed_got, up_own, up_got, *[value for _, value, _ in pieces])
 
@@ -1129,13 +1202,16 @@
     return (a.astype(jnp.float32) + b.astype(jnp.float32)).astype(jnp.bfloat16)
 
 
+def gather_turned(column, z):
+    return [
+        lax.ppermute(pick(column, lax.bitwise_xor(z, i), 0), "z", [(k, k ^ i) for k in range(4)])
+        for i in (1, 2, 3)
+    ]
+
+
 def z_summed(column, z):
-    shard = pick(column, z, 0).astype(jnp.float32)
-    for i in (1, 2, 3):
-        other = pick(column, lax.bitwise_xor(z, i), 0)
-        got = lax.ppermute(other, "z", [(k, k ^ i) for k in range(4)])
-        shard = shard + got.astype(jnp.float32)
-    return shard.astype(jnp.bfloat16)
+    parts = [pick(column, z, 0)] + gather_turned(column, z)
+    return sum(part.astype(jnp.float32) for part in parts).astype(jnp.bfloat16)
 
 
 def paired_body(
@@ -1260,6 +1336,7 @@
         [stream_zero, mixed_heads[0], swap(mixed_heads[1], "c"), norm_gain],
         [((count, 3 * width), bf16), whole_shape, wide_shape, ((count, width), f32), whole_shape],
         [pltpu.VMEM((rows, part, width), bf16)],
+        14,
     )
     normed_three, *ffn_across = together(normed_three, *across(ffn_x, ffn_y))
     ffn_pieces = ffn_pieces + across_pieces(*ffn_across)
@@ -1269,11 +1346,10 @@
         (jnp.arange(rows, dtype=jnp.int32) < rows_live)[:, None], (column < cols_live)[None, :]
     )
     up = jnp.where(live[..., None], up, jnp.zeros_like(up)).reshape(count, width)
-    out_own, out_other, da_own, da_other, *ffn_terms = feed_forward(
+    out_own, da_own, other_parts, *ffn_terms = feed_forward(
         place, normed_three, swap(normed_three, "c"), up, swap(up, "c"), ffn_pieces
     )
-    da_got = swap(da_other, "c")
-    out_got = swap(out_other, "c")
+    other_parts = swap(other_parts, "c")
     y_sent, y_kept, x_sent, x_kept = ffn_terms
     y_got, x_got = swap(y_sent, "y"), swap(x_sent, "x")
 
@@ -1283,12 +1359,13 @@
         info,
         place,
         col_pieces,
-        [up, da_own, da_got, out_own, out_got, resid_three, stream_one, qkv_two, norm_gain],
+        [up, da_own, out_own, other_parts, resid_three, stream_one, qkv_two, norm_gain],
         [whole_shape] * 2
         + [((count, half), bf16)] * 2
         + [((count, 5 * half), bf16)] * 2
         + [((4, width), f32)],
         [pltpu.VMEM((rows, part, 3 * width), bf16), pltpu.VMEM((rows, part, width), bf16)],
+        23,
     )
 
     result, x_got, y_got = together(result, x_got, y_got)
@@ -1312,6 +1389,7 @@
         place,
         [acts, acts_got, attn_mine, swap(attn_theirs, "c")],
         [((8, depth // 2, 5 * half), bf16)] * 2,
+        9,
     )
     ffn_column = jnp.concatenate([added(ffn_x, ffn_x_got), added(ffn_y, ffn_y_got)], axis=2)
     ffn_own = lax.all_to_all(ffn_column, "z", 0, 0, tiled=True)
@@ -1328,6 +1406,7 @@
         info,
         [near_part, near_got, far_got, stream_zero, grad_stream, norm_gain, col_norms],
         [((rows, part + 16, width), bf16)],
+        5,
     )[0]
     blocks, row_own = together(blocks, row_own)
     blocks = to_blocks(blocks)
@@ -1340,8 +1419,23 @@
     ]
     norm_grad = (norm_parts[0] + norm_parts[1]) + (norm_parts[2] + norm_parts[3])
     norm_grad = norm_grad[:6, :depth]
-    attn_own = z_summed(attn_column, z)
     row_grad = added(row_own, swap(row_own, "y"))
+    before = jnp.sum(jnp.square(ffn_own.astype(f32)))
+    before = before + 0.5 * jnp.sum(jnp.square(row_grad.astype(f32)))
+    before = before + 0.25 * jnp.sum(norm_grad * norm_grad)
+    attn_own, squares = whole_call(
+        last_sums_kernel,
+        place,
+        [
+            pick(attn_column, z, 0),
+            *gather_turned(attn_column, z),
+            jnp.broadcast_to(before, (8, TILE)),
+        ],
+        [((depth // 2, 5 * half), bf16), ((32, 8, TILE), f32)],
+        2,
+    )
+    attn_own, block_out = together(attn_own, block_out)
+    squares = lax.all_to_all(squares, ("z", "x", "y", "c"), 0, 0, tiled=True)
     attn_grad_b = joined(attn_own, swap(attn_own, "y"), y, 0)
     ffn_grads = [ffn_own, swap(ffn_own, "y")]
 
@@ -1349,26 +1443,19 @@
     attn_other = swap(attn_grad_b, "c")
     ffn_others = [swap(piece, "c") for piece in ffn_grads]
 
-    attn_own, block_out = together(attn_own, block_out)
-    squares = sum(jnp.sum(jnp.square(g.astype(f32))) for g in (attn_own, ffn_own))
-    squares = squares + 0.5 * jnp.sum(jnp.square(row_grad.astype(f32)))
-    squares = squares + 0.25 * jnp.sum(norm_grad * norm_grad)
-    squares = jnp.broadcast_to(squares, (32, 8, TILE))
-    squares = lax.all_to_all(squares, ("z", "x", "y", "c"), 0, 0, tiled=True)
     grad_norm = jnp.sqrt(jnp.sum(squares[:, 0, 0]))
     factor = clip_bound / jnp.maximum(grad_norm, clip_bound)
     attn_first_new, attn_second_new, attn_weight_new, attn_copy = attn_adam(
         place,
-        factor,
-        jnp.concatenate([row_grad, attn_grad_b], axis=1),
-        jnp.concatenate([row_other, attn_other], axis=1),
+        squares,
+        (row_grad, row_other, attn_grad_b, attn_other),
         attn_weight,
         attn_first,
         attn_second,
     )
     in_first_new, in_second_new, in_weight_new, in_copy, *turned = ffn_adam(
         place,
-        factor,
+        squares,
         [*ffn_grads, *ffn_others],
         (in_weight, in_first, in_second),
         (out_weight, out_first, out_second),

time: 403 us -> 397 us (0.985)
  waiting for transfers between devices: 141 us -> 133 us
  other arithmetic: 31.3 us -> 27.2 us
    ppermute x48 -> x47, waiting for transfers between devices: 61.7 us -> 66.9 us  [swap(): return lax.ppermute(value, axis, PAIR)]
    all_to_all x2, waiting for transfers between devices: 4.32 us -> 0.01 us  [to_blocks(): return lax.all_to_all(value, ('z', 'x'), 0, 0, tiled=True)]
    unnamed x81 -> x85, local copies, waits for them, and re-layouts: 4.65 us -> 8.37 us
    pallas_call x2 -> x3, Pallas kernels: 15 us -> 17.1 us  [whole_call(): pl.pallas_call(kernel, in_specs=[pl.BlockSpec(memory_space=pltpu.SMEM)] +...]
    ppermute x48 -> x47, starting transfers between devices: 24.4 us -> 26.5 us  [swap(): return lax.ppermute(value, axis, PAIR)]
  transfers between devices with their start and end apart: 74 -> 73, of which waited for: 35 -> 31; matrix products, arithmetic and copies ran while one was open for 11% -> 10% of each run, Pallas kernels for 24% -> 25%
where the time goes in v8:
time: 397 us; the launch traced here: 389 us
  waiting for transfers between devices  133 us (34%)
  Pallas kernels  124 us (31%)
  starting transfers between devices  73.8 us (19%)
  other arithmetic  27.2 us (7%)
  local copies, waits for them, and re-layouts  24.9 us (6%)
  between operations  6.59 us (2%)
    ppermute x47, waiting for transfers between devices, swap(): return lax.ppermute(value, axis, PAIR)  66.9 us
    pallas_call x2, Pallas kernels, column_call(): pl.pallas_call(partial(kernel, plan_of(pieces)), in_specs=[small] * 2 + [...  37.3 us
    ppermute x47, starting transfers between devices, swap(): return lax.ppermute(value, axis, PAIR)  26.5 us
    pallas_call x1, Pallas kernels, feed_forward(): pl.pallas_call(partial(ffn_kernel, plan_of(pieces)), in_specs=[pl.BlockSp...  22.2 us
    ppermute x6, waiting for transfers between devices, gather_turned(): lax.ppermute(pick(column, lax.bitwise_xor(z, i), 0), 'z', [(k, k ^ i) for...  21.2 us
    pallas_call x3, Pallas kernels, whole_call(): pl.pallas_call(kernel, in_specs=[pl.BlockSpec(memory_space=pltpu.SMEM)] +...  17.1 us
    pallas_call x1, Pallas kernels, row_attention_back(): pl.pallas_call(row_bwd_kernel, in_specs=[small, small] + [inside] * 4 + [...  16.1 us
    pallas_call x1, Pallas kernels, row_attention(): pl.pallas_call(partial(row_fwd_kernel, [step for step, _ in tokens], plan...  13.4 us
  transfers between devices with their start and end apart: 73, of which 31 were waited for; matrix products, arithmetic and copies ran while one was open for 10% of the time, Pallas kernels for 25%

profile of v8, /device:TPU:0, one launch (start us, length us, event | category | flops | bytes accessed | tf_op | source)
XLA Modules:
  0.0 389.4 jit_solution(12551729960891976524)
XLA Ops:
  4.3 5.0 %collective-permute-start.3 = (bf16[48,1152]{1,0:T(8,128)(2,1)}, bf16[48,1152]{1,0:T(8,128)(2,1)}, u32[]{:S(2)}, u32[]{:S(2)}) collective-permute-start(bf16[48,1152]{1,0:T(8,128)(2,1)} %fusion.18), channel_id=1, source_target_pairs={{0,24},{8,16},{16,8},{24,0},{1,25},{9,17},{17,9},{25,1},{2,26},{10... | collective-permute-start | bytes 331784 | tf_op jit(solution)/shard_map/ppermute | solution.py:368
  34.7 4.7 %collective-permute-done.7 = bf16[144,768]{1,0:T(8,128)(2,1)S(1)} collective-permute-done((bf16[144,768]{1,0:T(8,128)(2,1)S(1)}, bf16[144,768]{1,0:T(8,128)(2,1)S(1)}, u32[]{:S(2)}, u32[]{:S(2)}) %collective-permute-start.7) | collective-permute-done | bytes 221216 | tf_op jit(solution)/shard_map/ppermute | solution.py:1275
  39.5 5.5 %collective-permute-done.8 = bf16[144,768]{1,0:T(8,128)(2,1)S(1)} collective-permute-done((bf16[144,768]{1,0:T(8,128)(2,1)S(1)}, bf16[144,768]{1,0:T(8,128)(2,1)S(1)}, u32[]{:S(2)}, u32[]{:S(2)}) %collective-permute-start.8) | collective-permute-done | bytes 221216 | tf_op jit(solution)/shard_map/ppermute | solution.py:1275
  55.8 6.0 %collective-permute-done.15 = bf16[5,48,384]{2,1,0:T(8,128)(2,1)} collective-permute-done((bf16[5,48,384]{2,1,0:T(8,128)(2,1)S(1)}, bf16[5,48,384]{2,1,0:T(8,128)(2,1)}, u32[]{:S(2)}, u32[]{:S(2)}) %collective-permute-start.15) | collective-permute-done | bytes 184352 | tf_op jit(solution)/shard_map/ppermute | solution.py:368
  73.7 12.4 %collective-permute-done.17.refs_1_ = bf16[4,5,48,384]{3,2,1,0:T(8,128)(2,1)} collective-permute-done((bf16[4,5,48,384]{3,2,1,0:T(8,128)(2,1)}, bf16[4,5,48,384]{3,2,1,0:T(8,128)(2,1)}, u32[]{:S(2)}, u32[]{:S(2)}) %collective-permute-start.17) | collective-permute-done | bytes 737312 | tf_op jit(solution)/shard_map/ppermute | solution.py:319
  99.1 7.5 %collective-permute-done.20.refs_3_ = bf16[4,5,48,384]{3,2,1,0:T(8,128)(2,1)} collective-permute-done((bf16[4,5,48,384]{3,2,1,0:T(8,128)(2,1)}, bf16[4,5,48,384]{3,2,1,0:T(8,128)(2,1)}, u32[]{:S(2)}, u32[]{:S(2)}) %collective-permute-start.20) | collective-permute-done | bytes 737312 | tf_op jit(solution)/shard_map/ppermute | solution.py:319
  113.5 13.4 %shard_map.295 = (bf16[512,768]{1,0:T(8,128)(2,1)}, bf16[1024,768]{1,0:T(8,128)(2,1)}, bf16[1024,768]{1,0:T(8,128)(2,1)}, bf16[768,1152]{1,0:T(8,128)(2,1)}, f32...) custom-call(s32[4]{0:T(128)} %pad_add_fusion.1.place_ref, ...), custom_call_target="tpu_custom_call" | custom-call | flops 7539999744 | tf_op jit(solution)/shard_map/pallas_call | solution.py:709
  138.6 14.3 %shard_map.296 = (bf16[512,2304]{1,0:T(8,128)(2,1)}, bf16[512,768]{1,0:T(8,128)(2,1)}, bf16[8,64,2304]{2,1,0:T(8,128)(2,1)}, f32[512,768]{1,0:T(8,128)}, bf16[512,768]{1,0:T(8,128)(2,1)}) custom-call(s32[6]{0:T(128)} %concatenate.37.info_ref, s32[4]{0:T(128)} %pad_add_fusion.1.place_ref, bf16[4,5,48,384]{3,2,1,0:T(8,128)(2,1)} %pad_maximum_fusion.3.refs_0_, ...), custom_call_target="tpu_custom_call" | custom-call | flops 8120000000 | tf_op jit(solution)/shard_map/pallas_call | solution.py:988
  156.5 22.2 %shard_map.297 = (f32[512,768]{1,0:T(8,128)}, f32[512,768]{1,0:T(8,128)}, bf16[2,512,768]{2,1,0:T(8,128)(2,1)}, bf16[768,768]{1,0:T(8,128)(2,1)}, bf16[768,768]{...) custom-call(s32[4]{0:T(128)} %pad_add_fusion.1.place_ref, ...), custom_call_target="tpu_custom_call" | custom-call | flops 12760000512 | tf_op jit(solution)/shard_map/pallas_call | solution.py:1184
  183.7 23.0 %shard_map.298 = (bf16[512,768]{1,0:T(8,128)(2,1)}, bf16[512,768]{1,0:T(8,128)(2,1)}, bf16[512,384]{1,0:T(8,128)(2,1)}, bf16[512,384]{1,0:T(8,128)(2,1)}, bf16[5...) custom-call(s32[6]{0:T(128)} %concatenate.37.info_ref, s32[4]{0:T(128)} %pad_add_fusion.1.place_ref, ...), custom_call_target="tpu_custom_call" | custom-call | flops 13340000256 | tf_op jit(solution)/shard_map/pallas_call | solution.py:988
  207.6 6.3 %all-to-all-start.1 = ((bf16[8,64,768]{2,1,0:T(8,128)(2,1)}), bf16[8,64,768]{2,1,0:T(8,128)(2,1)S(1)}, u32[]{:S(2)}, u32[]{:S(2)}) async-start(bf16[8,64,768]{2,1,0:T(8,128)(2,1)} %bitcast.136), calls=%async_computation.1 | async-start | bytes 1572864 | tf_op jit(solution)/shard_map/all_to_all | solution.py:352
  223.2 16.1 %shard_map.299 = (f32[512,768]{1,0:T(8,128)}, bf16[512,768]{1,0:T(8,128)(2,1)}, f32[512,768]{1,0:T(8,128)}, bf16[512,768]{1,0:T(8,128)(2,1)}, bf16[4,96,1152]{2,...) custom-call(s32[6]{0:T(128)} %concatenate.37.info_ref, f32[1]{0:T(128)} %bitcast.39.tie_ref, ...), custom_call_target="tpu_custom_call" | custom-call | flops 9280000000 | tf_op jit(solution)/shard_map/pallas_call | solution.py:735
  240.9 4.8 %all-to-all-start.2 = ((bf16[4,96,1536]{2,1,0:T(8,128)(2,1)}), bf16[4,96,1536]{2,1,0:T(8,128)(2,1)S(1)}, u32[]{:S(2)}, u32[]{:S(2)}) async-start(bf16[4,96,1536]{2,1,0:T(8,128)(2,1)} %pad_maximum_fusion), calls=%async_computation.2 | async-start | bytes 2359296 | tf_op jit(solution)/shard_map/all_to_all | solution.py:1395
  251.2 9.4 %shard_map.301 = (bf16[8,48,1920]{2,1,0:T(8,128)(2,1)}, bf16[8,48,1920]{2,1,0:T(8,128)(2,1)}) custom-call(s32[4]{0:T(128)} %pad_add_fusion.1.place_ref, bf16[512,2304]{1,0:T(8,128)(2,1)} %get-tuple-element.154.acts_ref, bf16[512,2304]{1,0:T(8,128)(2,1)} %collective-permute-done.32.got_ref, bf16[512,1920]{1,0:T(8,128)(2,1)} %get-tuple-element.171.mine_ref, ...), custom_call_target="tpu_custom_call" | custom-call | flops 5219999744 | tf_op jit(solution)/shard_map/pallas_call | solution.py:1105
  260.6 8.1 %collective-permute-done.44 = bf16[4,96,1152]{2,1,0:T(8,128)(2,1)} collective-permute-done((bf16[4,96,1152]{2,1,0:T(8,128)(2,1)}, bf16[4,96,1152]{2,1,0:T(8,128)(2,1)}, u32[]{:S(2)}, u32[]{:S(2)}) %collective-permute-start.44) | collective-permute-done | bytes 884768 | tf_op jit(solution)/shard_map/ppermute | solution.py:319
  268.7 6.1 %all-to-all-done.2 = bf16[4,96,1536]{2,1,0:T(8,128)(2,1)S(1)} async-done(((bf16[4,96,1536]{2,1,0:T(8,128)(2,1)}), bf16[4,96,1536]{2,1,0:T(8,128)(2,1)S(1)}, u32[]{:S(2)}, u32[]{:S(2)}) %all-to-all-start.2) | async-done | bytes 1179680 | tf_op jit(solution)/shard_map/all_to_all | solution.py:1395
  284.9 5.5 %shard_map.302 = bf16[8,80,768]{2,1,0:T(8,128)(2,1)} custom-call(s32[6]{0:T(128)} %concatenate.37.info_ref, f32[512,768]{1,0:T(8,128)} %get-tuple-element.207.near_ref, bf16[512,768]{1,0:T(8,128)(2,1)} %collective-permute-done.50.near_got_ref, bf16[512,768]{1,0:T(8,128)(2,1)} %collective-permute-done.52.far_got_ref, ...), custom_call_target="tpu_custom_call" | custom-call | flops 2900000000 | tf_op jit(solution)/shard_map/pallas_call | solution.py:1105
  290.5 9.1 %collective-permute-done.54 = bf16[96,1152]{1,0:T(8,128)(2,1)S(1)} collective-permute-done((bf16[96,1152]{1,0:T(8,128)(2,1)S(1)}, bf16[96,1152]{1,0:T(8,128)(2,1)S(1)}, u32[]{:S(2)}, u32[]{:S(2)}) %collective-permute-start.54) | collective-permute-done | bytes 221216 | tf_op jit(solution)/shard_map/ppermute | solution.py:1207
  303.5 6.2 %collective-permute-done.45 = bf16[8,48,1920]{2,1,0:T(8,128)(2,1)} collective-permute-done((bf16[8,48,1920]{2,1,0:T(8,128)(2,1)}, bf16[8,48,1920]{2,1,0:T(8,128)(2,1)}, u32[]{:S(2)}, u32[]{:S(2)}) %collective-permute-start.45) | collective-permute-done | bytes 1474592 | tf_op jit(solution)/shard_map/ppermute | solution.py:319
  317.6 7.3 %collective-permute-done.56 = bf16[96,1152]{1,0:T(8,128)(2,1)S(1)} collective-permute-done((bf16[96,1152]{1,0:T(8,128)(2,1)S(1)}, bf16[96,1152]{1,0:T(8,128)(2,1)S(1)}, u32[]{:S(2)}, u32[]{:S(2)}) %collective-permute-start.56) | collective-permute-done | bytes 221216 | tf_op jit(solution)/shard_map/ppermute | solution.py:319
  344.3 8.4 %collective-permute-done.48.refs_1_ = bf16[48,1920]{1,0:T(8,128)(2,1)S(1)} collective-permute-done((bf16[48,1920]{1,0:T(8,128)(2,1)S(1)}, bf16[48,1920]{1,0:T(8,128)(2,1)S(1)}, u32[]{:S(2)}, u32[]{:S(2)}) %collective-permute-start.48) | collective-permute-done | bytes 184352 | tf_op jit(solution)/shard_map/ppermute | solution.py:1207
  362.8 6.1 %all-to-all-done.4.squares_ref = f32[32,8,128]{2,1,0:T(8,128)S(1)} async-done(((f32[32,8,128]{2,1,0:T(8,128)}), f32[32,8,128]{2,1,0:T(8,128)S(1)}, u32[]{:S(2)}, u32[]{:S(2)}) %all-to-all-start.4) | async-done | bytes 131104 | tf_op jit(solution)/shard_map/all_to_all | solution.py:1438
  371.2 7.8 %shard_map.305 = (f32[96,3072]{1,0:T(8,128)}, f32[96,3072]{1,0:T(8,128)}, f32[96,3072]{1,0:T(8,128)}, bf16[96,3072]{1,0:T(8,128)(2,1)}, f32[96,3072]{1,0:T(8,128...) custom-call(s32[4]{0:T(128)} %pad_add_fusion.1.place_ref, f32[32,8,128]{2,1,0:T(8,128)} %copy-done.3, ...), custom_call_target="tpu_custom_call" | custom-call | tf_op jit(solution)/shard_map/pallas_call | solution.py:1093
  382.2 5.6 %shard_map.304 = (f32[8,96,768]{2,1,0:T(8,128)}, f32[8,96,768]{2,1,0:T(8,128)}, f32[8,96,768]{2,1,0:T(8,128)}, bf16[8,96,768]{2,1,0:T(8,128)(2,1)}) custom-call(s32[4]{0:T(128)S(1)} %copy-done.5, f32[32,8,128]{2,1,0:T(8,128)S(1)} %copy-done.4, bf16[96,1152]{1,0:T(8,128)(2,1)S(1)} %get-tuple-element.238.row_ref, ...), custom_call_target="tpu_custom_call" | custom-call | tf_op jit(solution)/shard_map/pallas_call | solution.py:1053
  (297 shorter events, 162.0 us)
Async XLA Ops:
  64.7 29.8 %all-to-all-start = ((bf16[4,96,1536]{2,1,0:T(8,128)(2,1)}), bf16[4,96,1536]{2,1,0:T(8,128)(2,1)S(1)}, u32[]{:S(2)}, u32[]{:S(2)}) async-start(bf16[4,96,1536]{2,1,0:T(8,128)(2,1)} %broadcast_in_dim.39), calls=%async_computation | async-start | bytes 2359296 | tf_op jit(solution)/shard_map/all_to_all | solution.py:1292
  71.2 23.8 %collective-permute-start.21 = (bf16[4,144,768]{2,1,0:T(8,128)(2,1)S(1)}, bf16[4,144,768]{2,1,0:T(8,128)(2,1)}, u32[]{:S(2)}, u32[]{:S(2)}) collective-permute-start(bf16[4,144,768]{2,1,0:T(8,128)(2,1)S(1)} %pad_maximum_fusion.1.refs_0_), channel_id=1, source_target_pairs={{0,1},{1,0},{2,3},{3,2},{4,5},{5,4},{6,7},{7,6},{8,9},{9,8},{10,11... | collective-permute-start | bytes 2654216 | tf_op jit(solution)/shard_map/ppermute | solution.py:319
  71.7 26.7 %collective-permute-start.19 = (bf16[4,144,768]{2,1,0:T(8,128)(2,1)}, bf16[4,144,768]{2,1,0:T(8,128)(2,1)}, u32[]{:S(2)}, u32[]{:S(2)}) collective-permute-start(bf16[4,144,768]{2,1,0:T(8,128)(2,1)} %collective-permute-done.10.refs_1_), channel_id=1, source_target_pairs={{0,1},{1,0},{2,3},{3,2},{4,5},{5,4},{6,7},{7,6},{8,9},{9,8},{10,11... | collective-permute-start | bytes 2654216 | tf_op jit(solution)/shard_map/ppermute | solution.py:319
  73.6 22.8 %collective-permute-start.27 = (bf16[4,5,48,384]{3,2,1,0:T(8,128)(2,1)}, bf16[4,5,48,384]{3,2,1,0:T(8,128)(2,1)}, u32[]{:S(2)}, u32[]{:S(2)}) collective-permute-start(bf16[4,5,48,384]{3,2,1,0:T(8,128)(2,1)} %pad_maximum_fusion.3.refs_0_), channel_id=1, source_target_pairs={{0,1},{1,0},{2,3},{3,2},{4,5},{5,4},{6,7},{7,6},{8,9},{9,8},{10,11... | collective-permute-start | bytes 2211848 | tf_op jit(solution)/shard_map/ppermute | solution.py:319
  86.1 20.4 %collective-permute-start.20 = (bf16[4,5,48,384]{3,2,1,0:T(8,128)(2,1)}, bf16[4,5,48,384]{3,2,1,0:T(8,128)(2,1)}, u32[]{:S(2)}, u32[]{:S(2)}) collective-permute-start(bf16[4,5,48,384]{3,2,1,0:T(8,128)(2,1)} %collective-permute-done.17.refs_1_), channel_id=1, source_target_pairs={{0,2},{2,0},{1,3},{3,1},{4,6},{6,4},{5,7},{7,5},{8,10},{10,8},{9,1... | collective-permute-start | bytes 2211848 | tf_op jit(solution)/shard_map/ppermute | solution.py:319
  94.4 37.0 %collective-permute-start.23 = (bf16[4,96,1536]{2,1,0:T(8,128)(2,1)S(1)}, bf16[4,96,1536]{2,1,0:T(8,128)(2,1)}, u32[]{:S(2)}, u32[]{:S(2)}) collective-permute-start(bf16[4,96,1536]{2,1,0:T(8,128)(2,1)S(1)} %all-to-all-done.refs_0_), channel_id=1, source_target_pairs={{0,2},{2,0},{1,3},{3,1},{4,6},{6,4},{5,7},{7,5},{8,10},{10,8},{9,1... | collective-permute-start | bytes 3538952 | tf_op jit(solution)/shard_map/ppermute | solution.py:319
  94.9 36.5 %collective-permute-start.22 = (bf16[4,96,1536]{2,1,0:T(8,128)(2,1)S(1)}, bf16[4,96,1536]{2,1,0:T(8,128)(2,1)S(1)}, u32[]{:S(2)}, u32[]{:S(2)}) collective-permute-start(bf16[4,96,1536]{2,1,0:T(8,128)(2,1)S(1)} %all-to-all-done.refs_0_), channel_id=1, source_target_pairs={{0,4},{4,0},{1,5},{5,1},{2,6},{6,2},{3,7},{7,3},{8,12},{12,8},{9,1... | collective-permute-start | bytes 3538952 | tf_op jit(solution)/shard_map/ppermute | solution.py:319
  106.6 20.6 %collective-permute-start.28 = (bf16[4,5,48,384]{3,2,1,0:T(8,128)(2,1)}, bf16[4,5,48,384]{3,2,1,0:T(8,128)(2,1)}, u32[]{:S(2)}, u32[]{:S(2)}) collective-permute-start(bf16[4,5,48,384]{3,2,1,0:T(8,128)(2,1)} %collective-permute-done.17.refs_1_), channel_id=1, source_target_pairs={{0,1},{1,0},{2,3},{3,2},{4,5},{5,4},{6,7},{7,6},{8,9},{9,8},{10,11... | collective-permute-start | bytes 2211848 | tf_op jit(solution)/shard_map/ppermute | solution.py:319
  106.6 20.6 %collective-permute-start.29 = (bf16[4,5,48,384]{3,2,1,0:T(8,128)(2,1)}, bf16[4,5,48,384]{3,2,1,0:T(8,128)(2,1)}, u32[]{:S(2)}, u32[]{:S(2)}) collective-permute-start(bf16[4,5,48,384]{3,2,1,0:T(8,128)(2,1)} %collective-permute-done.18.refs_2_), channel_id=1, source_target_pairs={{0,1},{1,0},{2,3},{3,2},{4,5},{5,4},{6,7},{7,6},{8,9},{9,8},{10,11... | collective-permute-start | bytes 2211848 | tf_op jit(solution)/shard_map/ppermute | solution.py:319
  179.2 28.2 %collective-permute-start.39 = (bf16[4,2,96,768]{3,2,1,0:T(8,128)(2,1)}, bf16[4,2,96,768]{3,2,1,0:T(8,128)(2,1)S(1)}, u32[]{:S(2)}, u32[]{:S(2)}) collective-permute-start(bf16[4,2,96,768]{3,2,1,0:T(8,128)(2,1)} %get-tuple-element.184), channel_id=1, source_target_pairs={{0,4},{4,0},{1,5},{5,1},{2,6},{6,2},{3,7},{7,3},{8,12},{12,8},{9,1... | collective-permute-start | bytes 3538952 | tf_op jit(solution)/shard_map/ppermute | solution.py:319
  179.7 27.9 %collective-permute-start.40 = (bf16[768,768]{1,0:T(8,128)(2,1)}, bf16[768,768]{1,0:T(8,128)(2,1)S(1)}, u32[]{:S(2)}, u32[]{:S(2)}) collective-permute-start(bf16[768,768]{1,0:T(8,128)(2,1)} %get-tuple-element.185), channel_id=1, source_target_pairs={{0,2},{2,0},{1,3},{3,1},{4,6},{6,4},{5,7},{7,5},{8,10},{10,8},{9,1... | collective-permute-start | bytes 3538952 | tf_op jit(solution)/shard_map/ppermute | solution.py:319
  207.6 31.7 %all-to-all-start.1 = ((bf16[8,64,768]{2,1,0:T(8,128)(2,1)}), bf16[8,64,768]{2,1,0:T(8,128)(2,1)S(1)}, u32[]{:S(2)}, u32[]{:S(2)}) async-start(bf16[8,64,768]{2,1,0:T(8,128)(2,1)} %bitcast.136), calls=%async_computation.1 | async-start | bytes 1572864 | tf_op jit(solution)/shard_map/all_to_all | solution.py:352
  214.0 37.2 %collective-permute-start.32 = (bf16[512,2304]{1,0:T(8,128)(2,1)}, bf16[512,2304]{1,0:T(8,128)(2,1)}, u32[]{:S(2)}, u32[]{:S(2)}) collective-permute-start(bf16[512,2304]{1,0:T(8,128)(2,1)} %get-tuple-element.154.acts_ref), channel_id=1, source_target_pairs={{0,1},{1,0},{2,3},{3,2},{4,5},{5,4},{6,7},{7,6},{8,9},{9,8},{10,11... | collective-permute-start | bytes 7077896 | tf_op jit(solution)/shard_map/ppermute | solution.py:319
  218.9 20.5 %collective-permute-start.41 = (bf16[4,96,768]{2,1,0:T(8,128)(2,1)}, bf16[4,96,768]{2,1,0:T(8,128)(2,1)S(1)}, u32[]{:S(2)}, u32[]{:S(2)}) collective-permute-start(bf16[4,96,768]{2,1,0:T(8,128)(2,1)} %get-tuple-element.191), channel_id=1, source_target_pairs={{0,4},{4,0},{1,5},{5,1},{2,6},{6,2},{3,7},{7,3},{8,12},{12,8},{9,1... | collective-permute-start | bytes 1769480 | tf_op jit(solution)/shard_map/ppermute | solution.py:319
  240.9 34.0 %all-to-all-start.2 = ((bf16[4,96,1536]{2,1,0:T(8,128)(2,1)}), bf16[4,96,1536]{2,1,0:T(8,128)(2,1)S(1)}, u32[]{:S(2)}, u32[]{:S(2)}) async-start(bf16[4,96,1536]{2,1,0:T(8,128)(2,1)} %pad_maximum_fusion), calls=%async_computation.2 | async-start | bytes 2359296 | tf_op jit(solution)/shard_map/all_to_all | solution.py:1395
  245.9 22.8 %collective-permute-start.44 = (bf16[4,96,1152]{2,1,0:T(8,128)(2,1)}, bf16[4,96,1152]{2,1,0:T(8,128)(2,1)}, u32[]{:S(2)}, u32[]{:S(2)}) collective-permute-start(bf16[4,96,1152]{2,1,0:T(8,128)(2,1)} %get-tuple-element.200), channel_id=1, source_target_pairs={{0,4},{4,0},{1,5},{5,1},{2,6},{6,2},{3,7},{7,3},{8,12},{12,8},{9,1... | collective-permute-start | bytes 2654216 | tf_op jit(solution)/shard_map/ppermute | solution.py:319
  246.5 32.8 %collective-permute-start.50 = (bf16[512,768]{1,0:T(8,128)(2,1)}, bf16[512,768]{1,0:T(8,128)(2,1)}, u32[]{:S(2)}, u32[]{:S(2)}) collective-permute-start(bf16[512,768]{1,0:T(8,128)(2,1)} %get-tuple-element.208), channel_id=1, source_target_pairs={{0,1},{1,0},{2,3},{3,2},{4,5},{5,4},{6,7},{7,6},{8,9},{9,8},{10,11... | collective-permute-start | bytes 2359304 | tf_op jit(solution)/shard_map/ppermute | solution.py:319
  250.6 34.3 %collective-permute-start.52 = (bf16[512,768]{1,0:T(8,128)(2,1)}, bf16[512,768]{1,0:T(8,128)(2,1)}, u32[]{:S(2)}, u32[]{:S(2)}) collective-permute-start(bf16[512,768]{1,0:T(8,128)(2,1)} %add_convert_fusion.2), channel_id=1, source_target_pairs={{0,4},{4,0},{1,5},{5,1},{2,6},{6,2},{3,7},{7,3},{8,12},{12,8},{9,1... | collective-permute-start | bytes 2359304 | tf_op jit(solution)/shard_map/ppermute | solution.py:319
  275.8 33.9 %collective-permute-start.45 = (bf16[8,48,1920]{2,1,0:T(8,128)(2,1)}, bf16[8,48,1920]{2,1,0:T(8,128)(2,1)}, u32[]{:S(2)}, u32[]{:S(2)}) collective-permute-start(bf16[8,48,1920]{2,1,0:T(8,128)(2,1)} %get-tuple-element.202), channel_id=1, source_target_pairs={{0,2},{2,0},{1,3},{3,1},{4,6},{6,4},{5,7},{7,5},{8,10},{10,8},{9,1... | collective-permute-start | bytes 4423688 | tf_op jit(solution)/shard_map/ppermute | solution.py:319
  279.3 20.3 %collective-permute-start.54 = (bf16[96,1152]{1,0:T(8,128)(2,1)S(1)}, bf16[96,1152]{1,0:T(8,128)(2,1)S(1)}, u32[]{:S(2)}, u32[]{:S(2)}) collective-permute-start(bf16[96,1152]{1,0:T(8,128)(2,1)S(1)} %get-tuple-element.243), channel_id=1, source_target_pairs={{0,16},{8,24},{16,0},{24,8},{1,17},{9,25},{17,1},{25,9},{2,18},{10... | collective-permute-start | bytes 663560 | tf_op jit(solution)/shard_map/ppermute | solution.py:1207
  299.7 27.2 %all-to-all-start.3 = ((bf16[8,80,768]{2,1,0:T(8,128)(2,1)}), bf16[8,80,768]{2,1,0:T(8,128)(2,1)S(1)}, u32[]{:S(2)}, u32[]{:S(2)}) async-start(bf16[8,80,768]{2,1,0:T(8,128)(2,1)} %shard_map.302), calls=%async_computation.3 | async-start | bytes 1966080 | tf_op jit(solution)/shard_map/all_to_all | solution.py:352
  312.3 20.5 %collective-permute-start.46 = (bf16[4,48,1920]{2,1,0:T(8,128)(2,1)}, bf16[4,48,1920]{2,1,0:T(8,128)(2,1)}, u32[]{:S(2)}, u32[]{:S(2)}) collective-permute-start(bf16[4,48,1920]{2,1,0:T(8,128)(2,1)} %dynamic-slice_bitcast_fusion), channel_id=1, source_target_pairs={{0,4},{4,0},{1,5},{5,1},{2,6},{6,2},{3,7},{7,3},{8,12},{12,8},{9,1... | collective-permute-start | bytes 2211848 | tf_op jit(solution)/shard_map/ppermute | solution.py:319
  312.9 44.4 %collective-permute-start.65 = (bf16[96,1536]{1,0:T(8,128)(2,1)}, bf16[96,1536]{1,0:T(8,128)(2,1)}, u32[]{:S(2)}, u32[]{:S(2)}) collective-permute-start(bf16[96,1536]{1,0:T(8,128)(2,1)} %reduce_sum.57.refs_0_), channel_id=1, source_target_pairs={{0,2},{2,0},{1,3},{3,1},{4,6},{6,4},{5,7},{7,5},{8,10},{10,8},{9,1... | collective-permute-start | bytes 884744 | tf_op jit(solution)/shard_map/ppermute | solution.py:319
  357.4 22.2 %collective-permute-start.62 = (bf16[96,1152]{1,0:T(8,128)(2,1)S(1)}, bf16[96,1152]{1,0:T(8,128)(2,1)S(1)}, u32[]{:S(2)}, u32[]{:S(2)}) collective-permute-start(bf16[96,1152]{1,0:T(8,128)(2,1)S(1)} %get-tuple-element.238.row_ref), channel_id=1, source_target_pairs={{0,1},{1,0},{2,3},{3,2},{4,5},{5,4},{6,7},{7,6},{8,9},{9,8},{10,11... | collective-permute-start | bytes 663560 | tf_op jit(solution)/shard_map/ppermute | solution.py:319
  (92 other events, 875.4 us)

commit v9 on v8

--- a/solution.py
+++ b/solution.py
@@ -1292,10 +1292,10 @@
     ffn_z = lax.all_to_all(
         jnp.broadcast_to(ffn_quarter, (4, *ffn_quarter.shape)), "z", 0, 0, tiled=True
     )
-    col_x = swap(col_z, "x")
-    col_last = swap(col_x, "y")
-    col_x, col_y, ffn_z, up = together(col_x, swap(col_z, "y"), ffn_z, up)
-    tokens_far, col_last = together(swap(tokens_x, "c"), col_last)
+    col_x, col_y = swap(col_z, "x"), swap(col_z, "y")
+    col_across = across(col_x, col_y)
+    col_x, col_y, ffn_z, up = together(col_x, col_y, ffn_z, up)
+    tokens_far, *col_across = together(swap(tokens_x, "c"), *col_across)
     ffn_x, ffn_y = swap(ffn_z, "x"), swap(ffn_z, "y")
     ups = [pick(up, z, 0)] + [
         lax.ppermute(pick(up, lax.bitwise_xor(z, i), 0), "z", [(k, k ^ i) for k in range(4)])
@@ -1315,16 +1315,16 @@
     )
     mixed_heads = mixed_heads.reshape(2, count, half)
     col_stacks = [col_z, col_x, col_y]
-    mixed_heads, ffn_x, ffn_y, *rest = together(
-        mixed_heads, ffn_x, ffn_y, *ups, *[swap(value, "c") for value in col_stacks]
-    )
-    ups, col_others = rest[:4], rest[4:]
+    mixed_heads, ffn_x, ffn_y, *col_others = together(
+        mixed_heads, ffn_x, ffn_y, *[swap(value, "c") for value in col_stacks]
+    )
     ups = [jnp.where(z % 2 == 0, a, b) for a, b in zip(ups, (ups[1], ups[0], ups[3], ups[2]))]
     ups = [jnp.where(z < 2, a, b) for a, b in zip(ups, ups[2:] + ups[:2])]
     up = jnp.concatenate(ups)
-    col_stacks, col_others = [*col_stacks, col_last], [*col_others, swap(col_last, "c")]
-    col_pieces = [(step, v, 0) for step, v in zip(steps, col_stacks)]
-    col_pieces = col_pieces + [((j, m, 1), v, 0) for (j, m, _), v in zip(steps, col_others)]
+    col_pieces = [(step, v, 0) for step, v in zip(steps, col_stacks)] + across_pieces(*col_across)
+    col_others = [(step, v, 0) for step, v in zip(steps, col_others)]
+    col_others = col_others + across_pieces(*[swap(v, "c") for v in col_across])
+    col_pieces = col_pieces + [((j, m, 1), v, first) for (j, m, _), v, first in col_others]
     ffn_pieces = [(step, v, 0) for step, v in zip(steps, [ffn_z, ffn_x, ffn_y])]
 
     whole_shape, wide_shape = ((count, width), bf16), ((rows, part, 3 * width), bf16)
@@ -1382,6 +1382,7 @@
     )
     row_got = swap(row_sent, "x")
     far_sum = added(far_part, swap(far_theirs, "c"))
+    far_sum, attn_mine = together(far_sum, attn_mine)
     far_got = swap(far_sum, "x")
     near_got = swap(near_theirs, "c")
     attn_sent, attn_kept = whole_call(

time: 397 us -> 394 us (level)
  waiting for transfers between devices: 133 us -> 122 us
  starting transfers between devices: 73.8 us -> 78.3 us
    ppermute x47 -> x49, waiting for transfers between devices: 66.9 us -> 51.7 us  [swap(): return lax.ppermute(value, axis, PAIR)]
    ppermute x3, starting transfers between devices: 1.47 us -> 7.65 us  [paired_body(): lax.ppermute(pick(up, lax.bitwise_xor(z, i), 0), 'z', [(k, k ^ i) for k i...]
    ppermute x3, waiting for transfers between devices: 4.16 us -> 10.2 us  [paired_body(): lax.ppermute(pick(up, lax.bitwise_xor(z, i), 0), 'z', [(k, k ^ i) for k i...]
    slice x2 -> x4, local copies, waits for them, and re-layouts: 1.14 us -> 5.2 us  [across(): return (swap(over_x[:half], 'y'), swap(over_y[half:], 'x'))]
    ppermute x47 -> x49, starting transfers between devices: 26.5 us -> 27.3 us  [swap(): return lax.ppermute(value, axis, PAIR)]
    unnamed x85 -> x93, local copies, waits for them, and re-layouts: 8.37 us -> 8.74 us
  transfers between devices with their start and end apart: 73 -> 75, of which waited for: 31 -> 30; matrix products, arithmetic and copies ran while one was open for 10% -> 11% of each run, Pallas kernels for 25% -> 25%
where the time goes in v9:
time: 394 us; the launch traced here: 386 us
  Pallas kernels  124 us (31%)
  waiting for transfers between devices  122 us (31%)
  starting transfers between devices  78.3 us (20%)
  local copies, waits for them, and re-layouts  28 us (7%)
  other arithmetic  27.3 us (7%)
  between operations  6.68 us (2%)
    ppermute x49, waiting for transfers between devices, swap(): return lax.ppermute(value, axis, PAIR)  51.7 us
    pallas_call x2, Pallas kernels, column_call(): pl.pallas_call(partial(kernel, plan_of(pieces)), in_specs=[small] * 2 + [...  37.4 us
    ppermute x49, starting transfers between devices, swap(): return lax.ppermute(value, axis, PAIR)  27.3 us
    pallas_call x1, Pallas kernels, feed_forward(): pl.pallas_call(partial(ffn_kernel, plan_of(pieces)), in_specs=[pl.BlockSp...  22.2 us
    ppermute x6, waiting for transfers between devices, gather_turned(): lax.ppermute(pick(column, lax.bitwise_xor(z, i), 0), 'z', [(k, k ^ i) for...  21.8 us
    pallas_call x3, Pallas kernels, whole_call(): pl.pallas_call(kernel, in_specs=[pl.BlockSpec(memory_space=pltpu.SMEM)] +...  17.1 us
    pallas_call x1, Pallas kernels, row_attention_back(): pl.pallas_call(row_bwd_kernel, in_specs=[small, small] + [inside] * 4 + [...  16.1 us
    pallas_call x1, Pallas kernels, row_attention(): pl.pallas_call(partial(row_fwd_kernel, [step for step, _ in tokens], plan...  13.4 us
  transfers between devices with their start and end apart: 75, of which 30 were waited for; matrix products, arithmetic and copies ran while one was open for 11% of the time, Pallas kernels for 25%

profile of v9, /device:TPU:0, one launch (start us, length us, event | category | flops | bytes accessed | tf_op | source)
XLA Modules:
  0.0 386.4 jit_solution(9512395368497357487)
XLA Ops:
  4.3 5.0 %collective-permute-start.3 = (bf16[48,1152]{1,0:T(8,128)(2,1)}, bf16[48,1152]{1,0:T(8,128)(2,1)}, u32[]{:S(2)}, u32[]{:S(2)}) collective-permute-start(bf16[48,1152]{1,0:T(8,128)(2,1)} %fusion.18), channel_id=1, source_target_pairs={{0,24},{8,16},{16,8},{24,0},{1,25},{9,17},{17,9},{25,1},{2,26},{10... | collective-permute-start | bytes 331784 | tf_op jit(solution)/shard_map/ppermute | solution.py:368
  34.8 4.7 %collective-permute-done.7 = bf16[144,768]{1,0:T(8,128)(2,1)S(1)} collective-permute-done((bf16[144,768]{1,0:T(8,128)(2,1)S(1)}, bf16[144,768]{1,0:T(8,128)(2,1)S(1)}, u32[]{:S(2)}, u32[]{:S(2)}) %collective-permute-start.7) | collective-permute-done | bytes 221216 | tf_op jit(solution)/shard_map/ppermute | solution.py:1275
  39.6 5.5 %collective-permute-done.8 = bf16[144,768]{1,0:T(8,128)(2,1)S(1)} collective-permute-done((bf16[144,768]{1,0:T(8,128)(2,1)S(1)}, bf16[144,768]{1,0:T(8,128)(2,1)S(1)}, u32[]{:S(2)}, u32[]{:S(2)}) %collective-permute-start.8) | collective-permute-done | bytes 221216 | tf_op jit(solution)/shard_map/ppermute | solution.py:1275
  55.9 6.0 %collective-permute-done.15 = bf16[5,48,384]{2,1,0:T(8,128)(2,1)} collective-permute-done((bf16[5,48,384]{2,1,0:T(8,128)(2,1)S(1)}, bf16[5,48,384]{2,1,0:T(8,128)(2,1)}, u32[]{:S(2)}, u32[]{:S(2)}) %collective-permute-start.15) | collective-permute-done | bytes 184352 | tf_op jit(solution)/shard_map/ppermute | solution.py:368
  73.1 13.2 %collective-permute-done.18.refs_2_ = bf16[4,5,48,384]{3,2,1,0:T(8,128)(2,1)} collective-permute-done((bf16[4,5,48,384]{3,2,1,0:T(8,128)(2,1)}, bf16[4,5,48,384]{3,2,1,0:T(8,128)(2,1)}, u32[]{:S(2)}, u32[]{:S(2)}) %collective-permute-start.18) | collective-permute-done | bytes 737312 | tf_op jit(solution)/shard_map/ppermute | solution.py:319
  108.3 7.6 %collective-permute-done.33 = bf16[2,64,768]{2,1,0:T(8,128)(2,1)S(1)} collective-permute-done((bf16[2,64,768]{2,1,0:T(8,128)(2,1)}, bf16[2,64,768]{2,1,0:T(8,128)(2,1)S(1)}, u32[]{:S(2)}, u32[]{:S(2)}) %collective-permute-start.33) | collective-permute-done | bytes 196640 | tf_op jit(solution)/shard_map/ppermute | solution.py:1301
  115.9 13.4 %shard_map.295 = (bf16[512,768]{1,0:T(8,128)(2,1)}, bf16[1024,768]{1,0:T(8,128)(2,1)}, bf16[1024,768]{1,0:T(8,128)(2,1)}, bf16[768,1152]{1,0:T(8,128)(2,1)}, f32...) custom-call(s32[4]{0:T(128)} %pad_add_fusion.1.place_ref, ...), custom_call_target="tpu_custom_call" | custom-call | flops 7539999744 | tf_op jit(solution)/shard_map/pallas_call | solution.py:709
  138.7 14.4 %shard_map.296 = (bf16[512,2304]{1,0:T(8,128)(2,1)}, bf16[512,768]{1,0:T(8,128)(2,1)}, bf16[8,64,2304]{2,1,0:T(8,128)(2,1)}, f32[512,768]{1,0:T(8,128)}, bf16[512,768]{1,0:T(8,128)(2,1)}) custom-call(s32[6]{0:T(128)} %concatenate.37.info_ref, s32[4]{0:T(128)} %pad_add_fusion.1.place_ref, bf16[4,5,48,384]{3,2,1,0:T(8,128)(2,1)} %pad_maximum_fusion.3.refs_0_, ...), custom_call_target="tpu_custom_call" | custom-call | flops 8120000000 | tf_op jit(solution)/shard_map/pallas_call | solution.py:988
  156.6 22.2 %shard_map.297 = (f32[512,768]{1,0:T(8,128)}, f32[512,768]{1,0:T(8,128)}, bf16[2,512,768]{2,1,0:T(8,128)(2,1)}, bf16[768,768]{1,0:T(8,128)(2,1)}, bf16[768,768]{...) custom-call(s32[4]{0:T(128)} %pad_add_fusion.1.place_ref, ...), custom_call_target="tpu_custom_call" | custom-call | flops 12760000512 | tf_op jit(solution)/shard_map/pallas_call | solution.py:1184
  183.7 23.0 %shard_map.298 = (bf16[512,768]{1,0:T(8,128)(2,1)}, bf16[512,768]{1,0:T(8,128)(2,1)}, bf16[512,384]{1,0:T(8,128)(2,1)}, bf16[512,384]{1,0:T(8,128)(2,1)}, bf16[5...) custom-call(s32[6]{0:T(128)} %concatenate.37.info_ref, s32[4]{0:T(128)} %pad_add_fusion.1.place_ref, ...), custom_call_target="tpu_custom_call" | custom-call | flops 13340000256 | tf_op jit(solution)/shard_map/pallas_call | solution.py:988
  219.8 16.1 %shard_map.299 = (f32[512,768]{1,0:T(8,128)}, bf16[512,768]{1,0:T(8,128)(2,1)}, f32[512,768]{1,0:T(8,128)}, bf16[512,768]{1,0:T(8,128)(2,1)}, bf16[4,96,1152]{2,...) custom-call(s32[6]{0:T(128)} %concatenate.37.info_ref, f32[1]{0:T(128)} %bitcast.39.tie_ref, ...), custom_call_target="tpu_custom_call" | custom-call | flops 9280000000 | tf_op jit(solution)/shard_map/pallas_call | solution.py:735
  237.5 4.9 %all-to-all-start.2 = ((bf16[4,96,1536]{2,1,0:T(8,128)(2,1)}), bf16[4,96,1536]{2,1,0:T(8,128)(2,1)S(1)}, u32[]{:S(2)}, u32[]{:S(2)}) async-start(bf16[4,96,1536]{2,1,0:T(8,128)(2,1)} %pad_maximum_fusion), calls=%async_computation.2 | async-start | bytes 2359296 | tf_op jit(solution)/shard_map/all_to_all | solution.py:1396
  247.9 9.4 %shard_map.301 = (bf16[8,48,1920]{2,1,0:T(8,128)(2,1)}, bf16[8,48,1920]{2,1,0:T(8,128)(2,1)}) custom-call(s32[4]{0:T(128)} %pad_add_fusion.1.place_ref, bf16[512,2304]{1,0:T(8,128)(2,1)} %get-tuple-element.153.acts_ref, bf16[512,2304]{1,0:T(8,128)(2,1)} %collective-permute-done.31.got_ref, bf16[512,1920]{1,0:T(8,128)(2,1)} %get-tuple-element.191.mine_ref, ...), custom_call_target="tpu_custom_call" | custom-call | flops 5219999744 | tf_op jit(solution)/shard_map/pallas_call | solution.py:1105
  257.3 8.1 %collective-permute-done.47 = bf16[4,96,1152]{2,1,0:T(8,128)(2,1)} collective-permute-done((bf16[4,96,1152]{2,1,0:T(8,128)(2,1)}, bf16[4,96,1152]{2,1,0:T(8,128)(2,1)}, u32[]{:S(2)}, u32[]{:S(2)}) %collective-permute-start.47) | collective-permute-done | bytes 884768 | tf_op jit(solution)/shard_map/ppermute | solution.py:319
  265.4 6.1 %all-to-all-done.2 = bf16[4,96,1536]{2,1,0:T(8,128)(2,1)S(1)} async-done(((bf16[4,96,1536]{2,1,0:T(8,128)(2,1)}), bf16[4,96,1536]{2,1,0:T(8,128)(2,1)S(1)}, u32[]{:S(2)}, u32[]{:S(2)}) %all-to-all-start.2) | async-done | bytes 1179680 | tf_op jit(solution)/shard_map/all_to_all | solution.py:1396
  281.7 5.5 %shard_map.302 = bf16[8,80,768]{2,1,0:T(8,128)(2,1)} custom-call(s32[6]{0:T(128)} %concatenate.37.info_ref, f32[512,768]{1,0:T(8,128)} %get-tuple-element.206.near_ref, bf16[512,768]{1,0:T(8,128)(2,1)} %collective-permute-done.53.near_got_ref, bf16[512,768]{1,0:T(8,128)(2,1)} %collective-permute-done.54.far_got_ref, ...), custom_call_target="tpu_custom_call" | custom-call | flops 2900000000 | tf_op jit(solution)/shard_map/pallas_call | solution.py:1105
  288.0 9.2 %collective-permute-done.56 = bf16[96,1152]{1,0:T(8,128)(2,1)S(1)} collective-permute-done((bf16[96,1152]{1,0:T(8,128)(2,1)S(1)}, bf16[96,1152]{1,0:T(8,128)(2,1)S(1)}, u32[]{:S(2)}, u32[]{:S(2)}) %collective-permute-start.56) | collective-permute-done | bytes 221216 | tf_op jit(solution)/shard_map/ppermute | solution.py:1207
  301.0 5.3 %collective-permute-done.48 = bf16[8,48,1920]{2,1,0:T(8,128)(2,1)} collective-permute-done((bf16[8,48,1920]{2,1,0:T(8,128)(2,1)}, bf16[8,48,1920]{2,1,0:T(8,128)(2,1)}, u32[]{:S(2)}, u32[]{:S(2)}) %collective-permute-start.48) | collective-permute-done | bytes 1474592 | tf_op jit(solution)/shard_map/ppermute | solution.py:319
  314.3 7.3 %collective-permute-done.58 = bf16[96,1152]{1,0:T(8,128)(2,1)S(1)} collective-permute-done((bf16[96,1152]{1,0:T(8,128)(2,1)S(1)}, bf16[96,1152]{1,0:T(8,128)(2,1)S(1)}, u32[]{:S(2)}, u32[]{:S(2)}) %collective-permute-start.58) | collective-permute-done | bytes 221216 | tf_op jit(solution)/shard_map/ppermute | solution.py:319
  325.9 4.5 %collective-permute-done.49 = bf16[4,48,1920]{2,1,0:T(8,128)(2,1)} collective-permute-done((bf16[4,48,1920]{2,1,0:T(8,128)(2,1)}, bf16[4,48,1920]{2,1,0:T(8,128)(2,1)}, u32[]{:S(2)}, u32[]{:S(2)}) %collective-permute-start.49) | collective-permute-done | bytes 737312 | tf_op jit(solution)/shard_map/ppermute | solution.py:319
  341.9 8.0 %collective-permute-done.51.refs_1_ = bf16[48,1920]{1,0:T(8,128)(2,1)S(1)} collective-permute-done((bf16[48,1920]{1,0:T(8,128)(2,1)S(1)}, bf16[48,1920]{1,0:T(8,128)(2,1)S(1)}, u32[]{:S(2)}, u32[]{:S(2)}) %collective-permute-start.51) | collective-permute-done | bytes 184352 | tf_op jit(solution)/shard_map/ppermute | solution.py:1207
  360.1 5.8 %all-to-all-done.4.squares_ref = f32[32,8,128]{2,1,0:T(8,128)S(1)} async-done(((f32[32,8,128]{2,1,0:T(8,128)}), f32[32,8,128]{2,1,0:T(8,128)S(1)}, u32[]{:S(2)}, u32[]{:S(2)}) %all-to-all-start.4) | async-done | bytes 131104 | tf_op jit(solution)/shard_map/all_to_all | solution.py:1439
  368.1 7.8 %shard_map.305 = (f32[96,3072]{1,0:T(8,128)}, f32[96,3072]{1,0:T(8,128)}, f32[96,3072]{1,0:T(8,128)}, bf16[96,3072]{1,0:T(8,128)(2,1)}, f32[96,3072]{1,0:T(8,128...) custom-call(s32[4]{0:T(128)} %pad_add_fusion.1.place_ref, f32[32,8,128]{2,1,0:T(8,128)} %copy-done.3, ...), custom_call_target="tpu_custom_call" | custom-call | tf_op jit(solution)/shard_map/pallas_call | solution.py:1093
  379.2 5.6 %shard_map.304 = (f32[8,96,768]{2,1,0:T(8,128)}, f32[8,96,768]{2,1,0:T(8,128)}, f32[8,96,768]{2,1,0:T(8,128)}, bf16[8,96,768]{2,1,0:T(8,128)(2,1)}) custom-call(s32[4]{0:T(128)S(1)} %copy-done.5, f32[32,8,128]{2,1,0:T(8,128)S(1)} %copy-done.4, bf16[96,1152]{1,0:T(8,128)(2,1)S(1)} %get-tuple-element.236.row_ref, ...), custom_call_target="tpu_custom_call" | custom-call | tf_op jit(solution)/shard_map/pallas_call | solution.py:1053
  (311 shorter events, 161.0 us)
Async XLA Ops:
  31.3 19.8 %collective-permute-start.13 = (bf16[4,64,768]{2,1,0:T(8,128)(2,1)}, bf16[4,64,768]{2,1,0:T(8,128)(2,1)}, u32[]{:S(2)}, u32[]{:S(2)}) collective-permute-start(bf16[4,64,768]{2,1,0:T(8,128)(2,1)} %get-tuple-element.256), channel_id=1, source_target_pairs={{0,4},{4,0},{1,5},{5,1},{2,6},{6,2},{3,7},{7,3},{8,12},{12,8},{9,1... | collective-permute-start | bytes 1179656 | tf_op jit(solution)/shard_map/ppermute | solution.py:319
  64.8 29.8 %all-to-all-start = ((bf16[4,96,1536]{2,1,0:T(8,128)(2,1)}), bf16[4,96,1536]{2,1,0:T(8,128)(2,1)S(1)}, u32[]{:S(2)}, u32[]{:S(2)}) async-start(bf16[4,96,1536]{2,1,0:T(8,128)(2,1)} %broadcast_in_dim.39), calls=%async_computation | async-start | bytes 2359296 | tf_op jit(solution)/shard_map/all_to_all | solution.py:1292
  71.8 24.1 %collective-permute-start.22 = (bf16[4,144,768]{2,1,0:T(8,128)(2,1)S(1)}, bf16[4,144,768]{2,1,0:T(8,128)(2,1)}, u32[]{:S(2)}, u32[]{:S(2)}) collective-permute-start(bf16[4,144,768]{2,1,0:T(8,128)(2,1)S(1)} %pad_maximum_fusion.1.refs_0_), channel_id=1, source_target_pairs={{0,1},{1,0},{2,3},{3,2},{4,5},{5,4},{6,7},{7,6},{8,9},{9,8},{10,11... | collective-permute-start | bytes 2654216 | tf_op jit(solution)/shard_map/ppermute | solution.py:319
  71.8 24.6 %collective-permute-start.19 = (bf16[4,144,768]{2,1,0:T(8,128)(2,1)}, bf16[4,144,768]{2,1,0:T(8,128)(2,1)}, u32[]{:S(2)}, u32[]{:S(2)}) collective-permute-start(bf16[4,144,768]{2,1,0:T(8,128)(2,1)} %collective-permute-done.10.refs_1_), channel_id=1, source_target_pairs={{0,1},{1,0},{2,3},{3,2},{4,5},{5,4},{6,7},{7,6},{8,9},{9,8},{10,11... | collective-permute-start | bytes 2654216 | tf_op jit(solution)/shard_map/ppermute | solution.py:319
  94.5 35.5 %collective-permute-start.24 = (bf16[4,96,1536]{2,1,0:T(8,128)(2,1)S(1)}, bf16[4,96,1536]{2,1,0:T(8,128)(2,1)}, u32[]{:S(2)}, u32[]{:S(2)}) collective-permute-start(bf16[4,96,1536]{2,1,0:T(8,128)(2,1)S(1)} %all-to-all-done.refs_0_), channel_id=1, source_target_pairs={{0,2},{2,0},{1,3},{3,1},{4,6},{6,4},{5,7},{7,5},{8,10},{10,8},{9,1... | collective-permute-start | bytes 3538952 | tf_op jit(solution)/shard_map/ppermute | solution.py:319
  95.9 34.2 %collective-permute-start.23 = (bf16[4,96,1536]{2,1,0:T(8,128)(2,1)S(1)}, bf16[4,96,1536]{2,1,0:T(8,128)(2,1)}, u32[]{:S(2)}, u32[]{:S(2)}) collective-permute-start(bf16[4,96,1536]{2,1,0:T(8,128)(2,1)S(1)} %all-to-all-done.refs_0_), channel_id=1, source_target_pairs={{0,4},{4,0},{1,5},{5,1},{2,6},{6,2},{3,7},{7,3},{8,12},{12,8},{9,1... | collective-permute-start | bytes 3538952 | tf_op jit(solution)/shard_map/ppermute | solution.py:319
  105.7 23.7 %collective-permute-start.25 = (bf16[4,5,48,384]{3,2,1,0:T(8,128)(2,1)}, bf16[4,5,48,384]{3,2,1,0:T(8,128)(2,1)S(1)}, u32[]{:S(2)}, u32[]{:S(2)}) collective-permute-start(bf16[4,5,48,384]{3,2,1,0:T(8,128)(2,1)} %pad_maximum_fusion.3.refs_0_), channel_id=1, source_target_pairs={{0,1},{1,0},{2,3},{3,2},{4,5},{5,4},{6,7},{7,6},{8,9},{9,8},{10,11... | collective-permute-start | bytes 2211848 | tf_op jit(solution)/shard_map/ppermute | solution.py:319
  108.2 21.7 %collective-permute-start.26 = (bf16[4,5,48,384]{3,2,1,0:T(8,128)(2,1)}, bf16[4,5,48,384]{3,2,1,0:T(8,128)(2,1)S(1)}, u32[]{:S(2)}, u32[]{:S(2)}) collective-permute-start(bf16[4,5,48,384]{3,2,1,0:T(8,128)(2,1)} %collective-permute-done.17.refs_1_), channel_id=1, source_target_pairs={{0,1},{1,0},{2,3},{3,2},{4,5},{5,4},{6,7},{7,6},{8,9},{9,8},{10,11... | collective-permute-start | bytes 2211848 | tf_op jit(solution)/shard_map/ppermute | solution.py:319
  132.3 20.8 %collective-permute-start.38 = (bf16[512,768]{1,0:T(8,128)(2,1)S(1)}, bf16[512,768]{1,0:T(8,128)(2,1)S(1)}, u32[]{:S(2)}, u32[]{:S(2)}) collective-permute-start(bf16[512,768]{1,0:T(8,128)(2,1)S(1)} %bitcast_select_fusion.up_ref.refs_10_), channel_id=1, source_target_pairs={{0,1},{1,0},{2,3},{3,2},{4,5},{5,4},{6,7},{7,6},{8,9},{9,8},{10,11... | collective-permute-start | bytes 2359304 | tf_op jit(solution)/shard_map/ppermute | solution.py:319
  179.0 28.5 %collective-permute-start.41 = (bf16[4,2,96,768]{3,2,1,0:T(8,128)(2,1)}, bf16[4,2,96,768]{3,2,1,0:T(8,128)(2,1)S(1)}, u32[]{:S(2)}, u32[]{:S(2)}) collective-permute-start(bf16[4,2,96,768]{3,2,1,0:T(8,128)(2,1)} %get-tuple-element.180), channel_id=1, source_target_pairs={{0,4},{4,0},{1,5},{5,1},{2,6},{6,2},{3,7},{7,3},{8,12},{12,8},{9,1... | collective-permute-start | bytes 3538952 | tf_op jit(solution)/shard_map/ppermute | solution.py:319
  179.6 28.2 %collective-permute-start.42 = (bf16[768,768]{1,0:T(8,128)(2,1)}, bf16[768,768]{1,0:T(8,128)(2,1)S(1)}, u32[]{:S(2)}, u32[]{:S(2)}) collective-permute-start(bf16[768,768]{1,0:T(8,128)(2,1)} %get-tuple-element.181), channel_id=1, source_target_pairs={{0,2},{2,0},{1,3},{3,1},{4,6},{6,4},{5,7},{7,5},{8,10},{10,8},{9,1... | collective-permute-start | bytes 3538952 | tf_op jit(solution)/shard_map/ppermute | solution.py:319
  207.7 28.3 %all-to-all-start.1 = ((bf16[8,64,768]{2,1,0:T(8,128)(2,1)}), bf16[8,64,768]{2,1,0:T(8,128)(2,1)S(1)}, u32[]{:S(2)}, u32[]{:S(2)}) async-start(bf16[8,64,768]{2,1,0:T(8,128)(2,1)} %bitcast.145), calls=%async_computation.1 | async-start | bytes 1572864 | tf_op jit(solution)/shard_map/all_to_all | solution.py:352
  211.6 36.3 %collective-permute-start.31 = (bf16[512,2304]{1,0:T(8,128)(2,1)}, bf16[512,2304]{1,0:T(8,128)(2,1)}, u32[]{:S(2)}, u32[]{:S(2)}) collective-permute-start(bf16[512,2304]{1,0:T(8,128)(2,1)} %get-tuple-element.153.acts_ref), channel_id=1, source_target_pairs={{0,1},{1,0},{2,3},{3,2},{4,5},{5,4},{6,7},{7,6},{8,9},{9,8},{10,11... | collective-permute-start | bytes 7077896 | tf_op jit(solution)/shard_map/ppermute | solution.py:319
  216.4 19.5 %collective-permute-start.43 = (bf16[4,96,768]{2,1,0:T(8,128)(2,1)}, bf16[4,96,768]{2,1,0:T(8,128)(2,1)S(1)}, u32[]{:S(2)}, u32[]{:S(2)}) collective-permute-start(bf16[4,96,768]{2,1,0:T(8,128)(2,1)} %get-tuple-element.187), channel_id=1, source_target_pairs={{0,4},{4,0},{1,5},{5,1},{2,6},{6,2},{3,7},{7,3},{8,12},{12,8},{9,1... | collective-permute-start | bytes 1769480 | tf_op jit(solution)/shard_map/ppermute | solution.py:319
  237.5 34.0 %all-to-all-start.2 = ((bf16[4,96,1536]{2,1,0:T(8,128)(2,1)}), bf16[4,96,1536]{2,1,0:T(8,128)(2,1)S(1)}, u32[]{:S(2)}, u32[]{:S(2)}) async-start(bf16[4,96,1536]{2,1,0:T(8,128)(2,1)} %pad_maximum_fusion), calls=%async_computation.2 | async-start | bytes 2359296 | tf_op jit(solution)/shard_map/all_to_all | solution.py:1396
  242.6 22.8 %collective-permute-start.47 = (bf16[4,96,1152]{2,1,0:T(8,128)(2,1)}, bf16[4,96,1152]{2,1,0:T(8,128)(2,1)}, u32[]{:S(2)}, u32[]{:S(2)}) collective-permute-start(bf16[4,96,1152]{2,1,0:T(8,128)(2,1)} %get-tuple-element.199), channel_id=1, source_target_pairs={{0,4},{4,0},{1,5},{5,1},{2,6},{6,2},{3,7},{7,3},{8,12},{12,8},{9,1... | collective-permute-start | bytes 2654216 | tf_op jit(solution)/shard_map/ppermute | solution.py:319
  243.1 33.7 %collective-permute-start.53 = (bf16[512,768]{1,0:T(8,128)(2,1)}, bf16[512,768]{1,0:T(8,128)(2,1)}, u32[]{:S(2)}, u32[]{:S(2)}) collective-permute-start(bf16[512,768]{1,0:T(8,128)(2,1)} %get-tuple-element.207), channel_id=1, source_target_pairs={{0,1},{1,0},{2,3},{3,2},{4,5},{5,4},{6,7},{7,6},{8,9},{9,8},{10,11... | collective-permute-start | bytes 2359304 | tf_op jit(solution)/shard_map/ppermute | solution.py:319
  247.4 34.3 %collective-permute-start.54 = (bf16[512,768]{1,0:T(8,128)(2,1)}, bf16[512,768]{1,0:T(8,128)(2,1)}, u32[]{:S(2)}, u32[]{:S(2)}) collective-permute-start(bf16[512,768]{1,0:T(8,128)(2,1)} %add_convert_fusion.2), channel_id=1, source_target_pairs={{0,4},{4,0},{1,5},{5,1},{2,6},{6,2},{3,7},{7,3},{8,12},{12,8},{9,1... | collective-permute-start | bytes 2359304 | tf_op jit(solution)/shard_map/ppermute | solution.py:319
  272.5 33.9 %collective-permute-start.48 = (bf16[8,48,1920]{2,1,0:T(8,128)(2,1)}, bf16[8,48,1920]{2,1,0:T(8,128)(2,1)}, u32[]{:S(2)}, u32[]{:S(2)}) collective-permute-start(bf16[8,48,1920]{2,1,0:T(8,128)(2,1)} %get-tuple-element.201), channel_id=1, source_target_pairs={{0,2},{2,0},{1,3},{3,1},{4,6},{6,4},{5,7},{7,5},{8,10},{10,8},{9,1... | collective-permute-start | bytes 4423688 | tf_op jit(solution)/shard_map/ppermute | solution.py:319
  276.9 20.3 %collective-permute-start.56 = (bf16[96,1152]{1,0:T(8,128)(2,1)S(1)}, bf16[96,1152]{1,0:T(8,128)(2,1)S(1)}, u32[]{:S(2)}, u32[]{:S(2)}) collective-permute-start(bf16[96,1152]{1,0:T(8,128)(2,1)S(1)} %get-tuple-element.245), channel_id=1, source_target_pairs={{0,16},{8,24},{16,0},{24,8},{1,17},{9,25},{17,1},{25,9},{2,18},{10... | collective-permute-start | bytes 663560 | tf_op jit(solution)/shard_map/ppermute | solution.py:1207
  297.3 26.7 %all-to-all-start.3 = ((bf16[8,80,768]{2,1,0:T(8,128)(2,1)}), bf16[8,80,768]{2,1,0:T(8,128)(2,1)S(1)}, u32[]{:S(2)}, u32[]{:S(2)}) async-start(bf16[8,80,768]{2,1,0:T(8,128)(2,1)} %shard_map.302), calls=%async_computation.3 | async-start | bytes 1966080 | tf_op jit(solution)/shard_map/all_to_all | solution.py:352
  309.0 21.3 %collective-permute-start.49 = (bf16[4,48,1920]{2,1,0:T(8,128)(2,1)}, bf16[4,48,1920]{2,1,0:T(8,128)(2,1)}, u32[]{:S(2)}, u32[]{:S(2)}) collective-permute-start(bf16[4,48,1920]{2,1,0:T(8,128)(2,1)} %dynamic-slice_bitcast_fusion), channel_id=1, source_target_pairs={{0,4},{4,0},{1,5},{5,1},{2,6},{6,2},{3,7},{7,3},{8,12},{12,8},{9,1... | collective-permute-start | bytes 2211848 | tf_op jit(solution)/shard_map/ppermute | solution.py:319
  309.6 44.7 %collective-permute-start.67 = (bf16[96,1536]{1,0:T(8,128)(2,1)}, bf16[96,1536]{1,0:T(8,128)(2,1)}, u32[]{:S(2)}, u32[]{:S(2)}) collective-permute-start(bf16[96,1536]{1,0:T(8,128)(2,1)} %reduce_sum.57.refs_0_), channel_id=1, source_target_pairs={{0,2},{2,0},{1,3},{3,1},{4,6},{6,4},{5,7},{7,5},{8,10},{10,8},{9,1... | collective-permute-start | bytes 884744 | tf_op jit(solution)/shard_map/ppermute | solution.py:319
  354.3 22.3 %collective-permute-start.64 = (bf16[96,1152]{1,0:T(8,128)(2,1)S(1)}, bf16[96,1152]{1,0:T(8,128)(2,1)S(1)}, u32[]{:S(2)}, u32[]{:S(2)}) collective-permute-start(bf16[96,1152]{1,0:T(8,128)(2,1)S(1)} %get-tuple-element.236.row_ref), channel_id=1, source_target_pairs={{0,1},{1,0},{2,3},{3,2},{4,5},{5,4},{6,7},{7,6},{8,9},{9,8},{10,11... | collective-permute-start | bytes 663560 | tf_op jit(solution)/shard_map/ppermute | solution.py:319
  (98 other events, 899.9 us)

commit v10 on v9

--- a/solution.py
+++ b/solution.py
@@ -1297,10 +1297,7 @@
     col_x, col_y, ffn_z, up = together(col_x, col_y, ffn_z, up)
     tokens_far, *col_across = together(swap(tokens_x, "c"), *col_across)
     ffn_x, ffn_y = swap(ffn_z, "x"), swap(ffn_z, "y")
-    ups = [pick(up, z, 0)] + [
-        lax.ppermute(pick(up, lax.bitwise_xor(z, i), 0), "z", [(k, k ^ i) for k in range(4)])
-        for i in (1, 2, 3)
-    ]
+    up = lax.all_to_all(up, "z", 0, 0, tiled=True)
 
     rows = 8
     count = rows * part
@@ -1318,9 +1315,7 @@
     mixed_heads, ffn_x, ffn_y, *col_others = together(
         mixed_heads, ffn_x, ffn_y, *[swap(value, "c") for value in col_stacks]
     )
-    ups = [jnp.where(z % 2 == 0, a, b) for a, b in zip(ups, (ups[1], ups[0], ups[3], ups[2]))]
-    ups = [jnp.where(z < 2, a, b) for a, b in zip(ups, ups[2:] + ups[:2])]
-    up = jnp.concatenate(ups)
+    up = up.reshape(rows, part, width)
     col_pieces = [(step, v, 0) for step, v in zip(steps, col_stacks)] + across_pieces(*col_across)
     col_others = [(step, v, 0) for step, v in zip(steps, col_others)]
     col_others = col_others + across_pieces(*[swap(v, "c") for v in col_across])

time: 394 us -> 392 us (level)
  waiting for transfers between devices: 122 us -> 126 us
    ppermute x49, waiting for transfers between devices: 51.7 us -> 65.5 us  [swap(): return lax.ppermute(value, axis, PAIR)]
    ppermute x3 -> x0, waiting for transfers between devices: 10.2 us -> none  [paired_body(): lax.ppermute(pick(up, lax.bitwise_xor(z, i), 0), 'z', [(k, k ^ i) for k i...]
    ppermute x3 -> x0, starting transfers between devices: 7.65 us -> none  [paired_body(): lax.ppermute(pick(up, lax.bitwise_xor(z, i), 0), 'z', [(k, k ^ i) for k i...]
    all_to_all x0 -> x1, starting transfers between devices: none -> 5.1 us  [paired_body(): up = lax.all_to_all(up, 'z', 0, 0, tiled=True)]
    slice x4, local copies, waits for them, and re-layouts: 5.2 us -> 1.22 us  [across(): return (swap(over_x[:half], 'y'), swap(over_y[half:], 'x'))]
    unnamed x93 -> x87, local copies, waits for them, and re-layouts: 8.74 us -> 8.15 us
  transfers between devices with their start and end apart: 75 -> 73, of which waited for: 30 -> 31; matrix products, arithmetic and copies ran while one was open for 11% -> 10% of each run, Pallas kernels for 25% -> 25%
where the time goes in v10:
time: 392 us; the launch traced here: 385 us
  waiting for transfers between devices  126 us (32%)
  Pallas kernels  124 us (32%)
  starting transfers between devices  77.6 us (20%)
  other arithmetic  26.9 us (7%)
  local copies, waits for them, and re-layouts  24.1 us (6%)
  between operations  6.57 us (2%)
    ppermute x49, waiting for transfers between devices, swap(): return lax.ppermute(value, axis, PAIR)  65.5 us
    pallas_call x2, Pallas kernels, column_call(): pl.pallas_call(partial(kernel, plan_of(pieces)), in_specs=[small] * 2 + [...  37.3 us
    ppermute x49, starting transfers between devices, swap(): return lax.ppermute(value, axis, PAIR)  27.1 us
    pallas_call x1, Pallas kernels, feed_forward(): pl.pallas_call(partial(ffn_kernel, plan_of(pieces)), in_specs=[pl.BlockSp...  22.2 us
    ppermute x6, waiting for transfers between devices, gather_turned(): lax.ppermute(pick(column, lax.bitwise_xor(z, i), 0), 'z', [(k, k ^ i) for...  21.2 us
    pallas_call x3, Pallas kernels, whole_call(): pl.pallas_call(kernel, in_specs=[pl.BlockSpec(memory_space=pltpu.SMEM)] +...  17.1 us
    pallas_call x1, Pallas kernels, row_attention_back(): pl.pallas_call(row_bwd_kernel, in_specs=[small, small] + [inside] * 4 + [...  16.1 us
    pallas_call x1, Pallas kernels, row_attention(): pl.pallas_call(partial(row_fwd_kernel, [step for step, _ in tokens], plan...  13.4 us
  transfers between devices with their start and end apart: 73, of which 31 were waited for; matrix products, arithmetic and copies ran while one was open for 10% of the time, Pallas kernels for 25%

profile of v10, /device:TPU:0, one launch (start us, length us, event | category | flops | bytes accessed | tf_op | source)
XLA Modules:
  0.0 384.9 jit_solution(9428466966105123627)
XLA Ops:
  4.3 5.0 %collective-permute-start.3 = (bf16[48,1152]{1,0:T(8,128)(2,1)}, bf16[48,1152]{1,0:T(8,128)(2,1)}, u32[]{:S(2)}, u32[]{:S(2)}) collective-permute-start(bf16[48,1152]{1,0:T(8,128)(2,1)} %fusion.18), channel_id=1, source_target_pairs={{0,24},{8,16},{16,8},{24,0},{1,25},{9,17},{17,9},{25,1},{2,26},{10... | collective-permute-start | bytes 331784 | tf_op jit(solution)/shard_map/ppermute | solution.py:368
  34.7 4.7 %collective-permute-done.7 = bf16[144,768]{1,0:T(8,128)(2,1)S(1)} collective-permute-done((bf16[144,768]{1,0:T(8,128)(2,1)S(1)}, bf16[144,768]{1,0:T(8,128)(2,1)S(1)}, u32[]{:S(2)}, u32[]{:S(2)}) %collective-permute-start.7) | collective-permute-done | bytes 221216 | tf_op jit(solution)/shard_map/ppermute | solution.py:1275
  39.5 5.5 %collective-permute-done.8 = bf16[144,768]{1,0:T(8,128)(2,1)S(1)} collective-permute-done((bf16[144,768]{1,0:T(8,128)(2,1)S(1)}, bf16[144,768]{1,0:T(8,128)(2,1)S(1)}, u32[]{:S(2)}, u32[]{:S(2)}) %collective-permute-start.8) | collective-permute-done | bytes 221216 | tf_op jit(solution)/shard_map/ppermute | solution.py:1275
  55.8 5.9 %collective-permute-done.15 = bf16[5,48,384]{2,1,0:T(8,128)(2,1)S(1)} collective-permute-done((bf16[5,48,384]{2,1,0:T(8,128)(2,1)S(1)}, bf16[5,48,384]{2,1,0:T(8,128)(2,1)S(1)}, u32[]{:S(2)}, u32[]{:S(2)}) %collective-permute-start.15) | collective-permute-done | bytes 184352 | tf_op jit(solution)/shard_map/ppermute | solution.py:368
  71.3 17.5 %collective-permute-done.18.refs_2_ = bf16[4,5,48,384]{3,2,1,0:T(8,128)(2,1)S(1)} collective-permute-done((bf16[4,5,48,384]{3,2,1,0:T(8,128)(2,1)}, bf16[4,5,48,384]{3,2,1,0:T(8,128)(2,1)S(1)}, u32[]{:S(2)}, u32[]{:S(2)}) %collective-permute-start.18) | collective-permute-done | bytes 737312 | tf_op jit(solution)/shard_map/ppermute | solution.py:319
  103.7 5.1 %all-to-all-start.1 = ((bf16[4,2,64,768]{3,2,1,0:T(8,128)(2,1)}), bf16[4,2,64,768]{3,2,1,0:T(8,128)(2,1)S(1)}, u32[]{:S(2)}, u32[]{:S(2)}) async-start(bf16[4,2,64,768]{3,2,1,0:T(8,128)(2,1)} %maximum_select_fusion.2), calls=%async_computation.1 | async-start | bytes 1572864 | tf_op jit(solution)/shard_map/all_to_all | solution.py:1300
  108.9 13.4 %shard_map.295 = (bf16[512,768]{1,0:T(8,128)(2,1)}, bf16[1024,768]{1,0:T(8,128)(2,1)}, bf16[1024,768]{1,0:T(8,128)(2,1)}, bf16[768,1152]{1,0:T(8,128)(2,1)}, f32...) custom-call(s32[4]{0:T(128)} %pad_add_fusion.1.place_ref, ...), custom_call_target="tpu_custom_call" | custom-call | flops 7539999744 | tf_op jit(solution)/shard_map/pallas_call | solution.py:709
  134.1 14.3 %shard_map.296 = (bf16[512,2304]{1,0:T(8,128)(2,1)}, bf16[512,768]{1,0:T(8,128)(2,1)}, bf16[8,64,2304]{2,1,0:T(8,128)(2,1)}, f32[512,768]{1,0:T(8,128)}, bf16[512,768]{1,0:T(8,128)(2,1)}) custom-call(s32[6]{0:T(128)} %concatenate.32.info_ref, s32[4]{0:T(128)} %pad_add_fusion.1.place_ref, bf16[4,5,48,384]{3,2,1,0:T(8,128)(2,1)} %pad_maximum_fusion.2.refs_0_, ...), custom_call_target="tpu_custom_call" | custom-call | flops 8120000000 | tf_op jit(solution)/shard_map/pallas_call | solution.py:988
  152.1 22.2 %shard_map.297 = (f32[512,768]{1,0:T(8,128)}, f32[512,768]{1,0:T(8,128)}, bf16[2,512,768]{2,1,0:T(8,128)(2,1)}, bf16[768,768]{1,0:T(8,128)(2,1)}, bf16[768,768]{...) custom-call(s32[4]{0:T(128)} %pad_add_fusion.1.place_ref, ...), custom_call_target="tpu_custom_call" | custom-call | flops 12760000512 | tf_op jit(solution)/shard_map/pallas_call | solution.py:1184
  179.2 23.0 %shard_map.298 = (bf16[512,768]{1,0:T(8,128)(2,1)}, bf16[512,768]{1,0:T(8,128)(2,1)}, bf16[512,384]{1,0:T(8,128)(2,1)}, bf16[512,384]{1,0:T(8,128)(2,1)}, bf16[5...) custom-call(s32[6]{0:T(128)} %concatenate.32.info_ref, s32[4]{0:T(128)} %pad_add_fusion.1.place_ref, ...), custom_call_target="tpu_custom_call" | custom-call | flops 13340000256 | tf_op jit(solution)/shard_map/pallas_call | solution.py:988
  203.6 5.9 %all-to-all-start.2 = ((bf16[8,64,768]{2,1,0:T(8,128)(2,1)}), bf16[8,64,768]{2,1,0:T(8,128)(2,1)S(1)}, u32[]{:S(2)}, u32[]{:S(2)}) async-start(bf16[8,64,768]{2,1,0:T(8,128)(2,1)} %bitcast.128), calls=%async_computation.2 | async-start | bytes 1572864 | tf_op jit(solution)/shard_map/all_to_all | solution.py:352
  218.6 16.1 %shard_map.299 = (f32[512,768]{1,0:T(8,128)}, bf16[512,768]{1,0:T(8,128)(2,1)}, f32[512,768]{1,0:T(8,128)}, bf16[512,768]{1,0:T(8,128)(2,1)}, bf16[4,96,1152]{2,...) custom-call(s32[6]{0:T(128)} %concatenate.32.info_ref, f32[1]{0:T(128)} %bitcast.39.tie_ref, ...), custom_call_target="tpu_custom_call" | custom-call | flops 9280000000 | tf_op jit(solution)/shard_map/pallas_call | solution.py:735
  236.3 4.8 %all-to-all-start.3 = ((bf16[4,96,1536]{2,1,0:T(8,128)(2,1)}), bf16[4,96,1536]{2,1,0:T(8,128)(2,1)S(1)}, u32[]{:S(2)}, u32[]{:S(2)}) async-start(bf16[4,96,1536]{2,1,0:T(8,128)(2,1)} %pad_maximum_fusion), calls=%async_computation.3 | async-start | bytes 2359296 | tf_op jit(solution)/shard_map/all_to_all | solution.py:1391
  246.7 9.4 %shard_map.301 = (bf16[8,48,1920]{2,1,0:T(8,128)(2,1)}, bf16[8,48,1920]{2,1,0:T(8,128)(2,1)}) custom-call(s32[4]{0:T(128)} %pad_add_fusion.1.place_ref, bf16[512,2304]{1,0:T(8,128)(2,1)} %get-tuple-element.153.acts_ref, bf16[512,2304]{1,0:T(8,128)(2,1)} %collective-permute-done.31.got_ref, bf16[512,1920]{1,0:T(8,128)(2,1)} %get-tuple-element.191.mine_ref, ...), custom_call_target="tpu_custom_call" | custom-call | flops 5219999744 | tf_op jit(solution)/shard_map/pallas_call | solution.py:1105
  256.1 8.1 %collective-permute-done.44 = bf16[4,96,1152]{2,1,0:T(8,128)(2,1)} collective-permute-done((bf16[4,96,1152]{2,1,0:T(8,128)(2,1)}, bf16[4,96,1152]{2,1,0:T(8,128)(2,1)}, u32[]{:S(2)}, u32[]{:S(2)}) %collective-permute-start.44) | collective-permute-done | bytes 884768 | tf_op jit(solution)/shard_map/ppermute | solution.py:319
  264.1 6.1 %all-to-all-done.3 = bf16[4,96,1536]{2,1,0:T(8,128)(2,1)S(1)} async-done(((bf16[4,96,1536]{2,1,0:T(8,128)(2,1)}), bf16[4,96,1536]{2,1,0:T(8,128)(2,1)S(1)}, u32[]{:S(2)}, u32[]{:S(2)}) %all-to-all-start.3) | async-done | bytes 1179680 | tf_op jit(solution)/shard_map/all_to_all | solution.py:1391
  280.4 5.5 %shard_map.302 = bf16[8,80,768]{2,1,0:T(8,128)(2,1)} custom-call(s32[6]{0:T(128)} %concatenate.32.info_ref, f32[512,768]{1,0:T(8,128)} %get-tuple-element.206.near_ref, bf16[512,768]{1,0:T(8,128)(2,1)} %collective-permute-done.50.near_got_ref, bf16[512,768]{1,0:T(8,128)(2,1)} %collective-permute-done.51.far_got_ref, ...), custom_call_target="tpu_custom_call" | custom-call | flops 2900000000 | tf_op jit(solution)/shard_map/pallas_call | solution.py:1105
  286.0 9.2 %collective-permute-done.53 = bf16[96,1152]{1,0:T(8,128)(2,1)S(1)} collective-permute-done((bf16[96,1152]{1,0:T(8,128)(2,1)S(1)}, bf16[96,1152]{1,0:T(8,128)(2,1)S(1)}, u32[]{:S(2)}, u32[]{:S(2)}) %collective-permute-start.53) | collective-permute-done | bytes 221216 | tf_op jit(solution)/shard_map/ppermute | solution.py:1207
  299.0 6.0 %collective-permute-done.45 = bf16[8,48,1920]{2,1,0:T(8,128)(2,1)} collective-permute-done((bf16[8,48,1920]{2,1,0:T(8,128)(2,1)}, bf16[8,48,1920]{2,1,0:T(8,128)(2,1)}, u32[]{:S(2)}, u32[]{:S(2)}) %collective-permute-start.45) | collective-permute-done | bytes 1474592 | tf_op jit(solution)/shard_map/ppermute | solution.py:319
  313.0 7.3 %collective-permute-done.55 = bf16[96,1152]{1,0:T(8,128)(2,1)S(1)} collective-permute-done((bf16[96,1152]{1,0:T(8,128)(2,1)S(1)}, bf16[96,1152]{1,0:T(8,128)(2,1)S(1)}, u32[]{:S(2)}, u32[]{:S(2)}) %collective-permute-start.55) | collective-permute-done | bytes 221216 | tf_op jit(solution)/shard_map/ppermute | solution.py:319
  339.9 8.2 %collective-permute-done.48.refs_1_ = bf16[48,1920]{1,0:T(8,128)(2,1)S(1)} collective-permute-done((bf16[48,1920]{1,0:T(8,128)(2,1)S(1)}, bf16[48,1920]{1,0:T(8,128)(2,1)S(1)}, u32[]{:S(2)}, u32[]{:S(2)}) %collective-permute-start.48) | collective-permute-done | bytes 184352 | tf_op jit(solution)/shard_map/ppermute | solution.py:1207
  358.2 6.2 %all-to-all-done.5.squares_ref = f32[32,8,128]{2,1,0:T(8,128)S(1)} async-done(((f32[32,8,128]{2,1,0:T(8,128)}), f32[32,8,128]{2,1,0:T(8,128)S(1)}, u32[]{:S(2)}, u32[]{:S(2)}) %all-to-all-start.5) | async-done | bytes 131104 | tf_op jit(solution)/shard_map/all_to_all | solution.py:1434
  366.7 7.8 %shard_map.305 = (f32[96,3072]{1,0:T(8,128)}, f32[96,3072]{1,0:T(8,128)}, f32[96,3072]{1,0:T(8,128)}, bf16[96,3072]{1,0:T(8,128)(2,1)}, f32[96,3072]{1,0:T(8,128...) custom-call(s32[4]{0:T(128)} %pad_add_fusion.1.place_ref, f32[32,8,128]{2,1,0:T(8,128)} %copy-done.3, ...), custom_call_target="tpu_custom_call" | custom-call | tf_op jit(solution)/shard_map/pallas_call | solution.py:1093
  377.7 5.6 %shard_map.304 = (f32[8,96,768]{2,1,0:T(8,128)}, f32[8,96,768]{2,1,0:T(8,128)}, f32[8,96,768]{2,1,0:T(8,128)}, bf16[8,96,768]{2,1,0:T(8,128)(2,1)}) custom-call(s32[4]{0:T(128)S(1)} %copy-done.5, f32[32,8,128]{2,1,0:T(8,128)S(1)} %copy-done.4, bf16[96,1152]{1,0:T(8,128)(2,1)S(1)} %get-tuple-element.236.row_ref, ...), custom_call_target="tpu_custom_call" | custom-call | tf_op jit(solution)/shard_map/pallas_call | solution.py:1053
  (298 shorter events, 155.5 us)
Async XLA Ops:
  64.7 29.8 %all-to-all-start = ((bf16[4,96,1536]{2,1,0:T(8,128)(2,1)}), bf16[4,96,1536]{2,1,0:T(8,128)(2,1)S(1)}, u32[]{:S(2)}, u32[]{:S(2)}) async-start(bf16[4,96,1536]{2,1,0:T(8,128)(2,1)} %broadcast_in_dim.39), calls=%async_computation | async-start | bytes 2359296 | tf_op jit(solution)/shard_map/all_to_all | solution.py:1292
  68.6 26.3 %collective-permute-start.22 = (bf16[4,144,768]{2,1,0:T(8,128)(2,1)S(1)}, bf16[4,144,768]{2,1,0:T(8,128)(2,1)}, u32[]{:S(2)}, u32[]{:S(2)}) collective-permute-start(bf16[4,144,768]{2,1,0:T(8,128)(2,1)S(1)} %pad_maximum_fusion.1.refs_0_), channel_id=1, source_target_pairs={{0,1},{1,0},{2,3},{3,2},{4,5},{5,4},{6,7},{7,6},{8,9},{9,8},{10,11... | collective-permute-start | bytes 2654216 | tf_op jit(solution)/shard_map/ppermute | solution.py:319
  70.7 25.7 %collective-permute-start.19 = (bf16[4,144,768]{2,1,0:T(8,128)(2,1)}, bf16[4,144,768]{2,1,0:T(8,128)(2,1)}, u32[]{:S(2)}, u32[]{:S(2)}) collective-permute-start(bf16[4,144,768]{2,1,0:T(8,128)(2,1)} %collective-permute-done.10.refs_1_), channel_id=1, source_target_pairs={{0,1},{1,0},{2,3},{3,2},{4,5},{5,4},{6,7},{7,6},{8,9},{9,8},{10,11... | collective-permute-start | bytes 2654216 | tf_op jit(solution)/shard_map/ppermute | solution.py:319
  70.7 23.8 %collective-permute-start = (s32[2,2]{1,0:T(2,128)S(1)}, s32[2,2]{1,0:T(2,128)S(1)}, u32[]{:S(2)}, u32[]{:S(2)}) collective-permute-start(s32[2,2]{1,0:T(2,128)S(1)} %pad_add_fusion), channel_id=1, source_target_pairs={{0,1},{1,0},{2,3},{3,2},{4,5},{5,4},{6,7},{7,6},{8,9},{9,8},{10,11... | collective-permute-start | bytes 56 | tf_op jit(solution)/shard_map/ppermute | solution.py:319
  94.4 31.2 %collective-permute-start.24 = (bf16[4,96,1536]{2,1,0:T(8,128)(2,1)S(1)}, bf16[4,96,1536]{2,1,0:T(8,128)(2,1)}, u32[]{:S(2)}, u32[]{:S(2)}) collective-permute-start(bf16[4,96,1536]{2,1,0:T(8,128)(2,1)S(1)} %all-to-all-done.refs_0_), channel_id=1, source_target_pairs={{0,2},{2,0},{1,3},{3,1},{4,6},{6,4},{5,7},{7,5},{8,10},{10,8},{9,1... | collective-permute-start | bytes 3538952 | tf_op jit(solution)/shard_map/ppermute | solution.py:319
  95.0 30.7 %collective-permute-start.23 = (bf16[4,96,1536]{2,1,0:T(8,128)(2,1)S(1)}, bf16[4,96,1536]{2,1,0:T(8,128)(2,1)S(1)}, u32[]{:S(2)}, u32[]{:S(2)}) collective-permute-start(bf16[4,96,1536]{2,1,0:T(8,128)(2,1)S(1)} %all-to-all-done.refs_0_), channel_id=1, source_target_pairs={{0,4},{4,0},{1,5},{5,1},{2,6},{6,2},{3,7},{7,3},{8,12},{12,8},{9,1... | collective-permute-start | bytes 3538952 | tf_op jit(solution)/shard_map/ppermute | solution.py:319
  96.3 25.9 %collective-permute-start.25 = (bf16[4,5,48,384]{3,2,1,0:T(8,128)(2,1)}, bf16[4,5,48,384]{3,2,1,0:T(8,128)(2,1)}, u32[]{:S(2)}, u32[]{:S(2)}) collective-permute-start(bf16[4,5,48,384]{3,2,1,0:T(8,128)(2,1)} %pad_maximum_fusion.2.refs_0_), channel_id=1, source_target_pairs={{0,1},{1,0},{2,3},{3,2},{4,5},{5,4},{6,7},{7,6},{8,9},{9,8},{10,11... | collective-permute-start | bytes 2211848 | tf_op jit(solution)/shard_map/ppermute | solution.py:319
  100.4 21.8 %collective-permute-start.26 = (bf16[4,5,48,384]{3,2,1,0:T(8,128)(2,1)}, bf16[4,5,48,384]{3,2,1,0:T(8,128)(2,1)}, u32[]{:S(2)}, u32[]{:S(2)}) collective-permute-start(bf16[4,5,48,384]{3,2,1,0:T(8,128)(2,1)} %copy-done.23), channel_id=1, source_target_pairs={{0,1},{1,0},{2,3},{3,2},{4,5},{5,4},{6,7},{7,6},{8,9},{9,8},{10,11... | collective-permute-start | bytes 2211848 | tf_op jit(solution)/shard_map/ppermute | solution.py:319
  101.9 20.3 %collective-permute-start.27 = (bf16[4,5,48,384]{3,2,1,0:T(8,128)(2,1)}, bf16[4,5,48,384]{3,2,1,0:T(8,128)(2,1)}, u32[]{:S(2)}, u32[]{:S(2)}) collective-permute-start(bf16[4,5,48,384]{3,2,1,0:T(8,128)(2,1)} %copy-done.22), channel_id=1, source_target_pairs={{0,1},{1,0},{2,3},{3,2},{4,5},{5,4},{6,7},{7,6},{8,9},{9,8},{10,11... | collective-permute-start | bytes 2211848 | tf_op jit(solution)/shard_map/ppermute | solution.py:319
  103.7 26.4 %all-to-all-start.1 = ((bf16[4,2,64,768]{3,2,1,0:T(8,128)(2,1)}), bf16[4,2,64,768]{3,2,1,0:T(8,128)(2,1)S(1)}, u32[]{:S(2)}, u32[]{:S(2)}) async-start(bf16[4,2,64,768]{3,2,1,0:T(8,128)(2,1)} %maximum_select_fusion.2), calls=%async_computation.1 | async-start | bytes 1572864 | tf_op jit(solution)/shard_map/all_to_all | solution.py:1300
  174.5 28.4 %collective-permute-start.38 = (bf16[4,2,96,768]{3,2,1,0:T(8,128)(2,1)}, bf16[4,2,96,768]{3,2,1,0:T(8,128)(2,1)S(1)}, u32[]{:S(2)}, u32[]{:S(2)}) collective-permute-start(bf16[4,2,96,768]{3,2,1,0:T(8,128)(2,1)} %get-tuple-element.180), channel_id=1, source_target_pairs={{0,4},{4,0},{1,5},{5,1},{2,6},{6,2},{3,7},{7,3},{8,12},{12,8},{9,1... | collective-permute-start | bytes 3538952 | tf_op jit(solution)/shard_map/ppermute | solution.py:319
  175.5 28.2 %collective-permute-start.39 = (bf16[768,768]{1,0:T(8,128)(2,1)}, bf16[768,768]{1,0:T(8,128)(2,1)S(1)}, u32[]{:S(2)}, u32[]{:S(2)}) collective-permute-start(bf16[768,768]{1,0:T(8,128)(2,1)} %get-tuple-element.181), channel_id=1, source_target_pairs={{0,2},{2,0},{1,3},{3,1},{4,6},{6,4},{5,7},{7,5},{8,10},{10,8},{9,1... | collective-permute-start | bytes 3538952 | tf_op jit(solution)/shard_map/ppermute | solution.py:319
  203.6 31.2 %all-to-all-start.2 = ((bf16[8,64,768]{2,1,0:T(8,128)(2,1)}), bf16[8,64,768]{2,1,0:T(8,128)(2,1)S(1)}, u32[]{:S(2)}, u32[]{:S(2)}) async-start(bf16[8,64,768]{2,1,0:T(8,128)(2,1)} %bitcast.128), calls=%async_computation.2 | async-start | bytes 1572864 | tf_op jit(solution)/shard_map/all_to_all | solution.py:352
  209.6 37.1 %collective-permute-start.31 = (bf16[512,2304]{1,0:T(8,128)(2,1)}, bf16[512,2304]{1,0:T(8,128)(2,1)}, u32[]{:S(2)}, u32[]{:S(2)}) collective-permute-start(bf16[512,2304]{1,0:T(8,128)(2,1)} %get-tuple-element.153.acts_ref), channel_id=1, source_target_pairs={{0,1},{1,0},{2,3},{3,2},{4,5},{5,4},{6,7},{7,6},{8,9},{9,8},{10,11... | collective-permute-start | bytes 7077896 | tf_op jit(solution)/shard_map/ppermute | solution.py:319
  214.4 20.3 %collective-permute-start.40 = (bf16[4,96,768]{2,1,0:T(8,128)(2,1)}, bf16[4,96,768]{2,1,0:T(8,128)(2,1)S(1)}, u32[]{:S(2)}, u32[]{:S(2)}) collective-permute-start(bf16[4,96,768]{2,1,0:T(8,128)(2,1)} %get-tuple-element.187), channel_id=1, source_target_pairs={{0,4},{4,0},{1,5},{5,1},{2,6},{6,2},{3,7},{7,3},{8,12},{12,8},{9,1... | collective-permute-start | bytes 1769480 | tf_op jit(solution)/shard_map/ppermute | solution.py:319
  236.3 34.0 %all-to-all-start.3 = ((bf16[4,96,1536]{2,1,0:T(8,128)(2,1)}), bf16[4,96,1536]{2,1,0:T(8,128)(2,1)S(1)}, u32[]{:S(2)}, u32[]{:S(2)}) async-start(bf16[4,96,1536]{2,1,0:T(8,128)(2,1)} %pad_maximum_fusion), calls=%async_computation.3 | async-start | bytes 2359296 | tf_op jit(solution)/shard_map/all_to_all | solution.py:1391
  241.3 22.8 %collective-permute-start.44 = (bf16[4,96,1152]{2,1,0:T(8,128)(2,1)}, bf16[4,96,1152]{2,1,0:T(8,128)(2,1)}, u32[]{:S(2)}, u32[]{:S(2)}) collective-permute-start(bf16[4,96,1152]{2,1,0:T(8,128)(2,1)} %get-tuple-element.199), channel_id=1, source_target_pairs={{0,4},{4,0},{1,5},{5,1},{2,6},{6,2},{3,7},{7,3},{8,12},{12,8},{9,1... | collective-permute-start | bytes 2654216 | tf_op jit(solution)/shard_map/ppermute | solution.py:319
  241.9 33.0 %collective-permute-start.50 = (bf16[512,768]{1,0:T(8,128)(2,1)}, bf16[512,768]{1,0:T(8,128)(2,1)}, u32[]{:S(2)}, u32[]{:S(2)}) collective-permute-start(bf16[512,768]{1,0:T(8,128)(2,1)} %get-tuple-element.207), channel_id=1, source_target_pairs={{0,1},{1,0},{2,3},{3,2},{4,5},{5,4},{6,7},{7,6},{8,9},{9,8},{10,11... | collective-permute-start | bytes 2359304 | tf_op jit(solution)/shard_map/ppermute | solution.py:319
  246.1 34.3 %collective-permute-start.51 = (bf16[512,768]{1,0:T(8,128)(2,1)}, bf16[512,768]{1,0:T(8,128)(2,1)}, u32[]{:S(2)}, u32[]{:S(2)}) collective-permute-start(bf16[512,768]{1,0:T(8,128)(2,1)} %add_convert_fusion.2), channel_id=1, source_target_pairs={{0,4},{4,0},{1,5},{5,1},{2,6},{6,2},{3,7},{7,3},{8,12},{12,8},{9,1... | collective-permute-start | bytes 2359304 | tf_op jit(solution)/shard_map/ppermute | solution.py:319
  271.2 33.9 %collective-permute-start.45 = (bf16[8,48,1920]{2,1,0:T(8,128)(2,1)}, bf16[8,48,1920]{2,1,0:T(8,128)(2,1)}, u32[]{:S(2)}, u32[]{:S(2)}) collective-permute-start(bf16[8,48,1920]{2,1,0:T(8,128)(2,1)} %get-tuple-element.201), channel_id=1, source_target_pairs={{0,2},{2,0},{1,3},{3,1},{4,6},{6,4},{5,7},{7,5},{8,10},{10,8},{9,1... | collective-permute-start | bytes 4423688 | tf_op jit(solution)/shard_map/ppermute | solution.py:319
  295.3 27.1 %all-to-all-start.4 = ((bf16[8,80,768]{2,1,0:T(8,128)(2,1)}), bf16[8,80,768]{2,1,0:T(8,128)(2,1)S(1)}, u32[]{:S(2)}, u32[]{:S(2)}) async-start(bf16[8,80,768]{2,1,0:T(8,128)(2,1)} %shard_map.302), calls=%async_computation.4 | async-start | bytes 1966080 | tf_op jit(solution)/shard_map/all_to_all | solution.py:352
  307.8 20.6 %collective-permute-start.46 = (bf16[4,48,1920]{2,1,0:T(8,128)(2,1)}, bf16[4,48,1920]{2,1,0:T(8,128)(2,1)}, u32[]{:S(2)}, u32[]{:S(2)}) collective-permute-start(bf16[4,48,1920]{2,1,0:T(8,128)(2,1)} %dynamic-slice_bitcast_fusion), channel_id=1, source_target_pairs={{0,4},{4,0},{1,5},{5,1},{2,6},{6,2},{3,7},{7,3},{8,12},{12,8},{9,1... | collective-permute-start | bytes 2211848 | tf_op jit(solution)/shard_map/ppermute | solution.py:319
  308.3 44.5 %collective-permute-start.64 = (bf16[96,1536]{1,0:T(8,128)(2,1)}, bf16[96,1536]{1,0:T(8,128)(2,1)}, u32[]{:S(2)}, u32[]{:S(2)}) collective-permute-start(bf16[96,1536]{1,0:T(8,128)(2,1)} %reduce_sum.57.refs_0_), channel_id=1, source_target_pairs={{0,2},{2,0},{1,3},{3,1},{4,6},{6,4},{5,7},{7,5},{8,10},{10,8},{9,1... | collective-permute-start | bytes 884744 | tf_op jit(solution)/shard_map/ppermute | solution.py:319
  352.9 22.2 %collective-permute-start.61 = (bf16[96,1152]{1,0:T(8,128)(2,1)S(1)}, bf16[96,1152]{1,0:T(8,128)(2,1)S(1)}, u32[]{:S(2)}, u32[]{:S(2)}) collective-permute-start(bf16[96,1152]{1,0:T(8,128)(2,1)S(1)} %get-tuple-element.236.row_ref), channel_id=1, source_target_pairs={{0,1},{1,0},{2,3},{3,2},{4,5},{5,4},{6,7},{7,6},{8,9},{9,8},{10,11... | collective-permute-start | bytes 663560 | tf_op jit(solution)/shard_map/ppermute | solution.py:319
  (93 other events, 878.1 us)
